TPU v7x, 128 devices: a whole 4x4x4 slice. The times are simulated.
128 devices in a mesh: col: 32 (over y, x, core), row: 4 (over z).
Axes of the slice: x: 4, y: 4, z: 4, core: 2. Of those that a mesh axis runs over, the one named last changes fastest.
Arguments:
- base_rhs: float32 [256, 512, 128], P(('col', 'row')), may hold values from -6 to 6
- base_inverse: bfloat16 [256, 512, 512], P(('col', 'row')), may hold values from -0.5 to 1.2, as said below
- apex_righthand_vectors: float32 [5, 4, 512, 128], P(None, 'row'), may hold values from -6 to 6
- top_inverse: bfloat16 [5, 4, 512, 512], P(None, 'row'), may hold values from -0.5 to 1.2, as said below
- factor_blocks: bfloat16 [5, 768, 512, 512], P(None, ('col', 'row')), may hold values from -0.06187184 to 0.06187184
- block_source: int32 [5, 768], P(None, ('col', 'row')), may hold values from 0 to 23, as said below
- block_count: int32 [5, 128], P(None, ('col', 'row')), may hold values from 1 to 6, as said below
Outputs:
- base_solution: float32 [256, 512, 128], P(('col', 'row'))
- top_solution: float32 [5, 4, 512, 128], P(None, 'row')
Inputs may be any that keep to these rules, and one draw needn't show every extreme that they name: `base_inverse`: lower triangular; diagonal entries between 0.6 and 1.2. `top_inverse`: lower triangular; diagonal entries between 0.6 and 1.2. `block_source`: the first block_count entries of a list are strictly increasing. An entry below 8 names a base supernode of the device's process column; an entry q above names the top supernode of level u = (q - 8) // 4, lower than the list's level, and stands only on devices of process column u mod 32. The other entries are 0. `block_count`: every top level has a device with 6 live slots.
All inputs are finite; a program needn't handle non-finite values.
Results may differ from a plain program's by a relative error of at most 0.0075.
Values may be sent and summed in bfloat16 or wider, within the bound.
No kernel may reach another device: no remote copies, remote signals or barrier semaphores. Data moves between devices by JAX's collectives and lax.ppermute only.
A program may use at most 128 MiB of HBM per device.

v0:
```python
import jax
import jax.numpy as jnp
from jax import lax
from jax.sharding import PartitionSpec as P


def accumulate(factor_level, source_level, first_slot, end_slot, running_total, sources):

    def add_block(slot_index, summed):
        factor_block = lax.dynamic_index_in_dim(factor_level, slot_index, 0, keepdims=False)
        operand = lax.dynamic_index_in_dim(sources, source_level[slot_index], 0, keepdims=False)
        return summed + jnp.dot(factor_block, operand, preferred_element_type=jnp.float32)

    return lax.fori_loop(first_slot, end_slot, add_block, running_total)


def settle(partial_value, rhs_block, inverse_block):
    summed = lax.psum(partial_value, "col")
    correction = (rhs_block - summed).astype(jnp.bfloat16)
    return jnp.dot(inverse_block, correction, preferred_element_type=jnp.float32)


def on_device(
    base_rhs,
    base_inverse,
    apex_righthand_vectors,
    top_inverse,
    factor_blocks,
    block_source,
    block_count,
):
    row_devices = lax.axis_size("row")
    top_levels = apex_righthand_vectors.shape[0]
    base_solution = jnp.einsum(
        "sij,sjr->sir",
        base_inverse,
        base_rhs.astype(jnp.bfloat16),
        preferred_element_type=jnp.float32,
    )
    column_base = lax.all_gather(base_solution.astype(jnp.bfloat16), "row", axis=0, tiled=True)
    reference_aggregate = column_base.shape[0]
    sources = jnp.concatenate(
        [
            column_base,
            jnp.zeros(((top_levels - 1) * row_devices,) + column_base.shape[1:], jnp.bfloat16),
        ],
        axis=0,
    )
    zero_sums = jnp.zeros(base_rhs.shape[1:], jnp.float32)
    solutions = []
    for level_index in range(top_levels):
        live_count = block_count[level_index, 0]
        partial_value = accumulate(
            factor_blocks[level_index], block_source[level_index], 0, live_count, zero_sums, sources
        )
        top_solution = settle(
            partial_value, apex_righthand_vectors[level_index, 0], top_inverse[level_index, 0]
        )
        solutions.append(top_solution)
        if level_index + 1 < top_levels:
            gathered = lax.all_gather(
                top_solution.astype(jnp.bfloat16)[None], "row", axis=0, tiled=True
            )
            leading_row = reference_aggregate + level_index * row_devices
            sources = lax.dynamic_update_slice_in_dim(sources, gathered, leading_row, 0)
    return (base_solution, jnp.stack(solutions)[:, None])


def solution(mesh):
    placed = (
        P(("col", "row"), None, None),
        P(("col", "row"), None, None),
        P(None, "row", None, None),
        P(None, "row", None, None),
        P(None, ("col", "row"), None, None),
        P(None, ("col", "row")),
        P(None, ("col", "row")),
    )
    return jax.shard_map(
        on_device,
        mesh=mesh,
        in_specs=placed,
        out_specs=(P(("col", "row"), None, None), P(None, "row", None, None)),
        check_vma=False,
    )
```

profile of v0, /device:TPU:1, one launch (start us, length us, event | category | flops | bytes accessed | tf_op | source)
XLA Modules:
  0.0 756.6 jit_solution(6083641053875355539)
XLA Ops:
  8.4 2.4 fusion.53
  10.8 1.5 fusion.52
  13.2 11.6 %slice_bitcast_fusion = (bf16[6,512,512]{2,1,0:T(8,128)(2,1)}, bf16[6,512,512]{2,1,0:T(8,128)(2,1)}, bf16[6,512,512]{2,1,0:T(8,128)(2,1)}, bf16[6,512,512]{2,1,0:T(8,128)(2,1)}, bf16[6,512,512]{2,1,0:T(8,128)(2,1)}) fusion(bf16[5,6,512,512]{3,2,1,0:T(8,128)(2,1)} %param.21), kind=kLoop, calls=%fused_computation.30 | loop fusion | bytes 31457280 | tf_op jit(solution)/shard_map/squeeze | solution.py:54
  24.8 12.6 %all-gather.6.cloned.1.call-done = bf16[8,512,128]{2,1,0:T(8,128)(2,1)} async-done(((bf16[2,512,128]{2,1,0:T(8,128)(2,1)}), bf16[8,512,128]{2,1,0:T(8,128)(2,1)}) %all-gather.6.cloned.1.call-update) | async-done | bytes 1048592 | tf_op jit(solution)/shard_map/all_gather | solution.py:40
  37.4 3.3 concatenate.3
  40.8 9.5 %while.50 = (s32[]{:T(128)}, f32[512,128]{1,0:T(8,128)S(1)}, s32[]{:T(128)}, bf16[6,512,512]{2,1,0:T(8,128)(2,1)}, s32[6]{0:T(128)S(1)}, /*index=5*/bf16[24,512,...) while((s32[]{:T(128)}, f32[512,128]{1,0:T(8,128)S(1)}, s32[]{:T(128)}, ...), condition=%wide.region_1.2_spmd, body=%wide.region_0.1_spmd.sunk | while | flops 67174408 | bytes 1179837 | solution.py:14
  43.9 1.4 convolution_add_fusion.10
  51.1 118.8 %all-reduce.7.cloned.1.call-done = f32[512,128]{1,0:T(8,128)} async-done(((f32[512,128]{1,0:T(8,128)}), f32[512,128]{1,0:T(8,128)}) %all-reduce.7.cloned.1.call-update) | async-done | bytes 262160 | tf_op jit(solution)/shard_map/psum | solution.py:18
  169.9 1.5 bitcast_dynamic-update-slice_fusion.3
  171.4 11.8 %all-gather = bf16[2048,128]{0,1:T(8,128)(2,1)S(1)} all-gather(bf16[512,128]{0,1:T(8,128)(2,1)S(1)} %bitcast.190), channel_id=2, replica_groups=mesh['col'=32,'row'=4] {'row'}, dimensions={0}, use_global_device_ids=true | all-gather | bytes 655360 | tf_op jit(solution)/shard_map/all_gather | solution.py:61
  184.4 5.2 while.51
  187.5 1.4 convolution_add_fusion.11
  190.3 123.7 %all-reduce.9.cloned.1.call-done = f32[512,128]{1,0:T(8,128)} async-done(((f32[512,128]{1,0:T(8,128)}), f32[512,128]{1,0:T(8,128)}) %all-reduce.9.cloned.1.call-update) | async-done | bytes 262160 | tf_op jit(solution)/shard_map/psum | solution.py:18
  314.0 1.5 bitcast_dynamic-update-slice_fusion.2
  315.5 11.8 %all-gather.1 = bf16[2048,128]{0,1:T(8,128)(2,1)S(1)} all-gather(bf16[512,128]{0,1:T(8,128)(2,1)S(1)} %bitcast.187), channel_id=3, replica_groups=mesh['col'=32,'row'=4] {'row'}, dimensions={0}, use_global_device_ids=true | all-gather | bytes 655360 | tf_op jit(solution)/shard_map/all_gather | solution.py:61
  328.5 9.5 %while.52 = (s32[]{:T(128)}, f32[512,128]{1,0:T(8,128)S(1)}, s32[]{:T(128)}, bf16[6,512,512]{2,1,0:T(8,128)(2,1)}, s32[6]{0:T(128)S(1)}, /*index=5*/bf16[24,512,...) while((s32[]{:T(128)}, f32[512,128]{1,0:T(8,128)S(1)}, s32[]{:T(128)}, ...), condition=%wide.region_7.8_spmd, body=%wide.region_6.7_spmd.sunk | while | flops 67174408 | bytes 1179837 | solution.py:14
  336.1 1.4 convolution_add_fusion.12
  338.8 119.4 %all-reduce.11.cloned.1.call-done = f32[512,128]{1,0:T(8,128)} async-done(((f32[512,128]{1,0:T(8,128)}), f32[512,128]{1,0:T(8,128)}) %all-reduce.11.cloned.1.call-update) | async-done | bytes 262160 | tf_op jit(solution)/shard_map/psum | solution.py:18
  458.2 1.5 bitcast_dynamic-update-slice_fusion.1
  459.8 11.8 %all-gather.2 = bf16[2048,128]{0,1:T(8,128)(2,1)S(1)} all-gather(bf16[512,128]{0,1:T(8,128)(2,1)S(1)} %bitcast.188), channel_id=4, replica_groups=mesh['col'=32,'row'=4] {'row'}, dimensions={0}, use_global_device_ids=true | all-gather | bytes 655360 | tf_op jit(solution)/shard_map/all_gather | solution.py:61
  472.7 5.3 while.53
  475.9 1.4 convolution_add_fusion.13
  478.8 124.3 %all-reduce.13.cloned.1.call-done = f32[512,128]{1,0:T(8,128)} async-done(((f32[512,128]{1,0:T(8,128)}), f32[512,128]{1,0:T(8,128)}) %all-reduce.13.cloned.1.call-update) | async-done | bytes 262160 | tf_op jit(solution)/shard_map/psum | solution.py:18
  603.1 1.5 bitcast_dynamic-update-slice_fusion
  604.7 11.8 %all-gather.3 = bf16[2048,128]{0,1:T(8,128)(2,1)S(1)} all-gather(bf16[512,128]{0,1:T(8,128)(2,1)S(1)} %bitcast.189), channel_id=5, replica_groups=mesh['col'=32,'row'=4] {'row'}, dimensions={0}, use_global_device_ids=true | all-gather | bytes 655360 | tf_op jit(solution)/shard_map/all_gather | solution.py:61
  617.6 28.0 %while.54 = (s32[]{:T(128)}, f32[512,128]{1,0:T(8,128)S(1)}, s32[]{:T(128)}, bf16[6,512,512]{2,1,0:T(8,128)(2,1)}, s32[6]{0:T(128)S(1)}, /*index=5*/bf16[24,512,...) while((s32[]{:T(128)}, f32[512,128]{1,0:T(8,128)S(1)}, s32[]{:T(128)}, ...), condition=%wide.region_13.14_spmd, body=%wide.region_12.13_spmd.sunk | while | flops 67174408 | bytes 1179837 | solution.py:14
  620.8 1.4 convolution_add_fusion.14
  634.5 1.4 convolution_add_fusion.14
  639.1 1.4 convolution_add_fusion.14
  646.4 100.4 %all-reduce.15.cloned.1.call-done = f32[512,128]{1,0:T(8,128)} async-done(((f32[512,128]{1,0:T(8,128)}), f32[512,128]{1,0:T(8,128)}) %all-reduce.15.cloned.1.call-update) | async-done | bytes 262160 | tf_op jit(solution)/shard_map/psum | solution.py:18
  746.8 1.5 fusion.25
  748.3 1.5 copy.18
  (55 shorter events, 24.3 us)
Async XLA Ops:
  7.2 1.2 copy-start
  7.2 30.2 %all-gather.6.cloned.1.call-start = ((), (), s32[]{:S(2)}) async-start(), calls=%async_computation | async-start | bytes 1310720 | tf_op jit(solution)/shard_map/all_gather | solution.py:40
  10.8 159.1 %all-reduce.7.cloned.1.call-start = ((), (), s32[]{:S(2)}) async-start(), calls=%async_computation.1 | async-start | bytes 524288 | tf_op jit(solution)/shard_map/psum | solution.py:18
  50.3 0.7 copy-start.2
  51.0 263.0 %all-reduce.9.cloned.1.call-start = ((), (), s32[]{:S(2)}) async-start(), calls=%async_computation.2 | async-start | bytes 524288 | tf_op jit(solution)/shard_map/psum | solution.py:18
  189.6 0.7 copy-start.3
  190.3 268.0 %all-reduce.11.cloned.1.call-start = ((), (), s32[]{:S(2)}) async-start(), calls=%async_computation.3 | async-start | bytes 524288 | tf_op jit(solution)/shard_map/psum | solution.py:18
  338.0 0.7 copy-start.4
  338.8 264.4 %all-reduce.13.cloned.1.call-start = ((), (), s32[]{:S(2)}) async-start(), calls=%async_computation.4 | async-start | bytes 524288 | tf_op jit(solution)/shard_map/psum | solution.py:18
  478.0 0.7 copy-start.5
  478.7 268.0 %all-reduce.15.cloned.1.call-start = ((), (), s32[]{:S(2)}) async-start(), calls=%async_computation.5 | async-start | bytes 524288 | tf_op jit(solution)/shard_map/psum | solution.py:18
  645.6 0.7 copy-start.1
Sparse Core Ops, SparseCore 0:
  10.9 26.4 all-gather.5
  51.1 118.6 all-reduce.6
  190.4 123.5 all-reduce.8
  338.9 119.3 all-reduce.10
  478.9 124.2 all-reduce.12
  646.5 100.2 all-reduce.14
where the time goes:
time: 758 us; the launch traced here: 757 us
  waiting for transfers between devices  599 us (79%)
  blocking collectives  47.3 us (6%)
  local copies, waits for them, and re-layouts  35 us (5%)
  loops' own time  34 us (4%)
  matrix products  26.4 us (3%)
  between operations  14.3 us (2%)
    psum x5, waiting for transfers between devices, settle(): summed = lax.psum(partial_value, 'col')  587 us
    all_gather x4, blocking collectives, on_device(): lax.all_gather(top_solution.astype(jnp.bfloat16)[None], 'row', axis=0, ti...  47.3 us
    another operation x5, loops' own time, accumulate(): return lax.fori_loop(first_slot, end_slot, add_block, running_total)  34 us
    dot_general x12, matrix products, add_block(): jnp.dot(factor_block, operand, preferred_element_type=jnp.float32)  16.5 us
  transfers between devices with their start and end apart: 6, of which 6 were waited for; matrix products, arithmetic and copies ran while one was open for 2% of the time, Pallas kernels for 0%

commit v1 on v0

v1 whole, which is shorter than its diff:
```python
import functools

import jax
import jax.numpy as jnp
from jax import lax
from jax.experimental import pallas as pl
from jax.experimental.pallas import tpu as pltpu
from jax.sharding import PartitionSpec as P

BF16, F32 = jnp.bfloat16, jnp.float32
AXES = ("col", "row")
NX = NY = NZ = 4
BOTH = (0, 1)
ANY = pl.BlockSpec(memory_space=pl.ANY)
SMEM = pl.BlockSpec(memory_space=pltpu.SMEM)
VMEM = pl.BlockSpec(memory_space=pltpu.VMEM)


def column(x, y, core):
    return (y * NX + x) * 2 + core


def place(x, y, core, z):
    return column(x, y, core) * NZ + z


def dot(a, b):
    return jnp.dot(a, b, preferred_element_type=F32)


def params():
    return pltpu.CompilerParams(vmem_limit_bytes=48 * 1024 * 1024)


def live(source_ref, count_ref, level, slot, low, high):
    source = source_ref[level, slot]
    return (slot < count_ref[level, 0]) & (source >= low) & (source < high)


def block_copy(factor_ref, held, sems, level, slot, index):
    return pltpu.make_async_copy(factor_ref.at[level, slot], held.at[index], sems.at[index])


def products(levels, slots, low, high, row, source_ref, count_ref, factor_ref, piece_refs, per_row,
             held, operands, total, sems, piece_sems):
    for i, level in enumerate(levels):
        for slot in range(slots):
            @pl.when(live(source_ref, count_ref, level, slot, low, high))
            def _():
                block_copy(factor_ref, held, sems, level, slot, i * slots + slot).start()
    piece_copies = []
    for k, piece in enumerate(piece_refs):
        owner = lax.rem(row + NZ - k, NZ)
        copy = pltpu.make_async_copy(piece, operands.at[owner], piece_sems.at[k])
        copy.start()
        piece_copies.append(copy)
    total[...] = jnp.zeros_like(total)
    for copy in piece_copies:
        copy.wait()
    for i, level in enumerate(levels):
        for slot in range(slots):
            @pl.when(live(source_ref, count_ref, level, slot, low, high))
            def _():
                block_copy(factor_ref, held, sems, level, slot, i * slots + slot).wait()
                q = source_ref[level, slot] - low
                if per_row == 1:
                    operand = operands[q]
                else:
                    operand = operands[q // per_row, q % per_row]
                total[i] += dot(held[i * slots + slot], operand)


def base_kernel(levels, slots, place_ref, source_ref, count_ref, factor_ref, *rest):
    pieces, (keep_ref, send_ref), scratch = rest[:NZ], rest[NZ : NZ + 2], rest[NZ + 2 :]
    row, core = place_ref[0], place_ref[1]
    held, operands, total, sems, piece_sems = scratch
    per_row = operands.shape[1]
    products(range(levels), slots, 0, NZ * per_row, row, source_ref, count_ref, factor_ref, pieces, per_row,
             held, operands, total, sems, piece_sems)
    for i, (on_first, on_second) in enumerate(((0, 0), (1, 2), (3, 4))):
        keep_ref[i] = total[jnp.where(core == 0, on_first, on_second)]
        send_ref[i] = total[jnp.where(core == 0, on_second, on_first)].astype(BF16)


def solve_kernel(level, slots, low, place_ref, source_ref, count_ref, factor_ref, ahead_ref, inverse_ref, *rest):
    pieces, (out_ref,), scratch = rest[:NZ], rest[NZ : NZ + 1], rest[NZ + 1 :]
    held, operands, total, sems, piece_sems = scratch
    products((level,), slots, low, low + NZ, place_ref[0], source_ref, count_ref, factor_ref, pieces, 1,
             held, operands, total, sems, piece_sems)
    correction = (ahead_ref[...] - total[0]).astype(BF16)
    out_ref[...] = dot(inverse_ref[...], correction).astype(BF16)


def later_kernel(levels, slots, low, place_ref, source_ref, count_ref, factor_ref, *rest):
    pieces, (out_ref,), scratch = rest[:NZ], rest[NZ : NZ + 1], rest[NZ + 1 :]
    held, operands, total, sems, piece_sems = scratch
    products(levels, slots, low, low + NZ, place_ref[0], source_ref, count_ref, factor_ref, pieces, 1,
             held, operands, total, sems, piece_sems)
    out_ref[...] = total[...].astype(BF16)


def scratch(levels, slots, block, per_row, dtype_rows):
    shape = (NZ,) + ((per_row,) if per_row > 1 else ()) + dtype_rows
    return [
        pltpu.VMEM((levels * slots,) + block, BF16),
        pltpu.VMEM(shape, BF16),
        pltpu.VMEM((levels,) + dtype_rows, F32),
        pltpu.SemaphoreType.DMA((levels * slots,)),
        pltpu.SemaphoreType.DMA((NZ,)),
    ]


def send(value, pairs):
    return lax.ppermute(value, AXES, pairs)


def to_row_offset(sender, receiver, k):
    return [(sender * NZ + v, receiver * NZ + (v + k) % NZ) for v in range(NZ)]


def sum_to_root(value, root_x, cores):
    sent = value.astype(BF16)
    for dx in (1, 3, 2):
        value = value + send(sent, [
            (place((root_x + dx) % NX, y, core, z), place(root_x, y, core, z))
            for y in range(NY) for core in cores for z in range(NZ)
        ]).astype(F32)
    sent = value.astype(BF16)
    for y in (1, 3, 2):
        value = value + send(sent, [
            (place(root_x, y, core, z), place(root_x, 0, core, z)) for core in cores for z in range(NZ)
        ]).astype(F32)
    return value


def spread(value, x0, core, here):
    value = jnp.where(here == column(x0, 0, core), value, jnp.zeros_like(value))
    first = value
    for dx in (1, 3, 2):
        value = value + send(first, [(place(x0, 0, core, z), place((x0 + dx) % NX, 0, core, z)) for z in range(NZ)])
    first = value
    for y in (1, 3, 2):
        value = value + send(first, [
            (place(x, 0, core, z), place(x, y, core, z)) for x in range(NX) for z in range(NZ)
        ])
    return value + send(value, [
        (place(x, y, core, z), place(x, y, 1 - core, z)) for x in range(NX) for y in range(NY) for z in range(NZ)
    ])


def on_device(base_rhs, base_inverse, apex, top_inverse, factor_blocks, block_source, block_count):
    levels, slots = block_source.shape[0], factor_blocks.shape[1]
    per_row, size, samples = base_rhs.shape
    block = factor_blocks.shape[2:]
    here, row = lax.axis_index("col"), lax.axis_index("row")
    core = here % 2
    places = jnp.stack([row, core]).astype(jnp.int32)

    base_solution = jnp.einsum("sij,sjr->sir", base_inverse, base_rhs.astype(BF16), preferred_element_type=F32)
    rounded = base_solution.astype(BF16)
    pieces = [rounded] + [
        lax.ppermute(rounded, "row", [(z, (z + k) % NZ) for z in range(NZ)]) for k in (1, 2, 3)
    ]
    keep, give = pl.pallas_call(
        functools.partial(base_kernel, levels, slots),
        out_shape=(
            jax.ShapeDtypeStruct((3, size, samples), F32),
            jax.ShapeDtypeStruct((3, size, samples), BF16),
        ),
        in_specs=[SMEM, SMEM, SMEM, ANY] + [ANY] * NZ,
        out_specs=(VMEM, VMEM),
        scratch_shapes=scratch(levels, slots, block, per_row, (size, samples)),
        compiler_params=params(),
        name="base_products",
    )(places, block_source, block_count, factor_blocks, *pieces)
    got = lax.ppermute(give, "col", [(c, c ^ 1) for c in range(NX * NY * 2)])
    pair = keep + got.astype(F32)
    sums = [sum_to_root(pair[0], 0, (0,)), sum_to_root(pair[1], 0, BOTH), sum_to_root(pair[2], 1, BOTH)]
    sum_of = [sums[0], sums[1], sums[1], sums[2], sums[2]]
    ahead = [apex[t, 0] - sum_of[t] for t in range(levels)]

    first = dot(top_inverse[0, 0], ahead[0].astype(BF16)).astype(BF16)
    solved = [first]
    for u in range(levels - 1):
        sender = max(u - 1, 0)
        pieces = [
            solved[u] if sender == u and k == 0 else send(solved[u], to_row_offset(sender, u, k)) for k in range(NZ)
        ]
        common = (places, block_source, block_count, factor_blocks)
        low = per_row * NZ + u * NZ
        solved.append(
            pl.pallas_call(
                functools.partial(solve_kernel, u + 1, slots, low),
                out_shape=jax.ShapeDtypeStruct((size, samples), BF16),
                in_specs=[SMEM, SMEM, SMEM, ANY, VMEM, VMEM] + [ANY] * NZ,
                out_specs=VMEM,
                scratch_shapes=scratch(1, slots, block, 1, (size, samples)),
                compiler_params=params(),
                name=f"solve_{u + 1}",
            )(*common, ahead[u + 1], top_inverse[u + 1, 0], *pieces)
        )
        later = tuple(range(u + 2, levels))
        if later:
            made = pl.pallas_call(
                functools.partial(later_kernel, later, slots, low),
                out_shape=jax.ShapeDtypeStruct((len(later), size, samples), BF16),
                in_specs=[SMEM, SMEM, SMEM, ANY] + [ANY] * NZ,
                out_specs=VMEM,
                scratch_shapes=scratch(len(later), slots, block, 1, (size, samples)),
                compiler_params=params(),
                name=f"later_{u}",
            )(*common, *pieces)
            for i, t in enumerate(later):
                arrived = send(made[i], to_row_offset(u, t - 1, 0))
                ahead[t] = ahead[t] - arrived.astype(F32)
    out = [spread(jnp.stack(solved[:2]), 0, 0, here)]
    out += [spread(solved[t][None], (t - 1) // 2, (t - 1) % 2, here) for t in range(2, levels)]
    return base_solution, jnp.concatenate(out).astype(F32)[:, None]


def solution(mesh):
    placed = (
        P(AXES, None, None),
        P(AXES, None, None),
        P(None, "row", None, None),
        P(None, "row", None, None),
        P(None, AXES, None, None),
        P(None, AXES),
        P(None, AXES),
    )
    return jax.shard_map(
        on_device,
        mesh=mesh,
        in_specs=placed,
        out_specs=(P(AXES, None, None), P(None, "row", None, None)),
        check_vma=False,
    )
```

time: 758 us -> 370 us (0.49)
  waiting for transfers between devices: 599 us -> 19.2 us
  starting transfers between devices: 0.24 us -> 316 us
  blocking collectives: 47.3 us -> 0 us
  loops' own time: 34 us -> 0 us
  local copies, waits for them, and re-layouts: 35 us -> 4.77 us
  matrix products: 26.4 us -> 2.67 us
  Pallas kernels: 0 us -> 20.6 us
  between operations: 14.3 us -> 1.83 us
    psum x5 -> x0, waiting for transfers between devices: 587 us -> none  [settle(): summed = lax.psum(partial_value, 'col')]
    ppermute x0 -> x71, starting transfers between devices: none -> 316 us  [the longest x67 275 us: send(): return lax.ppermute(value, AXES, pairs)]
    all_gather x4 -> x0, blocking collectives: 47.3 us -> none  [on_device(): lax.all_gather(top_solution.astype(jnp.bfloat16)[None], 'row', axis=0, ti...]
    another operation x5 -> x0, loops' own time: 34 us -> none  [accumulate(): return lax.fori_loop(first_slot, end_slot, add_block, running_total)]
    dot_general x18 -> x2, matrix products: 26.4 us -> 2.67 us  [the longest x1 2.27 us: on_device(): jnp.einsum('sij,sjr->sir', base_inverse, base_rhs.astype(BF16), preferred...]
    pallas_call x0 -> x8, Pallas kernels: none -> 20.6 us  [the longest x4 8.81 us: on_device(): pl.pallas_call(functools.partial(solve_kernel, u + 1, slots, low), out_sh...]
    ppermute x0 -> x71, waiting for transfers between devices: none -> 19.2 us  [the longest x67 9.32 us: send(): return lax.ppermute(value, AXES, pairs)]
    all_gather x1 -> x0, waiting for transfers between devices: 12.6 us -> none  [on_device(): lax.all_gather(base_solution.astype(jnp.bfloat16), 'row', axis=0, tiled=T...]
  transfers between devices with their start and end apart: 6 -> 71, of which waited for: 6 -> 7; matrix products, arithmetic and copies ran while one was open for 2% -> 1% of each run, Pallas kernels for 0% -> 4%
where the time goes in v1:
time: 370 us; the launch traced here: 369 us
  starting transfers between devices  316 us (85%)
  Pallas kernels  20.6 us (6%)
  waiting for transfers between devices  19.2 us (5%)
  local copies, waits for them, and re-layouts  4.77 us (1%)
  other arithmetic  4.02 us (1%)
    ppermute x67, starting transfers between devices, send(): return lax.ppermute(value, AXES, pairs)  275 us
    ppermute x3, starting transfers between devices, on_device(): lax.ppermute(rounded, 'row', [(z, (z + k) % NZ) for z in range(NZ)])  28.4 us
    ppermute x1, starting transfers between devices, on_device(): got = lax.ppermute(give, 'col', [(c, c ^ 1) for c in range(NX * NY * 2)])  12.5 us
    ppermute x67, waiting for transfers between devices, send(): return lax.ppermute(value, AXES, pairs)  9.32 us
    pallas_call x4, Pallas kernels, on_device(): pl.pallas_call(functools.partial(solve_kernel, u + 1, slots, low), out_sh...  8.81 us
    pallas_call x3, Pallas kernels, on_device(): pl.pallas_call(functools.partial(later_kernel, later, slots, low), out_sh...  7.88 us
    ppermute x3, waiting for transfers between devices, on_device(): lax.ppermute(rounded, 'row', [(z, (z + k) % NZ) for z in range(NZ)])  7.72 us
  transfers between devices with their start and end apart: 71, of which 7 were waited for; matrix products, arithmetic and copies ran while one was open for 1% of the time, Pallas kernels for 4%

profile of v1, /device:TPU:1, one launch (start us, length us, event | category | flops | bytes accessed | tf_op | source)
XLA Modules:
  0.0 369.4 jit_solution(14179279879676682578)
XLA Ops:
  4.1 10.6 %collective-permute-start = (bf16[2,512,128]{2,1,0:T(8,128)(2,1)S(1)}, bf16[2,512,128]{2,1,0:T(8,128)(2,1)S(1)}, u32[]{:S(2)}, u32[]{:S(2)}) collective-permute-start(bf16[2,512,128]{2,1,0:T(8,128)(2,1)S(1)} %get-tuple-element.31.rest_0_), channel_id=1, source_target_pairs={{0,1},{1,2},{2,3},{3,0},{4,5},{5,6},{6,7},{7,4},{8,9},{9,10},{10,1... | collective-permute-start | bytes 786440 | tf_op jit(solution)/shard_map/ppermute | solution.py:162
  14.8 8.9 %collective-permute-start.1 = (bf16[2,512,128]{2,1,0:T(8,128)(2,1)S(1)}, bf16[2,512,128]{2,1,0:T(8,128)(2,1)S(1)}, u32[]{:S(2)}, u32[]{:S(2)}) collective-permute-start(bf16[2,512,128]{2,1,0:T(8,128)(2,1)S(1)} %get-tuple-element.31.rest_0_), channel_id=1, source_target_pairs={{0,2},{1,3},{2,0},{3,1},{4,6},{5,7},{6,4},{7,5},{8,10},{9,11},{10,... | collective-permute-start | bytes 786440 | tf_op jit(solution)/shard_map/ppermute | solution.py:162
  23.7 8.9 %collective-permute-start.2 = (bf16[2,512,128]{2,1,0:T(8,128)(2,1)S(1)}, bf16[2,512,128]{2,1,0:T(8,128)(2,1)S(1)}, u32[]{:S(2)}, u32[]{:S(2)}) collective-permute-start(bf16[2,512,128]{2,1,0:T(8,128)(2,1)S(1)} %get-tuple-element.31.rest_0_), channel_id=1, source_target_pairs={{0,3},{1,0},{2,1},{3,2},{4,7},{5,4},{6,5},{7,6},{8,11},{9,8},{10,9... | collective-permute-start | bytes 786440 | tf_op jit(solution)/shard_map/ppermute | solution.py:162
  33.3 7.1 %collective-permute-done.2.rest_3_ = bf16[2,512,128]{2,1,0:T(8,128)(2,1)S(1)} collective-permute-done((bf16[2,512,128]{2,1,0:T(8,128)(2,1)S(1)}, bf16[2,512,128]{2,1,0:T(8,128)(2,1)S(1)}, u32[]{:S(2)}, u32[]{:S(2)}) %collective-permute-start.2) | collective-permute-done | bytes 262176 | tf_op jit(solution)/shard_map/ppermute | solution.py:162
  40.5 3.9 %base_products.1 = (f32[3,512,128]{2,1,0:T(8,128)S(1)}, bf16[3,512,128]{2,1,0:T(8,128)(2,1)S(1)}) custom-call(s32[2]{0:T(128)S(1)} %pad_add_fusion.place_ref, s32[5,6]{1,0:T(8,128)S(1)} %copy-done.4, s32[5,1]{1,0:T(8,128)S(1)} %copy.9.count_ref, bf16[5,6,512,512]{3,2,1,0:T(8,128)(2,1)} %factor_ref.15, bf16[2,512,128]{2,1,0:T(8,128)(2,1)S(1)} %get-tuple-element.31.rest_0_, ...), custom_call_target="tpu_custom_call" | custom-call | tf_op jit(solution)/shard_map/base_products/pallas_call | solution.py:164
  44.3 12.5 %collective-permute-start.3 = (bf16[3,512,128]{2,1,0:T(8,128)(2,1)S(1)}, bf16[3,512,128]{2,1,0:T(8,128)(2,1)S(1)}, u32[]{:S(2)}, u32[]{:S(2)}) collective-permute-start(bf16[3,512,128]{2,1,0:T(8,128)(2,1)S(1)} %get-tuple-element.5), channel_id=1, source_target_pairs={{0,4},{4,0},{8,12},{12,8},{16,20},{20,16},{24,28},{28,24},{32,36},... | collective-permute-start | bytes 1179656 | tf_op jit(solution)/shard_map/ppermute | solution.py:176
  59.1 8.9 %collective-permute-start.10 = (bf16[512,128]{1,0:T(8,128)(2,1)S(1)}, bf16[512,128]{1,0:T(8,128)(2,1)S(1)}, u32[]{:S(2)}, u32[]{:S(2)}) collective-permute-start(bf16[512,128]{1,0:T(8,128)(2,1)S(1)} %get-tuple-element.24), channel_id=1, source_target_pairs={{8,0},{9,1},{10,2},{11,3},{12,4},{13,5},{14,6},{15,7},{40,32},{41,... | collective-permute-start | bytes 393224 | tf_op jit(solution)/shard_map/ppermute | solution.py:114
  68.0 9.6 %collective-permute-start.11 = (bf16[512,128]{1,0:T(8,128)(2,1)S(1)}, bf16[512,128]{1,0:T(8,128)(2,1)S(1)}, u32[]{:S(2)}, u32[]{:S(2)}) collective-permute-start(bf16[512,128]{1,0:T(8,128)(2,1)S(1)} %get-tuple-element.24), channel_id=1, source_target_pairs={{24,0},{25,1},{26,2},{27,3},{28,4},{29,5},{30,6},{31,7},{56,32},{5... | collective-permute-start | bytes 393224 | tf_op jit(solution)/shard_map/ppermute | solution.py:114
  77.5 9.9 %collective-permute-start.12 = (bf16[512,128]{1,0:T(8,128)(2,1)S(1)}, bf16[512,128]{1,0:T(8,128)(2,1)S(1)}, u32[]{:S(2)}, u32[]{:S(2)}) collective-permute-start(bf16[512,128]{1,0:T(8,128)(2,1)S(1)} %get-tuple-element.24), channel_id=1, source_target_pairs={{16,0},{17,1},{18,2},{19,3},{20,4},{21,5},{22,6},{23,7},{48,32},{4... | collective-permute-start | bytes 393224 | tf_op jit(solution)/shard_map/ppermute | solution.py:114
  87.5 10.2 %collective-permute-start.38 = (bf16[512,128]{1,0:T(8,128)(2,1)S(1)}, bf16[512,128]{1,0:T(8,128)(2,1)S(1)}, u32[]{:S(2)}, u32[]{:S(2)}) collective-permute-start(bf16[512,128]{1,0:T(8,128)(2,1)S(1)} %get-tuple-element.23), channel_id=1, source_target_pairs={{16,8},{17,9},{18,10},{19,11},{20,12},{21,13},{22,14},{23,15},{48,... | collective-permute-start | bytes 393224 | tf_op jit(solution)/shard_map/ppermute | solution.py:114
  97.7 10.8 %collective-permute-start.39 = (bf16[512,128]{1,0:T(8,128)(2,1)S(1)}, bf16[512,128]{1,0:T(8,128)(2,1)S(1)}, u32[]{:S(2)}, u32[]{:S(2)}) collective-permute-start(bf16[512,128]{1,0:T(8,128)(2,1)S(1)} %get-tuple-element.23), channel_id=1, source_target_pairs={{0,8},{1,9},{2,10},{3,11},{4,12},{5,13},{6,14},{7,15},{32,40},{33,... | collective-permute-start | bytes 393224 | tf_op jit(solution)/shard_map/ppermute | solution.py:114
  108.5 8.9 %collective-permute-start.40 = (bf16[512,128]{1,0:T(8,128)(2,1)S(1)}, bf16[512,128]{1,0:T(8,128)(2,1)S(1)}, u32[]{:S(2)}, u32[]{:S(2)}) collective-permute-start(bf16[512,128]{1,0:T(8,128)(2,1)S(1)} %get-tuple-element.23), channel_id=1, source_target_pairs={{24,8},{25,9},{26,10},{27,11},{28,12},{29,13},{30,14},{31,15},{56,... | collective-permute-start | bytes 393224 | tf_op jit(solution)/shard_map/ppermute | solution.py:114
  117.4 10.0 %collective-permute-start.4 = (bf16[512,128]{1,0:T(8,128)(2,1)S(1)}, bf16[512,128]{1,0:T(8,128)(2,1)S(1)}, u32[]{:S(2)}, u32[]{:S(2)}) collective-permute-start(bf16[512,128]{1,0:T(8,128)(2,1)S(1)} %get-tuple-element.25), channel_id=1, source_target_pairs={{8,0},{9,1},{10,2},{11,3},{40,32},{41,33},{42,34},{43,35},{72,64},... | collective-permute-start | bytes 393224 | tf_op jit(solution)/shard_map/ppermute | solution.py:114
  127.5 9.5 %collective-permute-start.5 = (bf16[512,128]{1,0:T(8,128)(2,1)S(1)}, bf16[512,128]{1,0:T(8,128)(2,1)S(1)}, u32[]{:S(2)}, u32[]{:S(2)}) collective-permute-start(bf16[512,128]{1,0:T(8,128)(2,1)S(1)} %get-tuple-element.25), channel_id=1, source_target_pairs={{24,0},{25,1},{26,2},{27,3},{56,32},{57,33},{58,34},{59,35},{88,64... | collective-permute-start | bytes 393224 | tf_op jit(solution)/shard_map/ppermute | solution.py:114
  137.1 9.9 %collective-permute-start.6 = (bf16[512,128]{1,0:T(8,128)(2,1)S(1)}, bf16[512,128]{1,0:T(8,128)(2,1)S(1)}, u32[]{:S(2)}, u32[]{:S(2)}) collective-permute-start(bf16[512,128]{1,0:T(8,128)(2,1)S(1)} %get-tuple-element.25), channel_id=1, source_target_pairs={{16,0},{17,1},{18,2},{19,3},{48,32},{49,33},{50,34},{51,35},{80,64... | collective-permute-start | bytes 393224 | tf_op jit(solution)/shard_map/ppermute | solution.py:114
  148.6 13.8 %collective-permute-start.8 = (bf16[512,128]{1,0:T(8,128)(2,1)S(1)}, bf16[512,128]{1,0:T(8,128)(2,1)S(1)}, u32[]{:S(2)}, u32[]{:S(2)}) collective-permute-start(bf16[512,128]{1,0:T(8,128)(2,1)S(1)} %get-tuple-element.22), channel_id=1, source_target_pairs={{96,0},{97,1},{98,2},{99,3}} | collective-permute-start | bytes 393224 | tf_op jit(solution)/shard_map/ppermute | solution.py:114
  165.5 19.4 %collective-permute-start.13 = (bf16[512,128]{1,0:T(8,128)(2,1)S(1)}, bf16[512,128]{1,0:T(8,128)(2,1)S(1)}, u32[]{:S(2)}, u32[]{:S(2)}) collective-permute-start(bf16[512,128]{1,0:T(8,128)(2,1)S(1)} %get-tuple-element.20), channel_id=1, source_target_pairs={{32,0},{33,1},{34,2},{35,3},{36,4},{37,5},{38,6},{39,7}} | collective-permute-start | bytes 393224 | tf_op jit(solution)/shard_map/ppermute | solution.py:114
  184.9 9.6 %collective-permute-start.14 = (bf16[512,128]{1,0:T(8,128)(2,1)S(1)}, bf16[512,128]{1,0:T(8,128)(2,1)S(1)}, u32[]{:S(2)}, u32[]{:S(2)}) collective-permute-start(bf16[512,128]{1,0:T(8,128)(2,1)S(1)} %get-tuple-element.20), channel_id=1, source_target_pairs={{96,0},{97,1},{98,2},{99,3},{100,4},{101,5},{102,6},{103,7}} | collective-permute-start | bytes 393224 | tf_op jit(solution)/shard_map/ppermute | solution.py:114
  194.5 9.6 %collective-permute-start.15 = (bf16[512,128]{1,0:T(8,128)(2,1)S(1)}, bf16[512,128]{1,0:T(8,128)(2,1)S(1)}, u32[]{:S(2)}, u32[]{:S(2)}) collective-permute-start(bf16[512,128]{1,0:T(8,128)(2,1)S(1)} %get-tuple-element.20), channel_id=1, source_target_pairs={{64,0},{65,1},{66,2},{67,3},{68,4},{69,5},{70,6},{71,7}} | collective-permute-start | bytes 393224 | tf_op jit(solution)/shard_map/ppermute | solution.py:114
  219.1 7.9 %collective-permute-start.41 = (bf16[512,128]{1,0:T(8,128)(2,1)}, bf16[512,128]{1,0:T(8,128)(2,1)}, u32[]{:S(2)}, u32[]{:S(2)}) collective-permute-start(bf16[512,128]{1,0:T(8,128)(2,1)} %get-tuple-element.8), channel_id=1, source_target_pairs={{40,8},{41,9},{42,10},{43,11},{44,12},{45,13},{46,14},{47,15}} | collective-permute-start | bytes 393224 | tf_op jit(solution)/shard_map/ppermute | solution.py:114
  242.4 4.2 %later_1.1 = bf16[2,512,128]{2,1,0:T(8,128)(2,1)S(1)} custom-call(s32[2]{0:T(128)S(1)} %pad_add_fusion.place_ref, s32[5,6]{1,0:T(8,128)S(1)} %copy-done.4, s32[5,1]{1,0:T(8,128)S(1)} %copy.9.count_ref, bf16[5,6,512,512]{3,2,1,0:T(8,128)(2,1)} %factor_ref.15, bf16[512,128]{1,0:T(8,128)(2,1)S(1)} %collective-permute-done.27.rest_0_, ...), custom_call_target="tpu_custom_call" | custom-call | tf_op jit(solution)/shard_map/later_1/pallas_call | solution.py:204
  253.0 4.0 %collective-permute-start.42 = (bf16[512,128]{1,0:T(8,128)(2,1)S(1)}, bf16[512,128]{1,0:T(8,128)(2,1)S(1)}, u32[]{:S(2)}, u32[]{:S(2)}) collective-permute-start(bf16[512,128]{1,0:T(8,128)(2,1)S(1)} %copy-done.8), channel_id=1, source_target_pairs={{104,8},{105,9},{106,10},{107,11},{108,12},{109,13},{110,14},{111,... | collective-permute-start | bytes 393224 | tf_op jit(solution)/shard_map/ppermute | solution.py:114
  257.0 9.5 %collective-permute-start.43 = (bf16[512,128]{1,0:T(8,128)(2,1)S(1)}, bf16[512,128]{1,0:T(8,128)(2,1)S(1)}, u32[]{:S(2)}, u32[]{:S(2)}) collective-permute-start(bf16[512,128]{1,0:T(8,128)(2,1)S(1)} %copy-done.8), channel_id=1, source_target_pairs={{72,8},{73,9},{74,10},{75,11},{76,12},{77,13},{78,14},{79,15}} | collective-permute-start | bytes 393224 | tf_op jit(solution)/shard_map/ppermute | solution.py:114
  268.0 10.2 %collective-permute-start.45 = (bf16[512,128]{1,0:T(8,128)(2,1)S(1)}, bf16[512,128]{1,0:T(8,128)(2,1)S(1)}, u32[]{:S(2)}, u32[]{:S(2)}) collective-permute-start(bf16[512,128]{1,0:T(8,128)(2,1)S(1)} %get-tuple-element.29), channel_id=1, source_target_pairs={{4,8},{5,9},{6,10},{7,11}} | collective-permute-start | bytes 393224 | tf_op jit(solution)/shard_map/ppermute | solution.py:114
  284.2 4.6 %collective-permute-start.22 = (bf16[2,512,128]{2,1,0:T(8,128)(2,1)S(1)}, bf16[2,512,128]{2,1,0:T(8,128)(2,1)S(1)}, u32[]{:S(2)}, u32[]{:S(2)}) collective-permute-start(bf16[2,512,128]{2,1,0:T(8,128)(2,1)S(1)} %add_add_fusion.1), channel_id=1, source_target_pairs={{0,32},{1,33},{2,34},{3,35},{8,40},{9,41},{10,42},{11,43},{16,48},... | collective-permute-start | bytes 786440 | tf_op jit(solution)/shard_map/ppermute | solution.py:114
  296.8 13.7 %collective-permute-start.23 = (bf16[2,512,128]{2,1,0:T(8,128)(2,1)S(1)}, bf16[2,512,128]{2,1,0:T(8,128)(2,1)S(1)}, u32[]{:S(2)}, u32[]{:S(2)}) collective-permute-start(bf16[2,512,128]{2,1,0:T(8,128)(2,1)S(1)} %add_add_fusion.1), channel_id=1, source_target_pairs={{0,96},{1,97},{2,98},{3,99},{8,104},{9,105},{10,106},{11,107},{16,... | collective-permute-start | bytes 786440 | tf_op jit(solution)/shard_map/ppermute | solution.py:114
  311.2 6.7 %collective-permute-start.37 = (bf16[1,512,128]{2,1,0:T(8,128)(2,1)S(1)}, bf16[1,512,128]{2,1,0:T(8,128)(2,1)S(1)}, u32[]{:S(2)}, u32[]{:S(2)}) collective-permute-start(bf16[1,512,128]{2,1,0:T(8,128)(2,1)S(1)} %add_add_fusion.6), channel_id=1, source_target_pairs={{4,0},{5,1},{6,2},{7,3},{36,32},{37,33},{38,34},{39,35},{68,64},{6... | collective-permute-start | bytes 393224 | tf_op jit(solution)/shard_map/ppermute | solution.py:114
  317.9 6.7 %collective-permute-start.53 = (bf16[1,512,128]{2,1,0:T(8,128)(2,1)S(1)}, bf16[1,512,128]{2,1,0:T(8,128)(2,1)S(1)}, u32[]{:S(2)}, u32[]{:S(2)}) collective-permute-start(bf16[1,512,128]{2,1,0:T(8,128)(2,1)S(1)} %add_add_fusion.5), channel_id=1, source_target_pairs={{0,32},{1,33},{2,34},{3,35},{8,40},{9,41},{10,42},{11,43},{16,48},... | collective-permute-start | bytes 393224 | tf_op jit(solution)/shard_map/ppermute | solution.py:114
  326.5 9.6 %collective-permute-start.54 = (bf16[1,512,128]{2,1,0:T(8,128)(2,1)S(1)}, bf16[1,512,128]{2,1,0:T(8,128)(2,1)S(1)}, u32[]{:S(2)}, u32[]{:S(2)}) collective-permute-start(bf16[1,512,128]{2,1,0:T(8,128)(2,1)S(1)} %add_add_fusion.5), channel_id=1, source_target_pairs={{0,96},{1,97},{2,98},{3,99},{8,104},{9,105},{10,106},{11,107},{16,... | collective-permute-start | bytes 393224 | tf_op jit(solution)/shard_map/ppermute | solution.py:114
  339.5 4.7 %collective-permute-done.65 = bf16[1,512,128]{2,1,0:T(8,128)(2,1)S(1)} collective-permute-done((bf16[1,512,128]{2,1,0:T(8,128)(2,1)S(1)}, bf16[1,512,128]{2,1,0:T(8,128)(2,1)S(1)}, u32[]{:S(2)}, u32[]{:S(2)}) %collective-permute-start.65) | collective-permute-done | bytes 131104 | tf_op jit(solution)/shard_map/ppermute | solution.py:114
  344.2 6.0 %collective-permute-start.25 = (bf16[2,512,128]{2,1,0:T(8,128)(2,1)S(1)}, bf16[2,512,128]{2,1,0:T(8,128)(2,1)S(1)}, u32[]{:S(2)}, u32[]{:S(2)}) collective-permute-start(bf16[2,512,128]{2,1,0:T(8,128)(2,1)S(1)} %add_add_fusion), channel_id=1, source_target_pairs={{0,4},{1,5},{2,6},{3,7},{32,36},{33,37},{34,38},{35,39},{64,68},{6... | collective-permute-start | bytes 786440 | tf_op jit(solution)/shard_map/ppermute | solution.py:114
  356.9 6.7 %collective-permute-start.56 = (bf16[1,512,128]{2,1,0:T(8,128)(2,1)S(1)}, bf16[1,512,128]{2,1,0:T(8,128)(2,1)S(1)}, u32[]{:S(2)}, u32[]{:S(2)}) collective-permute-start(bf16[1,512,128]{2,1,0:T(8,128)(2,1)S(1)} %add_add_fusion.4), channel_id=1, source_target_pairs={{0,4},{1,5},{2,6},{3,7},{32,36},{33,37},{34,38},{35,39},{64,68},{6... | collective-permute-start | bytes 393224 | tf_op jit(solution)/shard_map/ppermute | solution.py:114
  (171 shorter events, 81.1 us)
Async XLA Ops:
  4.1 28.6 %collective-permute-start = (bf16[2,512,128]{2,1,0:T(8,128)(2,1)S(1)}, bf16[2,512,128]{2,1,0:T(8,128)(2,1)S(1)}, u32[]{:S(2)}, u32[]{:S(2)}) collective-permute-start(bf16[2,512,128]{2,1,0:T(8,128)(2,1)S(1)} %get-tuple-element.31.rest_0_), channel_id=1, source_target_pairs={{0,1},{1,2},{2,3},{3,0},{4,5},{5,6},{6,7},{7,4},{8,9},{9,10},{10,1... | collective-permute-start | bytes 786440 | tf_op jit(solution)/shard_map/ppermute | solution.py:162
  14.8 18.6 %collective-permute-start.1 = (bf16[2,512,128]{2,1,0:T(8,128)(2,1)S(1)}, bf16[2,512,128]{2,1,0:T(8,128)(2,1)S(1)}, u32[]{:S(2)}, u32[]{:S(2)}) collective-permute-start(bf16[2,512,128]{2,1,0:T(8,128)(2,1)S(1)} %get-tuple-element.31.rest_0_), channel_id=1, source_target_pairs={{0,2},{1,3},{2,0},{3,1},{4,6},{5,7},{6,4},{7,5},{8,10},{9,11},{10,... | collective-permute-start | bytes 786440 | tf_op jit(solution)/shard_map/ppermute | solution.py:162
  23.7 16.8 %collective-permute-start.2 = (bf16[2,512,128]{2,1,0:T(8,128)(2,1)S(1)}, bf16[2,512,128]{2,1,0:T(8,128)(2,1)S(1)}, u32[]{:S(2)}, u32[]{:S(2)}) collective-permute-start(bf16[2,512,128]{2,1,0:T(8,128)(2,1)S(1)} %get-tuple-element.31.rest_0_), channel_id=1, source_target_pairs={{0,3},{1,0},{2,1},{3,2},{4,7},{5,4},{6,5},{7,6},{8,11},{9,8},{10,9... | collective-permute-start | bytes 786440 | tf_op jit(solution)/shard_map/ppermute | solution.py:162
  59.1 49.4 %collective-permute-start.10 = (bf16[512,128]{1,0:T(8,128)(2,1)S(1)}, bf16[512,128]{1,0:T(8,128)(2,1)S(1)}, u32[]{:S(2)}, u32[]{:S(2)}) collective-permute-start(bf16[512,128]{1,0:T(8,128)(2,1)S(1)} %get-tuple-element.24), channel_id=1, source_target_pairs={{8,0},{9,1},{10,2},{11,3},{12,4},{13,5},{14,6},{15,7},{40,32},{41,... | collective-permute-start | bytes 393224 | tf_op jit(solution)/shard_map/ppermute | solution.py:114
  68.0 49.4 %collective-permute-start.11 = (bf16[512,128]{1,0:T(8,128)(2,1)S(1)}, bf16[512,128]{1,0:T(8,128)(2,1)S(1)}, u32[]{:S(2)}, u32[]{:S(2)}) collective-permute-start(bf16[512,128]{1,0:T(8,128)(2,1)S(1)} %get-tuple-element.24), channel_id=1, source_target_pairs={{24,0},{25,1},{26,2},{27,3},{28,4},{29,5},{30,6},{31,7},{56,32},{5... | collective-permute-start | bytes 393224 | tf_op jit(solution)/shard_map/ppermute | solution.py:114
  77.5 49.9 %collective-permute-start.12 = (bf16[512,128]{1,0:T(8,128)(2,1)S(1)}, bf16[512,128]{1,0:T(8,128)(2,1)S(1)}, u32[]{:S(2)}, u32[]{:S(2)}) collective-permute-start(bf16[512,128]{1,0:T(8,128)(2,1)S(1)} %get-tuple-element.24), channel_id=1, source_target_pairs={{16,0},{17,1},{18,2},{19,3},{20,4},{21,5},{22,6},{23,7},{48,32},{4... | collective-permute-start | bytes 393224 | tf_op jit(solution)/shard_map/ppermute | solution.py:114
  87.5 49.6 %collective-permute-start.38 = (bf16[512,128]{1,0:T(8,128)(2,1)S(1)}, bf16[512,128]{1,0:T(8,128)(2,1)S(1)}, u32[]{:S(2)}, u32[]{:S(2)}) collective-permute-start(bf16[512,128]{1,0:T(8,128)(2,1)S(1)} %get-tuple-element.23), channel_id=1, source_target_pairs={{16,8},{17,9},{18,10},{19,11},{20,12},{21,13},{22,14},{23,15},{48,... | collective-permute-start | bytes 393224 | tf_op jit(solution)/shard_map/ppermute | solution.py:114
  97.7 49.3 %collective-permute-start.39 = (bf16[512,128]{1,0:T(8,128)(2,1)S(1)}, bf16[512,128]{1,0:T(8,128)(2,1)S(1)}, u32[]{:S(2)}, u32[]{:S(2)}) collective-permute-start(bf16[512,128]{1,0:T(8,128)(2,1)S(1)} %get-tuple-element.23), channel_id=1, source_target_pairs={{0,8},{1,9},{2,10},{3,11},{4,12},{5,13},{6,14},{7,15},{32,40},{33,... | collective-permute-start | bytes 393224 | tf_op jit(solution)/shard_map/ppermute | solution.py:114
  108.5 38.5 %collective-permute-start.40 = (bf16[512,128]{1,0:T(8,128)(2,1)S(1)}, bf16[512,128]{1,0:T(8,128)(2,1)S(1)}, u32[]{:S(2)}, u32[]{:S(2)}) collective-permute-start(bf16[512,128]{1,0:T(8,128)(2,1)S(1)} %get-tuple-element.23), channel_id=1, source_target_pairs={{24,8},{25,9},{26,10},{27,11},{28,12},{29,13},{30,14},{31,15},{56,... | collective-permute-start | bytes 393224 | tf_op jit(solution)/shard_map/ppermute | solution.py:114
  117.4 29.5 %collective-permute-start.4 = (bf16[512,128]{1,0:T(8,128)(2,1)S(1)}, bf16[512,128]{1,0:T(8,128)(2,1)S(1)}, u32[]{:S(2)}, u32[]{:S(2)}) collective-permute-start(bf16[512,128]{1,0:T(8,128)(2,1)S(1)} %get-tuple-element.25), channel_id=1, source_target_pairs={{8,0},{9,1},{10,2},{11,3},{40,32},{41,33},{42,34},{43,35},{72,64},... | collective-permute-start | bytes 393224 | tf_op jit(solution)/shard_map/ppermute | solution.py:114
  127.5 19.5 %collective-permute-start.5 = (bf16[512,128]{1,0:T(8,128)(2,1)S(1)}, bf16[512,128]{1,0:T(8,128)(2,1)S(1)}, u32[]{:S(2)}, u32[]{:S(2)}) collective-permute-start(bf16[512,128]{1,0:T(8,128)(2,1)S(1)} %get-tuple-element.25), channel_id=1, source_target_pairs={{24,0},{25,1},{26,2},{27,3},{56,32},{57,33},{58,34},{59,35},{88,64... | collective-permute-start | bytes 393224 | tf_op jit(solution)/shard_map/ppermute | solution.py:114
  163.5 31.0 %collective-permute-start.16 = (bf16[512,128]{1,0:T(8,128)(2,1)S(1)}, bf16[512,128]{1,0:T(8,128)(2,1)S(1)}, u32[]{:S(2)}, u32[]{:S(2)}) collective-permute-start(bf16[512,128]{1,0:T(8,128)(2,1)S(1)} %bitcast.110), channel_id=1, source_target_pairs={{0,1},{1,2},{2,3},{3,0}} | collective-permute-start | bytes 393224 | tf_op jit(solution)/shard_map/ppermute | solution.py:114
  164.2 39.8 %collective-permute-start.17 = (bf16[512,128]{1,0:T(8,128)(2,1)S(1)}, bf16[512,128]{1,0:T(8,128)(2,1)S(1)}, u32[]{:S(2)}, u32[]{:S(2)}) collective-permute-start(bf16[512,128]{1,0:T(8,128)(2,1)S(1)} %bitcast.111), channel_id=1, source_target_pairs={{0,2},{1,3},{2,0},{3,1}} | collective-permute-start | bytes 393224 | tf_op jit(solution)/shard_map/ppermute | solution.py:114
  164.9 39.2 %collective-permute-start.18 = (bf16[512,128]{1,0:T(8,128)(2,1)S(1)}, bf16[512,128]{1,0:T(8,128)(2,1)S(1)}, u32[]{:S(2)}, u32[]{:S(2)}) collective-permute-start(bf16[512,128]{1,0:T(8,128)(2,1)S(1)} %bitcast.112), channel_id=1, source_target_pairs={{0,3},{1,0},{2,1},{3,2}} | collective-permute-start | bytes 393224 | tf_op jit(solution)/shard_map/ppermute | solution.py:114
  165.5 42.8 %collective-permute-start.13 = (bf16[512,128]{1,0:T(8,128)(2,1)S(1)}, bf16[512,128]{1,0:T(8,128)(2,1)S(1)}, u32[]{:S(2)}, u32[]{:S(2)}) collective-permute-start(bf16[512,128]{1,0:T(8,128)(2,1)S(1)} %get-tuple-element.20), channel_id=1, source_target_pairs={{32,0},{33,1},{34,2},{35,3},{36,4},{37,5},{38,6},{39,7}} | collective-permute-start | bytes 393224 | tf_op jit(solution)/shard_map/ppermute | solution.py:114
  184.9 23.4 %collective-permute-start.14 = (bf16[512,128]{1,0:T(8,128)(2,1)S(1)}, bf16[512,128]{1,0:T(8,128)(2,1)S(1)}, u32[]{:S(2)}, u32[]{:S(2)}) collective-permute-start(bf16[512,128]{1,0:T(8,128)(2,1)S(1)} %get-tuple-element.20), channel_id=1, source_target_pairs={{96,0},{97,1},{98,2},{99,3},{100,4},{101,5},{102,6},{103,7}} | collective-permute-start | bytes 393224 | tf_op jit(solution)/shard_map/ppermute | solution.py:114
  194.5 16.7 %collective-permute-start.15 = (bf16[512,128]{1,0:T(8,128)(2,1)S(1)}, bf16[512,128]{1,0:T(8,128)(2,1)S(1)}, u32[]{:S(2)}, u32[]{:S(2)}) collective-permute-start(bf16[512,128]{1,0:T(8,128)(2,1)S(1)} %get-tuple-element.20), channel_id=1, source_target_pairs={{64,0},{65,1},{66,2},{67,3},{68,4},{69,5},{70,6},{71,7}} | collective-permute-start | bytes 393224 | tf_op jit(solution)/shard_map/ppermute | solution.py:114
  219.1 21.0 %collective-permute-start.41 = (bf16[512,128]{1,0:T(8,128)(2,1)}, bf16[512,128]{1,0:T(8,128)(2,1)}, u32[]{:S(2)}, u32[]{:S(2)}) collective-permute-start(bf16[512,128]{1,0:T(8,128)(2,1)} %get-tuple-element.8), channel_id=1, source_target_pairs={{40,8},{41,9},{42,10},{43,11},{44,12},{45,13},{46,14},{47,15}} | collective-permute-start | bytes 393224 | tf_op jit(solution)/shard_map/ppermute | solution.py:114
  246.6 21.3 %collective-permute-start.19 = (bf16[2,512,128]{2,1,0:T(8,128)(2,1)S(1)}, bf16[2,512,128]{2,1,0:T(8,128)(2,1)S(1)}, u32[]{:S(2)}, u32[]{:S(2)}) collective-permute-start(bf16[2,512,128]{2,1,0:T(8,128)(2,1)S(1)} %maximum_select_fusion), channel_id=1, source_target_pairs={{0,8},{1,9},{2,10},{3,11}} | collective-permute-start | bytes 786440 | tf_op jit(solution)/shard_map/ppermute | solution.py:114
  247.3 30.8 %collective-permute-start.20 = (bf16[2,512,128]{2,1,0:T(8,128)(2,1)S(1)}, bf16[2,512,128]{2,1,0:T(8,128)(2,1)S(1)}, u32[]{:S(2)}, u32[]{:S(2)}) collective-permute-start(bf16[2,512,128]{2,1,0:T(8,128)(2,1)S(1)} %maximum_select_fusion), channel_id=1, source_target_pairs={{0,24},{1,25},{2,26},{3,27}} | collective-permute-start | bytes 786440 | tf_op jit(solution)/shard_map/ppermute | solution.py:114
  248.0 31.5 %collective-permute-start.21 = (bf16[2,512,128]{2,1,0:T(8,128)(2,1)S(1)}, bf16[2,512,128]{2,1,0:T(8,128)(2,1)S(1)}, u32[]{:S(2)}, u32[]{:S(2)}) collective-permute-start(bf16[2,512,128]{2,1,0:T(8,128)(2,1)S(1)} %maximum_select_fusion), channel_id=1, source_target_pairs={{0,16},{1,17},{2,18},{3,19}} | collective-permute-start | bytes 786440 | tf_op jit(solution)/shard_map/ppermute | solution.py:114
  284.2 51.9 %collective-permute-start.22 = (bf16[2,512,128]{2,1,0:T(8,128)(2,1)S(1)}, bf16[2,512,128]{2,1,0:T(8,128)(2,1)S(1)}, u32[]{:S(2)}, u32[]{:S(2)}) collective-permute-start(bf16[2,512,128]{2,1,0:T(8,128)(2,1)S(1)} %add_add_fusion.1), channel_id=1, source_target_pairs={{0,32},{1,33},{2,34},{3,35},{8,40},{9,41},{10,42},{11,43},{16,48},... | collective-permute-start | bytes 786440 | tf_op jit(solution)/shard_map/ppermute | solution.py:114
  294.7 15.8 %collective-permute-start.61 = (bf16[512,128]{1,0:T(8,128)(2,1)S(1)}, bf16[512,128]{1,0:T(8,128)(2,1)S(1)}, u32[]{:S(2)}, u32[]{:S(2)}) collective-permute-start(bf16[512,128]{1,0:T(8,128)(2,1)S(1)} %solve_3.1), channel_id=1, source_target_pairs={{8,13},{9,14},{10,15},{11,12}} | collective-permute-start | bytes 393224 | tf_op jit(solution)/shard_map/ppermute | solution.py:114
  295.4 15.8 %collective-permute-start.62 = (bf16[512,128]{1,0:T(8,128)(2,1)S(1)}, bf16[512,128]{1,0:T(8,128)(2,1)S(1)}, u32[]{:S(2)}, u32[]{:S(2)}) collective-permute-start(bf16[512,128]{1,0:T(8,128)(2,1)S(1)} %solve_3.1), channel_id=1, source_target_pairs={{8,14},{9,15},{10,12},{11,13}} | collective-permute-start | bytes 393224 | tf_op jit(solution)/shard_map/ppermute | solution.py:114
  296.1 21.8 %collective-permute-start.63 = (bf16[512,128]{1,0:T(8,128)(2,1)S(1)}, bf16[512,128]{1,0:T(8,128)(2,1)S(1)}, u32[]{:S(2)}, u32[]{:S(2)}) collective-permute-start(bf16[512,128]{1,0:T(8,128)(2,1)S(1)} %solve_3.1), channel_id=1, source_target_pairs={{8,15},{9,12},{10,13},{11,14}} | collective-permute-start | bytes 393224 | tf_op jit(solution)/shard_map/ppermute | solution.py:114
  296.8 40.0 %collective-permute-start.23 = (bf16[2,512,128]{2,1,0:T(8,128)(2,1)S(1)}, bf16[2,512,128]{2,1,0:T(8,128)(2,1)S(1)}, u32[]{:S(2)}, u32[]{:S(2)}) collective-permute-start(bf16[2,512,128]{2,1,0:T(8,128)(2,1)S(1)} %add_add_fusion.1), channel_id=1, source_target_pairs={{0,96},{1,97},{2,98},{3,99},{8,104},{9,105},{10,106},{11,107},{16,... | collective-permute-start | bytes 786440 | tf_op jit(solution)/shard_map/ppermute | solution.py:114
  310.5 27.6 %collective-permute-start.24 = (bf16[2,512,128]{2,1,0:T(8,128)(2,1)S(1)}, bf16[2,512,128]{2,1,0:T(8,128)(2,1)S(1)}, u32[]{:S(2)}, u32[]{:S(2)}) collective-permute-start(bf16[2,512,128]{2,1,0:T(8,128)(2,1)S(1)} %add_add_fusion.1), channel_id=1, source_target_pairs={{0,64},{1,65},{2,66},{3,67},{8,72},{9,73},{10,74},{11,75},{16,80},... | collective-permute-start | bytes 786440 | tf_op jit(solution)/shard_map/ppermute | solution.py:114
  311.2 15.3 %collective-permute-start.37 = (bf16[1,512,128]{2,1,0:T(8,128)(2,1)S(1)}, bf16[1,512,128]{2,1,0:T(8,128)(2,1)S(1)}, u32[]{:S(2)}, u32[]{:S(2)}) collective-permute-start(bf16[1,512,128]{2,1,0:T(8,128)(2,1)S(1)} %add_add_fusion.6), channel_id=1, source_target_pairs={{4,0},{5,1},{6,2},{7,3},{36,32},{37,33},{38,34},{39,35},{68,64},{6... | collective-permute-start | bytes 393224 | tf_op jit(solution)/shard_map/ppermute | solution.py:114
  317.9 35.7 %collective-permute-start.53 = (bf16[1,512,128]{2,1,0:T(8,128)(2,1)S(1)}, bf16[1,512,128]{2,1,0:T(8,128)(2,1)S(1)}, u32[]{:S(2)}, u32[]{:S(2)}) collective-permute-start(bf16[1,512,128]{2,1,0:T(8,128)(2,1)S(1)} %add_add_fusion.5), channel_id=1, source_target_pairs={{0,32},{1,33},{2,34},{3,35},{8,40},{9,41},{10,42},{11,43},{16,48},... | collective-permute-start | bytes 393224 | tf_op jit(solution)/shard_map/ppermute | solution.py:114
  326.5 29.0 %collective-permute-start.54 = (bf16[1,512,128]{2,1,0:T(8,128)(2,1)S(1)}, bf16[1,512,128]{2,1,0:T(8,128)(2,1)S(1)}, u32[]{:S(2)}, u32[]{:S(2)}) collective-permute-start(bf16[1,512,128]{2,1,0:T(8,128)(2,1)S(1)} %add_add_fusion.5), channel_id=1, source_target_pairs={{0,96},{1,97},{2,98},{3,99},{8,104},{9,105},{10,106},{11,107},{16,... | collective-permute-start | bytes 393224 | tf_op jit(solution)/shard_map/ppermute | solution.py:114
  338.9 18.0 %collective-permute-start.55 = (bf16[1,512,128]{2,1,0:T(8,128)(2,1)S(1)}, bf16[1,512,128]{2,1,0:T(8,128)(2,1)S(1)}, u32[]{:S(2)}, u32[]{:S(2)}) collective-permute-start(bf16[1,512,128]{2,1,0:T(8,128)(2,1)S(1)} %add_add_fusion.5), channel_id=1, source_target_pairs={{0,64},{1,65},{2,66},{3,67},{8,72},{9,73},{10,74},{11,75},{16,80},... | collective-permute-start | bytes 393224 | tf_op jit(solution)/shard_map/ppermute | solution.py:114
  344.2 23.0 %collective-permute-start.25 = (bf16[2,512,128]{2,1,0:T(8,128)(2,1)S(1)}, bf16[2,512,128]{2,1,0:T(8,128)(2,1)S(1)}, u32[]{:S(2)}, u32[]{:S(2)}) collective-permute-start(bf16[2,512,128]{2,1,0:T(8,128)(2,1)S(1)} %add_add_fusion), channel_id=1, source_target_pairs={{0,4},{1,5},{2,6},{3,7},{32,36},{33,37},{34,38},{35,39},{64,68},{6... | collective-permute-start | bytes 786440 | tf_op jit(solution)/shard_map/ppermute | solution.py:114
  (51 other events, 670.1 us)

commit v2 on v1

--- a/solution.py
+++ b/solution.py
@@ -11,6 +11,7 @@
 AXES = ("col", "row")
 NX = NY = NZ = 4
 BOTH = (0, 1)
+CHAIN = 4
 ANY = pl.BlockSpec(memory_space=pl.ANY)
 SMEM = pl.BlockSpec(memory_space=pltpu.SMEM)
 VMEM = pl.BlockSpec(memory_space=pltpu.VMEM)
@@ -77,9 +78,14 @@
     per_row = operands.shape[1]
     products(range(levels), slots, 0, NZ * per_row, row, source_ref, count_ref, factor_ref, pieces, per_row,
              held, operands, total, sems, piece_sems)
-    for i, (on_first, on_second) in enumerate(((0, 0), (1, 2), (3, 4))):
-        keep_ref[i] = total[jnp.where(core == 0, on_first, on_second)]
-        send_ref[i] = total[jnp.where(core == 0, on_second, on_first)].astype(BF16)
+    shares, some = keep_ref.shape[0], keep_ref.shape[1] // levels
+    mine = pl.multiple_of(core * shares * some, shares * some)
+    other = pl.multiple_of((1 - core) * shares * some, shares * some)
+    for share in range(shares):
+        for level in range(levels):
+            place_in = pl.ds(level * some, some)
+            keep_ref[share, place_in] = total[level, pl.ds(mine + share * some, some)]
+            send_ref[share, place_in] = total[level, pl.ds(other + share * some, some)].astype(BF16)
 
 
 def solve_kernel(level, slots, low, place_ref, source_ref, count_ref, factor_ref, ahead_ref, inverse_ref, *rest):
@@ -96,7 +102,7 @@
     held, operands, total, sems, piece_sems = scratch
     products(levels, slots, low, low + NZ, place_ref[0], source_ref, count_ref, factor_ref, pieces, 1,
              held, operands, total, sems, piece_sems)
-    out_ref[...] = total[...].astype(BF16)
+    out_ref[...] = total[...]
 
 
 def scratch(levels, slots, block, per_row, dtype_rows):
@@ -118,22 +124,17 @@
     return [(sender * NZ + v, receiver * NZ + (v + k) % NZ) for v in range(NZ)]
 
 
-def sum_to_root(value, root_x, cores):
-    sent = value.astype(BF16)
-    for dx in (1, 3, 2):
-        value = value + send(sent, [
-            (place((root_x + dx) % NX, y, core, z), place(root_x, y, core, z))
-            for y in range(NY) for core in cores for z in range(NZ)
-        ]).astype(F32)
-    sent = value.astype(BF16)
-    for y in (1, 3, 2):
-        value = value + send(sent, [
-            (place(root_x, y, core, z), place(root_x, 0, core, z)) for core in cores for z in range(NZ)
-        ]).astype(F32)
-    return value
-
-
-def spread(value, x0, core, here):
+def other_core(value):
+    return lax.ppermute(value, "col", [(c, c ^ 1) for c in range(NX * NY * 2)])
+
+
+def over_plane(value):
+    groups = [[column(x, y, core) for y in range(NY) for x in range(NX)] for core in BOTH]
+    return lax.all_to_all(value, "col", 0, 0, axis_index_groups=groups, tiled=True)
+
+
+def spread(value, here):
+    x0, core = (CHAIN - 1) // 2, (CHAIN - 1) % 2
     value = jnp.where(here == column(x0, 0, core), value, jnp.zeros_like(value))
     first = value
     for dx in (1, 3, 2):
@@ -143,18 +144,20 @@
         value = value + send(first, [
             (place(x, 0, core, z), place(x, y, core, z)) for x in range(NX) for z in range(NZ)
         ])
-    return value + send(value, [
-        (place(x, y, core, z), place(x, y, 1 - core, z)) for x in range(NX) for y in range(NY) for z in range(NZ)
-    ])
+    return value + other_core(value)
 
 
 def on_device(base_rhs, base_inverse, apex, top_inverse, factor_blocks, block_source, block_count):
     levels, slots = block_source.shape[0], factor_blocks.shape[1]
     per_row, size, samples = base_rhs.shape
+    shares = NX * NY
+    some = size // 2 // shares
     block = factor_blocks.shape[2:]
     here, row = lax.axis_index("col"), lax.axis_index("row")
     core = here % 2
     places = jnp.stack([row, core]).astype(jnp.int32)
+    common = (places, block_source, block_count, factor_blocks)
+    after = lax.optimization_barrier
 
     base_solution = jnp.einsum("sij,sjr->sir", base_inverse, base_rhs.astype(BF16), preferred_element_type=F32)
     rounded = base_solution.astype(BF16)
@@ -164,30 +167,37 @@
     keep, give = pl.pallas_call(
         functools.partial(base_kernel, levels, slots),
         out_shape=(
-            jax.ShapeDtypeStruct((3, size, samples), F32),
-            jax.ShapeDtypeStruct((3, size, samples), BF16),
+            jax.ShapeDtypeStruct((shares, levels * some, samples), F32),
+            jax.ShapeDtypeStruct((shares, levels * some, samples), BF16),
         ),
         in_specs=[SMEM, SMEM, SMEM, ANY] + [ANY] * NZ,
         out_specs=(VMEM, VMEM),
         scratch_shapes=scratch(levels, slots, block, per_row, (size, samples)),
         compiler_params=params(),
         name="base_products",
-    )(places, block_source, block_count, factor_blocks, *pieces)
-    got = lax.ppermute(give, "col", [(c, c ^ 1) for c in range(NX * NY * 2)])
-    pair = keep + got.astype(F32)
-    sums = [sum_to_root(pair[0], 0, (0,)), sum_to_root(pair[1], 0, BOTH), sum_to_root(pair[2], 1, BOTH)]
-    sum_of = [sums[0], sums[1], sums[1], sums[2], sums[2]]
-    ahead = [apex[t, 0] - sum_of[t] for t in range(levels)]
-
-    first = dot(top_inverse[0, 0], ahead[0].astype(BF16)).astype(BF16)
-    solved = [first]
+    )(*common, *pieces)
+    pair = (keep + other_core(give).astype(F32)).astype(BF16)
+    share = jnp.sum(over_plane(pair).astype(F32), axis=0).astype(BF16)
+    half = over_plane(jnp.broadcast_to(share[None], (shares,) + share.shape))
+    other = other_core(half)
+    sums = jnp.where(core == 0, jnp.stack([half, other]), jnp.stack([other, half]))
+    sums = sums.reshape(2, shares, levels, some, samples)
+
+    def sum_of(t):
+        return sums[:, :, t].reshape(size, samples).astype(F32)
+
+    first = dot(top_inverse[0, 0], (apex[0, 0] - sum_of(0)).astype(BF16)).astype(BF16)
+    first, sums = after((first, sums))
+    ahead = [apex[t, 0] - sum_of(t) for t in range(levels)]
+
+    solved, kept, moving = [first], [], []
     for u in range(levels - 1):
         sender = max(u - 1, 0)
         pieces = [
             solved[u] if sender == u and k == 0 else send(solved[u], to_row_offset(sender, u, k)) for k in range(NZ)
         ]
-        common = (places, block_source, block_count, factor_blocks)
         low = per_row * NZ + u * NZ
+        target = ahead[u + 1] - moving[0].astype(F32) if u else ahead[u + 1]
         solved.append(
             pl.pallas_call(
                 functools.partial(solve_kernel, u + 1, slots, low),
@@ -197,25 +207,28 @@
                 scratch_shapes=scratch(1, slots, block, 1, (size, samples)),
                 compiler_params=params(),
                 name=f"solve_{u + 1}",
-            )(*common, ahead[u + 1], top_inverse[u + 1, 0], *pieces)
+            )(*common, target, top_inverse[u + 1, 0], *pieces)
         )
+        kept.append(pieces[0])
         later = tuple(range(u + 2, levels))
         if later:
+            pieces, solved[-1] = after((pieces, solved[-1]))
             made = pl.pallas_call(
                 functools.partial(later_kernel, later, slots, low),
-                out_shape=jax.ShapeDtypeStruct((len(later), size, samples), BF16),
+                out_shape=jax.ShapeDtypeStruct((len(later), size, samples), F32),
                 in_specs=[SMEM, SMEM, SMEM, ANY] + [ANY] * NZ,
                 out_specs=VMEM,
                 scratch_shapes=scratch(len(later), slots, block, 1, (size, samples)),
                 compiler_params=params(),
                 name=f"later_{u}",
             )(*common, *pieces)
-            for i, t in enumerate(later):
-                arrived = send(made[i], to_row_offset(u, t - 1, 0))
-                ahead[t] = ahead[t] - arrived.astype(F32)
-    out = [spread(jnp.stack(solved[:2]), 0, 0, here)]
-    out += [spread(solved[t][None], (t - 1) // 2, (t - 1) % 2, here) for t in range(2, levels)]
-    return base_solution, jnp.concatenate(out).astype(F32)[:, None]
+            if u:
+                made = made + moving[1:].astype(F32)
+            moving = send(jnp.concatenate([made.astype(BF16), jnp.stack(kept)]), to_row_offset(u, u + 1, 0))
+            moving, kept = moving[: len(later)], [moving[len(later) + i] for i in range(u + 1)]
+    old = spread(jnp.stack(kept[:-1]), here)
+    out = jnp.concatenate([old, spread(jnp.stack([kept[-1], solved[-1]]), here)])
+    return base_solution, out.astype(F32)[:, None]
 
 
 def solution(mesh):

time: 370 us -> 171 us (0.46)
  the two profiles are of different devices: /device:TPU:1 before, /device:TPU:23 now
where the time goes in v2:
time: 171 us; the launch traced here: 170 us
  waiting for transfers between devices  82.5 us (48%)
  starting transfers between devices  33 us (19%)
  blocking collectives  22.4 us (13%)
  Pallas kernels  18.2 us (11%)
  local copies, waits for them, and re-layouts  4.88 us (3%)
  other arithmetic  4.09 us (2%)
  matrix products  3.61 us (2%)
    ppermute x30, waiting for transfers between devices, send(): return lax.ppermute(value, AXES, pairs)  69.2 us
    all_to_all x2, blocking collectives, over_plane(): lax.all_to_all(value, 'col', 0, 0, axis_index_groups=groups, tiled=True)  22.4 us
    ppermute x30, starting transfers between devices, send(): return lax.ppermute(value, AXES, pairs)  21.7 us
    ppermute x3, waiting for transfers between devices, on_device(): lax.ppermute(rounded, 'row', [(z, (z + k) % NZ) for z in range(NZ)])  10.4 us
    pallas_call x4, Pallas kernels, on_device(): pl.pallas_call(functools.partial(solve_kernel, u + 1, slots, low), out_sh...  7.45 us
    ppermute x3, starting transfers between devices, on_device(): lax.ppermute(rounded, 'row', [(z, (z + k) % NZ) for z in range(NZ)])  5.67 us
    ppermute x4, starting transfers between devices, other_core(): return lax.ppermute(value, 'col', [(c, c ^ 1) for c in range(NX * NY * 2)])  5.58 us
    pallas_call x3, Pallas kernels, on_device(): pl.pallas_call(functools.partial(later_kernel, later, slots, low), out_sh...  5.38 us
  transfers between devices with their start and end apart: 37, of which 6 were waited for; matrix products, arithmetic and copies ran while one was open for 2% of the time, Pallas kernels for 0%

profile of v2, /device:TPU:23, one launch (start us, length us, event | category | flops | bytes accessed | tf_op | source)
XLA Modules:
  0.0 170.1 jit_solution(5846171764270998678)
XLA Ops:
  0.7 1.2 copy-done
  1.9 2.3 %fusion.10 = (bf16[2,512,128]{2,1,0:T(8,128)(2,1)S(1)}, f32[2,512,128]{2,1,0:T(8,128)}) fusion(bf16[2,512,512]{2,1,0:T(8,128)(2,1)S(1)} %copy-done, f32[2,512,128]{2,1,0:T(8,128)} %param.7), kind=kOutput, calls=%fused_computation.42 | convolution fusion | flops 134479872 | bytes 2359296 | tf_op jit(solution)/shard_map/sij,sjr->sir/dot_general | solution.py:162
  4.1 1.6 collective-permute-start
  5.8 3.3 %collective-permute-start.1 = (bf16[2,512,128]{2,1,0:T(8,128)(2,1)S(1)}, bf16[2,512,128]{2,1,0:T(8,128)(2,1)S(1)}, u32[]{:S(2)}, u32[]{:S(2)}) collective-permute-start(bf16[2,512,128]{2,1,0:T(8,128)(2,1)S(1)} %get-tuple-element.52.rest_0_), channel_id=1, source_target_pairs={{0,2},{1,3},{2,0},{3,1},{4,6},{5,7},{6,4},{7,5},{8,10},{9,11},{10,... | collective-permute-start | bytes 786440 | tf_op jit(solution)/shard_map/ppermute | solution.py:165
  9.1 0.7 collective-permute-start.2
  10.0 3.9 %collective-permute-done.rest_1_ = bf16[2,512,128]{2,1,0:T(8,128)(2,1)S(1)} collective-permute-done((bf16[2,512,128]{2,1,0:T(8,128)(2,1)S(1)}, bf16[2,512,128]{2,1,0:T(8,128)(2,1)S(1)}, u32[]{:S(2)}, u32[]{:S(2)}) %collective-permute-start) | collective-permute-done | bytes 262176 | tf_op jit(solution)/shard_map/ppermute | solution.py:165
  13.9 6.5 %collective-permute-done.1.rest_2_ = bf16[2,512,128]{2,1,0:T(8,128)(2,1)S(1)} collective-permute-done((bf16[2,512,128]{2,1,0:T(8,128)(2,1)S(1)}, bf16[2,512,128]{2,1,0:T(8,128)(2,1)S(1)}, u32[]{:S(2)}, u32[]{:S(2)}) %collective-permute-start.1) | collective-permute-done | bytes 262176 | tf_op jit(solution)/shard_map/ppermute | solution.py:165
  20.4 5.4 %base_products.1 = (f32[16,80,128]{2,1,0:T(8,128)S(1)}, bf16[16,80,128]{2,1,0:T(8,128)(2,1)S(1)}) custom-call(s32[2]{0:T(128)S(1)} %pad_add_fusion.place_ref, s32[5,6]{1,0:T(8,128)S(1)} %copy-done.1, s32[5,1]{1,0:T(8,128)S(1)} %copy.26.count_ref, bf16[5,6,512,512]{3,2,1,0:T(8,128)(2,1)} %factor_ref.15, bf16[2,512,128]{2,1,0:T(8,128)(2,1)S(1)} %get-tuple-element.52.rest_0_, ...), custom_call_target="tpu_custom_call" | custom-call | tf_op jit(solution)/shard_map/base_products/pallas_call | solution.py:167
  25.8 2.8 %collective-permute-start.3 = (bf16[16,80,128]{2,1,0:T(8,128)(2,1)S(1)}, bf16[16,80,128]{2,1,0:T(8,128)(2,1)S(1)}, u32[]{:S(2)}, u32[]{:S(2)}) collective-permute-start(bf16[16,80,128]{2,1,0:T(8,128)(2,1)S(1)} %get-tuple-element.22), channel_id=1, source_target_pairs={{0,4},{4,0},{8,12},{12,8},{16,20},{20,16},{24,28},{28,24},{32,36},... | collective-permute-start | bytes 983048 | tf_op jit(solution)/shard_map/ppermute | solution.py:128
  28.6 1.3 collective-permute-done.3
  29.9 11.5 %all_to_all.10 = bf16[16,80,128]{2,1,0:T(8,128)(2,1)S(1)} all-to-all(bf16[16,80,128]{2,1,0:T(8,128)(2,1)S(1)} %add_convert_fusion), channel_id=1, replica_groups={{0,8,16,24,32,40,48,56,64,72,80,88,96,104,112,120},{4,12,20,28,36,44,52..., dimensions={0} | all-to-all | bytes 655360 | tf_op jit(solution)/shard_map/all_to_all | solution.py:133
  41.5 11.0 %all_to_all.11 = bf16[16,80,128]{2,1,0:T(8,128)(2,1)S(1)} all-to-all(bf16[16,80,128]{2,1,0:T(8,128)(2,1)S(1)} %broadcast_in_dim.6), channel_id=1, replica_groups={{0,8,16,24,32,40,48,56,64,72,80,88,96,104,112,120},{4,12,20,28,36,44,52..., dimensions={0} | all-to-all | bytes 655360 | tf_op jit(solution)/shard_map/all_to_all | solution.py:133
  52.5 2.6 %collective-permute-start.4 = (bf16[16,80,128]{2,1,0:T(8,128)(2,1)S(1)}, bf16[16,80,128]{2,1,0:T(8,128)(2,1)S(1)}, u32[]{:S(2)}, u32[]{:S(2)}) collective-permute-start(bf16[16,80,128]{2,1,0:T(8,128)(2,1)S(1)} %all_to_all.11), channel_id=1, source_target_pairs={{0,4},{4,0},{8,12},{12,8},{16,20},{20,16},{24,28},{28,24},{32,36},... | collective-permute-start | bytes 983048 | tf_op jit(solution)/shard_map/ppermute | solution.py:128
  55.1 1.7 slice_bitcast_fusion
  56.9 1.2 copy-done.2
  58.1 1.3 fusion.rest_0_
  62.2 1.9 %solve_1.1 = bf16[512,128]{1,0:T(8,128)(2,1)S(1)} custom-call(s32[2]{0:T(128)S(1)} %pad_add_fusion.place_ref, s32[5,6]{1,0:T(8,128)S(1)} %copy-done.1, s32[5,1]{1,0:T(8,128)S(1)} %copy.26.count_ref, bf16[5,6,512,512]{3,2,1,0:T(8,128)(2,1)} %factor_ref.15, f32[512,128]{1,0:T(8,128)S(1)} %convert_subtract_fusion.6.ahead_ref, ...), custom_call_target="tpu_custom_call" | custom-call | tf_op jit(solution)/shard_map/solve_1/pallas_call | solution.py:202
  64.1 2.1 %later_0.1 = f32[3,512,128]{2,1,0:T(8,128)S(1)} custom-call(s32[2]{0:T(128)S(1)} %pad_add_fusion.place_ref, s32[5,6]{1,0:T(8,128)S(1)} %copy-done.1, s32[5,1]{1,0:T(8,128)S(1)} %copy.26.count_ref, bf16[5,6,512,512]{3,2,1,0:T(8,128)(2,1)} %factor_ref.15, bf16[512,128]{1,0:T(8,128)(2,1)S(1)} %fusion.rest_0_, ...), custom_call_target="tpu_custom_call" | custom-call | tf_op jit(solution)/shard_map/later_0/pallas_call | solution.py:216
  69.8 1.9 %solve_2.1 = bf16[512,128]{1,0:T(8,128)(2,1)S(1)} custom-call(s32[2]{0:T(128)S(1)} %pad_add_fusion.place_ref, s32[5,6]{1,0:T(8,128)S(1)} %copy-done.1, s32[5,1]{1,0:T(8,128)S(1)} %copy.26.count_ref, bf16[5,6,512,512]{3,2,1,0:T(8,128)(2,1)} %factor_ref.15, f32[512,128]{1,0:T(8,128)S(1)} %convert_subtract_fusion.4.ahead_ref, ...), custom_call_target="tpu_custom_call" | custom-call | tf_op jit(solution)/shard_map/solve_2/pallas_call | solution.py:202
  71.6 1.7 %later_1.1 = f32[2,512,128]{2,1,0:T(8,128)S(1)} custom-call(s32[2]{0:T(128)S(1)} %pad_add_fusion.place_ref, s32[5,6]{1,0:T(8,128)S(1)} %copy-done.1, s32[5,1]{1,0:T(8,128)S(1)} %copy.26.count_ref, bf16[5,6,512,512]{3,2,1,0:T(8,128)(2,1)} %factor_ref.15, bf16[512,128]{1,0:T(8,128)(2,1)S(1)} %collective-permute-done.8.rest_0_, ...), custom_call_target="tpu_custom_call" | custom-call | tf_op jit(solution)/shard_map/later_1/pallas_call | solution.py:216
  77.1 1.9 %solve_3.1 = bf16[512,128]{1,0:T(8,128)(2,1)S(1)} custom-call(s32[2]{0:T(128)S(1)} %pad_add_fusion.place_ref, s32[5,6]{1,0:T(8,128)S(1)} %copy-done.1, s32[5,1]{1,0:T(8,128)S(1)} %copy.26.count_ref, bf16[5,6,512,512]{3,2,1,0:T(8,128)(2,1)} %factor_ref.15, f32[512,128]{1,0:T(8,128)S(1)} %convert_subtract_fusion.2.ahead_ref, ...), custom_call_target="tpu_custom_call" | custom-call | tf_op jit(solution)/shard_map/solve_3/pallas_call | solution.py:202
  78.9 1.6 later_2.1
  80.6 0.9 pad_maximum_fusion.2
  82.1 0.9 collective-permute-start.26
  85.1 1.0 convert_subtract_fusion.ahead_ref
  86.1 1.9 %solve_4.1 = bf16[512,128]{1,0:T(8,128)(2,1)S(1)} custom-call(s32[2]{0:T(128)S(1)} %pad_add_fusion.place_ref, s32[5,6]{1,0:T(8,128)S(1)} %copy-done.1, s32[5,1]{1,0:T(8,128)S(1)} %copy.26.count_ref, bf16[5,6,512,512]{3,2,1,0:T(8,128)(2,1)} %factor_ref.15, f32[512,128]{1,0:T(8,128)S(1)} %convert_subtract_fusion.ahead_ref, ...), custom_call_target="tpu_custom_call" | custom-call | tf_op jit(solution)/shard_map/solve_4/pallas_call | solution.py:202
  93.6 1.3 collective-permute-start.35
  96.4 1.3 collective-permute-start.24
  97.7 58.0 %collective-permute-done.35 = bf16[2,512,128]{2,1,0:T(8,128)(2,1)S(1)} collective-permute-done((bf16[2,512,128]{2,1,0:T(8,128)(2,1)S(1)}, bf16[2,512,128]{2,1,0:T(8,128)(2,1)S(1)}, u32[]{:S(2)}, u32[]{:S(2)}) %collective-permute-start.35) | collective-permute-done | bytes 262176 | tf_op jit(solution)/shard_map/ppermute | solution.py:120
  155.9 11.1 %collective-permute-done.24 = bf16[3,512,128]{2,1,0:T(8,128)(2,1)S(1)} collective-permute-done((bf16[3,512,128]{2,1,0:T(8,128)(2,1)S(1)}, bf16[3,512,128]{2,1,0:T(8,128)(2,1)S(1)}, u32[]{:S(2)}, u32[]{:S(2)}) %collective-permute-start.24) | collective-permute-done | bytes 393248 | tf_op jit(solution)/shard_map/ppermute | solution.py:120
  167.2 1.7 collective-permute-done.25
  169.0 1.1 fusion.1
  (92 shorter events, 20.5 us)
Async XLA Ops:
  4.1 9.8 %collective-permute-start = (bf16[2,512,128]{2,1,0:T(8,128)(2,1)S(1)}, bf16[2,512,128]{2,1,0:T(8,128)(2,1)S(1)}, u32[]{:S(2)}, u32[]{:S(2)}) collective-permute-start(bf16[2,512,128]{2,1,0:T(8,128)(2,1)S(1)} %get-tuple-element.52.rest_0_), channel_id=1, source_target_pairs={{0,1},{1,2},{2,3},{3,0},{4,5},{5,6},{6,7},{7,4},{8,9},{9,10},{10,1... | collective-permute-start | bytes 786440 | tf_op jit(solution)/shard_map/ppermute | solution.py:165
  5.8 14.6 %collective-permute-start.1 = (bf16[2,512,128]{2,1,0:T(8,128)(2,1)S(1)}, bf16[2,512,128]{2,1,0:T(8,128)(2,1)S(1)}, u32[]{:S(2)}, u32[]{:S(2)}) collective-permute-start(bf16[2,512,128]{2,1,0:T(8,128)(2,1)S(1)} %get-tuple-element.52.rest_0_), channel_id=1, source_target_pairs={{0,2},{1,3},{2,0},{3,1},{4,6},{5,7},{6,4},{7,5},{8,10},{9,11},{10,... | collective-permute-start | bytes 786440 | tf_op jit(solution)/shard_map/ppermute | solution.py:165
  9.1 11.3 %collective-permute-start.2 = (bf16[2,512,128]{2,1,0:T(8,128)(2,1)S(1)}, bf16[2,512,128]{2,1,0:T(8,128)(2,1)S(1)}, u32[]{:S(2)}, u32[]{:S(2)}) collective-permute-start(bf16[2,512,128]{2,1,0:T(8,128)(2,1)S(1)} %get-tuple-element.52.rest_0_), channel_id=1, source_target_pairs={{0,3},{1,0},{2,1},{3,2},{4,7},{5,4},{6,5},{7,6},{8,11},{9,8},{10,9... | collective-permute-start | bytes 786440 | tf_op jit(solution)/shard_map/ppermute | solution.py:165
  25.8 4.1 %collective-permute-start.3 = (bf16[16,80,128]{2,1,0:T(8,128)(2,1)S(1)}, bf16[16,80,128]{2,1,0:T(8,128)(2,1)S(1)}, u32[]{:S(2)}, u32[]{:S(2)}) collective-permute-start(bf16[16,80,128]{2,1,0:T(8,128)(2,1)S(1)} %get-tuple-element.22), channel_id=1, source_target_pairs={{0,4},{4,0},{8,12},{12,8},{16,20},{20,16},{24,28},{28,24},{32,36},... | collective-permute-start | bytes 983048 | tf_op jit(solution)/shard_map/ppermute | solution.py:128
  52.5 4.3 %collective-permute-start.4 = (bf16[16,80,128]{2,1,0:T(8,128)(2,1)S(1)}, bf16[16,80,128]{2,1,0:T(8,128)(2,1)S(1)}, u32[]{:S(2)}, u32[]{:S(2)}) collective-permute-start(bf16[16,80,128]{2,1,0:T(8,128)(2,1)S(1)} %all_to_all.11), channel_id=1, source_target_pairs={{0,4},{4,0},{8,12},{12,8},{16,20},{20,16},{24,28},{28,24},{32,36},... | collective-permute-start | bytes 983048 | tf_op jit(solution)/shard_map/ppermute | solution.py:128
  59.4 2.8 %collective-permute-start.5 = (bf16[512,128]{1,0:T(8,128)(2,1)S(1)}, bf16[512,128]{1,0:T(8,128)(2,1)S(1)}, u32[]{:S(2)}, u32[]{:S(2)}) collective-permute-start(bf16[512,128]{1,0:T(8,128)(2,1)S(1)} %fusion.rest_0_), channel_id=1, source_target_pairs={{0,1},{1,2},{2,3},{3,0}} | collective-permute-start | bytes 393224 | tf_op jit(solution)/shard_map/ppermute | solution.py:120
  60.1 2.1 %collective-permute-start.6 = (bf16[512,128]{1,0:T(8,128)(2,1)S(1)}, bf16[512,128]{1,0:T(8,128)(2,1)S(1)}, u32[]{:S(2)}, u32[]{:S(2)}) collective-permute-start(bf16[512,128]{1,0:T(8,128)(2,1)S(1)} %fusion.rest_0_), channel_id=1, source_target_pairs={{0,2},{1,3},{2,0},{3,1}} | collective-permute-start | bytes 393224 | tf_op jit(solution)/shard_map/ppermute | solution.py:120
  66.3 3.4 %collective-permute-start.12 = (bf16[4,512,128]{2,1,0:T(8,128)(2,1)S(1)}, bf16[4,512,128]{2,1,0:T(8,128)(2,1)S(1)}, u32[]{:S(2)}, u32[]{:S(2)}) collective-permute-start(bf16[4,512,128]{2,1,0:T(8,128)(2,1)S(1)} %pad_maximum_fusion), channel_id=1, source_target_pairs={{0,4},{1,5},{2,6},{3,7}} | collective-permute-start | bytes 1572872 | tf_op jit(solution)/shard_map/ppermute | solution.py:120
  67.0 2.8 %collective-permute-start.10 = (bf16[512,128]{1,0:T(8,128)(2,1)S(1)}, bf16[512,128]{1,0:T(8,128)(2,1)S(1)}, u32[]{:S(2)}, u32[]{:S(2)}) collective-permute-start(bf16[512,128]{1,0:T(8,128)(2,1)S(1)} %solve_1.1), channel_id=1, source_target_pairs={{0,6},{1,7},{2,4},{3,5}} | collective-permute-start | bytes 393224 | tf_op jit(solution)/shard_map/ppermute | solution.py:120
  67.6 2.1 %collective-permute-start.11 = (bf16[512,128]{1,0:T(8,128)(2,1)S(1)}, bf16[512,128]{1,0:T(8,128)(2,1)S(1)}, u32[]{:S(2)}, u32[]{:S(2)}) collective-permute-start(bf16[512,128]{1,0:T(8,128)(2,1)S(1)} %solve_1.1), channel_id=1, source_target_pairs={{0,7},{1,4},{2,5},{3,6}} | collective-permute-start | bytes 393224 | tf_op jit(solution)/shard_map/ppermute | solution.py:120
  73.5 3.4 %collective-permute-start.17 = (bf16[4,512,128]{2,1,0:T(8,128)(2,1)S(1)}, bf16[4,512,128]{2,1,0:T(8,128)(2,1)S(1)}, u32[]{:S(2)}, u32[]{:S(2)}) collective-permute-start(bf16[4,512,128]{2,1,0:T(8,128)(2,1)S(1)} %pad_maximum_fusion.1), channel_id=1, source_target_pairs={{4,8},{5,9},{6,10},{7,11}} | collective-permute-start | bytes 1572872 | tf_op jit(solution)/shard_map/ppermute | solution.py:120
  74.2 2.8 %collective-permute-start.13 = (bf16[512,128]{1,0:T(8,128)(2,1)S(1)}, bf16[512,128]{1,0:T(8,128)(2,1)S(1)}, u32[]{:S(2)}, u32[]{:S(2)}) collective-permute-start(bf16[512,128]{1,0:T(8,128)(2,1)S(1)} %solve_2.1), channel_id=1, source_target_pairs={{4,8},{5,9},{6,10},{7,11}} | collective-permute-start | bytes 393224 | tf_op jit(solution)/shard_map/ppermute | solution.py:120
  74.9 2.1 %collective-permute-start.14 = (bf16[512,128]{1,0:T(8,128)(2,1)S(1)}, bf16[512,128]{1,0:T(8,128)(2,1)S(1)}, u32[]{:S(2)}, u32[]{:S(2)}) collective-permute-start(bf16[512,128]{1,0:T(8,128)(2,1)S(1)} %solve_2.1), channel_id=1, source_target_pairs={{4,9},{5,10},{6,11},{7,8}} | collective-permute-start | bytes 393224 | tf_op jit(solution)/shard_map/ppermute | solution.py:120
  81.4 3.6 %collective-permute-start.18 = (bf16[4,512,128]{2,1,0:T(8,128)(2,1)}, bf16[4,512,128]{2,1,0:T(8,128)(2,1)S(1)}, u32[]{:S(2)}, u32[]{:S(2)}) collective-permute-start(bf16[4,512,128]{2,1,0:T(8,128)(2,1)} %pad_maximum_fusion.2), channel_id=1, source_target_pairs={{8,12},{9,13},{10,14},{11,15}} | collective-permute-start | bytes 1572872 | tf_op jit(solution)/shard_map/ppermute | solution.py:120
  82.1 3.9 %collective-permute-start.26 = (bf16[512,128]{1,0:T(8,128)(2,1)S(1)}, bf16[512,128]{1,0:T(8,128)(2,1)S(1)}, u32[]{:S(2)}, u32[]{:S(2)}) collective-permute-start(bf16[512,128]{1,0:T(8,128)(2,1)S(1)} %solve_3.1), channel_id=1, source_target_pairs={{8,12},{9,13},{10,14},{11,15}} | collective-permute-start | bytes 393224 | tf_op jit(solution)/shard_map/ppermute | solution.py:120
  83.0 3.0 %collective-permute-start.27 = (bf16[512,128]{1,0:T(8,128)(2,1)S(1)}, bf16[512,128]{1,0:T(8,128)(2,1)S(1)}, u32[]{:S(2)}, u32[]{:S(2)}) collective-permute-start(bf16[512,128]{1,0:T(8,128)(2,1)S(1)} %solve_3.1), channel_id=1, source_target_pairs={{8,13},{9,14},{10,15},{11,12}} | collective-permute-start | bytes 393224 | tf_op jit(solution)/shard_map/ppermute | solution.py:120
  83.7 2.3 %collective-permute-start.28 = (bf16[512,128]{1,0:T(8,128)(2,1)S(1)}, bf16[512,128]{1,0:T(8,128)(2,1)S(1)}, u32[]{:S(2)}, u32[]{:S(2)}) collective-permute-start(bf16[512,128]{1,0:T(8,128)(2,1)S(1)} %solve_3.1), channel_id=1, source_target_pairs={{8,14},{9,15},{10,12},{11,13}} | collective-permute-start | bytes 393224 | tf_op jit(solution)/shard_map/ppermute | solution.py:120
  84.4 1.7 collective-permute-start.29
  88.0 3.5 %collective-permute-start.30 = (bf16[2,512,128]{2,1,0:T(8,128)(2,1)S(1)}, bf16[2,512,128]{2,1,0:T(8,128)(2,1)S(1)}, u32[]{:S(2)}, u32[]{:S(2)}) collective-permute-start(bf16[2,512,128]{2,1,0:T(8,128)(2,1)S(1)} %maximum_select_fusion.1), channel_id=1, source_target_pairs={{12,20},{13,21},{14,22},{15,23}} | collective-permute-start | bytes 786440 | tf_op jit(solution)/shard_map/ppermute | solution.py:120
  88.7 3.5 %collective-permute-start.31 = (bf16[2,512,128]{2,1,0:T(8,128)(2,1)S(1)}, bf16[2,512,128]{2,1,0:T(8,128)(2,1)S(1)}, u32[]{:S(2)}, u32[]{:S(2)}) collective-permute-start(bf16[2,512,128]{2,1,0:T(8,128)(2,1)S(1)} %maximum_select_fusion.1), channel_id=1, source_target_pairs={{12,4},{13,5},{14,6},{15,7}} | collective-permute-start | bytes 786440 | tf_op jit(solution)/shard_map/ppermute | solution.py:120
  89.4 2.8 %collective-permute-start.32 = (bf16[2,512,128]{2,1,0:T(8,128)(2,1)S(1)}, bf16[2,512,128]{2,1,0:T(8,128)(2,1)S(1)}, u32[]{:S(2)}, u32[]{:S(2)}) collective-permute-start(bf16[2,512,128]{2,1,0:T(8,128)(2,1)S(1)} %maximum_select_fusion.1), channel_id=1, source_target_pairs={{12,28},{13,29},{14,30},{15,31}} | collective-permute-start | bytes 786440 | tf_op jit(solution)/shard_map/ppermute | solution.py:120
  90.1 3.6 %collective-permute-start.19 = (bf16[3,512,128]{2,1,0:T(8,128)(2,1)S(1)}, bf16[3,512,128]{2,1,0:T(8,128)(2,1)S(1)}, u32[]{:S(2)}, u32[]{:S(2)}) collective-permute-start(bf16[3,512,128]{2,1,0:T(8,128)(2,1)S(1)} %slice_select_fusion), channel_id=1, source_target_pairs={{12,20},{13,21},{14,22},{15,23}} | collective-permute-start | bytes 1179656 | tf_op jit(solution)/shard_map/ppermute | solution.py:120
  90.8 4.2 %collective-permute-start.20 = (bf16[3,512,128]{2,1,0:T(8,128)(2,1)S(1)}, bf16[3,512,128]{2,1,0:T(8,128)(2,1)S(1)}, u32[]{:S(2)}, u32[]{:S(2)}) collective-permute-start(bf16[3,512,128]{2,1,0:T(8,128)(2,1)S(1)} %slice_select_fusion), channel_id=1, source_target_pairs={{12,4},{13,5},{14,6},{15,7}} | collective-permute-start | bytes 1179656 | tf_op jit(solution)/shard_map/ppermute | solution.py:120
  91.5 3.5 %collective-permute-start.21 = (bf16[3,512,128]{2,1,0:T(8,128)(2,1)S(1)}, bf16[3,512,128]{2,1,0:T(8,128)(2,1)S(1)}, u32[]{:S(2)}, u32[]{:S(2)}) collective-permute-start(bf16[3,512,128]{2,1,0:T(8,128)(2,1)S(1)} %slice_select_fusion), channel_id=1, source_target_pairs={{12,28},{13,29},{14,30},{15,31}} | collective-permute-start | bytes 1179656 | tf_op jit(solution)/shard_map/ppermute | solution.py:120
  92.3 4.2 %collective-permute-start.33 = (bf16[2,512,128]{2,1,0:T(8,128)(2,1)S(1)}, bf16[2,512,128]{2,1,0:T(8,128)(2,1)S(1)}, u32[]{:S(2)}, u32[]{:S(2)}) collective-permute-start(bf16[2,512,128]{2,1,0:T(8,128)(2,1)S(1)} %add_add_fusion.3), channel_id=1, source_target_pairs={{4,36},{5,37},{6,38},{7,39},{12,44},{13,45},{14,46},{15,47},{20,52... | collective-permute-start | bytes 786440 | tf_op jit(solution)/shard_map/ppermute | solution.py:120
  92.9 4.8 %collective-permute-start.34 = (bf16[2,512,128]{2,1,0:T(8,128)(2,1)S(1)}, bf16[2,512,128]{2,1,0:T(8,128)(2,1)S(1)}, u32[]{:S(2)}, u32[]{:S(2)}) collective-permute-start(bf16[2,512,128]{2,1,0:T(8,128)(2,1)S(1)} %add_add_fusion.3), channel_id=1, source_target_pairs={{4,100},{5,101},{6,102},{7,103},{12,108},{13,109},{14,110},{15,111... | collective-permute-start | bytes 786440 | tf_op jit(solution)/shard_map/ppermute | solution.py:120
  93.6 62.1 %collective-permute-start.35 = (bf16[2,512,128]{2,1,0:T(8,128)(2,1)S(1)}, bf16[2,512,128]{2,1,0:T(8,128)(2,1)S(1)}, u32[]{:S(2)}, u32[]{:S(2)}) collective-permute-start(bf16[2,512,128]{2,1,0:T(8,128)(2,1)S(1)} %add_add_fusion.3), channel_id=1, source_target_pairs={{4,68},{5,69},{6,70},{7,71},{12,76},{13,77},{14,78},{15,79},{20,84... | collective-permute-start | bytes 786440 | tf_op jit(solution)/shard_map/ppermute | solution.py:120
  95.0 60.9 %collective-permute-start.22 = (bf16[3,512,128]{2,1,0:T(8,128)(2,1)S(1)}, bf16[3,512,128]{2,1,0:T(8,128)(2,1)S(1)}, u32[]{:S(2)}, u32[]{:S(2)}) collective-permute-start(bf16[3,512,128]{2,1,0:T(8,128)(2,1)S(1)} %add_add_fusion.1), channel_id=1, source_target_pairs={{4,36},{5,37},{6,38},{7,39},{12,44},{13,45},{14,46},{15,47},{20,52... | collective-permute-start | bytes 1179656 | tf_op jit(solution)/shard_map/ppermute | solution.py:120
  95.7 60.2 %collective-permute-start.23 = (bf16[3,512,128]{2,1,0:T(8,128)(2,1)S(1)}, bf16[3,512,128]{2,1,0:T(8,128)(2,1)S(1)}, u32[]{:S(2)}, u32[]{:S(2)}) collective-permute-start(bf16[3,512,128]{2,1,0:T(8,128)(2,1)S(1)} %add_add_fusion.1), channel_id=1, source_target_pairs={{4,100},{5,101},{6,102},{7,103},{12,108},{13,109},{14,110},{15,111... | collective-permute-start | bytes 1179656 | tf_op jit(solution)/shard_map/ppermute | solution.py:120
  96.4 70.6 %collective-permute-start.24 = (bf16[3,512,128]{2,1,0:T(8,128)(2,1)S(1)}, bf16[3,512,128]{2,1,0:T(8,128)(2,1)S(1)}, u32[]{:S(2)}, u32[]{:S(2)}) collective-permute-start(bf16[3,512,128]{2,1,0:T(8,128)(2,1)S(1)} %add_add_fusion.1), channel_id=1, source_target_pairs={{4,68},{5,69},{6,70},{7,71},{12,76},{13,77},{14,78},{15,79},{20,84... | collective-permute-start | bytes 1179656 | tf_op jit(solution)/shard_map/ppermute | solution.py:120
  155.8 11.4 %collective-permute-start.36 = (bf16[2,512,128]{2,1,0:T(8,128)(2,1)S(1)}, bf16[2,512,128]{2,1,0:T(8,128)(2,1)S(1)}, u32[]{:S(2)}, u32[]{:S(2)}) collective-permute-start(bf16[2,512,128]{2,1,0:T(8,128)(2,1)S(1)} %add_add_fusion.2), channel_id=1, source_target_pairs={{0,4},{4,0},{8,12},{12,8},{16,20},{20,16},{24,28},{28,24},{32,36},... | collective-permute-start | bytes 786440 | tf_op jit(solution)/shard_map/ppermute | solution.py:128
  167.1 1.8 %collective-permute-start.25 = (bf16[3,512,128]{2,1,0:T(8,128)(2,1)S(1)}, bf16[3,512,128]{2,1,0:T(8,128)(2,1)S(1)}, u32[]{:S(2)}, u32[]{:S(2)}) collective-permute-start(bf16[3,512,128]{2,1,0:T(8,128)(2,1)S(1)} %add_add_fusion), channel_id=1, source_target_pairs={{0,4},{4,0},{8,12},{12,8},{16,20},{20,16},{24,28},{28,24},{32,36},... | collective-permute-start | bytes 1179656 | tf_op jit(solution)/shard_map/ppermute | solution.py:128
  (9 other events, 37.4 us)

commit v3 on v0

v3 whole, which is shorter than its diff:
```python
import functools

import jax
import jax.numpy as jnp
from jax import lax
from jax.experimental import pallas as pl
from jax.experimental.pallas import tpu as pltpu
from jax.sharding import PartitionSpec as P

BF16, F32 = jnp.bfloat16, jnp.float32
AXES = ("col", "row")
NX = NY = NZ = 4
BOTH = (0, 1)
SMEM = pl.BlockSpec(memory_space=pltpu.SMEM)
VMEM = pl.BlockSpec(memory_space=pltpu.VMEM)
ANY = pl.BlockSpec(memory_space=pl.ANY)


def column(x, y, core):
    return (y * NX + x) * 2 + core


def place(x, y, core, z):
    return column(x, y, core) * NZ + z


def dot(a, b):
    return jnp.dot(a, b, preferred_element_type=F32)


def call(body, name, outs, in_specs, args, scratch=(), flops=0, nbytes=0, out_specs=None):
    return pl.pallas_call(
        body,
        out_shape=outs,
        in_specs=in_specs,
        out_specs=out_specs or jax.tree.map(lambda _: VMEM, outs),
        scratch_shapes=list(scratch),
        compiler_params=pltpu.CompilerParams(vmem_limit_bytes=24 * 1024 * 1024),
        cost_estimate=pl.CostEstimate(flops=flops, bytes_accessed=nbytes, transcendentals=0),
        name=name,
    )(*args)


def base_solve_kernel(inverse_ref, rhs_ref, out_ref, rounded_ref):
    for i in range(rhs_ref.shape[0]):
        value = dot(inverse_ref[i], rhs_ref[i].astype(BF16))
        out_ref[i] = value
        rounded_ref[i] = value.astype(BF16)


def load_kernel(levels, slots, count_ref, factor_ref, inverse_ref, held_ref, kept_ref, sems, other_sem):
    inverses = pltpu.make_async_copy(inverse_ref, kept_ref, other_sem)
    inverses.start()

    def each(act):
        for level in range(levels):
            for slot in range(slots):
                @pl.when(slot < count_ref[level, 0])
                def _():
                    at = level * slots + slot
                    act(pltpu.make_async_copy(factor_ref.at[level, slot], held_ref.at[at], sems.at[at]))

    each(lambda copy: copy.start())
    each(lambda copy: copy.wait())
    inverses.wait()


def add_products(total, level, slots, low, high, operand_of, source_ref, count_ref, held_ref):
    for slot in range(slots):
        source = source_ref[level, slot]

        @pl.when((slot < count_ref[level, 0]) & (source >= low) & (source < high))
        def _():
            total[...] += dot(held_ref[level * slots + slot], operand_of(source - low))


def order_pieces(row, piece_refs, operands):
    for k, piece in enumerate(piece_refs):
        operands[lax.rem(row + NZ - k, NZ)] = piece[...]


def base_kernel(levels, slots, place_ref, source_ref, count_ref, held_ref, *rest):
    pieces, (keep_ref, send_ref), (operands, total) = rest[:NZ], rest[NZ : NZ + 2], rest[NZ + 2 :]
    core, per_row = place_ref[1], operands.shape[1]
    order_pieces(place_ref[0], pieces, operands)
    shares, some = keep_ref.shape[0], keep_ref.shape[1] // levels
    mine = pl.multiple_of(core * shares * some, shares * some)
    other = pl.multiple_of((1 - core) * shares * some, shares * some)
    for level in range(levels):
        total[...] = jnp.zeros_like(total)
        add_products(total, level, slots, 0, NZ * per_row, lambda q: operands[q // per_row, lax.rem(q, per_row)],
                     source_ref, count_ref, held_ref)
        for share in range(shares):
            place_in = pl.ds(level * some, some)
            keep_ref[share, place_in] = total[pl.ds(mine + share * some, some)]
            send_ref[share, place_in] = total[pl.ds(other + share * some, some)].astype(BF16)


def first_kernel(place_ref, half_ref, other_ref, apex_ref, inverse_ref, ahead_ref, out_ref, target):
    core = place_ref[1]
    levels = apex_ref.shape[0]
    shares, some = half_ref.shape[0], half_ref.shape[1] // levels
    for level in range(levels):
        to = target if level == 0 else ahead_ref.at[level - 1]
        for ref, side in ((half_ref, core), (other_ref, 1 - core)):
            for share in range(shares):
                rows = pl.ds(pl.multiple_of(side * shares * some, shares * some) + share * some, some)
                to[rows] = apex_ref[level, rows] - ref[share, pl.ds(level * some, some)].astype(F32)
        if level == 0:
            out_ref[...] = dot(inverse_ref[0], target[...].astype(BF16)).astype(BF16)


def sum_kernel(in_ref, out_ref):
    total = in_ref[0].astype(F32)
    for i in range(1, in_ref.shape[0]):
        total = total + in_ref[i].astype(F32)
    for i in range(in_ref.shape[0]):
        out_ref[i] = total.astype(BF16)


def solve_kernel(level, slots, low, extra, outs, place_ref, source_ref, count_ref, held_ref, ahead_ref, inverse_ref,
                 *rest):
    pieces, more, outs_refs = rest[:NZ], rest[NZ : NZ + extra], rest[NZ + extra : NZ + extra + len(outs)]
    operands, total = rest[NZ + extra + len(outs) :]
    named = dict(zip(outs, outs_refs))
    nearest = pieces[0]
    chained = len(nearest.shape) == 3
    row = place_ref[0]
    operands[row] = nearest[0] if chained else nearest[...]
    for k in range(1, NZ):
        operands[lax.rem(row + NZ - k, NZ)] = pieces[k][...]
    lists = (source_ref, count_ref, held_ref)
    total[...] = nearest[1].astype(F32) if chained else jnp.zeros_like(total)
    for ref in more:
        total[...] += ref[...].astype(F32)
    add_products(total, level, slots, low, low + NZ, lambda q: operands[q], *lists)
    correction = (ahead_ref[level - 1] - total[...]).astype(BF16)
    value = dot(inverse_ref[level], correction).astype(BF16)
    named["value"][...] = value
    if "packed" in named:
        named["packed"][0] = value
        total[...] = jnp.zeros_like(total)
        add_products(total, level + 1, slots, low, low + NZ, lambda q: operands[q], *lists)
        named["packed"][1] = total[...].astype(BF16)
    if "both" in named:
        named["both"][0] = operands[row]
        named["both"][1] = value
    if "kept" in named:
        for v in range(NZ):
            named["kept"][v] = operands[v]


def later_kernel(levels, slots, low, source_ref, count_ref, held_ref, operands, *rest):
    out_refs, total = rest[:-1], rest[-1]
    for level, out_ref in zip(levels, out_refs):
        total[...] = jnp.zeros_like(total)
        add_products(total, level, slots, low, low + NZ, lambda q: operands[q], source_ref, count_ref, held_ref)
        out_ref[...] = total[...].astype(BF16)


def pair_kernel(keep_ref, got_ref, out_ref):
    out_ref[...] = (keep_ref[...] + got_ref[...].astype(F32)).astype(BF16)


def pick_kernel(column_of, place_ref, value_ref, *rest):
    got, out_ref = rest[:-1], rest[-1]
    came = got[0][...]
    for ref in got[1:]:
        came = came + ref[...]
    out_ref[...] = jnp.where(place_ref[2] == column_of, value_ref[...], came)


def pick(column_of, places, value, got, name):
    return call(
        functools.partial(pick_kernel, column_of), name, jax.ShapeDtypeStruct(value.shape, value.dtype),
        [SMEM] + [VMEM] * (1 + len(got)), (places, value, *got),
    )


def send(value, pairs):
    return lax.ppermute(value, AXES, pairs)


def to_column(value, sender, receiver, k=0):
    return send(value, [(sender * NZ + z, receiver * NZ + (z + k) % NZ) for z in range(NZ)])


def to_next_rows(value):
    return [lax.ppermute(value, "row", [(z, (z + k) % NZ) for z in range(NZ)]) for k in (1, 2, 3)]


def other_core(value):
    return lax.ppermute(value, "col", [(c, c ^ 1) for c in range(NX * NY * 2)])


def over_plane(value):
    groups = [[column(x, y, core) for y in range(NY) for x in range(NX)] for core in BOTH]
    return lax.all_to_all(value, "col", 0, 0, axis_index_groups=groups, tiled=True)


def spread_x(value, x0, core, places):
    got = [
        send(value, [(place(x0, 0, core, z), place((x0 + dx) % NX, 0, core, z)) for z in range(NZ)])
        for dx in (1, 3, 2)
    ]
    return pick(column(x0, 0, core), places, value, got, "picked")


def spread_y(value, core, here):
    got = [
        send(value, [(place(x, 0, core, z), place(x, y, core, z)) for x in range(NX) for z in range(NZ)])
        for y in (1, 3, 2)
    ]
    own = (here < 2 * NX) & (here % 2 == core)
    return lambda: jnp.where(own, value, got[0] + got[1] + got[2])


def on_device(base_rhs, base_inverse, apex, top_inverse, factor_blocks, block_source, block_count):
    levels, slots = block_source.shape[0], factor_blocks.shape[1]
    per_row, size, samples = base_rhs.shape
    shares = NX * NY
    some = size // 2 // shares
    block = factor_blocks.shape[2:]
    here, row = lax.axis_index("col"), lax.axis_index("row")
    core = here % 2
    places = jnp.stack([row, core, here]).astype(jnp.int32)
    after = lax.optimization_barrier
    one = 2 * size * size * samples
    full = jax.ShapeDtypeStruct((size, samples), BF16)

    base_solution, rounded = call(
        base_solve_kernel, "base_solve",
        (jax.ShapeDtypeStruct(base_rhs.shape, F32), jax.ShapeDtypeStruct(base_rhs.shape, BF16)),
        [VMEM, VMEM], (base_inverse, base_rhs), flops=per_row * one, nbytes=6 * base_rhs.size + 2 * base_inverse.size,
    )
    rounded, counts, places = after((rounded, block_count, places))
    pieces = [rounded] + to_next_rows(rounded)
    held, inverses = (pltpu.with_memory_space_constraint(x, pltpu.VMEM) for x in call(
        functools.partial(load_kernel, levels, slots), "load_blocks",
        (pltpu.VMEM((levels * slots,) + block, BF16), pltpu.VMEM((levels,) + block, BF16)),
        [SMEM, ANY, ANY], (counts, factor_blocks, top_inverse[:, 0]),
        scratch=[pltpu.SemaphoreType.DMA((levels * slots,)), pltpu.SemaphoreType.DMA],
        nbytes=2 * factor_blocks.size, out_specs=(VMEM, VMEM),
    ))
    lists = (block_source, block_count, held)
    keep, give = call(
        functools.partial(base_kernel, levels, slots), "base_products",
        (
            jax.ShapeDtypeStruct((shares, levels * some, samples), F32),
            jax.ShapeDtypeStruct((shares, levels * some, samples), BF16),
        ),
        [SMEM] * 3 + [VMEM] * (1 + NZ), (places, *lists, *pieces),
        scratch=[pltpu.VMEM((NZ, per_row, size, samples), BF16), pltpu.VMEM((size, samples), F32)],
        flops=levels * slots * one // 2,
    )
    pair = call(
        pair_kernel, "pair_sums", jax.ShapeDtypeStruct(give.shape, BF16), [VMEM] * 2, (keep, other_core(give))
    )
    share = call(sum_kernel, "sum_shares", jax.ShapeDtypeStruct(pair.shape, BF16), [VMEM], (over_plane(pair),))
    half = over_plane(share)
    other = other_core(half)
    ahead, first = call(
        first_kernel, "solve_0", (jax.ShapeDtypeStruct((levels - 1, size, samples), F32), full),
        [SMEM] + [VMEM] * 4, (places, half, other, apex[:, 0], inverses),
        scratch=[pltpu.VMEM((size, samples), F32)], flops=one,
    )
    two = jax.ShapeDtypeStruct((2, size, samples), BF16)
    four = jax.ShapeDtypeStruct((NZ, size, samples), BF16)
    acc = pltpu.VMEM((size, samples), F32)

    def low(u):
        return per_row * NZ + u * NZ

    def solve(u, pieces, extra, outs):
        shapes = {"value": full, "packed": two, "both": two, "kept": four}
        return call(
            functools.partial(solve_kernel, u + 1, slots, low(u), len(extra), outs), f"solve_{u + 1}",
            tuple(shapes[o] for o in outs), [SMEM] * 3 + [VMEM] * (3 + NZ + len(extra)),
            (places, *lists, ahead, inverses, *pieces, *extra),
            scratch=[pltpu.VMEM(four.shape, BF16), acc], flops=5 * one,
        )

    def products(u, levels_made, kept):
        return call(
            functools.partial(later_kernel, levels_made, slots, low(u)), f"later_{u}",
            (full,) * len(levels_made), [SMEM] * 2 + [VMEM] * 2, (*lists, kept),
            scratch=[acc], flops=4 * len(levels_made) * one,
        )

    def onward(u, value, packed):
        return [to_column(packed, u - 1, u)] + [to_column(value, u - 1, u, k) for k in (1, 2, 3)]

    x1, packed, kept = solve(0, [first] + to_next_rows(first), [], ("value", "packed", "kept"))
    pieces = onward(1, x1, packed)
    pieces, kept = after((pieces, kept))
    p30, p40 = products(0, (3, 4), kept)
    x2, packed, both, kept = solve(1, pieces, [], ("value", "packed", "both", "kept"))
    pieces = onward(2, x2, packed)
    spread12 = spread_x(both, 0, 1, places)
    p30, p40 = to_column(p30, 0, 2), to_column(p40, 0, 3)
    pieces, kept = after((pieces, kept))
    p41, = products(1, (4,), kept)
    x3, packed = solve(2, pieces, [p30], ("value", "packed"))
    pieces = onward(3, x3, packed)
    spread12 = spread_y(after((spread12, x3))[0], 1, here)
    spread3 = spread_x(x3, 1, 0, places)
    p41 = to_column(p41, 1, 3)
    x4, = solve(3, pieces, [p40, p41], ("value",))
    spread4 = spread_x(x4, 1, 1, places)
    spread3 = spread_y(after((spread3, x4))[0], 0, here)
    spread4 = spread_y(spread4, 1, here)
    out = jnp.concatenate([spread12(), spread3()[None], spread4()[None]])
    out = out + other_core(out)
    out = jnp.concatenate([first[None], out])
    return base_solution, out.astype(F32)[:, None]


def solution(mesh):
    placed = (
        P(AXES, None, None),
        P(AXES, None, None),
        P(None, "row", None, None),
        P(None, "row", None, None),
        P(None, AXES, None, None),
        P(None, AXES),
        P(None, AXES),
    )
    return jax.shard_map(
        on_device,
        mesh=mesh,
        in_specs=placed,
        out_specs=(P(AXES, None, None), P(None, "row", None, None)),
        check_vma=False,
    )
```

time: 758 us -> 141 us (0.19)
  waiting for transfers between devices: 599 us -> 33.7 us
  starting transfers between devices: 0.24 us -> 48.8 us
  loops' own time: 34 us -> 0 us
  local copies, waits for them, and re-layouts: 35 us -> 5.49 us
  matrix products: 26.4 us -> 0 us
  Pallas kernels: 0 us -> 19.1 us
  blocking collectives: 47.3 us -> 29.3 us
  between operations: 14.3 us -> 1.25 us
    psum x5 -> x0, waiting for transfers between devices: 587 us -> none  [settle(): summed = lax.psum(partial_value, 'col')]
    ppermute x0 -> x42, starting transfers between devices: none -> 48.8 us  [the longest x33 38.5 us: send(): return lax.ppermute(value, AXES, pairs)]
    all_gather x4 -> x0, blocking collectives: 47.3 us -> none  [on_device(): lax.all_gather(top_solution.astype(jnp.bfloat16)[None], 'row', axis=0, ti...]
    another operation x5 -> x0, loops' own time: 34 us -> none  [accumulate(): return lax.fori_loop(first_slot, end_slot, add_block, running_total)]
    ppermute x0 -> x42, waiting for transfers between devices: none -> 33.7 us  [the longest x6 14.5 us: to_next_rows(): lax.ppermute(value, 'row', [(z, (z + k) % NZ) for z in range(NZ)])]
    all_to_all x0 -> x2, blocking collectives: none -> 29.3 us  [over_plane(): lax.all_to_all(value, 'col', 0, 0, axis_index_groups=groups, tiled=True)]
    dot_general x18 -> x0, matrix products: 26.4 us -> none  [the longest x12 16.5 us: add_block(): jnp.dot(factor_block, operand, preferred_element_type=jnp.float32)]
    pallas_call x0 -> x15, Pallas kernels: none -> 19.1 us  [call(): pl.pallas_call(body, out_shape=outs, in_specs=in_specs, out_specs=out_spe...]
  transfers between devices with their start and end apart: 6 -> 42, of which waited for: 6 -> 17; matrix products, arithmetic and copies ran while one was open for 2% -> 1% of each run, Pallas kernels for 0% -> 7%
where the time goes in v3:
time: 141 us; the launch traced here: 139 us
  starting transfers between devices  48.8 us (35%)
  waiting for transfers between devices  33.7 us (24%)
  blocking collectives  29.3 us (21%)
  Pallas kernels  19.1 us (14%)
  local copies, waits for them, and re-layouts  5.49 us (4%)
  other arithmetic  1.5 us (1%)
    ppermute x33, starting transfers between devices, send(): return lax.ppermute(value, AXES, pairs)  38.5 us
    all_to_all x2, blocking collectives, over_plane(): lax.all_to_all(value, 'col', 0, 0, axis_index_groups=groups, tiled=True)  29.3 us
    pallas_call x15, Pallas kernels, call(): pl.pallas_call(body, out_shape=outs, in_specs=in_specs, out_specs=out_spe...  19.1 us
    ppermute x6, waiting for transfers between devices, to_next_rows(): lax.ppermute(value, 'row', [(z, (z + k) % NZ) for z in range(NZ)])  14.5 us
    ppermute x33, waiting for transfers between devices, send(): return lax.ppermute(value, AXES, pairs)  14.4 us
    ppermute x6, starting transfers between devices, to_next_rows(): lax.ppermute(value, 'row', [(z, (z + k) % NZ) for z in range(NZ)])  7.64 us
    ppermute x3, waiting for transfers between devices, other_core(): return lax.ppermute(value, 'col', [(c, c ^ 1) for c in range(NX * NY * 2)])  4.77 us
    unnamed x11, local copies, waits for them, and re-layouts  4.75 us
  transfers between devices with their start and end apart: 42, of which 17 were waited for; matrix products, arithmetic and copies ran while one was open for 1% of the time, Pallas kernels for 7%

profile of v3, /device:TPU:1, one launch (start us, length us, event | category | flops | bytes accessed | tf_op | source)
XLA Modules:
  0.0 139.1 jit_solution(12240546032626930623)
XLA Ops:
  4.2 4.6 %collective-permute-start.2 = (bf16[2,512,128]{2,1,0:T(8,128)(2,1)S(1)}, bf16[2,512,128]{2,1,0:T(8,128)(2,1)S(1)}, u32[]{:S(2)}, u32[]{:S(2)}) collective-permute-start(bf16[2,512,128]{2,1,0:T(8,128)(2,1)S(1)} %get-tuple-element.41.rest_0_), channel_id=1, source_target_pairs={{0,3},{1,0},{2,1},{3,2},{4,7},{5,4},{6,5},{7,6},{8,11},{9,8},{10,9... | collective-permute-start | bytes 786440 | tf_op jit(solution)/shard_map/ppermute | solution.py:189
  11.0 1.7 %copy-done = bf16[5,1,512,512]{3,2,1,0:T(8,128)(2,1)S(1)} copy-done((bf16[5,1,512,512]{3,2,1,0:T(8,128)(2,1)S(1)}, bf16[5,1,512,512]{3,2,1,0:T(8,128)(2,1)}, u32[]{:S(2)}) %copy-start) | copy-done | bytes 2621464
  12.7 3.8 %load_blocks.1 = (bf16[30,512,512]{2,1,0:T(8,128)(2,1)S(1)}, bf16[5,512,512]{2,1,0:T(8,128)(2,1)S(1)}) custom-call(s32[5,1]{1,0:T(8,128)S(1)} %copy.9.count_ref, bf16[5,6,512,512]{3,2,1,0:T(8,128)(2,1)} %factor_ref.1, bf16[5,512,512]{2,1,0:T(8,128)(2,1)S(1)} %bitcast.17), custom_call_target="tpu_custom_call" | custom-call | bytes 15728640 | tf_op jit(solution)/shard_map/load_blocks/pallas_call | solution.py:32
  16.6 2.7 %collective-permute-done.2.rest_3_ = bf16[2,512,128]{2,1,0:T(8,128)(2,1)S(1)} collective-permute-done((bf16[2,512,128]{2,1,0:T(8,128)(2,1)S(1)}, bf16[2,512,128]{2,1,0:T(8,128)(2,1)S(1)}, u32[]{:S(2)}, u32[]{:S(2)}) %collective-permute-start.2) | collective-permute-done | bytes 262176 | tf_op jit(solution)/shard_map/ppermute | solution.py:189
  19.3 4.3 %collective-permute-done.rest_1_ = bf16[2,512,128]{2,1,0:T(8,128)(2,1)S(1)} collective-permute-done((bf16[2,512,128]{2,1,0:T(8,128)(2,1)S(1)}, bf16[2,512,128]{2,1,0:T(8,128)(2,1)S(1)}, u32[]{:S(2)}, u32[]{:S(2)}) %collective-permute-start) | collective-permute-done | bytes 262176 | tf_op jit(solution)/shard_map/ppermute | solution.py:189
  23.5 2.9 %base_products.1 = (f32[16,80,128]{2,1,0:T(8,128)S(1)}, bf16[16,80,128]{2,1,0:T(8,128)(2,1)S(1)}) custom-call(s32[3]{0:T(128)S(1)} %pad_add_fusion.place_ref, s32[5,6]{1,0:T(8,128)S(1)} %copy-done.4, s32[5,1]{1,0:T(8,128)S(1)} %copy.10.count_ref, bf16[30,512,512]{2,1,0:T(8,128)(2,1)S(1)} %get-tuple-element.40.held_ref, ...), custom_call_target="tpu_custom_call" | custom-call | flops 1006632960 | tf_op jit(solution)/shard_map/base_products/pallas_call | solution.py:32
  26.6 1.6 %collective-permute-done.3.got_ref = bf16[16,80,128]{2,1,0:T(8,128)(2,1)S(1)} collective-permute-done((bf16[16,80,128]{2,1,0:T(8,128)(2,1)S(1)}, bf16[16,80,128]{2,1,0:T(8,128)(2,1)S(1)}, u32[]{:S(2)}, u32[]{:S(2)}) %collective-permute-start.3) | collective-permute-done | bytes 327712 | tf_op jit(solution)/shard_map/ppermute | solution.py:193
  28.3 18.6 %all_to_all.10.in_ref = bf16[16,80,128]{2,1,0:T(8,128)(2,1)S(1)} all-to-all(bf16[16,80,128]{2,1,0:T(8,128)(2,1)S(1)} %pair_sums.1), channel_id=1, replica_groups={{0,8,16,24,32,40,48,56,64,72,80,88,96,104,112,120},{4,12,20,28,36,44,52..., dimensions={0} | all-to-all | bytes 655360 | tf_op jit(solution)/shard_map/all_to_all | solution.py:198
  46.9 10.7 %all_to_all.11.half_ref = bf16[16,80,128]{2,1,0:T(8,128)(2,1)S(1)} all-to-all(bf16[16,80,128]{2,1,0:T(8,128)(2,1)S(1)} %sum_shares.1), channel_id=1, replica_groups={{0,8,16,24,32,40,48,56,64,72,80,88,96,104,112,120},{4,12,20,28,36,44,52..., dimensions={0} | all-to-all | bytes 655360 | tf_op jit(solution)/shard_map/all_to_all | solution.py:198
  57.6 2.5 %collective-permute-start.4 = (bf16[16,80,128]{2,1,0:T(8,128)(2,1)S(1)}, bf16[16,80,128]{2,1,0:T(8,128)(2,1)S(1)}, u32[]{:S(2)}, u32[]{:S(2)}) collective-permute-start(bf16[16,80,128]{2,1,0:T(8,128)(2,1)S(1)} %all_to_all.11.half_ref), channel_id=1, source_target_pairs={{0,4},{4,0},{8,12},{12,8},{16,20},{20,16},{24,28},{28,24},{32,36},... | collective-permute-start | bytes 983048 | tf_op jit(solution)/shard_map/ppermute | solution.py:193
  63.0 1.7 %collective-permute-start.6 = (bf16[512,128]{1,0:T(8,128)(2,1)S(1)}, bf16[512,128]{1,0:T(8,128)(2,1)S(1)}, u32[]{:S(2)}, u32[]{:S(2)}) collective-permute-start(bf16[512,128]{1,0:T(8,128)(2,1)S(1)} %get-tuple-element.45.rest_0_), channel_id=1, source_target_pairs={{0,2},{1,3},{2,0},{3,1},{4,6},{5,7},{6,4},{7,5},{8,10},{9,11},{10,... | collective-permute-start | bytes 393224 | tf_op jit(solution)/shard_map/ppermute | solution.py:189
  64.7 2.4 %collective-permute-done.7.rest_3_ = bf16[512,128]{1,0:T(8,128)(2,1)S(1)} collective-permute-done((bf16[512,128]{1,0:T(8,128)(2,1)S(1)}, bf16[512,128]{1,0:T(8,128)(2,1)S(1)}, u32[]{:S(2)}, u32[]{:S(2)}) %collective-permute-start.7) | collective-permute-done | bytes 131104 | tf_op jit(solution)/shard_map/ppermute | solution.py:189
  67.1 1.8 %collective-permute-done.6.rest_2_ = bf16[512,128]{1,0:T(8,128)(2,1)S(1)} collective-permute-done((bf16[512,128]{1,0:T(8,128)(2,1)S(1)}, bf16[512,128]{1,0:T(8,128)(2,1)S(1)}, u32[]{:S(2)}, u32[]{:S(2)}) %collective-permute-start.6) | collective-permute-done | bytes 131104 | tf_op jit(solution)/shard_map/ppermute | solution.py:189
  68.9 3.3 %collective-permute-done.5.rest_1_ = bf16[512,128]{1,0:T(8,128)(2,1)S(1)} collective-permute-done((bf16[512,128]{1,0:T(8,128)(2,1)S(1)}, bf16[512,128]{1,0:T(8,128)(2,1)S(1)}, u32[]{:S(2)}, u32[]{:S(2)}) %collective-permute-start.5) | collective-permute-done | bytes 131104 | tf_op jit(solution)/shard_map/ppermute | solution.py:189
  72.2 1.4 solve_1.1
  78.8 2.4 %collective-permute-done.11.rest_3_ = bf16[512,128]{1,0:T(8,128)(2,1)S(1)} collective-permute-done((bf16[512,128]{1,0:T(8,128)(2,1)S(1)}, bf16[512,128]{1,0:T(8,128)(2,1)S(1)}, u32[]{:S(2)}, u32[]{:S(2)}) %collective-permute-start.11) | collective-permute-done | bytes 131104 | tf_op jit(solution)/shard_map/ppermute | solution.py:181
  81.2 2.8 %collective-permute-done.10.rest_2_ = bf16[512,128]{1,0:T(8,128)(2,1)S(1)} collective-permute-done((bf16[512,128]{1,0:T(8,128)(2,1)S(1)}, bf16[512,128]{1,0:T(8,128)(2,1)S(1)}, u32[]{:S(2)}, u32[]{:S(2)}) %collective-permute-start.10) | collective-permute-done | bytes 131104 | tf_op jit(solution)/shard_map/ppermute | solution.py:181
  84.0 1.4 collective-permute-done.9.rest_1_
  85.4 2.6 %solve_2.1 = (bf16[512,128]{1,0:T(8,128)(2,1)S(1)}, bf16[2,512,128]{2,1,0:T(8,128)(2,1)S(1)}, bf16[2,512,128]{2,1,0:T(8,128)(2,1)S(1)}, bf16[4,512,128]{2,1,0:T(8,128)(2,1)S(1)}) custom-call(s32[3]{0:T(128)S(1)} %pad_add_fusion.place_ref, s32[5,6]{1,0:T(8,128)S(1)} %copy-done.4, s32[5,1]{1,0:T(8,128)S(1)} %copy.10.count_ref, ...), custom_call_target="tpu_custom_call" | custom-call | flops 335544320 | tf_op jit(solution)/shard_map/solve_2/pallas_call | solution.py:32
  88.1 1.3 collective-permute-start.15
  89.4 1.3 collective-permute-start.18
  90.7 1.3 collective-permute-start.17
  92.0 1.3 collective-permute-start.16
  107.3 5.5 %collective-permute-start.31 = (bf16[512,128]{1,0:T(8,128)(2,1)S(1)}, bf16[512,128]{1,0:T(8,128)(2,1)S(1)}, u32[]{:S(2)}, u32[]{:S(2)}) collective-permute-start(bf16[512,128]{1,0:T(8,128)(2,1)S(1)} %later_1.1), channel_id=1, source_target_pairs={{4,12},{5,13},{6,14},{7,15}} | collective-permute-start | bytes 393224 | tf_op jit(solution)/shard_map/ppermute | solution.py:181
  113.6 1.3 collective-permute-start.22
  114.9 1.3 collective-permute-start.21
  116.2 1.3 collective-permute-start.20
  125.7 3.7 %collective-permute-done.36.rest_1_ = bf16[512,128]{1,0:T(8,128)(2,1)S(1)} collective-permute-done((bf16[512,128]{1,0:T(8,128)(2,1)S(1)}, bf16[512,128]{1,0:T(8,128)(2,1)S(1)}, u32[]{:S(2)}, u32[]{:S(2)}) %collective-permute-start.36) | collective-permute-done | bytes 131104 | tf_op jit(solution)/shard_map/ppermute | solution.py:181
  130.0 1.3 collective-permute-start.40
  132.6 1.3 collective-permute-start.38
  134.5 1.3 collective-permute-done.38
  136.0 1.9 %collective-permute-done.41 = bf16[4,512,128]{2,1,0:T(8,128)(2,1)S(1)} collective-permute-done((bf16[4,512,128]{2,1,0:T(8,128)(2,1)S(1)}, bf16[4,512,128]{2,1,0:T(8,128)(2,1)S(1)}, u32[]{:S(2)}, u32[]{:S(2)}) %collective-permute-start.41) | collective-permute-done | bytes 524320 | tf_op jit(solution)/shard_map/ppermute | solution.py:193
  (88 shorter events, 40.5 us)
Async XLA Ops:
  4.2 15.0 %collective-permute-start.2 = (bf16[2,512,128]{2,1,0:T(8,128)(2,1)S(1)}, bf16[2,512,128]{2,1,0:T(8,128)(2,1)S(1)}, u32[]{:S(2)}, u32[]{:S(2)}) collective-permute-start(bf16[2,512,128]{2,1,0:T(8,128)(2,1)S(1)} %get-tuple-element.41.rest_0_), channel_id=1, source_target_pairs={{0,3},{1,0},{2,1},{3,2},{4,7},{5,4},{6,5},{7,6},{8,11},{9,8},{10,9... | collective-permute-start | bytes 786440 | tf_op jit(solution)/shard_map/ppermute | solution.py:189
  8.8 10.5 %collective-permute-start.1 = (bf16[2,512,128]{2,1,0:T(8,128)(2,1)S(1)}, bf16[2,512,128]{2,1,0:T(8,128)(2,1)S(1)}, u32[]{:S(2)}, u32[]{:S(2)}) collective-permute-start(bf16[2,512,128]{2,1,0:T(8,128)(2,1)S(1)} %get-tuple-element.41.rest_0_), channel_id=1, source_target_pairs={{0,2},{1,3},{2,0},{3,1},{4,6},{5,7},{6,4},{7,5},{8,10},{9,11},{10,... | collective-permute-start | bytes 786440 | tf_op jit(solution)/shard_map/ppermute | solution.py:189
  8.8 14.7 %collective-permute-start = (bf16[2,512,128]{2,1,0:T(8,128)(2,1)S(1)}, bf16[2,512,128]{2,1,0:T(8,128)(2,1)S(1)}, u32[]{:S(2)}, u32[]{:S(2)}) collective-permute-start(bf16[2,512,128]{2,1,0:T(8,128)(2,1)S(1)} %get-tuple-element.41.rest_0_), channel_id=1, source_target_pairs={{0,1},{1,2},{2,3},{3,0},{4,5},{5,6},{6,7},{7,4},{8,9},{9,10},{10,1... | collective-permute-start | bytes 786440 | tf_op jit(solution)/shard_map/ppermute | solution.py:189
  62.3 4.8 %collective-permute-start.7 = (bf16[512,128]{1,0:T(8,128)(2,1)S(1)}, bf16[512,128]{1,0:T(8,128)(2,1)S(1)}, u32[]{:S(2)}, u32[]{:S(2)}) collective-permute-start(bf16[512,128]{1,0:T(8,128)(2,1)S(1)} %get-tuple-element.45.rest_0_), channel_id=1, source_target_pairs={{0,3},{1,0},{2,1},{3,2},{4,7},{5,4},{6,5},{7,6},{8,11},{9,8},{10,9... | collective-permute-start | bytes 393224 | tf_op jit(solution)/shard_map/ppermute | solution.py:189
  63.0 5.9 %collective-permute-start.6 = (bf16[512,128]{1,0:T(8,128)(2,1)S(1)}, bf16[512,128]{1,0:T(8,128)(2,1)S(1)}, u32[]{:S(2)}, u32[]{:S(2)}) collective-permute-start(bf16[512,128]{1,0:T(8,128)(2,1)S(1)} %get-tuple-element.45.rest_0_), channel_id=1, source_target_pairs={{0,2},{1,3},{2,0},{3,1},{4,6},{5,7},{6,4},{7,5},{8,10},{9,11},{10,... | collective-permute-start | bytes 393224 | tf_op jit(solution)/shard_map/ppermute | solution.py:189
  64.7 7.6 %collective-permute-start.5 = (bf16[512,128]{1,0:T(8,128)(2,1)S(1)}, bf16[512,128]{1,0:T(8,128)(2,1)S(1)}, u32[]{:S(2)}, u32[]{:S(2)}) collective-permute-start(bf16[512,128]{1,0:T(8,128)(2,1)S(1)} %get-tuple-element.45.rest_0_), channel_id=1, source_target_pairs={{0,1},{1,2},{2,3},{3,0},{4,5},{5,6},{6,7},{7,4},{8,9},{9,10},{10,1... | collective-permute-start | bytes 393224 | tf_op jit(solution)/shard_map/ppermute | solution.py:189
  73.6 11.8 %collective-permute-start.8 = (bf16[2,512,128]{2,1,0:T(8,128)(2,1)S(1)}, bf16[2,512,128]{2,1,0:T(8,128)(2,1)S(1)}, u32[]{:S(2)}, u32[]{:S(2)}) collective-permute-start(bf16[2,512,128]{2,1,0:T(8,128)(2,1)S(1)} %get-tuple-element.47), channel_id=1, source_target_pairs={{0,4},{1,5},{2,6},{3,7}} | collective-permute-start | bytes 786440 | tf_op jit(solution)/shard_map/ppermute | solution.py:181
  74.9 6.3 %collective-permute-start.11 = (bf16[512,128]{1,0:T(8,128)(2,1)S(1)}, bf16[512,128]{1,0:T(8,128)(2,1)S(1)}, u32[]{:S(2)}, u32[]{:S(2)}) collective-permute-start(bf16[512,128]{1,0:T(8,128)(2,1)S(1)} %get-tuple-element.48), channel_id=1, source_target_pairs={{0,7},{1,4},{2,5},{3,6}} | collective-permute-start | bytes 393224 | tf_op jit(solution)/shard_map/ppermute | solution.py:181
  76.2 7.8 %collective-permute-start.10 = (bf16[512,128]{1,0:T(8,128)(2,1)S(1)}, bf16[512,128]{1,0:T(8,128)(2,1)S(1)}, u32[]{:S(2)}, u32[]{:S(2)}) collective-permute-start(bf16[512,128]{1,0:T(8,128)(2,1)S(1)} %get-tuple-element.48), channel_id=1, source_target_pairs={{0,6},{1,7},{2,4},{3,5}} | collective-permute-start | bytes 393224 | tf_op jit(solution)/shard_map/ppermute | solution.py:181
  77.5 7.9 %collective-permute-start.9 = (bf16[512,128]{1,0:T(8,128)(2,1)S(1)}, bf16[512,128]{1,0:T(8,128)(2,1)S(1)}, u32[]{:S(2)}, u32[]{:S(2)}) collective-permute-start(bf16[512,128]{1,0:T(8,128)(2,1)S(1)} %get-tuple-element.48), channel_id=1, source_target_pairs={{0,5},{1,6},{2,7},{3,4}} | collective-permute-start | bytes 393224 | tf_op jit(solution)/shard_map/ppermute | solution.py:181
  88.1 12.9 %collective-permute-start.15 = (bf16[2,512,128]{2,1,0:T(8,128)(2,1)S(1)}, bf16[2,512,128]{2,1,0:T(8,128)(2,1)S(1)}, u32[]{:S(2)}, u32[]{:S(2)}) collective-permute-start(bf16[2,512,128]{2,1,0:T(8,128)(2,1)S(1)} %get-tuple-element.55), channel_id=1, source_target_pairs={{4,8},{5,9},{6,10},{7,11}} | collective-permute-start | bytes 786440 | tf_op jit(solution)/shard_map/ppermute | solution.py:181
  89.4 6.1 %collective-permute-start.18 = (bf16[512,128]{1,0:T(8,128)(2,1)S(1)}, bf16[512,128]{1,0:T(8,128)(2,1)S(1)}, u32[]{:S(2)}, u32[]{:S(2)}) collective-permute-start(bf16[512,128]{1,0:T(8,128)(2,1)S(1)} %get-tuple-element.56), channel_id=1, source_target_pairs={{4,11},{5,8},{6,9},{7,10}} | collective-permute-start | bytes 393224 | tf_op jit(solution)/shard_map/ppermute | solution.py:181
  90.7 7.3 %collective-permute-start.17 = (bf16[512,128]{1,0:T(8,128)(2,1)S(1)}, bf16[512,128]{1,0:T(8,128)(2,1)S(1)}, u32[]{:S(2)}, u32[]{:S(2)}) collective-permute-start(bf16[512,128]{1,0:T(8,128)(2,1)S(1)} %get-tuple-element.56), channel_id=1, source_target_pairs={{4,10},{5,11},{6,8},{7,9}} | collective-permute-start | bytes 393224 | tf_op jit(solution)/shard_map/ppermute | solution.py:181
  92.0 7.7 %collective-permute-start.16 = (bf16[512,128]{1,0:T(8,128)(2,1)S(1)}, bf16[512,128]{1,0:T(8,128)(2,1)S(1)}, u32[]{:S(2)}, u32[]{:S(2)}) collective-permute-start(bf16[512,128]{1,0:T(8,128)(2,1)S(1)} %get-tuple-element.56), channel_id=1, source_target_pairs={{4,9},{5,10},{6,11},{7,8}} | collective-permute-start | bytes 393224 | tf_op jit(solution)/shard_map/ppermute | solution.py:181
  94.1 7.5 %collective-permute-start.19 = (bf16[512,128]{1,0:T(8,128)(2,1)S(1)}, bf16[512,128]{1,0:T(8,128)(2,1)S(1)}, u32[]{:S(2)}, u32[]{:S(2)}) collective-permute-start(bf16[512,128]{1,0:T(8,128)(2,1)S(1)} %get-tuple-element.63), channel_id=1, source_target_pairs={{0,8},{1,9},{2,10},{3,11}} | collective-permute-start | bytes 393224 | tf_op jit(solution)/shard_map/ppermute | solution.py:181
  95.5 8.8 %collective-permute-start.14 = (bf16[2,512,128]{2,1,0:T(8,128)(2,1)S(1)}, bf16[2,512,128]{2,1,0:T(8,128)(2,1)S(1)}, u32[]{:S(2)}, u32[]{:S(2)}) collective-permute-start(bf16[2,512,128]{2,1,0:T(8,128)(2,1)S(1)} %get-tuple-element.54.value_ref), channel_id=1, source_target_pairs={{4,20},{5,21},{6,22},{7,23}} | collective-permute-start | bytes 786440 | tf_op jit(solution)/shard_map/ppermute | solution.py:181
  97.9 8.0 %collective-permute-start.13 = (bf16[2,512,128]{2,1,0:T(8,128)(2,1)S(1)}, bf16[2,512,128]{2,1,0:T(8,128)(2,1)S(1)}, u32[]{:S(2)}, u32[]{:S(2)}) collective-permute-start(bf16[2,512,128]{2,1,0:T(8,128)(2,1)S(1)} %get-tuple-element.54.value_ref), channel_id=1, source_target_pairs={{4,28},{5,29},{6,30},{7,31}} | collective-permute-start | bytes 786440 | tf_op jit(solution)/shard_map/ppermute | solution.py:181
  99.7 7.0 %collective-permute-start.12 = (bf16[2,512,128]{2,1,0:T(8,128)(2,1)S(1)}, bf16[2,512,128]{2,1,0:T(8,128)(2,1)S(1)}, u32[]{:S(2)}, u32[]{:S(2)}) collective-permute-start(bf16[2,512,128]{2,1,0:T(8,128)(2,1)S(1)} %get-tuple-element.54.value_ref), channel_id=1, source_target_pairs={{4,12},{5,13},{6,14},{7,15}} | collective-permute-start | bytes 786440 | tf_op jit(solution)/shard_map/ppermute | solution.py:181
  102.9 4.5 %collective-permute-start.29 = (bf16[512,128]{1,0:T(8,128)(2,1)S(1)}, bf16[512,128]{1,0:T(8,128)(2,1)S(1)}, u32[]{:S(2)}, u32[]{:S(2)}) collective-permute-start(bf16[512,128]{1,0:T(8,128)(2,1)S(1)} %get-tuple-element.64.value_ref), channel_id=1, source_target_pairs={{8,15},{9,12},{10,13},{11,14}} | collective-permute-start | bytes 393224 | tf_op jit(solution)/shard_map/ppermute | solution.py:181
  103.5 14.7 %collective-permute-start.26 = (bf16[2,512,128]{2,1,0:T(8,128)(2,1)S(1)}, bf16[2,512,128]{2,1,0:T(8,128)(2,1)S(1)}, u32[]{:S(2)}, u32[]{:S(2)}) collective-permute-start(bf16[2,512,128]{2,1,0:T(8,128)(2,1)S(1)} %get-tuple-element.66), channel_id=1, source_target_pairs={{8,12},{9,13},{10,14},{11,15}} | collective-permute-start | bytes 786440 | tf_op jit(solution)/shard_map/ppermute | solution.py:181
  104.2 9.3 %collective-permute-start.28 = (bf16[512,128]{1,0:T(8,128)(2,1)S(1)}, bf16[512,128]{1,0:T(8,128)(2,1)S(1)}, u32[]{:S(2)}, u32[]{:S(2)}) collective-permute-start(bf16[512,128]{1,0:T(8,128)(2,1)S(1)} %get-tuple-element.64.value_ref), channel_id=1, source_target_pairs={{8,14},{9,15},{10,12},{11,13}} | collective-permute-start | bytes 393224 | tf_op jit(solution)/shard_map/ppermute | solution.py:181
  106.0 8.9 %collective-permute-start.27 = (bf16[512,128]{1,0:T(8,128)(2,1)S(1)}, bf16[512,128]{1,0:T(8,128)(2,1)S(1)}, u32[]{:S(2)}, u32[]{:S(2)}) collective-permute-start(bf16[512,128]{1,0:T(8,128)(2,1)S(1)} %get-tuple-element.64.value_ref), channel_id=1, source_target_pairs={{8,13},{9,14},{10,15},{11,12}} | collective-permute-start | bytes 393224 | tf_op jit(solution)/shard_map/ppermute | solution.py:181
  106.6 9.6 %collective-permute-start.25 = (bf16[512,128]{1,0:T(8,128)(2,1)S(1)}, bf16[512,128]{1,0:T(8,128)(2,1)S(1)}, u32[]{:S(2)}, u32[]{:S(2)}) collective-permute-start(bf16[512,128]{1,0:T(8,128)(2,1)S(1)} %get-tuple-element.64.value_ref), channel_id=1, source_target_pairs={{8,24},{9,25},{10,26},{11,27}} | collective-permute-start | bytes 393224 | tf_op jit(solution)/shard_map/ppermute | solution.py:181
  107.3 10.2 %collective-permute-start.31 = (bf16[512,128]{1,0:T(8,128)(2,1)S(1)}, bf16[512,128]{1,0:T(8,128)(2,1)S(1)}, u32[]{:S(2)}, u32[]{:S(2)}) collective-permute-start(bf16[512,128]{1,0:T(8,128)(2,1)S(1)} %later_1.1), channel_id=1, source_target_pairs={{4,12},{5,13},{6,14},{7,15}} | collective-permute-start | bytes 393224 | tf_op jit(solution)/shard_map/ppermute | solution.py:181
  113.6 8.7 %collective-permute-start.22 = (bf16[2,512,128]{2,1,0:T(8,128)(2,1)S(1)}, bf16[2,512,128]{2,1,0:T(8,128)(2,1)S(1)}, u32[]{:S(2)}, u32[]{:S(2)}) collective-permute-start(bf16[2,512,128]{2,1,0:T(8,128)(2,1)S(1)} %picked.3), channel_id=1, source_target_pairs={{4,68},{5,69},{6,70},{7,71},{12,76},{13,77},{14,78},{15,79},{20,84... | collective-permute-start | bytes 786440 | tf_op jit(solution)/shard_map/ppermute | solution.py:181
  114.9 8.0 %collective-permute-start.21 = (bf16[2,512,128]{2,1,0:T(8,128)(2,1)S(1)}, bf16[2,512,128]{2,1,0:T(8,128)(2,1)S(1)}, u32[]{:S(2)}, u32[]{:S(2)}) collective-permute-start(bf16[2,512,128]{2,1,0:T(8,128)(2,1)S(1)} %picked.3), channel_id=1, source_target_pairs={{4,100},{5,101},{6,102},{7,103},{12,108},{13,109},{14,110},{15,111... | collective-permute-start | bytes 786440 | tf_op jit(solution)/shard_map/ppermute | solution.py:181
  116.2 7.4 %collective-permute-start.20 = (bf16[2,512,128]{2,1,0:T(8,128)(2,1)S(1)}, bf16[2,512,128]{2,1,0:T(8,128)(2,1)S(1)}, u32[]{:S(2)}, u32[]{:S(2)}) collective-permute-start(bf16[2,512,128]{2,1,0:T(8,128)(2,1)S(1)} %picked.3), channel_id=1, source_target_pairs={{4,36},{5,37},{6,38},{7,39},{12,44},{13,45},{14,46},{15,47},{20,52... | collective-permute-start | bytes 786440 | tf_op jit(solution)/shard_map/ppermute | solution.py:181
  120.3 4.7 %collective-permute-start.37 = (bf16[512,128]{1,0:T(8,128)(2,1)S(1)}, bf16[512,128]{1,0:T(8,128)(2,1)S(1)}, u32[]{:S(2)}, u32[]{:S(2)}) collective-permute-start(bf16[512,128]{1,0:T(8,128)(2,1)S(1)} %solve_4.1.value_ref), channel_id=1, source_target_pairs={{12,28},{13,29},{14,30},{15,31}} | collective-permute-start | bytes 393224 | tf_op jit(solution)/shard_map/ppermute | solution.py:181
  121.6 11.0 %collective-permute-start.34 = (bf16[512,128]{1,0:T(8,128)(2,1)S(1)}, bf16[512,128]{1,0:T(8,128)(2,1)S(1)}, u32[]{:S(2)}, u32[]{:S(2)}) collective-permute-start(bf16[512,128]{1,0:T(8,128)(2,1)S(1)} %picked.4), channel_id=1, source_target_pairs={{0,64},{1,65},{2,66},{3,67},{8,72},{9,73},{10,74},{11,75},{16,80},... | collective-permute-start | bytes 393224 | tf_op jit(solution)/shard_map/ppermute | solution.py:181
  122.3 11.6 %collective-permute-start.33 = (bf16[512,128]{1,0:T(8,128)(2,1)S(1)}, bf16[512,128]{1,0:T(8,128)(2,1)S(1)}, u32[]{:S(2)}, u32[]{:S(2)}) collective-permute-start(bf16[512,128]{1,0:T(8,128)(2,1)S(1)} %picked.4), channel_id=1, source_target_pairs={{0,96},{1,97},{2,98},{3,99},{8,104},{9,105},{10,106},{11,107},{16,... | collective-permute-start | bytes 393224 | tf_op jit(solution)/shard_map/ppermute | solution.py:181
  123.0 11.0 %collective-permute-start.32 = (bf16[512,128]{1,0:T(8,128)(2,1)S(1)}, bf16[512,128]{1,0:T(8,128)(2,1)S(1)}, u32[]{:S(2)}, u32[]{:S(2)}) collective-permute-start(bf16[512,128]{1,0:T(8,128)(2,1)S(1)} %picked.4), channel_id=1, source_target_pairs={{0,32},{1,33},{2,34},{3,35},{8,40},{9,41},{10,42},{11,43},{16,48},... | collective-permute-start | bytes 393224 | tf_op jit(solution)/shard_map/ppermute | solution.py:181
  123.7 5.7 %collective-permute-start.36 = (bf16[512,128]{1,0:T(8,128)(2,1)S(1)}, bf16[512,128]{1,0:T(8,128)(2,1)S(1)}, u32[]{:S(2)}, u32[]{:S(2)}) collective-permute-start(bf16[512,128]{1,0:T(8,128)(2,1)S(1)} %solve_4.1.value_ref), channel_id=1, source_target_pairs={{12,4},{13,5},{14,6},{15,7}} | collective-permute-start | bytes 393224 | tf_op jit(solution)/shard_map/ppermute | solution.py:181
  (15 other events, 80.0 us)

commit v4 on v3

v4 whole, which is shorter than its diff:
```python
import functools

import jax
import jax.numpy as jnp
from jax import lax
from jax.experimental import pallas as pl
from jax.experimental.pallas import tpu as pltpu
from jax.sharding import PartitionSpec as P

BF16, F32 = jnp.bfloat16, jnp.float32
AXES = ("col", "row")
NX = NY = NZ = 4
BOTH = (0, 1)
SMEM = pl.BlockSpec(memory_space=pltpu.SMEM)
VMEM = pl.BlockSpec(memory_space=pltpu.VMEM)
HBM = pl.BlockSpec(memory_space=pltpu.HBM)


def column(x, y, core):
    return (y * NX + x) * 2 + core


def place(x, y, core, z):
    return column(x, y, core) * NZ + z


def dot(a, b):
    return jnp.dot(a, b, preferred_element_type=F32)


def call(body, name, outs, in_specs, args, scratch=(), flops=0, nbytes=0, out_specs=None):
    return pl.pallas_call(
        body,
        out_shape=outs,
        in_specs=in_specs,
        out_specs=out_specs or jax.tree.map(lambda _: VMEM, outs),
        scratch_shapes=list(scratch),
        compiler_params=pltpu.CompilerParams(vmem_limit_bytes=24 * 1024 * 1024),
        cost_estimate=pl.CostEstimate(flops=flops, bytes_accessed=nbytes, transcendentals=0),
        name=name,
    )(*args)


def base_solve_kernel(inverse_ref, rhs_ref, out_ref, rounded_ref, inverse, rhs, value, sems):
    count = rhs_ref.shape[0]
    reads, writes = [], []
    for i in range(count):
        reads.append((
            pltpu.make_async_copy(inverse_ref.at[i], inverse.at[i], sems.at[0, i]),
            pltpu.make_async_copy(rhs_ref.at[i], rhs.at[i], sems.at[1, i]),
        ))
        for copy in reads[-1]:
            copy.start()
    for i in range(count):
        for copy in reads[i]:
            copy.wait()
        value[i] = dot(inverse[i], rhs[i].astype(BF16))
        writes.append(pltpu.make_async_copy(value.at[i], out_ref.at[i], sems.at[2, i]))
        writes[-1].start()
        rounded = value[i].astype(BF16)
        for v in range(rounded_ref.shape[0]):
            rounded_ref[v, i] = rounded
    for copy in writes:
        copy.wait()


def add_products(total, level, slots, low, high, operand_of, table, held_ref, ready=None):
    for slot in range(slots):
        source = table[level, slot]

        @pl.when(slot < table[level, slots])
        def _():
            if ready is not None:
                ready(level, slot).wait()

            @pl.when((source >= low) & (source < high))
            def _():
                total[...] += dot(held_ref[level * slots + slot], operand_of(source - low))


def base_kernel(levels, slots, table, factor_ref, inverse_ref, operands, keep_ref, send_ref, held_ref, kept_ref,
                total, sems, other_sem):
    def block_copy(level, slot):
        at = level * slots + slot
        return pltpu.make_async_copy(factor_ref.at[level, slot], held_ref.at[at], sems.at[at])

    for level in range(levels):
        for slot in range(slots):
            @pl.when(slot < table[level, slots])
            def _():
                block_copy(level, slot).start()
    inverses = pltpu.make_async_copy(inverse_ref, kept_ref, other_sem)
    inverses.start()
    core, per_row = table[levels, 1], operands.shape[1]
    shares, some = keep_ref.shape[0], keep_ref.shape[1] // levels
    mine = pl.multiple_of(core * shares * some, shares * some)
    other = pl.multiple_of((1 - core) * shares * some, shares * some)
    for level in range(levels):
        total[...] = jnp.zeros_like(total)
        add_products(total, level, slots, 0, NZ * per_row, lambda q: operands[q // per_row, lax.rem(q, per_row)],
                     table, held_ref, block_copy)
        for share in range(shares):
            place_in = pl.ds(level * some, some)
            keep_ref[share, place_in] = total[pl.ds(mine + share * some, some)]
            send_ref[share, place_in] = total[pl.ds(other + share * some, some)].astype(BF16)
    inverses.wait()


def first_kernel(table, half_ref, other_ref, apex_ref, inverse_ref, ahead_ref, out_ref, target):
    levels = apex_ref.shape[0]
    core = table[levels, 1]
    shares, some = half_ref.shape[0], half_ref.shape[1] // levels
    for level in range(levels):
        to = target if level == 0 else ahead_ref.at[level - 1]
        for ref, side in ((half_ref, core), (other_ref, 1 - core)):
            for share in range(shares):
                rows = pl.ds(pl.multiple_of(side * shares * some, shares * some) + share * some, some)
                to[rows] = apex_ref[level, rows] - ref[share, pl.ds(level * some, some)].astype(F32)
        if level == 0:
            out_ref[...] = dot(inverse_ref[0], target[...].astype(BF16)).astype(BF16)


def sum_kernel(in_ref, out_ref):
    total = in_ref[0].astype(F32)
    for i in range(1, in_ref.shape[0]):
        total = total + in_ref[i].astype(F32)
    for i in range(in_ref.shape[0]):
        out_ref[i] = total.astype(BF16)


def solve_kernel(level, slots, low, extra, outs, table, held_ref, ahead_ref, inverse_ref,
                 *rest):
    pieces, more, outs_refs = rest[:NZ], rest[NZ : NZ + extra], rest[NZ + extra : NZ + extra + len(outs)]
    operands, total = rest[NZ + extra + len(outs) :]
    named = dict(zip(outs, outs_refs))
    nearest = pieces[0]
    chained = len(nearest.shape) == 3
    row = table[inverse_ref.shape[0], 0]
    operands[row] = nearest[0] if chained else nearest[...]
    for k in range(1, NZ):
        operands[lax.rem(row + NZ - k, NZ)] = pieces[k][...]
    lists = (table, held_ref)
    total[...] = nearest[1].astype(F32) if chained else jnp.zeros_like(total)
    for ref in more:
        total[...] += ref[...].astype(F32)
    add_products(total, level, slots, low, low + NZ, lambda q: operands[q], *lists)
    correction = (ahead_ref[level - 1] - total[...]).astype(BF16)
    value = dot(inverse_ref[level], correction).astype(BF16)
    named["value"][...] = value
    if "packed" in named:
        named["packed"][0] = value
        total[...] = jnp.zeros_like(total)
        add_products(total, level + 1, slots, low, low + NZ, lambda q: operands[q], *lists)
        named["packed"][1] = total[...].astype(BF16)
    if "both" in named:
        named["both"][0] = operands[row]
        named["both"][1] = value
    if "kept" in named:
        for v in range(NZ):
            named["kept"][v] = operands[v]


def later_kernel(levels, slots, low, table, held_ref, operands, *rest):
    out_refs, total = rest[:-1], rest[-1]
    for level, out_ref in zip(levels, out_refs):
        total[...] = jnp.zeros_like(total)
        add_products(total, level, slots, low, low + NZ, lambda q: operands[q], table, held_ref)
        out_ref[...] = total[...].astype(BF16)


def pair_kernel(keep_ref, got_ref, out_ref):
    out_ref[...] = (keep_ref[...] + got_ref[...].astype(F32)).astype(BF16)


def pick_kernel(levels, column_of, table, value_ref, *rest):
    got, out_ref = rest[:-1], rest[-1]
    came = got[0][...]
    for ref in got[1:]:
        came = came + ref[...]
    out_ref[...] = jnp.where(table[levels, 2] == column_of, value_ref[...], came)


def pick(column_of, table, value, got, name):
    return call(
        functools.partial(pick_kernel, table.shape[0] - 1, column_of), name, jax.ShapeDtypeStruct(value.shape, value.dtype),
        [SMEM] + [VMEM] * (1 + len(got)), (table, value, *got),
    )


def send(value, pairs):
    return lax.ppermute(value, AXES, pairs)


def to_column(value, sender, receiver, k=0):
    return send(value, [(sender * NZ + z, receiver * NZ + (z + k) % NZ) for z in range(NZ)])


def other_core(value):
    return lax.ppermute(value, "col", [(c, c ^ 1) for c in range(NX * NY * 2)])


def over_plane(value):
    groups = [[column(x, y, core) for y in range(NY) for x in range(NX)] for core in BOTH]
    return lax.all_to_all(value, "col", 0, 0, axis_index_groups=groups, tiled=True)


def spread_x(value, x0, core, table):
    got = [
        send(value, [(place(x0, 0, core, z), place((x0 + dx) % NX, 0, core, z)) for z in range(NZ)])
        for dx in (1, 3, 2)
    ]
    return pick(column(x0, 0, core), table, value, got, "picked")


def spread_y(value, core, here):
    got = [
        send(value, [(place(x, 0, core, z), place(x, y, core, z)) for x in range(NX) for z in range(NZ)])
        for y in (1, 3, 2)
    ]
    own = (here < 2 * NX) & (here % 2 == core)
    return lambda: jnp.where(own, value, got[0] + got[1] + got[2])


def on_device(base_rhs, base_inverse, apex, top_inverse, factor_blocks, block_source, block_count):
    levels, slots = block_source.shape[0], factor_blocks.shape[1]
    per_row, size, samples = base_rhs.shape
    shares = NX * NY
    some = size // 2 // shares
    block = factor_blocks.shape[2:]
    here, row = lax.axis_index("col"), lax.axis_index("row")
    core = here % 2
    table = jnp.concatenate([block_source, block_count], axis=1)
    table = jnp.concatenate([table, jnp.pad(jnp.stack([row, core, here]), (0, slots - 2))[None].astype(jnp.int32)])
    after = lax.optimization_barrier
    in_hbm = functools.partial(pltpu.with_memory_space_constraint, memory_space=pltpu.HBM)
    one = 2 * size * size * samples
    full = jax.ShapeDtypeStruct((size, samples), BF16)

    base_solution, rounded = call(
        base_solve_kernel, "base_solve",
        (jax.ShapeDtypeStruct(base_rhs.shape, F32), jax.ShapeDtypeStruct((NZ,) + base_rhs.shape, BF16)),
        [HBM, HBM], (in_hbm(base_inverse), in_hbm(base_rhs)), flops=per_row * one, nbytes=6 * base_rhs.size + 2 * base_inverse.size,
        scratch=[
            pltpu.VMEM(base_inverse.shape, BF16), pltpu.VMEM(base_rhs.shape, F32), pltpu.VMEM(base_rhs.shape, F32),
            pltpu.SemaphoreType.DMA((3, per_row)),
        ],
        out_specs=(HBM, VMEM),
    )
    rounded, table = after((rounded, table))
    operands = lax.all_to_all(rounded, "row", 0, 0, tiled=True)
    keep, give, held, inverses = call(
        functools.partial(base_kernel, levels, slots), "base_products",
        (
            jax.ShapeDtypeStruct((shares, levels * some, samples), F32),
            jax.ShapeDtypeStruct((shares, levels * some, samples), BF16),
            pltpu.VMEM((levels * slots,) + block, BF16),
            pltpu.VMEM((levels,) + block, BF16),
        ),
        [SMEM, HBM, HBM, VMEM], (table, factor_blocks, in_hbm(top_inverse[:, 0]), operands),
        scratch=[
            pltpu.VMEM((size, samples), F32), pltpu.SemaphoreType.DMA((levels * slots,)), pltpu.SemaphoreType.DMA,
        ],
        flops=levels * slots * one // 2, nbytes=2 * factor_blocks.size,
    )
    held, inverses = (pltpu.with_memory_space_constraint(x, pltpu.VMEM) for x in (held, inverses))
    lists = (table, held)
    pair = call(
        pair_kernel, "pair_sums", jax.ShapeDtypeStruct(give.shape, BF16), [VMEM] * 2, (keep, other_core(give))
    )
    share = call(sum_kernel, "sum_shares", jax.ShapeDtypeStruct(pair.shape, BF16), [VMEM], (over_plane(pair),))
    half = over_plane(share)
    other = other_core(half)
    ahead, first = call(
        first_kernel, "solve_0", (jax.ShapeDtypeStruct((levels - 1, size, samples), F32), full),
        [SMEM] + [VMEM] * 4, (table, half, other, apex[:, 0], inverses),
        scratch=[pltpu.VMEM((size, samples), F32)], flops=one,
    )
    two = jax.ShapeDtypeStruct((2, size, samples), BF16)
    four = jax.ShapeDtypeStruct((NZ, size, samples), BF16)
    acc = pltpu.VMEM((size, samples), F32)

    def low(u):
        return per_row * NZ + u * NZ

    def solve(u, pieces, extra, outs):
        shapes = {"value": full, "packed": two, "both": two, "kept": four}
        return call(
            functools.partial(solve_kernel, u + 1, slots, low(u), len(extra), outs), f"solve_{u + 1}",
            tuple(shapes[o] for o in outs), [SMEM] + [VMEM] * (3 + NZ + len(extra)),
            (*lists, ahead, inverses, *pieces, *extra),
            scratch=[pltpu.VMEM(four.shape, BF16), acc], flops=5 * one,
        )

    def products(u, levels_made, kept):
        return call(
            functools.partial(later_kernel, levels_made, slots, low(u)), f"later_{u}",
            (full,) * len(levels_made), [SMEM] + [VMEM] * 2, (*lists, kept),
            scratch=[acc], flops=4 * len(levels_made) * one,
        )

    def onward(u, value, packed):
        return [to_column(packed, u - 1, u)] + [to_column(value, u - 1, u, k) for k in (1, 2, 3)]

    x1, packed, kept = solve(0, [first] + [to_column(first, 1, 0, k) for k in (1, 2, 3)], [], ("value", "packed", "kept"))
    pieces = onward(1, x1, packed)
    pieces, kept = after((pieces, kept))
    p30, p40 = products(0, (3, 4), kept)
    x2, packed, both, kept = solve(1, pieces, [], ("value", "packed", "both", "kept"))
    pieces = onward(2, x2, packed)
    spread12 = spread_x(both, 0, 1, table)
    p30, p40 = to_column(p30, 0, 2), to_column(p40, 0, 3)
    pieces, kept = after((pieces, kept))
    p41, = products(1, (4,), kept)
    x3, packed = solve(2, pieces, [p30], ("value", "packed"))
    pieces = onward(3, x3, packed)
    p41 = to_column(p41, 1, 3)
    x4, = solve(3, pieces, [p40, p41], ("value",))
    spread4 = spread_x(x4, 1, 1, table)
    spread12 = spread_y(after((spread12, x4))[0], 1, here)
    spread3 = spread_x(after((x3, x4))[0], 1, 0, table)
    spread3 = spread_y(spread3, 0, here)
    spread4 = spread_y(spread4, 1, here)
    out = jnp.concatenate([spread12(), spread3()[None], spread4()[None]])
    out = out + other_core(out)
    out = jnp.concatenate([first[None], out])
    return base_solution, out.astype(F32)[:, None]


def solution(mesh):
    placed = (
        P(AXES, None, None),
        P(AXES, None, None),
        P(None, "row", None, None),
        P(None, "row", None, None),
        P(None, AXES, None, None),
        P(None, AXES),
        P(None, AXES),
    )
    return jax.shard_map(
        on_device,
        mesh=mesh,
        in_specs=placed,
        out_specs=(P(AXES, None, None), P(None, "row", None, None)),
        check_vma=False,
    )
```

time: 141 us -> 146 us (1.035)
  blocking collectives: 29.3 us -> 47.6 us
  waiting for transfers between devices: 33.7 us -> 23.1 us
  local copies, waits for them, and re-layouts: 5.49 us -> 0.76 us
    all_to_all x0 -> x1, blocking collectives: none -> 19.8 us  [on_device(): operands = lax.all_to_all(rounded, 'row', 0, 0, tiled=True)]
    ppermute x6 -> x0, waiting for transfers between devices: 14.5 us -> none  [to_next_rows(): lax.ppermute(value, 'row', [(z, (z + k) % NZ) for z in range(NZ)])]
    ppermute x33 -> x36, starting transfers between devices: 38.5 us -> 46.5 us  [send(): return lax.ppermute(value, AXES, pairs)]
    ppermute x6 -> x0, starting transfers between devices: 7.64 us -> none  [to_next_rows(): lax.ppermute(value, 'row', [(z, (z + k) % NZ) for z in range(NZ)])]
    ppermute x33 -> x36, waiting for transfers between devices: 14.4 us -> 18.7 us  [send(): return lax.ppermute(value, AXES, pairs)]
    unnamed x11 -> x3, local copies, waits for them, and re-layouts: 4.75 us -> 0.75 us
    all_to_all x2, blocking collectives: 29.3 us -> 27.8 us  [over_plane(): lax.all_to_all(value, 'col', 0, 0, axis_index_groups=groups, tiled=True)]
    pallas_call x15 -> x14, Pallas kernels: 19.1 us -> 19.6 us  [call(): pl.pallas_call(body, out_shape=outs, in_specs=in_specs, out_specs=out_spe...]
  transfers between devices with their start and end apart: 42 -> 39, of which waited for: 17 -> 13; matrix products, arithmetic and copies ran while one was open for 1% -> 0% of each run, Pallas kernels for 7% -> 4%
where the time goes in v4:
time: 146 us; the launch traced here: 145 us
  starting transfers between devices  50.1 us (34%)
  blocking collectives  47.6 us (33%)
  waiting for transfers between devices  23.1 us (16%)
  Pallas kernels  19.6 us (13%)
  other arithmetic  2.26 us (2%)
    ppermute x36, starting transfers between devices, send(): return lax.ppermute(value, AXES, pairs)  46.5 us
    all_to_all x2, blocking collectives, over_plane(): lax.all_to_all(value, 'col', 0, 0, axis_index_groups=groups, tiled=True)  27.8 us
    all_to_all x1, blocking collectives, on_device(): operands = lax.all_to_all(rounded, 'row', 0, 0, tiled=True)  19.8 us
    pallas_call x14, Pallas kernels, call(): pl.pallas_call(body, out_shape=outs, in_specs=in_specs, out_specs=out_spe...  19.6 us
    ppermute x36, waiting for transfers between devices, send(): return lax.ppermute(value, AXES, pairs)  18.7 us
    ppermute x3, waiting for transfers between devices, other_core(): return lax.ppermute(value, 'col', [(c, c ^ 1) for c in range(NX * NY * 2)])  4.41 us
    ppermute x3, starting transfers between devices, other_core(): return lax.ppermute(value, 'col', [(c, c ^ 1) for c in range(NX * NY * 2)])  3.68 us
  transfers between devices with their start and end apart: 39, of which 13 were waited for; matrix products, arithmetic and copies ran while one was open for 0% of the time, Pallas kernels for 4%

profile of v4, /device:TPU:1, one launch (start us, length us, event | category | flops | bytes accessed | tf_op | source)
XLA Modules:
  0.0 144.7 jit_solution(13842062909188924119)
XLA Ops:
  1.5 2.7 %base_solve.1 = (f32[2,512,128]{2,1,0:T(8,128)}, bf16[4,2,512,128]{3,2,1,0:T(8,128)(2,1)S(1)}) custom-call(bf16[2,512,512]{2,1,0:T(8,128)(2,1)} %inverse_ref.1, f32[2,512,128]{2,1,0:T(8,128)} %rhs_ref.1), custom_call_target="tpu_custom_call" | custom-call | flops 134217728 | bytes 1835008 | tf_op jit(solution)/shard_map/base_solve/pallas_call | solution.py:32
  4.9 19.8 %all_to_all.15.operands = bf16[4,2,512,128]{3,2,1,0:T(8,128)(2,1)S(1)} all-to-all(bf16[4,2,512,128]{3,2,1,0:T(8,128)(2,1)S(1)} %get-tuple-element.38), channel_id=1, replica_groups=mesh['col'=32,'row'=4] {'row'}, dimensions={0} | all-to-all | bytes 2097152 | tf_op jit(solution)/shard_map/all_to_all | solution.py:250
  24.8 5.4 %base_products.1 = (f32[16,80,128]{2,1,0:T(8,128)S(1)}, bf16[16,80,128]{2,1,0:T(8,128)(2,1)S(1)}, bf16[30,512,512]{2,1,0:T(8,128)(2,1)S(1)}, bf16[5,512,512]{2,1,0:T(8,128)(2,1)S(1)}) custom-call(s32[6,7]{1,0:T(8,128)S(1)} %pad_add_fusion.table, bf16[5,6,512,512]{3,2,1,0:T(8,128)(2,1)} %factor_ref.1, bf16[5,512,512]{2,1,0:T(8,128)(2,1)} %bitcast.21, ...), custom_call_target="tpu_custom_call" | custom-call | flops 1006632960 | bytes 15728640 | tf_op jit(solution)/shard_map/base_products/pallas_call | solution.py:32
  32.4 17.0 %all_to_all.16.in_ref = bf16[16,80,128]{2,1,0:T(8,128)(2,1)S(1)} all-to-all(bf16[16,80,128]{2,1,0:T(8,128)(2,1)S(1)} %pair_sums.1), channel_id=1, replica_groups={{0,8,16,24,32,40,48,56,64,72,80,88,96,104,112,120},{4,12,20,28,36,44,52..., dimensions={0} | all-to-all | bytes 655360 | tf_op jit(solution)/shard_map/all_to_all | solution.py:204
  49.5 10.7 %all_to_all.17.half_ref = bf16[16,80,128]{2,1,0:T(8,128)(2,1)S(1)} all-to-all(bf16[16,80,128]{2,1,0:T(8,128)(2,1)S(1)} %sum_shares.1), channel_id=1, replica_groups={{0,8,16,24,32,40,48,56,64,72,80,88,96,104,112,120},{4,12,20,28,36,44,52..., dimensions={0} | all-to-all | bytes 655360 | tf_op jit(solution)/shard_map/all_to_all | solution.py:204
  60.3 2.7 %collective-permute-start.1 = (bf16[16,80,128]{2,1,0:T(8,128)(2,1)S(1)}, bf16[16,80,128]{2,1,0:T(8,128)(2,1)S(1)}, u32[]{:S(2)}, u32[]{:S(2)}) collective-permute-start(bf16[16,80,128]{2,1,0:T(8,128)(2,1)S(1)} %all_to_all.17.half_ref), channel_id=1, source_target_pairs={{0,4},{4,0},{8,12},{12,8},{16,20},{20,16},{24,28},{28,24},{32,36},... | collective-permute-start | bytes 983048 | tf_op jit(solution)/shard_map/ppermute | solution.py:199
  65.2 3.2 %collective-permute-start.4 = (bf16[512,128]{1,0:T(8,128)(2,1)S(1)}, bf16[512,128]{1,0:T(8,128)(2,1)S(1)}, u32[]{:S(2)}, u32[]{:S(2)}) collective-permute-start(bf16[512,128]{1,0:T(8,128)(2,1)S(1)} %get-tuple-element.42.rest_0_), channel_id=1, source_target_pairs={{4,3},{5,0},{6,1},{7,2}} | collective-permute-start | bytes 393224 | tf_op jit(solution)/shard_map/ppermute | solution.py:191
  68.4 1.4 collective-permute-start.3
  69.8 1.3 collective-permute-start.2
  71.7 1.4 collective-permute-done.2.rest_1_
  79.4 4.4 %collective-permute-done.8.rest_3_ = bf16[512,128]{1,0:T(8,128)(2,1)S(1)} collective-permute-done((bf16[512,128]{1,0:T(8,128)(2,1)S(1)}, bf16[512,128]{1,0:T(8,128)(2,1)S(1)}, u32[]{:S(2)}, u32[]{:S(2)}) %collective-permute-start.8) | collective-permute-done | bytes 131104 | tf_op jit(solution)/shard_map/ppermute | solution.py:191
  83.8 2.5 %collective-permute-done.7.rest_2_ = bf16[512,128]{1,0:T(8,128)(2,1)S(1)} collective-permute-done((bf16[512,128]{1,0:T(8,128)(2,1)S(1)}, bf16[512,128]{1,0:T(8,128)(2,1)S(1)}, u32[]{:S(2)}, u32[]{:S(2)}) %collective-permute-start.7) | collective-permute-done | bytes 131104 | tf_op jit(solution)/shard_map/ppermute | solution.py:191
  86.3 1.3 collective-permute-done.6.rest_1_
  87.6 2.8 %solve_2.1 = (bf16[512,128]{1,0:T(8,128)(2,1)S(1)}, bf16[2,512,128]{2,1,0:T(8,128)(2,1)S(1)}, bf16[2,512,128]{2,1,0:T(8,128)(2,1)S(1)}, bf16[4,512,128]{2,1,0:T(8,128)(2,1)S(1)}) custom-call(s32[6,7]{1,0:T(8,128)S(1)} %pad_add_fusion.table, bf16[30,512,512]{2,1,0:T(8,128)(2,1)S(1)} %get-tuple-element.43.held_ref, ...), custom_call_target="tpu_custom_call" | custom-call | flops 335544320 | tf_op jit(solution)/shard_map/solve_2/pallas_call | solution.py:32
  90.4 1.3 collective-permute-start.12
  91.7 1.3 collective-permute-start.15
  93.0 1.3 collective-permute-start.14
  94.3 1.3 collective-permute-start.13
  98.8 1.8 %collective-permute-done.14.rest_2_ = bf16[512,128]{1,0:T(8,128)(2,1)S(1)} collective-permute-done((bf16[512,128]{1,0:T(8,128)(2,1)S(1)}, bf16[512,128]{1,0:T(8,128)(2,1)S(1)}, u32[]{:S(2)}, u32[]{:S(2)}) %collective-permute-start.14) | collective-permute-done | bytes 131104 | tf_op jit(solution)/shard_map/ppermute | solution.py:191
  100.6 1.4 collective-permute-done.13.rest_1_
  105.8 1.5 %later_1.1 = bf16[512,128]{1,0:T(8,128)(2,1)S(1)} custom-call(s32[6,7]{1,0:T(8,128)S(1)} %pad_add_fusion.table, bf16[30,512,512]{2,1,0:T(8,128)(2,1)S(1)} %get-tuple-element.43.held_ref, bf16[4,512,128]{2,1,0:T(8,128)(2,1)S(1)} %get-tuple-element.65.operands), custom_call_target="tpu_custom_call" | custom-call | flops 268435456 | tf_op jit(solution)/shard_map/later_1/pallas_call | solution.py:32
  107.4 1.3 collective-permute-start.22
  108.7 1.3 collective-permute-start.11
  110.0 1.3 collective-permute-start.10
  111.3 7.9 %collective-permute-start.9 = (bf16[2,512,128]{2,1,0:T(8,128)(2,1)S(1)}, bf16[2,512,128]{2,1,0:T(8,128)(2,1)S(1)}, u32[]{:S(2)}, u32[]{:S(2)}) collective-permute-start(bf16[2,512,128]{2,1,0:T(8,128)(2,1)S(1)} %get-tuple-element.52.value_ref), channel_id=1, source_target_pairs={{4,12},{5,13},{6,14},{7,15}} | collective-permute-start | bytes 786440 | tf_op jit(solution)/shard_map/ppermute | solution.py:191
  123.7 1.3 collective-permute-start.25
  125.1 1.3 collective-permute-start.24
  126.4 1.3 collective-permute-start.23
  130.4 3.0 %collective-permute-done.33.rest_1_ = bf16[512,128]{1,0:T(8,128)(2,1)S(1)} collective-permute-done((bf16[512,128]{1,0:T(8,128)(2,1)S(1)}, bf16[512,128]{1,0:T(8,128)(2,1)S(1)}, u32[]{:S(2)}, u32[]{:S(2)}) %collective-permute-start.33) | collective-permute-done | bytes 131104 | tf_op jit(solution)/shard_map/ppermute | solution.py:191
  135.5 1.3 collective-permute-start.37
  138.1 1.3 collective-permute-start.35
  141.6 1.9 %collective-permute-done.38 = bf16[4,512,128]{2,1,0:T(8,128)(2,1)S(1)} collective-permute-done((bf16[4,512,128]{2,1,0:T(8,128)(2,1)S(1)}, bf16[4,512,128]{2,1,0:T(8,128)(2,1)S(1)}, u32[]{:S(2)}, u32[]{:S(2)}) %collective-permute-start.38) | collective-permute-done | bytes 524320 | tf_op jit(solution)/shard_map/ppermute | solution.py:199
  (75 shorter events, 33.7 us)
Async XLA Ops:
  60.3 3.9 %collective-permute-start.1 = (bf16[16,80,128]{2,1,0:T(8,128)(2,1)S(1)}, bf16[16,80,128]{2,1,0:T(8,128)(2,1)S(1)}, u32[]{:S(2)}, u32[]{:S(2)}) collective-permute-start(bf16[16,80,128]{2,1,0:T(8,128)(2,1)S(1)} %all_to_all.17.half_ref), channel_id=1, source_target_pairs={{0,4},{4,0},{8,12},{12,8},{16,20},{20,16},{24,28},{28,24},{32,36},... | collective-permute-start | bytes 983048 | tf_op jit(solution)/shard_map/ppermute | solution.py:199
  65.2 5.9 %collective-permute-start.4 = (bf16[512,128]{1,0:T(8,128)(2,1)S(1)}, bf16[512,128]{1,0:T(8,128)(2,1)S(1)}, u32[]{:S(2)}, u32[]{:S(2)}) collective-permute-start(bf16[512,128]{1,0:T(8,128)(2,1)S(1)} %get-tuple-element.42.rest_0_), channel_id=1, source_target_pairs={{4,3},{5,0},{6,1},{7,2}} | collective-permute-start | bytes 393224 | tf_op jit(solution)/shard_map/ppermute | solution.py:191
  74.2 13.4 %collective-permute-start.5 = (bf16[2,512,128]{2,1,0:T(8,128)(2,1)S(1)}, bf16[2,512,128]{2,1,0:T(8,128)(2,1)S(1)}, u32[]{:S(2)}, u32[]{:S(2)}) collective-permute-start(bf16[2,512,128]{2,1,0:T(8,128)(2,1)S(1)} %get-tuple-element.45), channel_id=1, source_target_pairs={{0,4},{1,5},{2,6},{3,7}} | collective-permute-start | bytes 786440 | tf_op jit(solution)/shard_map/ppermute | solution.py:191
  75.5 8.3 %collective-permute-start.8 = (bf16[512,128]{1,0:T(8,128)(2,1)S(1)}, bf16[512,128]{1,0:T(8,128)(2,1)S(1)}, u32[]{:S(2)}, u32[]{:S(2)}) collective-permute-start(bf16[512,128]{1,0:T(8,128)(2,1)S(1)} %get-tuple-element.46), channel_id=1, source_target_pairs={{0,7},{1,4},{2,5},{3,6}} | collective-permute-start | bytes 393224 | tf_op jit(solution)/shard_map/ppermute | solution.py:191
  76.8 9.5 %collective-permute-start.7 = (bf16[512,128]{1,0:T(8,128)(2,1)S(1)}, bf16[512,128]{1,0:T(8,128)(2,1)S(1)}, u32[]{:S(2)}, u32[]{:S(2)}) collective-permute-start(bf16[512,128]{1,0:T(8,128)(2,1)S(1)} %get-tuple-element.46), channel_id=1, source_target_pairs={{0,6},{1,7},{2,4},{3,5}} | collective-permute-start | bytes 393224 | tf_op jit(solution)/shard_map/ppermute | solution.py:191
  78.1 9.5 %collective-permute-start.6 = (bf16[512,128]{1,0:T(8,128)(2,1)S(1)}, bf16[512,128]{1,0:T(8,128)(2,1)S(1)}, u32[]{:S(2)}, u32[]{:S(2)}) collective-permute-start(bf16[512,128]{1,0:T(8,128)(2,1)S(1)} %get-tuple-element.46), channel_id=1, source_target_pairs={{0,5},{1,6},{2,7},{3,4}} | collective-permute-start | bytes 393224 | tf_op jit(solution)/shard_map/ppermute | solution.py:191
  90.4 11.6 %collective-permute-start.12 = (bf16[2,512,128]{2,1,0:T(8,128)(2,1)S(1)}, bf16[2,512,128]{2,1,0:T(8,128)(2,1)S(1)}, u32[]{:S(2)}, u32[]{:S(2)}) collective-permute-start(bf16[2,512,128]{2,1,0:T(8,128)(2,1)S(1)} %get-tuple-element.53), channel_id=1, source_target_pairs={{4,8},{5,9},{6,10},{7,11}} | collective-permute-start | bytes 786440 | tf_op jit(solution)/shard_map/ppermute | solution.py:191
  91.7 6.4 %collective-permute-start.15 = (bf16[512,128]{1,0:T(8,128)(2,1)S(1)}, bf16[512,128]{1,0:T(8,128)(2,1)S(1)}, u32[]{:S(2)}, u32[]{:S(2)}) collective-permute-start(bf16[512,128]{1,0:T(8,128)(2,1)S(1)} %get-tuple-element.54), channel_id=1, source_target_pairs={{4,11},{5,8},{6,9},{7,10}} | collective-permute-start | bytes 393224 | tf_op jit(solution)/shard_map/ppermute | solution.py:191
  93.0 7.6 %collective-permute-start.14 = (bf16[512,128]{1,0:T(8,128)(2,1)S(1)}, bf16[512,128]{1,0:T(8,128)(2,1)S(1)}, u32[]{:S(2)}, u32[]{:S(2)}) collective-permute-start(bf16[512,128]{1,0:T(8,128)(2,1)S(1)} %get-tuple-element.54), channel_id=1, source_target_pairs={{4,10},{5,11},{6,8},{7,9}} | collective-permute-start | bytes 393224 | tf_op jit(solution)/shard_map/ppermute | solution.py:191
  94.3 7.7 %collective-permute-start.13 = (bf16[512,128]{1,0:T(8,128)(2,1)S(1)}, bf16[512,128]{1,0:T(8,128)(2,1)S(1)}, u32[]{:S(2)}, u32[]{:S(2)}) collective-permute-start(bf16[512,128]{1,0:T(8,128)(2,1)S(1)} %get-tuple-element.54), channel_id=1, source_target_pairs={{4,9},{5,10},{6,11},{7,8}} | collective-permute-start | bytes 393224 | tf_op jit(solution)/shard_map/ppermute | solution.py:191
  96.4 5.6 %collective-permute-start.16 = (bf16[512,128]{1,0:T(8,128)(2,1)S(1)}, bf16[512,128]{1,0:T(8,128)(2,1)S(1)}, u32[]{:S(2)}, u32[]{:S(2)}) collective-permute-start(bf16[512,128]{1,0:T(8,128)(2,1)S(1)} %get-tuple-element.61), channel_id=1, source_target_pairs={{0,8},{1,9},{2,10},{3,11}} | collective-permute-start | bytes 393224 | tf_op jit(solution)/shard_map/ppermute | solution.py:191
  98.2 9.2 %collective-permute-start.21 = (bf16[512,128]{1,0:T(8,128)(2,1)S(1)}, bf16[512,128]{1,0:T(8,128)(2,1)S(1)}, u32[]{:S(2)}, u32[]{:S(2)}) collective-permute-start(bf16[512,128]{1,0:T(8,128)(2,1)S(1)} %get-tuple-element.64), channel_id=1, source_target_pairs={{0,12},{1,13},{2,14},{3,15}} | collective-permute-start | bytes 393224 | tf_op jit(solution)/shard_map/ppermute | solution.py:191
  103.1 16.1 %collective-permute-start.17 = (bf16[2,512,128]{2,1,0:T(8,128)(2,1)S(1)}, bf16[2,512,128]{2,1,0:T(8,128)(2,1)S(1)}, u32[]{:S(2)}, u32[]{:S(2)}) collective-permute-start(bf16[2,512,128]{2,1,0:T(8,128)(2,1)S(1)} %get-tuple-element.62), channel_id=1, source_target_pairs={{8,12},{9,13},{10,14},{11,15}} | collective-permute-start | bytes 786440 | tf_op jit(solution)/shard_map/ppermute | solution.py:191
  103.8 4.9 %collective-permute-start.20 = (bf16[512,128]{1,0:T(8,128)(2,1)S(1)}, bf16[512,128]{1,0:T(8,128)(2,1)S(1)}, u32[]{:S(2)}, u32[]{:S(2)}) collective-permute-start(bf16[512,128]{1,0:T(8,128)(2,1)S(1)} %get-tuple-element.67.value_ref), channel_id=1, source_target_pairs={{8,15},{9,12},{10,13},{11,14}} | collective-permute-start | bytes 393224 | tf_op jit(solution)/shard_map/ppermute | solution.py:191
  104.5 5.5 %collective-permute-start.19 = (bf16[512,128]{1,0:T(8,128)(2,1)S(1)}, bf16[512,128]{1,0:T(8,128)(2,1)S(1)}, u32[]{:S(2)}, u32[]{:S(2)}) collective-permute-start(bf16[512,128]{1,0:T(8,128)(2,1)S(1)} %get-tuple-element.67.value_ref), channel_id=1, source_target_pairs={{8,14},{9,15},{10,12},{11,13}} | collective-permute-start | bytes 393224 | tf_op jit(solution)/shard_map/ppermute | solution.py:191
  105.1 6.2 %collective-permute-start.18 = (bf16[512,128]{1,0:T(8,128)(2,1)S(1)}, bf16[512,128]{1,0:T(8,128)(2,1)S(1)}, u32[]{:S(2)}, u32[]{:S(2)}) collective-permute-start(bf16[512,128]{1,0:T(8,128)(2,1)S(1)} %get-tuple-element.67.value_ref), channel_id=1, source_target_pairs={{8,13},{9,14},{10,15},{11,12}} | collective-permute-start | bytes 393224 | tf_op jit(solution)/shard_map/ppermute | solution.py:191
  107.4 11.8 %collective-permute-start.22 = (bf16[512,128]{1,0:T(8,128)(2,1)S(1)}, bf16[512,128]{1,0:T(8,128)(2,1)S(1)}, u32[]{:S(2)}, u32[]{:S(2)}) collective-permute-start(bf16[512,128]{1,0:T(8,128)(2,1)S(1)} %later_1.1), channel_id=1, source_target_pairs={{4,12},{5,13},{6,14},{7,15}} | collective-permute-start | bytes 393224 | tf_op jit(solution)/shard_map/ppermute | solution.py:191
  108.7 12.9 %collective-permute-start.11 = (bf16[2,512,128]{2,1,0:T(8,128)(2,1)S(1)}, bf16[2,512,128]{2,1,0:T(8,128)(2,1)S(1)}, u32[]{:S(2)}, u32[]{:S(2)}) collective-permute-start(bf16[2,512,128]{2,1,0:T(8,128)(2,1)S(1)} %get-tuple-element.52.value_ref), channel_id=1, source_target_pairs={{4,20},{5,21},{6,22},{7,23}} | collective-permute-start | bytes 786440 | tf_op jit(solution)/shard_map/ppermute | solution.py:191
  110.0 12.3 %collective-permute-start.10 = (bf16[2,512,128]{2,1,0:T(8,128)(2,1)S(1)}, bf16[2,512,128]{2,1,0:T(8,128)(2,1)S(1)}, u32[]{:S(2)}, u32[]{:S(2)}) collective-permute-start(bf16[2,512,128]{2,1,0:T(8,128)(2,1)S(1)} %get-tuple-element.52.value_ref), channel_id=1, source_target_pairs={{4,28},{5,29},{6,30},{7,31}} | collective-permute-start | bytes 786440 | tf_op jit(solution)/shard_map/ppermute | solution.py:191
  111.3 11.7 %collective-permute-start.9 = (bf16[2,512,128]{2,1,0:T(8,128)(2,1)S(1)}, bf16[2,512,128]{2,1,0:T(8,128)(2,1)S(1)}, u32[]{:S(2)}, u32[]{:S(2)}) collective-permute-start(bf16[2,512,128]{2,1,0:T(8,128)(2,1)S(1)} %get-tuple-element.52.value_ref), channel_id=1, source_target_pairs={{4,12},{5,13},{6,14},{7,15}} | collective-permute-start | bytes 786440 | tf_op jit(solution)/shard_map/ppermute | solution.py:191
  120.3 4.8 %collective-permute-start.28 = (bf16[512,128]{1,0:T(8,128)(2,1)S(1)}, bf16[512,128]{1,0:T(8,128)(2,1)S(1)}, u32[]{:S(2)}, u32[]{:S(2)}) collective-permute-start(bf16[512,128]{1,0:T(8,128)(2,1)S(1)} %get-tuple-element.67.value_ref), channel_id=1, source_target_pairs={{8,24},{9,25},{10,26},{11,27}} | collective-permute-start | bytes 393224 | tf_op jit(solution)/shard_map/ppermute | solution.py:191
  121.0 5.4 %collective-permute-start.27 = (bf16[512,128]{1,0:T(8,128)(2,1)S(1)}, bf16[512,128]{1,0:T(8,128)(2,1)S(1)}, u32[]{:S(2)}, u32[]{:S(2)}) collective-permute-start(bf16[512,128]{1,0:T(8,128)(2,1)S(1)} %get-tuple-element.67.value_ref), channel_id=1, source_target_pairs={{8,0},{9,1},{10,2},{11,3}} | collective-permute-start | bytes 393224 | tf_op jit(solution)/shard_map/ppermute | solution.py:191
  121.6 6.1 %collective-permute-start.26 = (bf16[512,128]{1,0:T(8,128)(2,1)S(1)}, bf16[512,128]{1,0:T(8,128)(2,1)S(1)}, u32[]{:S(2)}, u32[]{:S(2)}) collective-permute-start(bf16[512,128]{1,0:T(8,128)(2,1)S(1)} %get-tuple-element.67.value_ref), channel_id=1, source_target_pairs={{8,16},{9,17},{10,18},{11,19}} | collective-permute-start | bytes 393224 | tf_op jit(solution)/shard_map/ppermute | solution.py:191
  122.3 6.7 %collective-permute-start.34 = (bf16[512,128]{1,0:T(8,128)(2,1)S(1)}, bf16[512,128]{1,0:T(8,128)(2,1)S(1)}, u32[]{:S(2)}, u32[]{:S(2)}) collective-permute-start(bf16[512,128]{1,0:T(8,128)(2,1)S(1)} %solve_4.1.value_ref), channel_id=1, source_target_pairs={{12,28},{13,29},{14,30},{15,31}} | collective-permute-start | bytes 393224 | tf_op jit(solution)/shard_map/ppermute | solution.py:191
  123.7 11.7 %collective-permute-start.25 = (bf16[2,512,128]{2,1,0:T(8,128)(2,1)S(1)}, bf16[2,512,128]{2,1,0:T(8,128)(2,1)S(1)}, u32[]{:S(2)}, u32[]{:S(2)}) collective-permute-start(bf16[2,512,128]{2,1,0:T(8,128)(2,1)S(1)} %picked.3), channel_id=1, source_target_pairs={{4,68},{5,69},{6,70},{7,71},{12,76},{13,77},{14,78},{15,79},{20,84... | collective-permute-start | bytes 786440 | tf_op jit(solution)/shard_map/ppermute | solution.py:191
  125.1 11.7 %collective-permute-start.24 = (bf16[2,512,128]{2,1,0:T(8,128)(2,1)S(1)}, bf16[2,512,128]{2,1,0:T(8,128)(2,1)S(1)}, u32[]{:S(2)}, u32[]{:S(2)}) collective-permute-start(bf16[2,512,128]{2,1,0:T(8,128)(2,1)S(1)} %picked.3), channel_id=1, source_target_pairs={{4,100},{5,101},{6,102},{7,103},{12,108},{13,109},{14,110},{15,111... | collective-permute-start | bytes 786440 | tf_op jit(solution)/shard_map/ppermute | solution.py:191
  126.4 11.7 %collective-permute-start.23 = (bf16[2,512,128]{2,1,0:T(8,128)(2,1)S(1)}, bf16[2,512,128]{2,1,0:T(8,128)(2,1)S(1)}, u32[]{:S(2)}, u32[]{:S(2)}) collective-permute-start(bf16[2,512,128]{2,1,0:T(8,128)(2,1)S(1)} %picked.3), channel_id=1, source_target_pairs={{4,36},{5,37},{6,38},{7,39},{12,44},{13,45},{14,46},{15,47},{20,52... | collective-permute-start | bytes 786440 | tf_op jit(solution)/shard_map/ppermute | solution.py:191
  127.7 5.7 %collective-permute-start.33 = (bf16[512,128]{1,0:T(8,128)(2,1)S(1)}, bf16[512,128]{1,0:T(8,128)(2,1)S(1)}, u32[]{:S(2)}, u32[]{:S(2)}) collective-permute-start(bf16[512,128]{1,0:T(8,128)(2,1)S(1)} %solve_4.1.value_ref), channel_id=1, source_target_pairs={{12,4},{13,5},{14,6},{15,7}} | collective-permute-start | bytes 393224 | tf_op jit(solution)/shard_map/ppermute | solution.py:191
  129.0 5.1 %collective-permute-start.32 = (bf16[512,128]{1,0:T(8,128)(2,1)S(1)}, bf16[512,128]{1,0:T(8,128)(2,1)S(1)}, u32[]{:S(2)}, u32[]{:S(2)}) collective-permute-start(bf16[512,128]{1,0:T(8,128)(2,1)S(1)} %solve_4.1.value_ref), channel_id=1, source_target_pairs={{12,20},{13,21},{14,22},{15,23}} | collective-permute-start | bytes 393224 | tf_op jit(solution)/shard_map/ppermute | solution.py:191
  133.4 7.9 %collective-permute-start.31 = (bf16[512,128]{1,0:T(8,128)(2,1)S(1)}, bf16[512,128]{1,0:T(8,128)(2,1)S(1)}, u32[]{:S(2)}, u32[]{:S(2)}) collective-permute-start(bf16[512,128]{1,0:T(8,128)(2,1)S(1)} %picked.4), channel_id=1, source_target_pairs={{0,64},{1,65},{2,66},{3,67},{8,72},{9,73},{10,74},{11,75},{16,80},... | collective-permute-start | bytes 393224 | tf_op jit(solution)/shard_map/ppermute | solution.py:191
  134.1 7.3 %collective-permute-start.30 = (bf16[512,128]{1,0:T(8,128)(2,1)S(1)}, bf16[512,128]{1,0:T(8,128)(2,1)S(1)}, u32[]{:S(2)}, u32[]{:S(2)}) collective-permute-start(bf16[512,128]{1,0:T(8,128)(2,1)S(1)} %picked.4), channel_id=1, source_target_pairs={{0,96},{1,97},{2,98},{3,99},{8,104},{9,105},{10,106},{11,107},{16,... | collective-permute-start | bytes 393224 | tf_op jit(solution)/shard_map/ppermute | solution.py:191
  135.5 4.0 %collective-permute-start.37 = (bf16[512,128]{1,0:T(8,128)(2,1)S(1)}, bf16[512,128]{1,0:T(8,128)(2,1)S(1)}, u32[]{:S(2)}, u32[]{:S(2)}) collective-permute-start(bf16[512,128]{1,0:T(8,128)(2,1)S(1)} %picked.5), channel_id=1, source_target_pairs={{4,68},{5,69},{6,70},{7,71},{12,76},{13,77},{14,78},{15,79},{20,84... | collective-permute-start | bytes 393224 | tf_op jit(solution)/shard_map/ppermute | solution.py:191
  (8 other events, 53.3 us)

commit v5 on v4

--- a/solution.py
+++ b/solution.py
@@ -41,8 +41,9 @@
     )(*args)
 
 
-def base_solve_kernel(inverse_ref, rhs_ref, out_ref, rounded_ref, inverse, rhs, value, sems):
+def base_solve_kernel(inverse_ref, rhs_ref, out_ref, *rest):
     count = rhs_ref.shape[0]
+    rounded_refs, (inverse, rhs, value, sems) = rest[:count], rest[count:]
     reads, writes = [], []
     for i in range(count):
         reads.append((
@@ -57,53 +58,54 @@
         value[i] = dot(inverse[i], rhs[i].astype(BF16))
         writes.append(pltpu.make_async_copy(value.at[i], out_ref.at[i], sems.at[2, i]))
         writes[-1].start()
-        rounded = value[i].astype(BF16)
-        for v in range(rounded_ref.shape[0]):
-            rounded_ref[v, i] = rounded
+        rounded_refs[i][...] = value[i].astype(BF16)
     for copy in writes:
         copy.wait()
 
 
-def add_products(total, level, slots, low, high, operand_of, table, held_ref, ready=None):
+def load_kernel(levels, slots, table, factor_ref, inverse_ref, held_ref, kept_ref, sems, other_sem):
+    inverses = pltpu.make_async_copy(inverse_ref, kept_ref, other_sem)
+    inverses.start()
+
+    def each(act):
+        for level in range(levels):
+            for slot in range(slots):
+                @pl.when(slot < table[level, slots])
+                def _():
+                    at = level * slots + slot
+                    act(pltpu.make_async_copy(factor_ref.at[level, slot], held_ref.at[at], sems.at[at]))
+
+    each(lambda copy: copy.start())
+    each(lambda copy: copy.wait())
+    inverses.wait()
+
+
+def add_products(total, level, slots, low, high, operand_of, table, held_ref):
     for slot in range(slots):
         source = table[level, slot]
 
-        @pl.when(slot < table[level, slots])
+        @pl.when((slot < table[level, slots]) & (source >= low) & (source < high))
         def _():
-            if ready is not None:
-                ready(level, slot).wait()
-
-            @pl.when((source >= low) & (source < high))
-            def _():
-                total[...] += dot(held_ref[level * slots + slot], operand_of(source - low))
-
-
-def base_kernel(levels, slots, table, factor_ref, inverse_ref, operands, keep_ref, send_ref, held_ref, kept_ref,
-                total, sems, other_sem):
-    def block_copy(level, slot):
-        at = level * slots + slot
-        return pltpu.make_async_copy(factor_ref.at[level, slot], held_ref.at[at], sems.at[at])
-
-    for level in range(levels):
-        for slot in range(slots):
-            @pl.when(slot < table[level, slots])
-            def _():
-                block_copy(level, slot).start()
-    inverses = pltpu.make_async_copy(inverse_ref, kept_ref, other_sem)
-    inverses.start()
-    core, per_row = table[levels, 1], operands.shape[1]
+            total[...] += dot(held_ref[level * slots + slot], operand_of(source - low))
+
+
+def base_kernel(levels, slots, table, held_ref, *rest):
+    pieces, (keep_ref, send_ref, operands, total) = rest[:-4], rest[-4:]
+    row, core = table[levels, 0], table[levels, 1]
+    per_row = len(pieces) // NZ
+    for k in range(NZ):
+        for i in range(per_row):
+            operands[lax.rem(row + NZ - k, NZ) * per_row + i] = pieces[k * per_row + i][...]
     shares, some = keep_ref.shape[0], keep_ref.shape[1] // levels
     mine = pl.multiple_of(core * shares * some, shares * some)
     other = pl.multiple_of((1 - core) * shares * some, shares * some)
     for level in range(levels):
         total[...] = jnp.zeros_like(total)
-        add_products(total, level, slots, 0, NZ * per_row, lambda q: operands[q // per_row, lax.rem(q, per_row)],
-                     table, held_ref, block_copy)
+        add_products(total, level, slots, 0, NZ * per_row, lambda q: operands[q], table, held_ref)
         for share in range(shares):
             place_in = pl.ds(level * some, some)
             keep_ref[share, place_in] = total[pl.ds(mine + share * some, some)]
             send_ref[share, place_in] = total[pl.ds(other + share * some, some)].astype(BF16)
-    inverses.wait()
 
 
 def first_kernel(table, half_ref, other_ref, apex_ref, inverse_ref, ahead_ref, out_ref, target):
@@ -141,7 +143,7 @@
         operands[lax.rem(row + NZ - k, NZ)] = pieces[k][...]
     lists = (table, held_ref)
     total[...] = nearest[1].astype(F32) if chained else jnp.zeros_like(total)
-    for ref in more:
+    for ref in more[1 if "mixed" in named else 0 :]:
         total[...] += ref[...].astype(F32)
     add_products(total, level, slots, low, low + NZ, lambda q: operands[q], *lists)
     correction = (ahead_ref[level - 1] - total[...]).astype(BF16)
@@ -152,9 +154,8 @@
         total[...] = jnp.zeros_like(total)
         add_products(total, level + 1, slots, low, low + NZ, lambda q: operands[q], *lists)
         named["packed"][1] = total[...].astype(BF16)
-    if "both" in named:
-        named["both"][0] = operands[row]
-        named["both"][1] = value
+    if "mixed" in named:
+        named["mixed"][...] = jnp.where(table[inverse_ref.shape[0], 1] == 0, more[0][...], value)
     if "kept" in named:
         for v in range(NZ):
             named["kept"][v] = operands[v]
@@ -177,12 +178,32 @@
     came = got[0][...]
     for ref in got[1:]:
         came = came + ref[...]
-    out_ref[...] = jnp.where(table[levels, 2] == column_of, value_ref[...], came)
-
-
-def pick(column_of, table, value, got, name):
+    out_ref[...] = jnp.where(table[levels, 2] // 2 == column_of // 2, value_ref[...], came)
+
+
+def merge_kernel(levels, table, *rest):
+    refs, out_ref = rest[:-1], rest[-1]
+    each = len(refs) // out_ref.shape[0]
+    for i in range(out_ref.shape[0]):
+        value, *got = refs[i * each : (i + 1) * each]
+        came = got[0][...]
+        for ref in got[1:]:
+            came = came + ref[...]
+        out_ref[i] = jnp.where(table[levels, 2] < 2 * NX, value[...], came)
+
+
+def final_kernel(table, first_ref, mine_ref, other_ref, out_ref):
+    levels = out_ref.shape[0]
+    core = table[levels, 1]
+    out_ref[0] = first_ref[...].astype(F32)
+    for level in range(1, levels):
+        i, side = (level - 1) // 2, (level - 1) % 2
+        out_ref[level] = jnp.where(core == side, mine_ref[i], other_ref[i]).astype(F32)
+
+
+def pick(column_of, table, value, got):
     return call(
-        functools.partial(pick_kernel, table.shape[0] - 1, column_of), name, jax.ShapeDtypeStruct(value.shape, value.dtype),
+        functools.partial(pick_kernel, table.shape[0] - 1, column_of), "picked", jax.ShapeDtypeStruct(value.shape, value.dtype),
         [SMEM] + [VMEM] * (1 + len(got)), (table, value, *got),
     )
 
@@ -193,6 +214,10 @@
 
 def to_column(value, sender, receiver, k=0):
     return send(value, [(sender * NZ + z, receiver * NZ + (z + k) % NZ) for z in range(NZ)])
+
+
+def to_row(value, step):
+    return lax.ppermute(value, "row", [(z, (z + step) % NZ) for z in range(NZ)])
 
 
 def other_core(value):
@@ -204,21 +229,22 @@
     return lax.all_to_all(value, "col", 0, 0, axis_index_groups=groups, tiled=True)
 
 
-def spread_x(value, x0, core, table):
+def spread_x(value, x0, table):
     got = [
-        send(value, [(place(x0, 0, core, z), place((x0 + dx) % NX, 0, core, z)) for z in range(NZ)])
+        send(value, [(place(x0, 0, core, z), place((x0 + dx) % NX, 0, core, z)) for core in BOTH for z in range(NZ)])
         for dx in (1, 3, 2)
     ]
-    return pick(column(x0, 0, core), table, value, got, "picked")
-
-
-def spread_y(value, core, here):
+    return pick(column(x0, 0, 0), table, value, got)
+
+
+def spread_y(value):
     got = [
-        send(value, [(place(x, 0, core, z), place(x, y, core, z)) for x in range(NX) for z in range(NZ)])
+        send(value, [
+            (place(x, 0, core, z), place(x, y, core, z)) for x in range(NX) for core in BOTH for z in range(NZ)
+        ])
         for y in (1, 3, 2)
     ]
-    own = (here < 2 * NX) & (here % 2 == core)
-    return lambda: jnp.where(own, value, got[0] + got[1] + got[2])
+    return [value] + got
 
 
 def on_device(base_rhs, base_inverse, apex, top_inverse, factor_blocks, block_source, block_count):
@@ -236,34 +262,38 @@
     one = 2 * size * size * samples
     full = jax.ShapeDtypeStruct((size, samples), BF16)
 
-    base_solution, rounded = call(
-        base_solve_kernel, "base_solve",
-        (jax.ShapeDtypeStruct(base_rhs.shape, F32), jax.ShapeDtypeStruct((NZ,) + base_rhs.shape, BF16)),
-        [HBM, HBM], (in_hbm(base_inverse), in_hbm(base_rhs)), flops=per_row * one, nbytes=6 * base_rhs.size + 2 * base_inverse.size,
+    base_solution, *rounded = call(
+        base_solve_kernel, "base_solve", (jax.ShapeDtypeStruct(base_rhs.shape, F32),) + (full,) * per_row,
+        [HBM, HBM], (in_hbm(base_inverse), in_hbm(base_rhs)), flops=per_row * one,
+        nbytes=6 * base_rhs.size + 2 * base_inverse.size,
         scratch=[
             pltpu.VMEM(base_inverse.shape, BF16), pltpu.VMEM(base_rhs.shape, F32), pltpu.VMEM(base_rhs.shape, F32),
             pltpu.SemaphoreType.DMA((3, per_row)),
         ],
-        out_specs=(HBM, VMEM),
-    )
-    rounded, table = after((rounded, table))
-    operands = lax.all_to_all(rounded, "row", 0, 0, tiled=True)
-    keep, give, held, inverses = call(
+        out_specs=(HBM,) + (VMEM,) * per_row,
+    )
+    near = [to_row(rounded[0], 1), to_row(rounded[1], -1)]
+    near += [to_row(rounded[1], 1), to_row(rounded[0], -1)]
+    far = [to_row(near[0], 1), to_row(near[1], -1)]
+    pieces = rounded + [near[0], near[2]] + far + [near[3], near[1]]
+    held, inverses = (pltpu.with_memory_space_constraint(x, pltpu.VMEM) for x in call(
+        functools.partial(load_kernel, levels, slots), "load_blocks",
+        (pltpu.VMEM((levels * slots,) + block, BF16), pltpu.VMEM((levels,) + block, BF16)),
+        [SMEM, HBM, HBM], (table, factor_blocks, in_hbm(top_inverse[:, 0])),
+        scratch=[pltpu.SemaphoreType.DMA((levels * slots,)), pltpu.SemaphoreType.DMA],
+        nbytes=2 * factor_blocks.size, out_specs=(VMEM, VMEM),
+    ))
+    lists = (table, held)
+    keep, give = call(
         functools.partial(base_kernel, levels, slots), "base_products",
         (
             jax.ShapeDtypeStruct((shares, levels * some, samples), F32),
             jax.ShapeDtypeStruct((shares, levels * some, samples), BF16),
-            pltpu.VMEM((levels * slots,) + block, BF16),
-            pltpu.VMEM((levels,) + block, BF16),
         ),
-        [SMEM, HBM, HBM, VMEM], (table, factor_blocks, in_hbm(top_inverse[:, 0]), operands),
-        scratch=[
-            pltpu.VMEM((size, samples), F32), pltpu.SemaphoreType.DMA((levels * slots,)), pltpu.SemaphoreType.DMA,
-        ],
-        flops=levels * slots * one // 2, nbytes=2 * factor_blocks.size,
-    )
-    held, inverses = (pltpu.with_memory_space_constraint(x, pltpu.VMEM) for x in (held, inverses))
-    lists = (table, held)
+        [SMEM] + [VMEM] * (1 + len(pieces)), (*lists, *pieces),
+        scratch=[pltpu.VMEM((NZ * per_row, size, samples), BF16), pltpu.VMEM((size, samples), F32)],
+        flops=levels * slots * one // 2,
+    )
     pair = call(
         pair_kernel, "pair_sums", jax.ShapeDtypeStruct(give.shape, BF16), [VMEM] * 2, (keep, other_core(give))
     )
@@ -283,7 +313,7 @@
         return per_row * NZ + u * NZ
 
     def solve(u, pieces, extra, outs):
-        shapes = {"value": full, "packed": two, "both": two, "kept": four}
+        shapes = {"value": full, "packed": two, "mixed": full, "kept": four}
         return call(
             functools.partial(solve_kernel, u + 1, slots, low(u), len(extra), outs), f"solve_{u + 1}",
             tuple(shapes[o] for o in outs), [SMEM] + [VMEM] * (3 + NZ + len(extra)),
@@ -301,29 +331,31 @@
     def onward(u, value, packed):
         return [to_column(packed, u - 1, u)] + [to_column(value, u - 1, u, k) for k in (1, 2, 3)]
 
-    x1, packed, kept = solve(0, [first] + [to_column(first, 1, 0, k) for k in (1, 2, 3)], [], ("value", "packed", "kept"))
+    x1, packed, kept = solve(0, [first] + [to_row(first, k) for k in (1, 2, 3)], [], ("value", "packed", "kept"))
     pieces = onward(1, x1, packed)
     pieces, kept = after((pieces, kept))
     p30, p40 = products(0, (3, 4), kept)
-    x2, packed, both, kept = solve(1, pieces, [], ("value", "packed", "both", "kept"))
+    x2, packed, mixed12, kept = solve(1, pieces, [x1], ("value", "packed", "mixed", "kept"))
     pieces = onward(2, x2, packed)
-    spread12 = spread_x(both, 0, 1, table)
+    mixed12 = spread_x(mixed12, 0, table)
     p30, p40 = to_column(p30, 0, 2), to_column(p40, 0, 3)
     pieces, kept = after((pieces, kept))
     p41, = products(1, (4,), kept)
     x3, packed = solve(2, pieces, [p30], ("value", "packed"))
     pieces = onward(3, x3, packed)
+    spread12 = spread_y(after((mixed12, x3))[0])
     p41 = to_column(p41, 1, 3)
-    x4, = solve(3, pieces, [p40, p41], ("value",))
-    spread4 = spread_x(x4, 1, 1, table)
-    spread12 = spread_y(after((spread12, x4))[0], 1, here)
-    spread3 = spread_x(after((x3, x4))[0], 1, 0, table)
-    spread3 = spread_y(spread3, 0, here)
-    spread4 = spread_y(spread4, 1, here)
-    out = jnp.concatenate([spread12(), spread3()[None], spread4()[None]])
-    out = out + other_core(out)
-    out = jnp.concatenate([first[None], out])
-    return base_solution, out.astype(F32)[:, None]
+    x4, mixed34 = solve(3, pieces, [x3, p40, p41], ("value", "mixed"))
+    spread34 = spread_y(spread_x(mixed34, 1, table))
+    spreads = spread12 + spread34
+    mine = call(
+        functools.partial(merge_kernel, levels), "merged", two, [SMEM] + [VMEM] * len(spreads), (table, *spreads)
+    )
+    out = call(
+        final_kernel, "final", jax.ShapeDtypeStruct((levels, size, samples), F32), [SMEM] + [VMEM] * 3,
+        (table, first, mine, other_core(mine)),
+    )
+    return base_solution, out[:, None]
 
 
 def solution(mesh):

time: 146 us -> 140 us (0.959)
  blocking collectives: 47.6 us -> 30.2 us
  waiting for transfers between devices: 23.1 us -> 28.8 us
  starting transfers between devices: 50.1 us -> 54.8 us
  Pallas kernels: 19.6 us -> 22.9 us
    all_to_all x1 -> x0, blocking collectives: 19.8 us -> none  [on_device(): operands = lax.all_to_all(rounded, 'row', 0, 0, tiled=True)]
    ppermute x0 -> x9, starting transfers between devices: none -> 13.7 us  [to_row(): return lax.ppermute(value, 'row', [(z, (z + step) % NZ) for z in range(NZ)])]
    ppermute x36 -> x27, starting transfers between devices: 46.5 us -> 36 us  [send(): return lax.ppermute(value, AXES, pairs)]
    ppermute x0 -> x9, waiting for transfers between devices: none -> 10.1 us  [to_row(): return lax.ppermute(value, 'row', [(z, (z + step) % NZ) for z in range(NZ)])]
    ppermute x36 -> x27, waiting for transfers between devices: 18.7 us -> 15 us  [send(): return lax.ppermute(value, AXES, pairs)]
    pallas_call x14 -> x16, Pallas kernels: 19.6 us -> 22.9 us  [call(): pl.pallas_call(body, out_shape=outs, in_specs=in_specs, out_specs=out_spe...]
    all_to_all x2, blocking collectives: 27.8 us -> 30.2 us  [over_plane(): lax.all_to_all(value, 'col', 0, 0, axis_index_groups=groups, tiled=True)]
  transfers between devices with their start and end apart: 39 -> 39, of which waited for: 13 -> 17; matrix products, arithmetic and copies ran while one was open for 0% -> 1% of each run, Pallas kernels for 4% -> 8%
where the time goes in v5:
time: 140 us; the launch traced here: 139 us
  starting transfers between devices  54.8 us (39%)
  blocking collectives  30.2 us (22%)
  waiting for transfers between devices  28.8 us (21%)
  Pallas kernels  22.9 us (16%)
    ppermute x27, starting transfers between devices, send(): return lax.ppermute(value, AXES, pairs)  36 us
    all_to_all x2, blocking collectives, over_plane(): lax.all_to_all(value, 'col', 0, 0, axis_index_groups=groups, tiled=True)  30.2 us
    pallas_call x16, Pallas kernels, call(): pl.pallas_call(body, out_shape=outs, in_specs=in_specs, out_specs=out_spe...  22.9 us
    ppermute x27, waiting for transfers between devices, send(): return lax.ppermute(value, AXES, pairs)  15 us
    ppermute x9, starting transfers between devices, to_row(): return lax.ppermute(value, 'row', [(z, (z + step) % NZ) for z in range(NZ)])  13.7 us
    ppermute x9, waiting for transfers between devices, to_row(): return lax.ppermute(value, 'row', [(z, (z + step) % NZ) for z in range(NZ)])  10.1 us
    ppermute x3, starting transfers between devices, other_core(): return lax.ppermute(value, 'col', [(c, c ^ 1) for c in range(NX * NY * 2)])  5.12 us
    ppermute x3, waiting for transfers between devices, other_core(): return lax.ppermute(value, 'col', [(c, c ^ 1) for c in range(NX * NY * 2)])  3.67 us
  transfers between devices with their start and end apart: 39, of which 17 were waited for; matrix products, arithmetic and copies ran while one was open for 1% of the time, Pallas kernels for 8%

profile of v5, /device:TPU:1, one launch (start us, length us, event | category | flops | bytes accessed | tf_op | source)
XLA Modules:
  0.0 139.3 jit_solution(22533225152022135)
XLA Ops:
  0.6 2.7 %base_solve.1 = (f32[2,512,128]{2,1,0:T(8,128)}, bf16[512,128]{1,0:T(8,128)(2,1)S(1)}, bf16[512,128]{1,0:T(8,128)(2,1)S(1)}) custom-call(bf16[2,512,512]{2,1,0:T(8,128)(2,1)} %inverse_ref.1, f32[2,512,128]{2,1,0:T(8,128)} %rhs_ref.1), custom_call_target="tpu_custom_call" | custom-call | flops 134217728 | bytes 1835008 | tf_op jit(solution)/shard_map/base_solve/pallas_call | solution.py:32
  3.3 2.5 %collective-permute-start = (bf16[512,128]{1,0:T(8,128)(2,1)S(1)}, bf16[512,128]{1,0:T(8,128)(2,1)S(1)}, u32[]{:S(2)}, u32[]{:S(2)}) collective-permute-start(bf16[512,128]{1,0:T(8,128)(2,1)S(1)} %get-tuple-element.36.rest_0_), channel_id=1, source_target_pairs={{0,1},{1,2},{2,3},{3,0},{4,5},{5,6},{6,7},{7,4},{8,9},{9,10},{10,1... | collective-permute-start | bytes 393224 | tf_op jit(solution)/shard_map/ppermute | solution.py:220
  5.9 2.2 %collective-permute-start.3 = (bf16[512,128]{1,0:T(8,128)(2,1)S(1)}, bf16[512,128]{1,0:T(8,128)(2,1)S(1)}, u32[]{:S(2)}, u32[]{:S(2)}) collective-permute-start(bf16[512,128]{1,0:T(8,128)(2,1)S(1)} %get-tuple-element.37.rest_1_), channel_id=1, source_target_pairs={{0,3},{1,0},{2,1},{3,2},{4,7},{5,4},{6,5},{7,6},{8,11},{9,8},{10,9... | collective-permute-start | bytes 393224 | tf_op jit(solution)/shard_map/ppermute | solution.py:220
  8.1 1.4 collective-permute-start.5
  9.6 1.6 %collective-permute-done.rest_2_ = bf16[512,128]{1,0:T(8,128)(2,1)S(1)} collective-permute-done((bf16[512,128]{1,0:T(8,128)(2,1)S(1)}, bf16[512,128]{1,0:T(8,128)(2,1)S(1)}, u32[]{:S(2)}, u32[]{:S(2)}) %collective-permute-start) | collective-permute-done | bytes 131104 | tf_op jit(solution)/shard_map/ppermute | solution.py:220
  11.2 2.7 %collective-permute-start.4 = (bf16[512,128]{1,0:T(8,128)(2,1)S(1)}, bf16[512,128]{1,0:T(8,128)(2,1)S(1)}, u32[]{:S(2)}, u32[]{:S(2)}) collective-permute-start(bf16[512,128]{1,0:T(8,128)(2,1)S(1)} %collective-permute-done.3.rest_7_), channel_id=1, source_target_pairs={{0,3},{1,0},{2,1},{3,2},{4,7},{5,4},{6,5},{7,6},{8,11},{9,8},{10,9... | collective-permute-start | bytes 393224 | tf_op jit(solution)/shard_map/ppermute | solution.py:220
  15.4 4.2 %load_blocks.1 = (bf16[30,512,512]{2,1,0:T(8,128)(2,1)S(1)}, bf16[5,512,512]{2,1,0:T(8,128)(2,1)S(1)}) custom-call(s32[6,7]{1,0:T(8,128)S(1)} %pad_add_fusion.table, bf16[5,6,512,512]{3,2,1,0:T(8,128)(2,1)} %factor_ref.1, bf16[5,512,512]{2,1,0:T(8,128)(2,1)} %bitcast.11), custom_call_target="tpu_custom_call" | custom-call | bytes 15728640 | tf_op jit(solution)/shard_map/load_blocks/pallas_call | solution.py:32
  19.7 2.0 %base_products.1 = (f32[16,80,128]{2,1,0:T(8,128)S(1)}, bf16[16,80,128]{2,1,0:T(8,128)(2,1)S(1)}) custom-call(s32[6,7]{1,0:T(8,128)S(1)} %pad_add_fusion.table, bf16[30,512,512]{2,1,0:T(8,128)(2,1)S(1)} %get-tuple-element.35.held_ref, bf16[512,128]{1,0:T(8,128)(2,1)S(1)} %get-tuple-element.36.rest_0_, bf16[512,128]{1,0:T(8,128)(2,1)S(1)} %get-tuple-element.37.rest_1_, ...), custom_call_target="tpu_custom_call" | custom-call | flops 1006632960 | tf_op jit(solution)/shard_map/base_products/pallas_call | solution.py:32
  21.7 1.9 %collective-permute-start.6 = (bf16[16,80,128]{2,1,0:T(8,128)(2,1)S(1)}, bf16[16,80,128]{2,1,0:T(8,128)(2,1)S(1)}, u32[]{:S(2)}, u32[]{:S(2)}) collective-permute-start(bf16[16,80,128]{2,1,0:T(8,128)(2,1)S(1)} %get-tuple-element.39), channel_id=1, source_target_pairs={{0,4},{4,0},{8,12},{12,8},{16,20},{20,16},{24,28},{28,24},{32,36},... | collective-permute-start | bytes 983048 | tf_op jit(solution)/shard_map/ppermute | solution.py:224
  24.9 19.4 %all_to_all.10.in_ref = bf16[16,80,128]{2,1,0:T(8,128)(2,1)S(1)} all-to-all(bf16[16,80,128]{2,1,0:T(8,128)(2,1)S(1)} %pair_sums.1), channel_id=1, replica_groups={{0,8,16,24,32,40,48,56,64,72,80,88,96,104,112,120},{4,12,20,28,36,44,52..., dimensions={0} | all-to-all | bytes 655360 | tf_op jit(solution)/shard_map/all_to_all | solution.py:229
  44.4 10.7 %all_to_all.11.half_ref = bf16[16,80,128]{2,1,0:T(8,128)(2,1)S(1)} all-to-all(bf16[16,80,128]{2,1,0:T(8,128)(2,1)S(1)} %sum_shares.1), channel_id=1, replica_groups={{0,8,16,24,32,40,48,56,64,72,80,88,96,104,112,120},{4,12,20,28,36,44,52..., dimensions={0} | all-to-all | bytes 655360 | tf_op jit(solution)/shard_map/all_to_all | solution.py:229
  55.2 2.7 %collective-permute-start.7 = (bf16[16,80,128]{2,1,0:T(8,128)(2,1)S(1)}, bf16[16,80,128]{2,1,0:T(8,128)(2,1)S(1)}, u32[]{:S(2)}, u32[]{:S(2)}) collective-permute-start(bf16[16,80,128]{2,1,0:T(8,128)(2,1)S(1)} %all_to_all.11.half_ref), channel_id=1, source_target_pairs={{0,4},{4,0},{8,12},{12,8},{16,20},{20,16},{24,28},{28,24},{32,36},... | collective-permute-start | bytes 983048 | tf_op jit(solution)/shard_map/ppermute | solution.py:224
  60.2 4.1 %collective-permute-start.10 = (bf16[512,128]{1,0:T(8,128)(2,1)S(1)}, bf16[512,128]{1,0:T(8,128)(2,1)S(1)}, u32[]{:S(2)}, u32[]{:S(2)}) collective-permute-start(bf16[512,128]{1,0:T(8,128)(2,1)S(1)} %get-tuple-element.41.rest_0_.first_ref), channel_id=1, source_target_pairs={{0,3},{1,0},{2,1},{3,2},{4,7},{5,4},{6,5},{7,6},{8,11},{9,8},{10,9... | collective-permute-start | bytes 393224 | tf_op jit(solution)/shard_map/ppermute | solution.py:220
  65.0 5.0 %collective-permute-done.10.rest_3_ = bf16[512,128]{1,0:T(8,128)(2,1)S(1)} collective-permute-done((bf16[512,128]{1,0:T(8,128)(2,1)S(1)}, bf16[512,128]{1,0:T(8,128)(2,1)S(1)}, u32[]{:S(2)}, u32[]{:S(2)}) %collective-permute-start.10) | collective-permute-done | bytes 131104 | tf_op jit(solution)/shard_map/ppermute | solution.py:220
  70.3 3.2 %collective-permute-done.8.rest_1_ = bf16[512,128]{1,0:T(8,128)(2,1)S(1)} collective-permute-done((bf16[512,128]{1,0:T(8,128)(2,1)S(1)}, bf16[512,128]{1,0:T(8,128)(2,1)S(1)}, u32[]{:S(2)}, u32[]{:S(2)}) %collective-permute-start.8) | collective-permute-done | bytes 131104 | tf_op jit(solution)/shard_map/ppermute | solution.py:220
  79.9 2.4 %collective-permute-done.14.rest_3_ = bf16[512,128]{1,0:T(8,128)(2,1)S(1)} collective-permute-done((bf16[512,128]{1,0:T(8,128)(2,1)S(1)}, bf16[512,128]{1,0:T(8,128)(2,1)S(1)}, u32[]{:S(2)}, u32[]{:S(2)}) %collective-permute-start.14) | collective-permute-done | bytes 131104 | tf_op jit(solution)/shard_map/ppermute | solution.py:212
  82.3 2.8 %collective-permute-done.13.rest_2_ = bf16[512,128]{1,0:T(8,128)(2,1)S(1)} collective-permute-done((bf16[512,128]{1,0:T(8,128)(2,1)S(1)}, bf16[512,128]{1,0:T(8,128)(2,1)S(1)}, u32[]{:S(2)}, u32[]{:S(2)}) %collective-permute-start.13) | collective-permute-done | bytes 131104 | tf_op jit(solution)/shard_map/ppermute | solution.py:212
  85.2 1.4 collective-permute-done.12.rest_1_
  86.5 2.6 %solve_2.1 = (bf16[512,128]{1,0:T(8,128)(2,1)S(1)}, bf16[2,512,128]{2,1,0:T(8,128)(2,1)S(1)}, bf16[512,128]{1,0:T(8,128)(2,1)S(1)}, bf16[4,512,128]{2,1,0:T(8,128)(2,1)S(1)}) custom-call(s32[6,7]{1,0:T(8,128)S(1)} %pad_add_fusion.table, bf16[30,512,512]{2,1,0:T(8,128)(2,1)S(1)} %get-tuple-element.35.held_ref, ...), custom_call_target="tpu_custom_call" | custom-call | flops 335544320 | tf_op jit(solution)/shard_map/solve_2/pallas_call | solution.py:32
  89.1 1.3 collective-permute-start.18
  90.4 1.3 collective-permute-start.21
  95.8 2.1 %collective-permute-done.21.rest_3_ = bf16[512,128]{1,0:T(8,128)(2,1)S(1)} collective-permute-done((bf16[512,128]{1,0:T(8,128)(2,1)S(1)}, bf16[512,128]{1,0:T(8,128)(2,1)S(1)}, u32[]{:S(2)}, u32[]{:S(2)}) %collective-permute-start.21) | collective-permute-done | bytes 131104 | tf_op jit(solution)/shard_map/ppermute | solution.py:212
  99.3 1.7 %collective-permute-done.19.rest_1_ = bf16[512,128]{1,0:T(8,128)(2,1)S(1)} collective-permute-done((bf16[512,128]{1,0:T(8,128)(2,1)S(1)}, bf16[512,128]{1,0:T(8,128)(2,1)S(1)}, u32[]{:S(2)}, u32[]{:S(2)}) %collective-permute-start.19) | collective-permute-done | bytes 131104 | tf_op jit(solution)/shard_map/ppermute | solution.py:212
  104.9 1.5 %later_1.1 = bf16[512,128]{1,0:T(8,128)(2,1)S(1)} custom-call(s32[6,7]{1,0:T(8,128)S(1)} %pad_add_fusion.table, bf16[30,512,512]{2,1,0:T(8,128)(2,1)S(1)} %get-tuple-element.35.held_ref, bf16[4,512,128]{2,1,0:T(8,128)(2,1)S(1)} %get-tuple-element.64.operands), custom_call_target="tpu_custom_call" | custom-call | flops 268435456 | tf_op jit(solution)/shard_map/later_1/pallas_call | solution.py:32
  107.7 1.3 collective-permute-start.17
  110.4 7.3 %collective-permute-start.15 = (bf16[512,128]{1,0:T(8,128)(2,1)S(1)}, bf16[512,128]{1,0:T(8,128)(2,1)S(1)}, u32[]{:S(2)}, u32[]{:S(2)}) collective-permute-start(bf16[512,128]{1,0:T(8,128)(2,1)S(1)} %get-tuple-element.50.value_ref), channel_id=1, source_target_pairs={{0,8},{1,9},{2,10},{3,11},{4,12},{5,13},{6,14},{7,15}} | collective-permute-start | bytes 393224 | tf_op jit(solution)/shard_map/ppermute | solution.py:212
  117.7 1.7 %solve_4.1 = (bf16[512,128]{1,0:T(8,128)(2,1)}, bf16[512,128]{1,0:T(8,128)(2,1)S(1)}) custom-call(s32[6,7]{1,0:T(8,128)S(1)} %pad_add_fusion.table, bf16[30,512,512]{2,1,0:T(8,128)(2,1)S(1)} %get-tuple-element.35.held_ref, f32[4,512,128]{2,1,0:T(8,128)S(1)} %get-tuple-element.42.ahead_ref, bf16[5,512,512]{2,1,0:T(8,128)(2,1)S(1)} %get-tuple-element.40.inverse_ref, ...), custom_call_target="tpu_custom_call" | custom-call | flops 335544320 | tf_op jit(solution)/shard_map/solve_4/pallas_call | solution.py:32
  125.4 1.3 collective-permute-start.23
  127.7 1.3 collective-permute-start.37
  132.3 1.3 collective-permute-done.36.rest_6_
  133.6 1.5 %collective-permute-done.35.rest_5_ = bf16[512,128]{1,0:T(8,128)(2,1)S(1)} collective-permute-done((bf16[512,128]{1,0:T(8,128)(2,1)S(1)}, bf16[512,128]{1,0:T(8,128)(2,1)S(1)}, u32[]{:S(2)}, u32[]{:S(2)}) %collective-permute-start.35) | collective-permute-done | bytes 131104 | tf_op jit(solution)/shard_map/ppermute | solution.py:212
  137.5 1.8 %final.1 = f32[5,512,128]{2,1,0:T(8,128)} custom-call(s32[6,7]{1,0:T(8,128)S(1)} %pad_add_fusion.table, bf16[512,128]{1,0:T(8,128)(2,1)S(1)} %get-tuple-element.41.rest_0_.first_ref, bf16[2,512,128]{2,1,0:T(8,128)(2,1)S(1)} %merged.1.mine_ref, bf16[2,512,128]{2,1,0:T(8,128)(2,1)S(1)} %collective-permute-done.38.other_ref), custom_call_target="tpu_custom_call" | custom-call | tf_op jit(solution)/shard_map/final/pallas_call | solution.py:32
  (70 shorter events, 37.2 us)
Async XLA Ops:
  3.3 7.9 %collective-permute-start = (bf16[512,128]{1,0:T(8,128)(2,1)S(1)}, bf16[512,128]{1,0:T(8,128)(2,1)S(1)}, u32[]{:S(2)}, u32[]{:S(2)}) collective-permute-start(bf16[512,128]{1,0:T(8,128)(2,1)S(1)} %get-tuple-element.36.rest_0_), channel_id=1, source_target_pairs={{0,1},{1,2},{2,3},{3,0},{4,5},{5,6},{6,7},{7,4},{8,9},{9,10},{10,1... | collective-permute-start | bytes 393224 | tf_op jit(solution)/shard_map/ppermute | solution.py:220
  5.9 5.3 %collective-permute-start.3 = (bf16[512,128]{1,0:T(8,128)(2,1)S(1)}, bf16[512,128]{1,0:T(8,128)(2,1)S(1)}, u32[]{:S(2)}, u32[]{:S(2)}) collective-permute-start(bf16[512,128]{1,0:T(8,128)(2,1)S(1)} %get-tuple-element.37.rest_1_), channel_id=1, source_target_pairs={{0,3},{1,0},{2,1},{3,2},{4,7},{5,4},{6,5},{7,6},{8,11},{9,8},{10,9... | collective-permute-start | bytes 393224 | tf_op jit(solution)/shard_map/ppermute | solution.py:220
  8.1 11.6 %collective-permute-start.5 = (bf16[512,128]{1,0:T(8,128)(2,1)S(1)}, bf16[512,128]{1,0:T(8,128)(2,1)S(1)}, u32[]{:S(2)}, u32[]{:S(2)}) collective-permute-start(bf16[512,128]{1,0:T(8,128)(2,1)S(1)} %get-tuple-element.36.rest_0_), channel_id=1, source_target_pairs={{0,3},{1,0},{2,1},{3,2},{4,7},{5,4},{6,5},{7,6},{8,11},{9,8},{10,9... | collective-permute-start | bytes 393224 | tf_op jit(solution)/shard_map/ppermute | solution.py:220
  9.5 10.2 %collective-permute-start.1 = (bf16[512,128]{1,0:T(8,128)(2,1)S(1)}, bf16[512,128]{1,0:T(8,128)(2,1)S(1)}, u32[]{:S(2)}, u32[]{:S(2)}) collective-permute-start(bf16[512,128]{1,0:T(8,128)(2,1)S(1)} %get-tuple-element.37.rest_1_), channel_id=1, source_target_pairs={{0,1},{1,2},{2,3},{3,0},{4,5},{5,6},{6,7},{7,4},{8,9},{9,10},{10,1... | collective-permute-start | bytes 393224 | tf_op jit(solution)/shard_map/ppermute | solution.py:220
  11.2 8.4 %collective-permute-start.2 = (bf16[512,128]{1,0:T(8,128)(2,1)S(1)}, bf16[512,128]{1,0:T(8,128)(2,1)S(1)}, u32[]{:S(2)}, u32[]{:S(2)}) collective-permute-start(bf16[512,128]{1,0:T(8,128)(2,1)S(1)} %collective-permute-done.rest_2_), channel_id=1, source_target_pairs={{0,1},{1,2},{2,3},{3,0},{4,5},{5,6},{6,7},{7,4},{8,9},{9,10},{10,1... | collective-permute-start | bytes 393224 | tf_op jit(solution)/shard_map/ppermute | solution.py:220
  11.2 8.5 %collective-permute-start.4 = (bf16[512,128]{1,0:T(8,128)(2,1)S(1)}, bf16[512,128]{1,0:T(8,128)(2,1)S(1)}, u32[]{:S(2)}, u32[]{:S(2)}) collective-permute-start(bf16[512,128]{1,0:T(8,128)(2,1)S(1)} %collective-permute-done.3.rest_7_), channel_id=1, source_target_pairs={{0,3},{1,0},{2,1},{3,2},{4,7},{5,4},{6,5},{7,6},{8,11},{9,8},{10,9... | collective-permute-start | bytes 393224 | tf_op jit(solution)/shard_map/ppermute | solution.py:220
  60.2 9.8 %collective-permute-start.10 = (bf16[512,128]{1,0:T(8,128)(2,1)S(1)}, bf16[512,128]{1,0:T(8,128)(2,1)S(1)}, u32[]{:S(2)}, u32[]{:S(2)}) collective-permute-start(bf16[512,128]{1,0:T(8,128)(2,1)S(1)} %get-tuple-element.41.rest_0_.first_ref), channel_id=1, source_target_pairs={{0,3},{1,0},{2,1},{3,2},{4,7},{5,4},{6,5},{7,6},{8,11},{9,8},{10,9... | collective-permute-start | bytes 393224 | tf_op jit(solution)/shard_map/ppermute | solution.py:220
  64.3 6.0 %collective-permute-start.9 = (bf16[512,128]{1,0:T(8,128)(2,1)S(1)}, bf16[512,128]{1,0:T(8,128)(2,1)S(1)}, u32[]{:S(2)}, u32[]{:S(2)}) collective-permute-start(bf16[512,128]{1,0:T(8,128)(2,1)S(1)} %get-tuple-element.41.rest_0_.first_ref), channel_id=1, source_target_pairs={{0,2},{1,3},{2,0},{3,1},{4,6},{5,7},{6,4},{7,5},{8,10},{9,11},{10,... | collective-permute-start | bytes 393224 | tf_op jit(solution)/shard_map/ppermute | solution.py:220
  64.3 9.1 %collective-permute-start.8 = (bf16[512,128]{1,0:T(8,128)(2,1)S(1)}, bf16[512,128]{1,0:T(8,128)(2,1)S(1)}, u32[]{:S(2)}, u32[]{:S(2)}) collective-permute-start(bf16[512,128]{1,0:T(8,128)(2,1)S(1)} %get-tuple-element.41.rest_0_.first_ref), channel_id=1, source_target_pairs={{0,1},{1,2},{2,3},{3,0},{4,5},{5,6},{6,7},{7,4},{8,9},{9,10},{10,1... | collective-permute-start | bytes 393224 | tf_op jit(solution)/shard_map/ppermute | solution.py:220
  74.7 11.8 %collective-permute-start.11 = (bf16[2,512,128]{2,1,0:T(8,128)(2,1)S(1)}, bf16[2,512,128]{2,1,0:T(8,128)(2,1)S(1)}, u32[]{:S(2)}, u32[]{:S(2)}) collective-permute-start(bf16[2,512,128]{2,1,0:T(8,128)(2,1)S(1)} %get-tuple-element.43), channel_id=1, source_target_pairs={{0,4},{1,5},{2,6},{3,7}} | collective-permute-start | bytes 786440 | tf_op jit(solution)/shard_map/ppermute | solution.py:212
  76.0 6.3 %collective-permute-start.14 = (bf16[512,128]{1,0:T(8,128)(2,1)S(1)}, bf16[512,128]{1,0:T(8,128)(2,1)S(1)}, u32[]{:S(2)}, u32[]{:S(2)}) collective-permute-start(bf16[512,128]{1,0:T(8,128)(2,1)S(1)} %get-tuple-element.44.rest_4_), channel_id=1, source_target_pairs={{0,7},{1,4},{2,5},{3,6}} | collective-permute-start | bytes 393224 | tf_op jit(solution)/shard_map/ppermute | solution.py:212
  77.3 7.8 %collective-permute-start.13 = (bf16[512,128]{1,0:T(8,128)(2,1)S(1)}, bf16[512,128]{1,0:T(8,128)(2,1)S(1)}, u32[]{:S(2)}, u32[]{:S(2)}) collective-permute-start(bf16[512,128]{1,0:T(8,128)(2,1)S(1)} %get-tuple-element.44.rest_4_), channel_id=1, source_target_pairs={{0,6},{1,7},{2,4},{3,5}} | collective-permute-start | bytes 393224 | tf_op jit(solution)/shard_map/ppermute | solution.py:212
  78.6 7.9 %collective-permute-start.12 = (bf16[512,128]{1,0:T(8,128)(2,1)S(1)}, bf16[512,128]{1,0:T(8,128)(2,1)S(1)}, u32[]{:S(2)}, u32[]{:S(2)}) collective-permute-start(bf16[512,128]{1,0:T(8,128)(2,1)S(1)} %get-tuple-element.44.rest_4_), channel_id=1, source_target_pairs={{0,5},{1,6},{2,7},{3,4}} | collective-permute-start | bytes 393224 | tf_op jit(solution)/shard_map/ppermute | solution.py:212
  89.1 12.0 %collective-permute-start.18 = (bf16[2,512,128]{2,1,0:T(8,128)(2,1)S(1)}, bf16[2,512,128]{2,1,0:T(8,128)(2,1)S(1)}, u32[]{:S(2)}, u32[]{:S(2)}) collective-permute-start(bf16[2,512,128]{2,1,0:T(8,128)(2,1)S(1)} %get-tuple-element.51), channel_id=1, source_target_pairs={{4,8},{5,9},{6,10},{7,11}} | collective-permute-start | bytes 786440 | tf_op jit(solution)/shard_map/ppermute | solution.py:212
  90.4 7.5 %collective-permute-start.21 = (bf16[512,128]{1,0:T(8,128)(2,1)S(1)}, bf16[512,128]{1,0:T(8,128)(2,1)S(1)}, u32[]{:S(2)}, u32[]{:S(2)}) collective-permute-start(bf16[512,128]{1,0:T(8,128)(2,1)S(1)} %get-tuple-element.52), channel_id=1, source_target_pairs={{4,11},{5,8},{6,9},{7,10}} | collective-permute-start | bytes 393224 | tf_op jit(solution)/shard_map/ppermute | solution.py:212
  91.7 7.6 %collective-permute-start.20 = (bf16[512,128]{1,0:T(8,128)(2,1)S(1)}, bf16[512,128]{1,0:T(8,128)(2,1)S(1)}, u32[]{:S(2)}, u32[]{:S(2)}) collective-permute-start(bf16[512,128]{1,0:T(8,128)(2,1)S(1)} %get-tuple-element.52), channel_id=1, source_target_pairs={{4,10},{5,11},{6,8},{7,9}} | collective-permute-start | bytes 393224 | tf_op jit(solution)/shard_map/ppermute | solution.py:212
  93.1 8.0 %collective-permute-start.19 = (bf16[512,128]{1,0:T(8,128)(2,1)S(1)}, bf16[512,128]{1,0:T(8,128)(2,1)S(1)}, u32[]{:S(2)}, u32[]{:S(2)}) collective-permute-start(bf16[512,128]{1,0:T(8,128)(2,1)S(1)} %get-tuple-element.52), channel_id=1, source_target_pairs={{4,9},{5,10},{6,11},{7,8}} | collective-permute-start | bytes 393224 | tf_op jit(solution)/shard_map/ppermute | solution.py:212
  95.1 6.0 %collective-permute-start.22 = (bf16[512,128]{1,0:T(8,128)(2,1)S(1)}, bf16[512,128]{1,0:T(8,128)(2,1)S(1)}, u32[]{:S(2)}, u32[]{:S(2)}) collective-permute-start(bf16[512,128]{1,0:T(8,128)(2,1)S(1)} %get-tuple-element.59), channel_id=1, source_target_pairs={{0,8},{1,9},{2,10},{3,11}} | collective-permute-start | bytes 393224 | tf_op jit(solution)/shard_map/ppermute | solution.py:212
  97.9 8.5 %collective-permute-start.30 = (bf16[512,128]{1,0:T(8,128)(2,1)S(1)}, bf16[512,128]{1,0:T(8,128)(2,1)S(1)}, u32[]{:S(2)}, u32[]{:S(2)}) collective-permute-start(bf16[512,128]{1,0:T(8,128)(2,1)S(1)} %get-tuple-element.63), channel_id=1, source_target_pairs={{0,12},{1,13},{2,14},{3,15}} | collective-permute-start | bytes 393224 | tf_op jit(solution)/shard_map/ppermute | solution.py:212
  102.2 15.5 %collective-permute-start.26 = (bf16[2,512,128]{2,1,0:T(8,128)(2,1)S(1)}, bf16[2,512,128]{2,1,0:T(8,128)(2,1)S(1)}, u32[]{:S(2)}, u32[]{:S(2)}) collective-permute-start(bf16[2,512,128]{2,1,0:T(8,128)(2,1)S(1)} %get-tuple-element.62), channel_id=1, source_target_pairs={{8,12},{9,13},{10,14},{11,15}} | collective-permute-start | bytes 786440 | tf_op jit(solution)/shard_map/ppermute | solution.py:212
  103.6 5.5 %collective-permute-start.28 = (bf16[512,128]{1,0:T(8,128)(2,1)S(1)}, bf16[512,128]{1,0:T(8,128)(2,1)S(1)}, u32[]{:S(2)}, u32[]{:S(2)}) collective-permute-start(bf16[512,128]{1,0:T(8,128)(2,1)S(1)} %get-tuple-element.60.rest_4_), channel_id=1, source_target_pairs={{8,14},{9,15},{10,12},{11,13}} | collective-permute-start | bytes 393224 | tf_op jit(solution)/shard_map/ppermute | solution.py:212
  104.2 6.1 %collective-permute-start.27 = (bf16[512,128]{1,0:T(8,128)(2,1)S(1)}, bf16[512,128]{1,0:T(8,128)(2,1)S(1)}, u32[]{:S(2)}, u32[]{:S(2)}) collective-permute-start(bf16[512,128]{1,0:T(8,128)(2,1)S(1)} %get-tuple-element.60.rest_4_), channel_id=1, source_target_pairs={{8,13},{9,14},{10,15},{11,12}} | collective-permute-start | bytes 393224 | tf_op jit(solution)/shard_map/ppermute | solution.py:212
  106.4 11.3 %collective-permute-start.31 = (bf16[512,128]{1,0:T(8,128)(2,1)S(1)}, bf16[512,128]{1,0:T(8,128)(2,1)S(1)}, u32[]{:S(2)}, u32[]{:S(2)}) collective-permute-start(bf16[512,128]{1,0:T(8,128)(2,1)S(1)} %later_1.1), channel_id=1, source_target_pairs={{4,12},{5,13},{6,14},{7,15}} | collective-permute-start | bytes 393224 | tf_op jit(solution)/shard_map/ppermute | solution.py:212
  107.7 12.4 %collective-permute-start.17 = (bf16[512,128]{1,0:T(8,128)(2,1)S(1)}, bf16[512,128]{1,0:T(8,128)(2,1)S(1)}, u32[]{:S(2)}, u32[]{:S(2)}) collective-permute-start(bf16[512,128]{1,0:T(8,128)(2,1)S(1)} %get-tuple-element.50.value_ref), channel_id=1, source_target_pairs={{0,16},{1,17},{2,18},{3,19},{4,20},{5,21},{6,22},{7,23}} | collective-permute-start | bytes 393224 | tf_op jit(solution)/shard_map/ppermute | solution.py:212
  109.0 11.1 %collective-permute-start.16 = (bf16[512,128]{1,0:T(8,128)(2,1)S(1)}, bf16[512,128]{1,0:T(8,128)(2,1)S(1)}, u32[]{:S(2)}, u32[]{:S(2)}) collective-permute-start(bf16[512,128]{1,0:T(8,128)(2,1)S(1)} %get-tuple-element.50.value_ref), channel_id=1, source_target_pairs={{0,24},{1,25},{2,26},{3,27},{4,28},{5,29},{6,30},{7,31}} | collective-permute-start | bytes 393224 | tf_op jit(solution)/shard_map/ppermute | solution.py:212
  110.4 9.8 %collective-permute-start.15 = (bf16[512,128]{1,0:T(8,128)(2,1)S(1)}, bf16[512,128]{1,0:T(8,128)(2,1)S(1)}, u32[]{:S(2)}, u32[]{:S(2)}) collective-permute-start(bf16[512,128]{1,0:T(8,128)(2,1)S(1)} %get-tuple-element.50.value_ref), channel_id=1, source_target_pairs={{0,8},{1,9},{2,10},{3,11},{4,12},{5,13},{6,14},{7,15}} | collective-permute-start | bytes 393224 | tf_op jit(solution)/shard_map/ppermute | solution.py:212
  119.4 6.0 %collective-permute-start.34 = (bf16[512,128]{1,0:T(8,128)(2,1)S(1)}, bf16[512,128]{1,0:T(8,128)(2,1)S(1)}, u32[]{:S(2)}, u32[]{:S(2)}) collective-permute-start(bf16[512,128]{1,0:T(8,128)(2,1)S(1)} %get-tuple-element.65.value_ref), channel_id=1, source_target_pairs={{8,24},{9,25},{10,26},{11,27},{12,28},{13,29},{14,30},{15,31}} | collective-permute-start | bytes 393224 | tf_op jit(solution)/shard_map/ppermute | solution.py:212
  120.8 6.2 %collective-permute-start.33 = (bf16[512,128]{1,0:T(8,128)(2,1)S(1)}, bf16[512,128]{1,0:T(8,128)(2,1)S(1)}, u32[]{:S(2)}, u32[]{:S(2)}) collective-permute-start(bf16[512,128]{1,0:T(8,128)(2,1)S(1)} %get-tuple-element.65.value_ref), channel_id=1, source_target_pairs={{8,0},{9,1},{10,2},{11,3},{12,4},{13,5},{14,6},{15,7}} | collective-permute-start | bytes 393224 | tf_op jit(solution)/shard_map/ppermute | solution.py:212
  122.1 4.9 %collective-permute-start.32 = (bf16[512,128]{1,0:T(8,128)(2,1)S(1)}, bf16[512,128]{1,0:T(8,128)(2,1)S(1)}, u32[]{:S(2)}, u32[]{:S(2)}) collective-permute-start(bf16[512,128]{1,0:T(8,128)(2,1)S(1)} %get-tuple-element.65.value_ref), channel_id=1, source_target_pairs={{8,16},{9,17},{10,18},{11,19},{12,20},{13,21},{14,22},{15,23}} | collective-permute-start | bytes 393224 | tf_op jit(solution)/shard_map/ppermute | solution.py:212
  122.8 7.5 %collective-permute-start.25 = (bf16[512,128]{1,0:T(8,128)(2,1)S(1)}, bf16[512,128]{1,0:T(8,128)(2,1)S(1)}, u32[]{:S(2)}, u32[]{:S(2)}) collective-permute-start(bf16[512,128]{1,0:T(8,128)(2,1)S(1)} %picked.2.rest_0_), channel_id=1, source_target_pairs={{0,64},{1,65},{2,66},{3,67},{4,68},{5,69},{6,70},{7,71},{8,72},{9,... | collective-permute-start | bytes 393224 | tf_op jit(solution)/shard_map/ppermute | solution.py:212
  124.1 7.6 %collective-permute-start.24 = (bf16[512,128]{1,0:T(8,128)(2,1)S(1)}, bf16[512,128]{1,0:T(8,128)(2,1)S(1)}, u32[]{:S(2)}, u32[]{:S(2)}) collective-permute-start(bf16[512,128]{1,0:T(8,128)(2,1)S(1)} %picked.2.rest_0_), channel_id=1, source_target_pairs={{0,96},{1,97},{2,98},{3,99},{4,100},{5,101},{6,102},{7,103},{8,104... | collective-permute-start | bytes 393224 | tf_op jit(solution)/shard_map/ppermute | solution.py:212
  125.4 6.3 %collective-permute-start.23 = (bf16[512,128]{1,0:T(8,128)(2,1)S(1)}, bf16[512,128]{1,0:T(8,128)(2,1)S(1)}, u32[]{:S(2)}, u32[]{:S(2)}) collective-permute-start(bf16[512,128]{1,0:T(8,128)(2,1)S(1)} %picked.2.rest_0_), channel_id=1, source_target_pairs={{0,32},{1,33},{2,34},{3,35},{4,36},{5,37},{6,38},{7,39},{8,40},{9,... | collective-permute-start | bytes 393224 | tf_op jit(solution)/shard_map/ppermute | solution.py:212
  (8 other events, 65.0 us)

commit v6 on v5

--- a/solution.py
+++ b/solution.py
@@ -63,34 +63,34 @@
         copy.wait()
 
 
-def load_kernel(levels, slots, table, factor_ref, inverse_ref, held_ref, kept_ref, sems, other_sem):
+def add_products(total, level, slots, low, high, operand_of, table, held_ref, copy_of=None):
+    for slot in range(slots):
+        source = table[level, slot]
+
+        @pl.when(slot < table[level, slots])
+        def _():
+            if copy_of is not None:
+                copy_of(level, slot).wait()
+
+            @pl.when((source >= low) & (source < high))
+            def _():
+                total[...] += dot(held_ref[level * slots + slot], operand_of(source - low))
+
+
+def base_kernel(levels, slots, table, factor_ref, inverse_ref, *rest):
+    pieces, (keep_ref, send_ref, held_ref, kept_ref, operands, total, sems, other_sem) = rest[:-8], rest[-8:]
+
+    def copy_of(level, slot):
+        at = level * slots + slot
+        return pltpu.make_async_copy(factor_ref.at[level, slot], held_ref.at[at], sems.at[at])
+
+    for level in range(levels):
+        for slot in range(slots):
+            @pl.when(slot < table[level, slots])
+            def _():
+                copy_of(level, slot).start()
     inverses = pltpu.make_async_copy(inverse_ref, kept_ref, other_sem)
     inverses.start()
-
-    def each(act):
-        for level in range(levels):
-            for slot in range(slots):
-                @pl.when(slot < table[level, slots])
-                def _():
-                    at = level * slots + slot
-                    act(pltpu.make_async_copy(factor_ref.at[level, slot], held_ref.at[at], sems.at[at]))
-
-    each(lambda copy: copy.start())
-    each(lambda copy: copy.wait())
-    inverses.wait()
-
-
-def add_products(total, level, slots, low, high, operand_of, table, held_ref):
-    for slot in range(slots):
-        source = table[level, slot]
-
-        @pl.when((slot < table[level, slots]) & (source >= low) & (source < high))
-        def _():
-            total[...] += dot(held_ref[level * slots + slot], operand_of(source - low))
-
-
-def base_kernel(levels, slots, table, held_ref, *rest):
-    pieces, (keep_ref, send_ref, operands, total) = rest[:-4], rest[-4:]
     row, core = table[levels, 0], table[levels, 1]
     per_row = len(pieces) // NZ
     for k in range(NZ):
@@ -101,11 +101,12 @@
     other = pl.multiple_of((1 - core) * shares * some, shares * some)
     for level in range(levels):
         total[...] = jnp.zeros_like(total)
-        add_products(total, level, slots, 0, NZ * per_row, lambda q: operands[q], table, held_ref)
+        add_products(total, level, slots, 0, NZ * per_row, lambda q: operands[q], table, held_ref, copy_of)
         for share in range(shares):
             place_in = pl.ds(level * some, some)
             keep_ref[share, place_in] = total[pl.ds(mine + share * some, some)]
             send_ref[share, place_in] = total[pl.ds(other + share * some, some)].astype(BF16)
+    inverses.wait()
 
 
 def first_kernel(table, half_ref, other_ref, apex_ref, inverse_ref, ahead_ref, out_ref, target):
@@ -229,12 +230,11 @@
     return lax.all_to_all(value, "col", 0, 0, axis_index_groups=groups, tiled=True)
 
 
-def spread_x(value, x0, table):
-    got = [
+def spread_x(value, x0):
+    return [value] + [
         send(value, [(place(x0, 0, core, z), place((x0 + dx) % NX, 0, core, z)) for core in BOTH for z in range(NZ)])
         for dx in (1, 3, 2)
     ]
-    return pick(column(x0, 0, 0), table, value, got)
 
 
 def spread_y(value):
@@ -276,24 +276,23 @@
     near += [to_row(rounded[1], 1), to_row(rounded[0], -1)]
     far = [to_row(near[0], 1), to_row(near[1], -1)]
     pieces = rounded + [near[0], near[2]] + far + [near[3], near[1]]
-    held, inverses = (pltpu.with_memory_space_constraint(x, pltpu.VMEM) for x in call(
-        functools.partial(load_kernel, levels, slots), "load_blocks",
-        (pltpu.VMEM((levels * slots,) + block, BF16), pltpu.VMEM((levels,) + block, BF16)),
-        [SMEM, HBM, HBM], (table, factor_blocks, in_hbm(top_inverse[:, 0])),
-        scratch=[pltpu.SemaphoreType.DMA((levels * slots,)), pltpu.SemaphoreType.DMA],
-        nbytes=2 * factor_blocks.size, out_specs=(VMEM, VMEM),
-    ))
-    lists = (table, held)
-    keep, give = call(
+    keep, give, held, inverses = call(
         functools.partial(base_kernel, levels, slots), "base_products",
         (
             jax.ShapeDtypeStruct((shares, levels * some, samples), F32),
             jax.ShapeDtypeStruct((shares, levels * some, samples), BF16),
+            pltpu.VMEM((levels * slots,) + block, BF16),
+            pltpu.VMEM((levels,) + block, BF16),
         ),
-        [SMEM] + [VMEM] * (1 + len(pieces)), (*lists, *pieces),
-        scratch=[pltpu.VMEM((NZ * per_row, size, samples), BF16), pltpu.VMEM((size, samples), F32)],
-        flops=levels * slots * one // 2,
-    )
+        [SMEM, HBM, HBM] + [VMEM] * len(pieces), (table, factor_blocks, in_hbm(top_inverse[:, 0]), *pieces),
+        scratch=[
+            pltpu.VMEM((NZ * per_row, size, samples), BF16), pltpu.VMEM((size, samples), F32),
+            pltpu.SemaphoreType.DMA((levels * slots,)), pltpu.SemaphoreType.DMA,
+        ],
+        flops=levels * slots * one // 2, nbytes=2 * factor_blocks.size,
+    )
+    held, inverses = (pltpu.with_memory_space_constraint(x, pltpu.VMEM) for x in (held, inverses))
+    lists = (table, held)
     pair = call(
         pair_kernel, "pair_sums", jax.ShapeDtypeStruct(give.shape, BF16), [VMEM] * 2, (keep, other_core(give))
     )
@@ -337,16 +336,22 @@
     p30, p40 = products(0, (3, 4), kept)
     x2, packed, mixed12, kept = solve(1, pieces, [x1], ("value", "packed", "mixed", "kept"))
     pieces = onward(2, x2, packed)
-    mixed12 = spread_x(mixed12, 0, table)
+    mixed12, pieces[3] = after((mixed12, pieces[3]))
+    mixed12 = spread_x(mixed12, 0)
     p30, p40 = to_column(p30, 0, 2), to_column(p40, 0, 3)
     pieces, kept = after((pieces, kept))
     p41, = products(1, (4,), kept)
+    pieces, mixed12 = after((pieces, mixed12))
+    mixed12 = pick(column(0, 0, 0), table, mixed12[0], mixed12[1:])
     x3, packed = solve(2, pieces, [p30], ("value", "packed"))
     pieces = onward(3, x3, packed)
-    spread12 = spread_y(after((mixed12, x3))[0])
+    mixed12, pieces[3] = after((mixed12, pieces[3]))
+    spread12 = spread_y(mixed12)
     p41 = to_column(p41, 1, 3)
+    pieces, spread12 = after((pieces, spread12))
     x4, mixed34 = solve(3, pieces, [x3, p40, p41], ("value", "mixed"))
-    spread34 = spread_y(spread_x(mixed34, 1, table))
+    mixed34 = spread_x(mixed34, 1)
+    spread34 = spread_y(pick(column(1, 0, 0), table, mixed34[0], mixed34[1:]))
     spreads = spread12 + spread34
     mine = call(
         functools.partial(merge_kernel, levels), "merged", two, [SMEM] + [VMEM] * len(spreads), (table, *spreads)

time: 140 us -> 149 us (1.064); the launches traced: 139 us -> 146 us
  starting transfers between devices: 54.8 us -> 61.4 us
  waiting for transfers between devices: 28.8 us -> 32.1 us
  blocking collectives: 30.2 us -> 28.1 us
    ppermute x27, starting transfers between devices: 36 us -> 41.4 us  [send(): return lax.ppermute(value, AXES, pairs)]
    ppermute x27, waiting for transfers between devices: 15 us -> 19.4 us  [send(): return lax.ppermute(value, AXES, pairs)]
    all_to_all x2, blocking collectives: 30.2 us -> 28.1 us  [over_plane(): lax.all_to_all(value, 'col', 0, 0, axis_index_groups=groups, tiled=True)]
    pallas_call x16 -> x15, Pallas kernels: 22.9 us -> 21.9 us  [call(): pl.pallas_call(body, out_shape=outs, in_specs=in_specs, out_specs=out_spe...]
  transfers between devices with their start and end apart: 39 -> 39, of which waited for: 17 -> 15; matrix products, arithmetic and copies ran while one was open for 1% -> 1% of each run, Pallas kernels for 8% -> 2%
where the time goes in v6:
time: 149 us; the launch traced here: 146 us
  starting transfers between devices  61.4 us (41%)
  waiting for transfers between devices  32.1 us (22%)
  blocking collectives  28.1 us (19%)
  Pallas kernels  21.9 us (15%)
    ppermute x27, starting transfers between devices, send(): return lax.ppermute(value, AXES, pairs)  41.4 us
    all_to_all x2, blocking collectives, over_plane(): lax.all_to_all(value, 'col', 0, 0, axis_index_groups=groups, tiled=True)  28.1 us
    pallas_call x15, Pallas kernels, call(): pl.pallas_call(body, out_shape=outs, in_specs=in_specs, out_specs=out_spe...  21.9 us
    ppermute x27, waiting for transfers between devices, send(): return lax.ppermute(value, AXES, pairs)  19.4 us
    ppermute x9, starting transfers between devices, to_row(): return lax.ppermute(value, 'row', [(z, (z + step) % NZ) for z in range(NZ)])  14.7 us
    ppermute x9, waiting for transfers between devices, to_row(): return lax.ppermute(value, 'row', [(z, (z + step) % NZ) for z in range(NZ)])  8.64 us
    ppermute x3, starting transfers between devices, other_core(): return lax.ppermute(value, 'col', [(c, c ^ 1) for c in range(NX * NY * 2)])  5.23 us
    ppermute x3, waiting for transfers between devices, other_core(): return lax.ppermute(value, 'col', [(c, c ^ 1) for c in range(NX * NY * 2)])  4.03 us
  transfers between devices with their start and end apart: 39, of which 15 were waited for; matrix products, arithmetic and copies ran while one was open for 1% of the time, Pallas kernels for 2%

profile of v6, /device:TPU:1, one launch (start us, length us, event | category | flops | bytes accessed | tf_op | source)
XLA Modules:
  0.0 146.1 jit_solution(933605899824094536)
XLA Ops:
  0.6 2.7 %base_solve.1 = (f32[2,512,128]{2,1,0:T(8,128)}, bf16[512,128]{1,0:T(8,128)(2,1)S(1)}, bf16[512,128]{1,0:T(8,128)(2,1)S(1)}) custom-call(bf16[2,512,512]{2,1,0:T(8,128)(2,1)} %inverse_ref.1, f32[2,512,128]{2,1,0:T(8,128)} %rhs_ref.1), custom_call_target="tpu_custom_call" | custom-call | flops 134217728 | bytes 1835008 | tf_op jit(solution)/shard_map/base_solve/pallas_call | solution.py:32
  3.3 2.5 %collective-permute-start = (bf16[512,128]{1,0:T(8,128)(2,1)S(1)}, bf16[512,128]{1,0:T(8,128)(2,1)S(1)}, u32[]{:S(2)}, u32[]{:S(2)}) collective-permute-start(bf16[512,128]{1,0:T(8,128)(2,1)S(1)} %get-tuple-element.54.rest_0_), channel_id=1, source_target_pairs={{0,1},{1,2},{2,3},{3,0},{4,5},{5,6},{6,7},{7,4},{8,9},{9,10},{10,1... | collective-permute-start | bytes 393224 | tf_op jit(solution)/shard_map/ppermute | solution.py:221
  5.9 2.2 %collective-permute-start.3 = (bf16[512,128]{1,0:T(8,128)(2,1)S(1)}, bf16[512,128]{1,0:T(8,128)(2,1)S(1)}, u32[]{:S(2)}, u32[]{:S(2)}) collective-permute-start(bf16[512,128]{1,0:T(8,128)(2,1)S(1)} %get-tuple-element.55.rest_1_), channel_id=1, source_target_pairs={{0,3},{1,0},{2,1},{3,2},{4,7},{5,4},{6,5},{7,6},{8,11},{9,8},{10,9... | collective-permute-start | bytes 393224 | tf_op jit(solution)/shard_map/ppermute | solution.py:221
  8.1 2.7 %collective-permute-start.5 = (bf16[512,128]{1,0:T(8,128)(2,1)S(1)}, bf16[512,128]{1,0:T(8,128)(2,1)S(1)}, u32[]{:S(2)}, u32[]{:S(2)}) collective-permute-start(bf16[512,128]{1,0:T(8,128)(2,1)S(1)} %get-tuple-element.54.rest_0_), channel_id=1, source_target_pairs={{0,3},{1,0},{2,1},{3,2},{4,7},{5,4},{6,5},{7,6},{8,11},{9,8},{10,9... | collective-permute-start | bytes 393224 | tf_op jit(solution)/shard_map/ppermute | solution.py:221
  11.2 2.7 %collective-permute-start.4 = (bf16[512,128]{1,0:T(8,128)(2,1)S(1)}, bf16[512,128]{1,0:T(8,128)(2,1)S(1)}, u32[]{:S(2)}, u32[]{:S(2)}) collective-permute-start(bf16[512,128]{1,0:T(8,128)(2,1)S(1)} %collective-permute-done.3.rest_7_), channel_id=1, source_target_pairs={{0,3},{1,0},{2,1},{3,2},{4,7},{5,4},{6,5},{7,6},{8,11},{9,8},{10,9... | collective-permute-start | bytes 393224 | tf_op jit(solution)/shard_map/ppermute | solution.py:221
  16.3 5.0 %base_products.1 = (f32[16,80,128]{2,1,0:T(8,128)S(1)}, bf16[16,80,128]{2,1,0:T(8,128)(2,1)S(1)}, bf16[30,512,512]{2,1,0:T(8,128)(2,1)S(1)}, bf16[5,512,512]{2,1,0:T(8,128)(2,1)S(1)}) custom-call(s32[6,7]{1,0:T(8,128)S(1)} %pad_add_fusion.table, bf16[5,6,512,512]{3,2,1,0:T(8,128)(2,1)} %factor_ref.1, bf16[5,512,512]{2,1,0:T(8,128)(2,1)} %bitcast.11, ...), custom_call_target="tpu_custom_call" | custom-call | flops 1006632960 | bytes 15728640 | tf_op jit(solution)/shard_map/base_products/pallas_call | solution.py:32
  21.3 2.5 %collective-permute-start.6 = (bf16[16,80,128]{2,1,0:T(8,128)(2,1)S(1)}, bf16[16,80,128]{2,1,0:T(8,128)(2,1)S(1)}, u32[]{:S(2)}, u32[]{:S(2)}) collective-permute-start(bf16[16,80,128]{2,1,0:T(8,128)(2,1)S(1)} %get-tuple-element.57), channel_id=1, source_target_pairs={{0,4},{4,0},{8,12},{12,8},{16,20},{20,16},{24,28},{28,24},{32,36},... | collective-permute-start | bytes 983048 | tf_op jit(solution)/shard_map/ppermute | solution.py:225
  25.0 17.4 %all_to_all.10.in_ref = bf16[16,80,128]{2,1,0:T(8,128)(2,1)S(1)} all-to-all(bf16[16,80,128]{2,1,0:T(8,128)(2,1)S(1)} %pair_sums.1), channel_id=1, replica_groups={{0,8,16,24,32,40,48,56,64,72,80,88,96,104,112,120},{4,12,20,28,36,44,52..., dimensions={0} | all-to-all | bytes 655360 | tf_op jit(solution)/shard_map/all_to_all | solution.py:230
  42.5 10.7 %all_to_all.11.half_ref = bf16[16,80,128]{2,1,0:T(8,128)(2,1)S(1)} all-to-all(bf16[16,80,128]{2,1,0:T(8,128)(2,1)S(1)} %sum_shares.1), channel_id=1, replica_groups={{0,8,16,24,32,40,48,56,64,72,80,88,96,104,112,120},{4,12,20,28,36,44,52..., dimensions={0} | all-to-all | bytes 655360 | tf_op jit(solution)/shard_map/all_to_all | solution.py:230
  53.2 2.7 %collective-permute-start.7 = (bf16[16,80,128]{2,1,0:T(8,128)(2,1)S(1)}, bf16[16,80,128]{2,1,0:T(8,128)(2,1)S(1)}, u32[]{:S(2)}, u32[]{:S(2)}) collective-permute-start(bf16[16,80,128]{2,1,0:T(8,128)(2,1)S(1)} %all_to_all.11.half_ref), channel_id=1, source_target_pairs={{0,4},{4,0},{8,12},{12,8},{16,20},{20,16},{24,28},{28,24},{32,36},... | collective-permute-start | bytes 983048 | tf_op jit(solution)/shard_map/ppermute | solution.py:225
  58.2 3.4 %collective-permute-start.10 = (bf16[512,128]{1,0:T(8,128)(2,1)S(1)}, bf16[512,128]{1,0:T(8,128)(2,1)S(1)}, u32[]{:S(2)}, u32[]{:S(2)}) collective-permute-start(bf16[512,128]{1,0:T(8,128)(2,1)S(1)} %get-tuple-element.59.rest_0_.first_ref), channel_id=1, source_target_pairs={{0,3},{1,0},{2,1},{3,2},{4,7},{5,4},{6,5},{7,6},{8,11},{9,8},{10,9... | collective-permute-start | bytes 393224 | tf_op jit(solution)/shard_map/ppermute | solution.py:221
  62.8 1.5 %collective-permute-done.10.rest_3_ = bf16[512,128]{1,0:T(8,128)(2,1)S(1)} collective-permute-done((bf16[512,128]{1,0:T(8,128)(2,1)S(1)}, bf16[512,128]{1,0:T(8,128)(2,1)S(1)}, u32[]{:S(2)}, u32[]{:S(2)}) %collective-permute-start.10) | collective-permute-done | bytes 131104 | tf_op jit(solution)/shard_map/ppermute | solution.py:221
  64.3 5.9 %collective-permute-done.8.rest_1_ = bf16[512,128]{1,0:T(8,128)(2,1)S(1)} collective-permute-done((bf16[512,128]{1,0:T(8,128)(2,1)S(1)}, bf16[512,128]{1,0:T(8,128)(2,1)S(1)}, u32[]{:S(2)}, u32[]{:S(2)}) %collective-permute-start.8) | collective-permute-done | bytes 131104 | tf_op jit(solution)/shard_map/ppermute | solution.py:221
  76.7 3.6 %collective-permute-done.12.rest_1_ = bf16[512,128]{1,0:T(8,128)(2,1)S(1)} collective-permute-done((bf16[512,128]{1,0:T(8,128)(2,1)S(1)}, bf16[512,128]{1,0:T(8,128)(2,1)S(1)}, u32[]{:S(2)}, u32[]{:S(2)}) %collective-permute-start.12) | collective-permute-done | bytes 131104 | tf_op jit(solution)/shard_map/ppermute | solution.py:213
  80.3 1.6 %collective-permute-done.13.rest_2_ = bf16[512,128]{1,0:T(8,128)(2,1)S(1)} collective-permute-done((bf16[512,128]{1,0:T(8,128)(2,1)S(1)}, bf16[512,128]{1,0:T(8,128)(2,1)S(1)}, u32[]{:S(2)}, u32[]{:S(2)}) %collective-permute-start.13) | collective-permute-done | bytes 131104 | tf_op jit(solution)/shard_map/ppermute | solution.py:213
  81.9 2.9 %solve_2.1 = (bf16[512,128]{1,0:T(8,128)(2,1)S(1)}, bf16[2,512,128]{2,1,0:T(8,128)(2,1)S(1)}, bf16[512,128]{1,0:T(8,128)(2,1)S(1)}, bf16[4,512,128]{2,1,0:T(8,128)(2,1)S(1)}) custom-call(s32[6,7]{1,0:T(8,128)S(1)} %pad_add_fusion.table, bf16[30,512,512]{2,1,0:T(8,128)(2,1)S(1)} %get-tuple-element.60.held_ref, ...), custom_call_target="tpu_custom_call" | custom-call | flops 335544320 | tf_op jit(solution)/shard_map/solve_2/pallas_call | solution.py:32
  84.8 1.3 collective-permute-start.18
  86.1 1.3 collective-permute-start.16
  87.4 1.3 collective-permute-start.15
  90.1 1.3 collective-permute-start.19
  91.4 1.3 collective-permute-start.20
  95.7 2.8 %collective-permute-done.21.rest_2_ = bf16[512,128]{1,0:T(8,128)(2,1)S(1)} collective-permute-done((bf16[512,128]{1,0:T(8,128)(2,1)S(1)}, bf16[512,128]{1,0:T(8,128)(2,1)S(1)}, u32[]{:S(2)}, u32[]{:S(2)}) %collective-permute-start.21) | collective-permute-done | bytes 131104 | tf_op jit(solution)/shard_map/ppermute | solution.py:213
  102.4 1.5 %later_1.1 = bf16[512,128]{1,0:T(8,128)(2,1)S(1)} custom-call(s32[6,7]{1,0:T(8,128)S(1)} %pad_add_fusion.table, bf16[30,512,512]{2,1,0:T(8,128)(2,1)S(1)} %get-tuple-element.60.held_ref, bf16[4,512,128]{2,1,0:T(8,128)(2,1)S(1)} %get-tuple-element.102.operands), custom_call_target="tpu_custom_call" | custom-call | flops 268435456 | tf_op jit(solution)/shard_map/later_1/pallas_call | solution.py:32
  107.2 1.3 collective-permute-start.29
  109.2 12.7 %collective-permute-start.31 = (bf16[512,128]{1,0:T(8,128)(2,1)S(1)}, bf16[512,128]{1,0:T(8,128)(2,1)S(1)}, u32[]{:S(2)}, u32[]{:S(2)}) collective-permute-start(bf16[512,128]{1,0:T(8,128)(2,1)S(1)} %later_1.1), channel_id=1, source_target_pairs={{4,12},{5,13},{6,14},{7,15}} | collective-permute-start | bytes 393224 | tf_op jit(solution)/shard_map/ppermute | solution.py:213
  121.9 2.5 %collective-permute-done.31.rest_6_ = bf16[512,128]{1,0:T(8,128)(2,1)S(1)} collective-permute-done((bf16[512,128]{1,0:T(8,128)(2,1)S(1)}, bf16[512,128]{1,0:T(8,128)(2,1)S(1)}, u32[]{:S(2)}, u32[]{:S(2)}) %collective-permute-start.31) | collective-permute-done | bytes 131104 | tf_op jit(solution)/shard_map/ppermute | solution.py:213
  124.5 1.7 %solve_4.1 = (bf16[512,128]{1,0:T(8,128)(2,1)}, bf16[512,128]{1,0:T(8,128)(2,1)S(1)}) custom-call(s32[6,7]{1,0:T(8,128)S(1)} %pad_add_fusion.table, bf16[30,512,512]{2,1,0:T(8,128)(2,1)S(1)} %get-tuple-element.60.held_ref, f32[4,512,128]{2,1,0:T(8,128)S(1)} %get-tuple-element.61.ahead_ref, bf16[5,512,512]{2,1,0:T(8,128)(2,1)S(1)} %get-tuple-element.58.inverse_ref, ...), custom_call_target="tpu_custom_call" | custom-call | flops 335544320 | tf_op jit(solution)/shard_map/solve_4/pallas_call | solution.py:32
  128.8 6.5 %collective-permute-done.33.rest_1_ = bf16[512,128]{1,0:T(8,128)(2,1)S(1)} collective-permute-done((bf16[512,128]{1,0:T(8,128)(2,1)S(1)}, bf16[512,128]{1,0:T(8,128)(2,1)S(1)}, u32[]{:S(2)}, u32[]{:S(2)}) %collective-permute-start.33) | collective-permute-done | bytes 131104 | tf_op jit(solution)/shard_map/ppermute | solution.py:213
  136.0 1.3 collective-permute-start.35
  140.5 1.5 %collective-permute-done.37.rest_7_ = bf16[512,128]{1,0:T(8,128)(2,1)S(1)} collective-permute-done((bf16[512,128]{1,0:T(8,128)(2,1)S(1)}, bf16[512,128]{1,0:T(8,128)(2,1)S(1)}, u32[]{:S(2)}, u32[]{:S(2)}) %collective-permute-start.37) | collective-permute-done | bytes 131104 | tf_op jit(solution)/shard_map/ppermute | solution.py:213
  142.8 1.5 %collective-permute-done.38.other_ref = bf16[2,512,128]{2,1,0:T(8,128)(2,1)S(1)} collective-permute-done((bf16[2,512,128]{2,1,0:T(8,128)(2,1)S(1)}, bf16[2,512,128]{2,1,0:T(8,128)(2,1)S(1)}, u32[]{:S(2)}, u32[]{:S(2)}) %collective-permute-start.38) | collective-permute-done | bytes 262176 | tf_op jit(solution)/shard_map/ppermute | solution.py:225
  144.3 1.8 %final.1 = f32[5,512,128]{2,1,0:T(8,128)} custom-call(s32[6,7]{1,0:T(8,128)S(1)} %pad_add_fusion.table, bf16[512,128]{1,0:T(8,128)(2,1)S(1)} %get-tuple-element.59.rest_0_.first_ref, bf16[2,512,128]{2,1,0:T(8,128)(2,1)S(1)} %merged.1.mine_ref, bf16[2,512,128]{2,1,0:T(8,128)(2,1)S(1)} %collective-permute-done.38.other_ref), custom_call_target="tpu_custom_call" | custom-call | tf_op jit(solution)/shard_map/final/pallas_call | solution.py:32
  (69 shorter events, 33.5 us)
Async XLA Ops:
  3.3 7.9 %collective-permute-start = (bf16[512,128]{1,0:T(8,128)(2,1)S(1)}, bf16[512,128]{1,0:T(8,128)(2,1)S(1)}, u32[]{:S(2)}, u32[]{:S(2)}) collective-permute-start(bf16[512,128]{1,0:T(8,128)(2,1)S(1)} %get-tuple-element.54.rest_0_), channel_id=1, source_target_pairs={{0,1},{1,2},{2,3},{3,0},{4,5},{5,6},{6,7},{7,4},{8,9},{9,10},{10,1... | collective-permute-start | bytes 393224 | tf_op jit(solution)/shard_map/ppermute | solution.py:221
  5.9 5.3 %collective-permute-start.3 = (bf16[512,128]{1,0:T(8,128)(2,1)S(1)}, bf16[512,128]{1,0:T(8,128)(2,1)S(1)}, u32[]{:S(2)}, u32[]{:S(2)}) collective-permute-start(bf16[512,128]{1,0:T(8,128)(2,1)S(1)} %get-tuple-element.55.rest_1_), channel_id=1, source_target_pairs={{0,3},{1,0},{2,1},{3,2},{4,7},{5,4},{6,5},{7,6},{8,11},{9,8},{10,9... | collective-permute-start | bytes 393224 | tf_op jit(solution)/shard_map/ppermute | solution.py:221
  8.1 7.3 %collective-permute-start.1 = (bf16[512,128]{1,0:T(8,128)(2,1)S(1)}, bf16[512,128]{1,0:T(8,128)(2,1)S(1)}, u32[]{:S(2)}, u32[]{:S(2)}) collective-permute-start(bf16[512,128]{1,0:T(8,128)(2,1)S(1)} %get-tuple-element.55.rest_1_), channel_id=1, source_target_pairs={{0,1},{1,2},{2,3},{3,0},{4,5},{5,6},{6,7},{7,4},{8,9},{9,10},{10,1... | collective-permute-start | bytes 393224 | tf_op jit(solution)/shard_map/ppermute | solution.py:221
  8.1 7.3 %collective-permute-start.5 = (bf16[512,128]{1,0:T(8,128)(2,1)S(1)}, bf16[512,128]{1,0:T(8,128)(2,1)S(1)}, u32[]{:S(2)}, u32[]{:S(2)}) collective-permute-start(bf16[512,128]{1,0:T(8,128)(2,1)S(1)} %get-tuple-element.54.rest_0_), channel_id=1, source_target_pairs={{0,3},{1,0},{2,1},{3,2},{4,7},{5,4},{6,5},{7,6},{8,11},{9,8},{10,9... | collective-permute-start | bytes 393224 | tf_op jit(solution)/shard_map/ppermute | solution.py:221
  11.2 5.0 %collective-permute-start.2 = (bf16[512,128]{1,0:T(8,128)(2,1)S(1)}, bf16[512,128]{1,0:T(8,128)(2,1)S(1)}, u32[]{:S(2)}, u32[]{:S(2)}) collective-permute-start(bf16[512,128]{1,0:T(8,128)(2,1)S(1)} %collective-permute-done.rest_2_), channel_id=1, source_target_pairs={{0,1},{1,2},{2,3},{3,0},{4,5},{5,6},{6,7},{7,4},{8,9},{9,10},{10,1... | collective-permute-start | bytes 393224 | tf_op jit(solution)/shard_map/ppermute | solution.py:221
  11.2 5.0 %collective-permute-start.4 = (bf16[512,128]{1,0:T(8,128)(2,1)S(1)}, bf16[512,128]{1,0:T(8,128)(2,1)S(1)}, u32[]{:S(2)}, u32[]{:S(2)}) collective-permute-start(bf16[512,128]{1,0:T(8,128)(2,1)S(1)} %collective-permute-done.3.rest_7_), channel_id=1, source_target_pairs={{0,3},{1,0},{2,1},{3,2},{4,7},{5,4},{6,5},{7,6},{8,11},{9,8},{10,9... | collective-permute-start | bytes 393224 | tf_op jit(solution)/shard_map/ppermute | solution.py:221
  53.2 3.9 %collective-permute-start.7 = (bf16[16,80,128]{2,1,0:T(8,128)(2,1)S(1)}, bf16[16,80,128]{2,1,0:T(8,128)(2,1)S(1)}, u32[]{:S(2)}, u32[]{:S(2)}) collective-permute-start(bf16[16,80,128]{2,1,0:T(8,128)(2,1)S(1)} %all_to_all.11.half_ref), channel_id=1, source_target_pairs={{0,4},{4,0},{8,12},{12,8},{16,20},{20,16},{24,28},{28,24},{32,36},... | collective-permute-start | bytes 983048 | tf_op jit(solution)/shard_map/ppermute | solution.py:225
  58.2 6.1 %collective-permute-start.10 = (bf16[512,128]{1,0:T(8,128)(2,1)S(1)}, bf16[512,128]{1,0:T(8,128)(2,1)S(1)}, u32[]{:S(2)}, u32[]{:S(2)}) collective-permute-start(bf16[512,128]{1,0:T(8,128)(2,1)S(1)} %get-tuple-element.59.rest_0_.first_ref), channel_id=1, source_target_pairs={{0,3},{1,0},{2,1},{3,2},{4,7},{5,4},{6,5},{7,6},{8,11},{9,8},{10,9... | collective-permute-start | bytes 393224 | tf_op jit(solution)/shard_map/ppermute | solution.py:221
  61.6 8.7 %collective-permute-start.8 = (bf16[512,128]{1,0:T(8,128)(2,1)S(1)}, bf16[512,128]{1,0:T(8,128)(2,1)S(1)}, u32[]{:S(2)}, u32[]{:S(2)}) collective-permute-start(bf16[512,128]{1,0:T(8,128)(2,1)S(1)} %get-tuple-element.59.rest_0_.first_ref), channel_id=1, source_target_pairs={{0,1},{1,2},{2,3},{3,0},{4,5},{5,6},{6,7},{7,4},{8,9},{9,10},{10,1... | collective-permute-start | bytes 393224 | tf_op jit(solution)/shard_map/ppermute | solution.py:221
  61.6 8.7 %collective-permute-start.9 = (bf16[512,128]{1,0:T(8,128)(2,1)S(1)}, bf16[512,128]{1,0:T(8,128)(2,1)S(1)}, u32[]{:S(2)}, u32[]{:S(2)}) collective-permute-start(bf16[512,128]{1,0:T(8,128)(2,1)S(1)} %get-tuple-element.59.rest_0_.first_ref), channel_id=1, source_target_pairs={{0,2},{1,3},{2,0},{3,1},{4,6},{5,7},{6,4},{7,5},{8,10},{9,11},{10,... | collective-permute-start | bytes 393224 | tf_op jit(solution)/shard_map/ppermute | solution.py:221
  71.5 10.4 %collective-permute-start.11 = (bf16[2,512,128]{2,1,0:T(8,128)(2,1)S(1)}, bf16[2,512,128]{2,1,0:T(8,128)(2,1)S(1)}, u32[]{:S(2)}, u32[]{:S(2)}) collective-permute-start(bf16[2,512,128]{2,1,0:T(8,128)(2,1)S(1)} %get-tuple-element.62), channel_id=1, source_target_pairs={{0,4},{1,5},{2,6},{3,7}} | collective-permute-start | bytes 786440 | tf_op jit(solution)/shard_map/ppermute | solution.py:213
  72.8 7.5 %collective-permute-start.12 = (bf16[512,128]{1,0:T(8,128)(2,1)S(1)}, bf16[512,128]{1,0:T(8,128)(2,1)S(1)}, u32[]{:S(2)}, u32[]{:S(2)}) collective-permute-start(bf16[512,128]{1,0:T(8,128)(2,1)S(1)} %get-tuple-element.63.rest_4_), channel_id=1, source_target_pairs={{0,5},{1,6},{2,7},{3,4}} | collective-permute-start | bytes 393224 | tf_op jit(solution)/shard_map/ppermute | solution.py:213
  74.1 7.8 %collective-permute-start.13 = (bf16[512,128]{1,0:T(8,128)(2,1)S(1)}, bf16[512,128]{1,0:T(8,128)(2,1)S(1)}, u32[]{:S(2)}, u32[]{:S(2)}) collective-permute-start(bf16[512,128]{1,0:T(8,128)(2,1)S(1)} %get-tuple-element.63.rest_4_), channel_id=1, source_target_pairs={{0,6},{1,7},{2,4},{3,5}} | collective-permute-start | bytes 393224 | tf_op jit(solution)/shard_map/ppermute | solution.py:213
  75.4 6.5 %collective-permute-start.14 = (bf16[512,128]{1,0:T(8,128)(2,1)S(1)}, bf16[512,128]{1,0:T(8,128)(2,1)S(1)}, u32[]{:S(2)}, u32[]{:S(2)}) collective-permute-start(bf16[512,128]{1,0:T(8,128)(2,1)S(1)} %get-tuple-element.63.rest_4_), channel_id=1, source_target_pairs={{0,7},{1,4},{2,5},{3,6}} | collective-permute-start | bytes 393224 | tf_op jit(solution)/shard_map/ppermute | solution.py:213
  84.8 5.2 %collective-permute-start.18 = (bf16[512,128]{1,0:T(8,128)(2,1)S(1)}, bf16[512,128]{1,0:T(8,128)(2,1)S(1)}, u32[]{:S(2)}, u32[]{:S(2)}) collective-permute-start(bf16[512,128]{1,0:T(8,128)(2,1)S(1)} %get-tuple-element.70), channel_id=1, source_target_pairs={{4,11},{5,8},{6,9},{7,10}} | collective-permute-start | bytes 393224 | tf_op jit(solution)/shard_map/ppermute | solution.py:213
  86.1 6.5 %collective-permute-start.16 = (bf16[512,128]{1,0:T(8,128)(2,1)S(1)}, bf16[512,128]{1,0:T(8,128)(2,1)S(1)}, u32[]{:S(2)}, u32[]{:S(2)}) collective-permute-start(bf16[512,128]{1,0:T(8,128)(2,1)S(1)} %get-tuple-element.70), channel_id=1, source_target_pairs={{4,9},{5,10},{6,11},{7,8}} | collective-permute-start | bytes 393224 | tf_op jit(solution)/shard_map/ppermute | solution.py:213
  87.4 8.0 %collective-permute-start.15 = (bf16[2,512,128]{2,1,0:T(8,128)(2,1)S(1)}, bf16[2,512,128]{2,1,0:T(8,128)(2,1)S(1)}, u32[]{:S(2)}, u32[]{:S(2)}) collective-permute-start(bf16[2,512,128]{2,1,0:T(8,128)(2,1)S(1)} %get-tuple-element.69), channel_id=1, source_target_pairs={{4,8},{5,9},{6,10},{7,11}} | collective-permute-start | bytes 786440 | tf_op jit(solution)/shard_map/ppermute | solution.py:213
  88.7 6.0 %collective-permute-start.17 = (bf16[512,128]{1,0:T(8,128)(2,1)S(1)}, bf16[512,128]{1,0:T(8,128)(2,1)S(1)}, u32[]{:S(2)}, u32[]{:S(2)}) collective-permute-start(bf16[512,128]{1,0:T(8,128)(2,1)S(1)} %get-tuple-element.70), channel_id=1, source_target_pairs={{4,10},{5,11},{6,8},{7,9}} | collective-permute-start | bytes 393224 | tf_op jit(solution)/shard_map/ppermute | solution.py:213
  90.1 5.7 %collective-permute-start.19 = (bf16[512,128]{1,0:T(8,128)(2,1)S(1)}, bf16[512,128]{1,0:T(8,128)(2,1)S(1)}, u32[]{:S(2)}, u32[]{:S(2)}) collective-permute-start(bf16[512,128]{1,0:T(8,128)(2,1)S(1)} %get-tuple-element.87.value_ref), channel_id=1, source_target_pairs={{0,8},{1,9},{2,10},{3,11},{4,12},{5,13},{6,14},{7,15}} | collective-permute-start | bytes 393224 | tf_op jit(solution)/shard_map/ppermute | solution.py:213
  91.4 4.4 %collective-permute-start.20 = (bf16[512,128]{1,0:T(8,128)(2,1)S(1)}, bf16[512,128]{1,0:T(8,128)(2,1)S(1)}, u32[]{:S(2)}, u32[]{:S(2)}) collective-permute-start(bf16[512,128]{1,0:T(8,128)(2,1)S(1)} %get-tuple-element.87.value_ref), channel_id=1, source_target_pairs={{0,24},{1,25},{2,26},{3,27},{4,28},{5,29},{6,30},{7,31}} | collective-permute-start | bytes 393224 | tf_op jit(solution)/shard_map/ppermute | solution.py:213
  92.7 5.9 %collective-permute-start.21 = (bf16[512,128]{1,0:T(8,128)(2,1)S(1)}, bf16[512,128]{1,0:T(8,128)(2,1)S(1)}, u32[]{:S(2)}, u32[]{:S(2)}) collective-permute-start(bf16[512,128]{1,0:T(8,128)(2,1)S(1)} %get-tuple-element.87.value_ref), channel_id=1, source_target_pairs={{0,16},{1,17},{2,18},{3,19},{4,20},{5,21},{6,22},{7,23}} | collective-permute-start | bytes 393224 | tf_op jit(solution)/shard_map/ppermute | solution.py:213
  99.7 9.5 %collective-permute-start.23 = (bf16[2,512,128]{2,1,0:T(8,128)(2,1)S(1)}, bf16[2,512,128]{2,1,0:T(8,128)(2,1)S(1)}, u32[]{:S(2)}, u32[]{:S(2)}) collective-permute-start(bf16[2,512,128]{2,1,0:T(8,128)(2,1)S(1)} %get-tuple-element.85), channel_id=1, source_target_pairs={{8,12},{9,13},{10,14},{11,15}} | collective-permute-start | bytes 786440 | tf_op jit(solution)/shard_map/ppermute | solution.py:213
  100.3 4.2 %collective-permute-start.26 = (bf16[512,128]{1,0:T(8,128)(2,1)S(1)}, bf16[512,128]{1,0:T(8,128)(2,1)S(1)}, u32[]{:S(2)}, u32[]{:S(2)}) collective-permute-start(bf16[512,128]{1,0:T(8,128)(2,1)S(1)} %get-tuple-element.86.rest_4_), channel_id=1, source_target_pairs={{8,15},{9,12},{10,13},{11,14}} | collective-permute-start | bytes 393224 | tf_op jit(solution)/shard_map/ppermute | solution.py:213
  101.0 6.1 %collective-permute-start.24 = (bf16[512,128]{1,0:T(8,128)(2,1)S(1)}, bf16[512,128]{1,0:T(8,128)(2,1)S(1)}, u32[]{:S(2)}, u32[]{:S(2)}) collective-permute-start(bf16[512,128]{1,0:T(8,128)(2,1)S(1)} %get-tuple-element.86.rest_4_), channel_id=1, source_target_pairs={{8,13},{9,14},{10,15},{11,12}} | collective-permute-start | bytes 393224 | tf_op jit(solution)/shard_map/ppermute | solution.py:213
  101.7 6.8 %collective-permute-start.25 = (bf16[512,128]{1,0:T(8,128)(2,1)S(1)}, bf16[512,128]{1,0:T(8,128)(2,1)S(1)}, u32[]{:S(2)}, u32[]{:S(2)}) collective-permute-start(bf16[512,128]{1,0:T(8,128)(2,1)S(1)} %get-tuple-element.86.rest_4_), channel_id=1, source_target_pairs={{8,14},{9,15},{10,12},{11,13}} | collective-permute-start | bytes 393224 | tf_op jit(solution)/shard_map/ppermute | solution.py:213
  104.5 17.4 %collective-permute-start.27 = (bf16[512,128]{1,0:T(8,128)(2,1)S(1)}, bf16[512,128]{1,0:T(8,128)(2,1)S(1)}, u32[]{:S(2)}, u32[]{:S(2)}) collective-permute-start(bf16[512,128]{1,0:T(8,128)(2,1)S(1)} %picked.2.rest_0_), channel_id=1, source_target_pairs={{0,32},{1,33},{2,34},{3,35},{4,36},{5,37},{6,38},{7,39},{8,40},{9,... | collective-permute-start | bytes 393224 | tf_op jit(solution)/shard_map/ppermute | solution.py:213
  105.8 16.1 %collective-permute-start.28 = (bf16[512,128]{1,0:T(8,128)(2,1)S(1)}, bf16[512,128]{1,0:T(8,128)(2,1)S(1)}, u32[]{:S(2)}, u32[]{:S(2)}) collective-permute-start(bf16[512,128]{1,0:T(8,128)(2,1)S(1)} %picked.2.rest_0_), channel_id=1, source_target_pairs={{0,96},{1,97},{2,98},{3,99},{4,100},{5,101},{6,102},{7,103},{8,104... | collective-permute-start | bytes 393224 | tf_op jit(solution)/shard_map/ppermute | solution.py:213
  107.2 14.8 %collective-permute-start.29 = (bf16[512,128]{1,0:T(8,128)(2,1)S(1)}, bf16[512,128]{1,0:T(8,128)(2,1)S(1)}, u32[]{:S(2)}, u32[]{:S(2)}) collective-permute-start(bf16[512,128]{1,0:T(8,128)(2,1)S(1)} %picked.2.rest_0_), channel_id=1, source_target_pairs={{0,64},{1,65},{2,66},{3,67},{4,68},{5,69},{6,70},{7,71},{8,72},{9,... | collective-permute-start | bytes 393224 | tf_op jit(solution)/shard_map/ppermute | solution.py:213
  108.5 13.5 %collective-permute-start.30 = (bf16[512,128]{1,0:T(8,128)(2,1)S(1)}, bf16[512,128]{1,0:T(8,128)(2,1)S(1)}, u32[]{:S(2)}, u32[]{:S(2)}) collective-permute-start(bf16[512,128]{1,0:T(8,128)(2,1)S(1)} %get-tuple-element.101), channel_id=1, source_target_pairs={{0,12},{1,13},{2,14},{3,15}} | collective-permute-start | bytes 393224 | tf_op jit(solution)/shard_map/ppermute | solution.py:213
  109.2 15.3 %collective-permute-start.31 = (bf16[512,128]{1,0:T(8,128)(2,1)S(1)}, bf16[512,128]{1,0:T(8,128)(2,1)S(1)}, u32[]{:S(2)}, u32[]{:S(2)}) collective-permute-start(bf16[512,128]{1,0:T(8,128)(2,1)S(1)} %later_1.1), channel_id=1, source_target_pairs={{4,12},{5,13},{6,14},{7,15}} | collective-permute-start | bytes 393224 | tf_op jit(solution)/shard_map/ppermute | solution.py:213
  126.8 8.5 %collective-permute-start.33 = (bf16[512,128]{1,0:T(8,128)(2,1)S(1)}, bf16[512,128]{1,0:T(8,128)(2,1)S(1)}, u32[]{:S(2)}, u32[]{:S(2)}) collective-permute-start(bf16[512,128]{1,0:T(8,128)(2,1)S(1)} %get-tuple-element.103.value_ref), channel_id=1, source_target_pairs={{8,0},{9,1},{10,2},{11,3},{12,4},{13,5},{14,6},{15,7}} | collective-permute-start | bytes 393224 | tf_op jit(solution)/shard_map/ppermute | solution.py:213
  128.1 7.2 %collective-permute-start.34 = (bf16[512,128]{1,0:T(8,128)(2,1)S(1)}, bf16[512,128]{1,0:T(8,128)(2,1)S(1)}, u32[]{:S(2)}, u32[]{:S(2)}) collective-permute-start(bf16[512,128]{1,0:T(8,128)(2,1)S(1)} %get-tuple-element.103.value_ref), channel_id=1, source_target_pairs={{8,24},{9,25},{10,26},{11,27},{12,28},{13,29},{14,30},{15,31}} | collective-permute-start | bytes 393224 | tf_op jit(solution)/shard_map/ppermute | solution.py:213
  (8 other events, 58.2 us)

commit v7 on v6

--- a/solution.py
+++ b/solution.py
@@ -336,19 +336,16 @@
     p30, p40 = products(0, (3, 4), kept)
     x2, packed, mixed12, kept = solve(1, pieces, [x1], ("value", "packed", "mixed", "kept"))
     pieces = onward(2, x2, packed)
-    mixed12, pieces[3] = after((mixed12, pieces[3]))
     mixed12 = spread_x(mixed12, 0)
+    mixed12 = pick(column(0, 0, 0), table, mixed12[0], mixed12[1:])
     p30, p40 = to_column(p30, 0, 2), to_column(p40, 0, 3)
     pieces, kept = after((pieces, kept))
     p41, = products(1, (4,), kept)
-    pieces, mixed12 = after((pieces, mixed12))
-    mixed12 = pick(column(0, 0, 0), table, mixed12[0], mixed12[1:])
+    pieces, p40 = after((pieces, p40))
     x3, packed = solve(2, pieces, [p30], ("value", "packed"))
     pieces = onward(3, x3, packed)
-    mixed12, pieces[3] = after((mixed12, pieces[3]))
-    spread12 = spread_y(mixed12)
+    spread12 = spread_y(after((mixed12, x3))[0])
     p41 = to_column(p41, 1, 3)
-    pieces, spread12 = after((pieces, spread12))
     x4, mixed34 = solve(3, pieces, [x3, p40, p41], ("value", "mixed"))
     mixed34 = spread_x(mixed34, 1)
     spread34 = spread_y(pick(column(1, 0, 0), table, mixed34[0], mixed34[1:]))

time: 149 us -> 142 us (0.953)
  waiting for transfers between devices: 32.1 us -> 29.3 us
  starting transfers between devices: 61.4 us -> 59.3 us
  Pallas kernels: 21.9 us -> 20.1 us
    ppermute x27, waiting for transfers between devices: 19.4 us -> 12.9 us  [send(): return lax.ppermute(value, AXES, pairs)]
    ppermute x9, waiting for transfers between devices: 8.64 us -> 12.4 us  [to_row(): return lax.ppermute(value, 'row', [(z, (z + step) % NZ) for z in range(NZ)])]
    pallas_call x15, Pallas kernels: 21.9 us -> 20.1 us  [call(): pl.pallas_call(body, out_shape=outs, in_specs=in_specs, out_specs=out_spe...]
    ppermute x9, starting transfers between devices: 14.7 us -> 13 us  [to_row(): return lax.ppermute(value, 'row', [(z, (z + step) % NZ) for z in range(NZ)])]
  transfers between devices with their start and end apart: 39 -> 39, of which waited for: 15 -> 16; matrix products, arithmetic and copies ran while one was open for 1% -> 1% of each run, Pallas kernels for 2% -> 4%
where the time goes in v7:
time: 142 us; the launch traced here: 140 us
  starting transfers between devices  59.3 us (42%)
  waiting for transfers between devices  29.3 us (21%)
  blocking collectives  28.3 us (20%)
  Pallas kernels  20.1 us (14%)
    ppermute x27, starting transfers between devices, send(): return lax.ppermute(value, AXES, pairs)  41.4 us
    all_to_all x2, blocking collectives, over_plane(): lax.all_to_all(value, 'col', 0, 0, axis_index_groups=groups, tiled=True)  28.3 us
    pallas_call x15, Pallas kernels, call(): pl.pallas_call(body, out_shape=outs, in_specs=in_specs, out_specs=out_spe...  20.1 us
    ppermute x9, starting transfers between devices, to_row(): return lax.ppermute(value, 'row', [(z, (z + step) % NZ) for z in range(NZ)])  13 us
    ppermute x27, waiting for transfers between devices, send(): return lax.ppermute(value, AXES, pairs)  12.9 us
    ppermute x9, waiting for transfers between devices, to_row(): return lax.ppermute(value, 'row', [(z, (z + step) % NZ) for z in range(NZ)])  12.4 us
    ppermute x3, starting transfers between devices, other_core(): return lax.ppermute(value, 'col', [(c, c ^ 1) for c in range(NX * NY * 2)])  4.87 us
    ppermute x3, waiting for transfers between devices, other_core(): return lax.ppermute(value, 'col', [(c, c ^ 1) for c in range(NX * NY * 2)])  4.03 us
  transfers between devices with their start and end apart: 39, of which 16 were waited for; matrix products, arithmetic and copies ran while one was open for 1% of the time, Pallas kernels for 4%

profile of v7, /device:TPU:1, one launch (start us, length us, event | category | flops | bytes accessed | tf_op | source)
XLA Modules:
  0.0 139.6 jit_solution(1122547490889229425)
XLA Ops:
  0.6 2.7 %base_solve.1 = (f32[2,512,128]{2,1,0:T(8,128)}, bf16[512,128]{1,0:T(8,128)(2,1)S(1)}, bf16[512,128]{1,0:T(8,128)(2,1)S(1)}) custom-call(bf16[2,512,512]{2,1,0:T(8,128)(2,1)} %inverse_ref.1, f32[2,512,128]{2,1,0:T(8,128)} %rhs_ref.1), custom_call_target="tpu_custom_call" | custom-call | flops 134217728 | bytes 1835008 | tf_op jit(solution)/shard_map/base_solve/pallas_call | solution.py:32
  3.3 2.5 %collective-permute-start = (bf16[512,128]{1,0:T(8,128)(2,1)S(1)}, bf16[512,128]{1,0:T(8,128)(2,1)S(1)}, u32[]{:S(2)}, u32[]{:S(2)}) collective-permute-start(bf16[512,128]{1,0:T(8,128)(2,1)S(1)} %get-tuple-element.40.rest_0_), channel_id=1, source_target_pairs={{0,1},{1,2},{2,3},{3,0},{4,5},{5,6},{6,7},{7,4},{8,9},{9,10},{10,1... | collective-permute-start | bytes 393224 | tf_op jit(solution)/shard_map/ppermute | solution.py:221
  5.9 2.2 %collective-permute-start.3 = (bf16[512,128]{1,0:T(8,128)(2,1)S(1)}, bf16[512,128]{1,0:T(8,128)(2,1)S(1)}, u32[]{:S(2)}, u32[]{:S(2)}) collective-permute-start(bf16[512,128]{1,0:T(8,128)(2,1)S(1)} %get-tuple-element.41.rest_1_), channel_id=1, source_target_pairs={{0,3},{1,0},{2,1},{3,2},{4,7},{5,4},{6,5},{7,6},{8,11},{9,8},{10,9... | collective-permute-start | bytes 393224 | tf_op jit(solution)/shard_map/ppermute | solution.py:221
  8.1 1.4 collective-permute-start.5
  9.6 1.6 %collective-permute-done.rest_2_ = bf16[512,128]{1,0:T(8,128)(2,1)S(1)} collective-permute-done((bf16[512,128]{1,0:T(8,128)(2,1)S(1)}, bf16[512,128]{1,0:T(8,128)(2,1)S(1)}, u32[]{:S(2)}, u32[]{:S(2)}) %collective-permute-start) | collective-permute-done | bytes 131104 | tf_op jit(solution)/shard_map/ppermute | solution.py:221
  11.2 2.7 %collective-permute-start.4 = (bf16[512,128]{1,0:T(8,128)(2,1)S(1)}, bf16[512,128]{1,0:T(8,128)(2,1)S(1)}, u32[]{:S(2)}, u32[]{:S(2)}) collective-permute-start(bf16[512,128]{1,0:T(8,128)(2,1)S(1)} %collective-permute-done.3.rest_7_), channel_id=1, source_target_pairs={{0,3},{1,0},{2,1},{3,2},{4,7},{5,4},{6,5},{7,6},{8,11},{9,8},{10,9... | collective-permute-start | bytes 393224 | tf_op jit(solution)/shard_map/ppermute | solution.py:221
  15.4 2.3 %collective-permute-done.2.rest_4_ = bf16[512,128]{1,0:T(8,128)(2,1)S(1)} collective-permute-done((bf16[512,128]{1,0:T(8,128)(2,1)S(1)}, bf16[512,128]{1,0:T(8,128)(2,1)S(1)}, u32[]{:S(2)}, u32[]{:S(2)}) %collective-permute-start.2) | collective-permute-done | bytes 131104 | tf_op jit(solution)/shard_map/ppermute | solution.py:221
  17.7 4.1 %base_products.1 = (f32[16,80,128]{2,1,0:T(8,128)S(1)}, bf16[16,80,128]{2,1,0:T(8,128)(2,1)S(1)}, bf16[30,512,512]{2,1,0:T(8,128)(2,1)S(1)}, bf16[5,512,512]{2,1,0:T(8,128)(2,1)S(1)}) custom-call(s32[6,7]{1,0:T(8,128)S(1)} %pad_add_fusion.table, bf16[5,6,512,512]{3,2,1,0:T(8,128)(2,1)} %factor_ref.1, bf16[5,512,512]{2,1,0:T(8,128)(2,1)} %bitcast.11, ...), custom_call_target="tpu_custom_call" | custom-call | flops 1006632960 | bytes 15728640 | tf_op jit(solution)/shard_map/base_products/pallas_call | solution.py:32
  21.8 2.1 %collective-permute-start.6 = (bf16[16,80,128]{2,1,0:T(8,128)(2,1)S(1)}, bf16[16,80,128]{2,1,0:T(8,128)(2,1)S(1)}, u32[]{:S(2)}, u32[]{:S(2)}) collective-permute-start(bf16[16,80,128]{2,1,0:T(8,128)(2,1)S(1)} %get-tuple-element.43), channel_id=1, source_target_pairs={{0,4},{4,0},{8,12},{12,8},{16,20},{20,16},{24,28},{28,24},{32,36},... | collective-permute-start | bytes 983048 | tf_op jit(solution)/shard_map/ppermute | solution.py:225
  25.3 17.5 %all_to_all.10.in_ref = bf16[16,80,128]{2,1,0:T(8,128)(2,1)S(1)} all-to-all(bf16[16,80,128]{2,1,0:T(8,128)(2,1)S(1)} %pair_sums.1), channel_id=1, replica_groups={{0,8,16,24,32,40,48,56,64,72,80,88,96,104,112,120},{4,12,20,28,36,44,52..., dimensions={0} | all-to-all | bytes 655360 | tf_op jit(solution)/shard_map/all_to_all | solution.py:230
  42.8 10.7 %all_to_all.11.half_ref = bf16[16,80,128]{2,1,0:T(8,128)(2,1)S(1)} all-to-all(bf16[16,80,128]{2,1,0:T(8,128)(2,1)S(1)} %sum_shares.1), channel_id=1, replica_groups={{0,8,16,24,32,40,48,56,64,72,80,88,96,104,112,120},{4,12,20,28,36,44,52..., dimensions={0} | all-to-all | bytes 655360 | tf_op jit(solution)/shard_map/all_to_all | solution.py:230
  53.6 2.7 %collective-permute-start.7 = (bf16[16,80,128]{2,1,0:T(8,128)(2,1)S(1)}, bf16[16,80,128]{2,1,0:T(8,128)(2,1)S(1)}, u32[]{:S(2)}, u32[]{:S(2)}) collective-permute-start(bf16[16,80,128]{2,1,0:T(8,128)(2,1)S(1)} %all_to_all.11.half_ref), channel_id=1, source_target_pairs={{0,4},{4,0},{8,12},{12,8},{16,20},{20,16},{24,28},{28,24},{32,36},... | collective-permute-start | bytes 983048 | tf_op jit(solution)/shard_map/ppermute | solution.py:225
  58.6 3.5 %collective-permute-start.10 = (bf16[512,128]{1,0:T(8,128)(2,1)S(1)}, bf16[512,128]{1,0:T(8,128)(2,1)S(1)}, u32[]{:S(2)}, u32[]{:S(2)}) collective-permute-start(bf16[512,128]{1,0:T(8,128)(2,1)S(1)} %get-tuple-element.45.rest_0_.first_ref), channel_id=1, source_target_pairs={{0,3},{1,0},{2,1},{3,2},{4,7},{5,4},{6,5},{7,6},{8,11},{9,8},{10,9... | collective-permute-start | bytes 393224 | tf_op jit(solution)/shard_map/ppermute | solution.py:221
  62.7 4.8 %collective-permute-done.10.rest_3_ = bf16[512,128]{1,0:T(8,128)(2,1)S(1)} collective-permute-done((bf16[512,128]{1,0:T(8,128)(2,1)S(1)}, bf16[512,128]{1,0:T(8,128)(2,1)S(1)}, u32[]{:S(2)}, u32[]{:S(2)}) %collective-permute-start.10) | collective-permute-done | bytes 131104 | tf_op jit(solution)/shard_map/ppermute | solution.py:221
  68.0 3.2 %collective-permute-done.8.rest_1_ = bf16[512,128]{1,0:T(8,128)(2,1)S(1)} collective-permute-done((bf16[512,128]{1,0:T(8,128)(2,1)S(1)}, bf16[512,128]{1,0:T(8,128)(2,1)S(1)}, u32[]{:S(2)}, u32[]{:S(2)}) %collective-permute-start.8) | collective-permute-done | bytes 131104 | tf_op jit(solution)/shard_map/ppermute | solution.py:221
  77.7 2.4 %collective-permute-done.14.rest_3_ = bf16[512,128]{1,0:T(8,128)(2,1)S(1)} collective-permute-done((bf16[512,128]{1,0:T(8,128)(2,1)S(1)}, bf16[512,128]{1,0:T(8,128)(2,1)S(1)}, u32[]{:S(2)}, u32[]{:S(2)}) %collective-permute-start.14) | collective-permute-done | bytes 131104 | tf_op jit(solution)/shard_map/ppermute | solution.py:213
  80.0 2.8 %collective-permute-done.13.rest_2_ = bf16[512,128]{1,0:T(8,128)(2,1)S(1)} collective-permute-done((bf16[512,128]{1,0:T(8,128)(2,1)S(1)}, bf16[512,128]{1,0:T(8,128)(2,1)S(1)}, u32[]{:S(2)}, u32[]{:S(2)}) %collective-permute-start.13) | collective-permute-done | bytes 131104 | tf_op jit(solution)/shard_map/ppermute | solution.py:213
  82.9 1.4 collective-permute-done.12.rest_1_
  84.3 2.3 %solve_2.1 = (bf16[512,128]{1,0:T(8,128)(2,1)S(1)}, bf16[2,512,128]{2,1,0:T(8,128)(2,1)S(1)}, bf16[512,128]{1,0:T(8,128)(2,1)S(1)}, bf16[4,512,128]{2,1,0:T(8,128)(2,1)S(1)}) custom-call(s32[6,7]{1,0:T(8,128)S(1)} %pad_add_fusion.table, bf16[30,512,512]{2,1,0:T(8,128)(2,1)S(1)} %get-tuple-element.46.held_ref, ...), custom_call_target="tpu_custom_call" | custom-call | flops 335544320 | tf_op jit(solution)/shard_map/solve_2/pallas_call | solution.py:32
  86.6 1.3 collective-permute-start.18
  89.2 1.3 collective-permute-start.20
  90.5 1.3 collective-permute-start.19
  95.5 1.7 %collective-permute-done.19.rest_1_ = bf16[512,128]{1,0:T(8,128)(2,1)S(1)} collective-permute-done((bf16[512,128]{1,0:T(8,128)(2,1)S(1)}, bf16[512,128]{1,0:T(8,128)(2,1)S(1)}, u32[]{:S(2)}, u32[]{:S(2)}) %collective-permute-start.19) | collective-permute-done | bytes 131104 | tf_op jit(solution)/shard_map/ppermute | solution.py:213
  102.3 1.5 %collective-permute-start.31 = (bf16[512,128]{1,0:T(8,128)(2,1)S(1)}, bf16[512,128]{1,0:T(8,128)(2,1)S(1)}, u32[]{:S(2)}, u32[]{:S(2)}) collective-permute-start(bf16[512,128]{1,0:T(8,128)(2,1)S(1)} %later_1.1), channel_id=1, source_target_pairs={{4,12},{5,13},{6,14},{7,15}} | collective-permute-start | bytes 393224 | tf_op jit(solution)/shard_map/ppermute | solution.py:213
  105.1 1.3 collective-permute-start.16
  106.5 12.5 %collective-permute-start.15 = (bf16[512,128]{1,0:T(8,128)(2,1)S(1)}, bf16[512,128]{1,0:T(8,128)(2,1)S(1)}, u32[]{:S(2)}, u32[]{:S(2)}) collective-permute-start(bf16[512,128]{1,0:T(8,128)(2,1)S(1)} %get-tuple-element.55.value_ref), channel_id=1, source_target_pairs={{0,8},{1,9},{2,10},{3,11},{4,12},{5,13},{6,14},{7,15}} | collective-permute-start | bytes 393224 | tf_op jit(solution)/shard_map/ppermute | solution.py:213
  119.0 1.7 %solve_4.1 = (bf16[512,128]{1,0:T(8,128)(2,1)}, bf16[512,128]{1,0:T(8,128)(2,1)S(1)}) custom-call(s32[6,7]{1,0:T(8,128)S(1)} %pad_add_fusion.table, bf16[30,512,512]{2,1,0:T(8,128)(2,1)S(1)} %get-tuple-element.46.held_ref, f32[4,512,128]{2,1,0:T(8,128)S(1)} %get-tuple-element.47.ahead_ref, bf16[5,512,512]{2,1,0:T(8,128)(2,1)S(1)} %get-tuple-element.44.inverse_ref, ...), custom_call_target="tpu_custom_call" | custom-call | flops 335544320 | tf_op jit(solution)/shard_map/solve_4/pallas_call | solution.py:32
  124.0 1.3 collective-permute-start.26
  128.7 1.3 collective-permute-start.37
  133.8 1.7 %collective-permute-done.35.rest_5_ = bf16[512,128]{1,0:T(8,128)(2,1)S(1)} collective-permute-done((bf16[512,128]{1,0:T(8,128)(2,1)S(1)}, bf16[512,128]{1,0:T(8,128)(2,1)S(1)}, u32[]{:S(2)}, u32[]{:S(2)}) %collective-permute-start.35) | collective-permute-done | bytes 131104 | tf_op jit(solution)/shard_map/ppermute | solution.py:213
  136.3 1.5 %collective-permute-done.38.other_ref = bf16[2,512,128]{2,1,0:T(8,128)(2,1)S(1)} collective-permute-done((bf16[2,512,128]{2,1,0:T(8,128)(2,1)S(1)}, bf16[2,512,128]{2,1,0:T(8,128)(2,1)S(1)}, u32[]{:S(2)}, u32[]{:S(2)}) %collective-permute-start.38) | collective-permute-done | bytes 262176 | tf_op jit(solution)/shard_map/ppermute | solution.py:225
  137.8 1.8 %final.1 = f32[5,512,128]{2,1,0:T(8,128)} custom-call(s32[6,7]{1,0:T(8,128)S(1)} %pad_add_fusion.table, bf16[512,128]{1,0:T(8,128)(2,1)S(1)} %get-tuple-element.45.rest_0_.first_ref, bf16[2,512,128]{2,1,0:T(8,128)(2,1)S(1)} %merged.1.mine_ref, bf16[2,512,128]{2,1,0:T(8,128)(2,1)S(1)} %collective-permute-done.38.other_ref), custom_call_target="tpu_custom_call" | custom-call | tf_op jit(solution)/shard_map/final/pallas_call | solution.py:32
  (69 shorter events, 35.4 us)
Async XLA Ops:
  3.3 7.9 %collective-permute-start = (bf16[512,128]{1,0:T(8,128)(2,1)S(1)}, bf16[512,128]{1,0:T(8,128)(2,1)S(1)}, u32[]{:S(2)}, u32[]{:S(2)}) collective-permute-start(bf16[512,128]{1,0:T(8,128)(2,1)S(1)} %get-tuple-element.40.rest_0_), channel_id=1, source_target_pairs={{0,1},{1,2},{2,3},{3,0},{4,5},{5,6},{6,7},{7,4},{8,9},{9,10},{10,1... | collective-permute-start | bytes 393224 | tf_op jit(solution)/shard_map/ppermute | solution.py:221
  5.9 5.3 %collective-permute-start.3 = (bf16[512,128]{1,0:T(8,128)(2,1)S(1)}, bf16[512,128]{1,0:T(8,128)(2,1)S(1)}, u32[]{:S(2)}, u32[]{:S(2)}) collective-permute-start(bf16[512,128]{1,0:T(8,128)(2,1)S(1)} %get-tuple-element.41.rest_1_), channel_id=1, source_target_pairs={{0,3},{1,0},{2,1},{3,2},{4,7},{5,4},{6,5},{7,6},{8,11},{9,8},{10,9... | collective-permute-start | bytes 393224 | tf_op jit(solution)/shard_map/ppermute | solution.py:221
  8.1 7.3 %collective-permute-start.5 = (bf16[512,128]{1,0:T(8,128)(2,1)S(1)}, bf16[512,128]{1,0:T(8,128)(2,1)S(1)}, u32[]{:S(2)}, u32[]{:S(2)}) collective-permute-start(bf16[512,128]{1,0:T(8,128)(2,1)S(1)} %get-tuple-element.40.rest_0_), channel_id=1, source_target_pairs={{0,3},{1,0},{2,1},{3,2},{4,7},{5,4},{6,5},{7,6},{8,11},{9,8},{10,9... | collective-permute-start | bytes 393224 | tf_op jit(solution)/shard_map/ppermute | solution.py:221
  9.5 6.0 %collective-permute-start.1 = (bf16[512,128]{1,0:T(8,128)(2,1)S(1)}, bf16[512,128]{1,0:T(8,128)(2,1)S(1)}, u32[]{:S(2)}, u32[]{:S(2)}) collective-permute-start(bf16[512,128]{1,0:T(8,128)(2,1)S(1)} %get-tuple-element.41.rest_1_), channel_id=1, source_target_pairs={{0,1},{1,2},{2,3},{3,0},{4,5},{5,6},{6,7},{7,4},{8,9},{9,10},{10,1... | collective-permute-start | bytes 393224 | tf_op jit(solution)/shard_map/ppermute | solution.py:221
  11.2 6.5 %collective-permute-start.2 = (bf16[512,128]{1,0:T(8,128)(2,1)S(1)}, bf16[512,128]{1,0:T(8,128)(2,1)S(1)}, u32[]{:S(2)}, u32[]{:S(2)}) collective-permute-start(bf16[512,128]{1,0:T(8,128)(2,1)S(1)} %collective-permute-done.rest_2_), channel_id=1, source_target_pairs={{0,1},{1,2},{2,3},{3,0},{4,5},{5,6},{6,7},{7,4},{8,9},{9,10},{10,1... | collective-permute-start | bytes 393224 | tf_op jit(solution)/shard_map/ppermute | solution.py:221
  11.2 6.5 %collective-permute-start.4 = (bf16[512,128]{1,0:T(8,128)(2,1)S(1)}, bf16[512,128]{1,0:T(8,128)(2,1)S(1)}, u32[]{:S(2)}, u32[]{:S(2)}) collective-permute-start(bf16[512,128]{1,0:T(8,128)(2,1)S(1)} %collective-permute-done.3.rest_7_), channel_id=1, source_target_pairs={{0,3},{1,0},{2,1},{3,2},{4,7},{5,4},{6,5},{7,6},{8,11},{9,8},{10,9... | collective-permute-start | bytes 393224 | tf_op jit(solution)/shard_map/ppermute | solution.py:221
  58.6 8.9 %collective-permute-start.10 = (bf16[512,128]{1,0:T(8,128)(2,1)S(1)}, bf16[512,128]{1,0:T(8,128)(2,1)S(1)}, u32[]{:S(2)}, u32[]{:S(2)}) collective-permute-start(bf16[512,128]{1,0:T(8,128)(2,1)S(1)} %get-tuple-element.45.rest_0_.first_ref), channel_id=1, source_target_pairs={{0,3},{1,0},{2,1},{3,2},{4,7},{5,4},{6,5},{7,6},{8,11},{9,8},{10,9... | collective-permute-start | bytes 393224 | tf_op jit(solution)/shard_map/ppermute | solution.py:221
  62.0 6.0 %collective-permute-start.9 = (bf16[512,128]{1,0:T(8,128)(2,1)S(1)}, bf16[512,128]{1,0:T(8,128)(2,1)S(1)}, u32[]{:S(2)}, u32[]{:S(2)}) collective-permute-start(bf16[512,128]{1,0:T(8,128)(2,1)S(1)} %get-tuple-element.45.rest_0_.first_ref), channel_id=1, source_target_pairs={{0,2},{1,3},{2,0},{3,1},{4,6},{5,7},{6,4},{7,5},{8,10},{9,11},{10,... | collective-permute-start | bytes 393224 | tf_op jit(solution)/shard_map/ppermute | solution.py:221
  62.0 9.1 %collective-permute-start.8 = (bf16[512,128]{1,0:T(8,128)(2,1)S(1)}, bf16[512,128]{1,0:T(8,128)(2,1)S(1)}, u32[]{:S(2)}, u32[]{:S(2)}) collective-permute-start(bf16[512,128]{1,0:T(8,128)(2,1)S(1)} %get-tuple-element.45.rest_0_.first_ref), channel_id=1, source_target_pairs={{0,1},{1,2},{2,3},{3,0},{4,5},{5,6},{6,7},{7,4},{8,9},{9,10},{10,1... | collective-permute-start | bytes 393224 | tf_op jit(solution)/shard_map/ppermute | solution.py:221
  72.5 11.8 %collective-permute-start.11 = (bf16[2,512,128]{2,1,0:T(8,128)(2,1)S(1)}, bf16[2,512,128]{2,1,0:T(8,128)(2,1)S(1)}, u32[]{:S(2)}, u32[]{:S(2)}) collective-permute-start(bf16[2,512,128]{2,1,0:T(8,128)(2,1)S(1)} %get-tuple-element.48), channel_id=1, source_target_pairs={{0,4},{1,5},{2,6},{3,7}} | collective-permute-start | bytes 786440 | tf_op jit(solution)/shard_map/ppermute | solution.py:213
  73.8 6.3 %collective-permute-start.14 = (bf16[512,128]{1,0:T(8,128)(2,1)S(1)}, bf16[512,128]{1,0:T(8,128)(2,1)S(1)}, u32[]{:S(2)}, u32[]{:S(2)}) collective-permute-start(bf16[512,128]{1,0:T(8,128)(2,1)S(1)} %get-tuple-element.49.rest_4_), channel_id=1, source_target_pairs={{0,7},{1,4},{2,5},{3,6}} | collective-permute-start | bytes 393224 | tf_op jit(solution)/shard_map/ppermute | solution.py:213
  75.1 7.8 %collective-permute-start.13 = (bf16[512,128]{1,0:T(8,128)(2,1)S(1)}, bf16[512,128]{1,0:T(8,128)(2,1)S(1)}, u32[]{:S(2)}, u32[]{:S(2)}) collective-permute-start(bf16[512,128]{1,0:T(8,128)(2,1)S(1)} %get-tuple-element.49.rest_4_), channel_id=1, source_target_pairs={{0,6},{1,7},{2,4},{3,5}} | collective-permute-start | bytes 393224 | tf_op jit(solution)/shard_map/ppermute | solution.py:213
  76.4 7.9 %collective-permute-start.12 = (bf16[512,128]{1,0:T(8,128)(2,1)S(1)}, bf16[512,128]{1,0:T(8,128)(2,1)S(1)}, u32[]{:S(2)}, u32[]{:S(2)}) collective-permute-start(bf16[512,128]{1,0:T(8,128)(2,1)S(1)} %get-tuple-element.49.rest_4_), channel_id=1, source_target_pairs={{0,5},{1,6},{2,7},{3,4}} | collective-permute-start | bytes 393224 | tf_op jit(solution)/shard_map/ppermute | solution.py:213
  86.6 10.7 %collective-permute-start.18 = (bf16[2,512,128]{2,1,0:T(8,128)(2,1)S(1)}, bf16[2,512,128]{2,1,0:T(8,128)(2,1)S(1)}, u32[]{:S(2)}, u32[]{:S(2)}) collective-permute-start(bf16[2,512,128]{2,1,0:T(8,128)(2,1)S(1)} %get-tuple-element.56), channel_id=1, source_target_pairs={{4,8},{5,9},{6,10},{7,11}} | collective-permute-start | bytes 786440 | tf_op jit(solution)/shard_map/ppermute | solution.py:213
  87.9 6.3 %collective-permute-start.21 = (bf16[512,128]{1,0:T(8,128)(2,1)S(1)}, bf16[512,128]{1,0:T(8,128)(2,1)S(1)}, u32[]{:S(2)}, u32[]{:S(2)}) collective-permute-start(bf16[512,128]{1,0:T(8,128)(2,1)S(1)} %get-tuple-element.57), channel_id=1, source_target_pairs={{4,11},{5,8},{6,9},{7,10}} | collective-permute-start | bytes 393224 | tf_op jit(solution)/shard_map/ppermute | solution.py:213
  89.2 6.4 %collective-permute-start.20 = (bf16[512,128]{1,0:T(8,128)(2,1)S(1)}, bf16[512,128]{1,0:T(8,128)(2,1)S(1)}, u32[]{:S(2)}, u32[]{:S(2)}) collective-permute-start(bf16[512,128]{1,0:T(8,128)(2,1)S(1)} %get-tuple-element.57), channel_id=1, source_target_pairs={{4,10},{5,11},{6,8},{7,9}} | collective-permute-start | bytes 393224 | tf_op jit(solution)/shard_map/ppermute | solution.py:213
  90.5 6.8 %collective-permute-start.19 = (bf16[512,128]{1,0:T(8,128)(2,1)S(1)}, bf16[512,128]{1,0:T(8,128)(2,1)S(1)}, u32[]{:S(2)}, u32[]{:S(2)}) collective-permute-start(bf16[512,128]{1,0:T(8,128)(2,1)S(1)} %get-tuple-element.57), channel_id=1, source_target_pairs={{4,9},{5,10},{6,11},{7,8}} | collective-permute-start | bytes 393224 | tf_op jit(solution)/shard_map/ppermute | solution.py:213
  92.5 4.7 %collective-permute-start.22 = (bf16[512,128]{1,0:T(8,128)(2,1)S(1)}, bf16[512,128]{1,0:T(8,128)(2,1)S(1)}, u32[]{:S(2)}, u32[]{:S(2)}) collective-permute-start(bf16[512,128]{1,0:T(8,128)(2,1)S(1)} %get-tuple-element.64), channel_id=1, source_target_pairs={{0,12},{1,13},{2,14},{3,15}} | collective-permute-start | bytes 393224 | tf_op jit(solution)/shard_map/ppermute | solution.py:213
  98.4 20.6 %collective-permute-start.27 = (bf16[2,512,128]{2,1,0:T(8,128)(2,1)S(1)}, bf16[2,512,128]{2,1,0:T(8,128)(2,1)S(1)}, u32[]{:S(2)}, u32[]{:S(2)}) collective-permute-start(bf16[2,512,128]{2,1,0:T(8,128)(2,1)S(1)} %get-tuple-element.72), channel_id=1, source_target_pairs={{8,12},{9,13},{10,14},{11,15}} | collective-permute-start | bytes 786440 | tf_op jit(solution)/shard_map/ppermute | solution.py:213
  99.1 4.8 %collective-permute-start.30 = (bf16[512,128]{1,0:T(8,128)(2,1)S(1)}, bf16[512,128]{1,0:T(8,128)(2,1)S(1)}, u32[]{:S(2)}, u32[]{:S(2)}) collective-permute-start(bf16[512,128]{1,0:T(8,128)(2,1)S(1)} %get-tuple-element.70.rest_4_), channel_id=1, source_target_pairs={{8,15},{9,12},{10,13},{11,14}} | collective-permute-start | bytes 393224 | tf_op jit(solution)/shard_map/ppermute | solution.py:213
  99.7 5.4 %collective-permute-start.29 = (bf16[512,128]{1,0:T(8,128)(2,1)S(1)}, bf16[512,128]{1,0:T(8,128)(2,1)S(1)}, u32[]{:S(2)}, u32[]{:S(2)}) collective-permute-start(bf16[512,128]{1,0:T(8,128)(2,1)S(1)} %get-tuple-element.70.rest_4_), channel_id=1, source_target_pairs={{8,14},{9,15},{10,12},{11,13}} | collective-permute-start | bytes 393224 | tf_op jit(solution)/shard_map/ppermute | solution.py:213
  100.4 6.0 %collective-permute-start.28 = (bf16[512,128]{1,0:T(8,128)(2,1)S(1)}, bf16[512,128]{1,0:T(8,128)(2,1)S(1)}, u32[]{:S(2)}, u32[]{:S(2)}) collective-permute-start(bf16[512,128]{1,0:T(8,128)(2,1)S(1)} %get-tuple-element.70.rest_4_), channel_id=1, source_target_pairs={{8,13},{9,14},{10,15},{11,12}} | collective-permute-start | bytes 393224 | tf_op jit(solution)/shard_map/ppermute | solution.py:213
  102.3 16.7 %collective-permute-start.31 = (bf16[512,128]{1,0:T(8,128)(2,1)S(1)}, bf16[512,128]{1,0:T(8,128)(2,1)S(1)}, u32[]{:S(2)}, u32[]{:S(2)}) collective-permute-start(bf16[512,128]{1,0:T(8,128)(2,1)S(1)} %later_1.1), channel_id=1, source_target_pairs={{4,12},{5,13},{6,14},{7,15}} | collective-permute-start | bytes 393224 | tf_op jit(solution)/shard_map/ppermute | solution.py:213
  103.8 17.5 %collective-permute-start.17 = (bf16[512,128]{1,0:T(8,128)(2,1)S(1)}, bf16[512,128]{1,0:T(8,128)(2,1)S(1)}, u32[]{:S(2)}, u32[]{:S(2)}) collective-permute-start(bf16[512,128]{1,0:T(8,128)(2,1)S(1)} %get-tuple-element.55.value_ref), channel_id=1, source_target_pairs={{0,16},{1,17},{2,18},{3,19},{4,20},{5,21},{6,22},{7,23}} | collective-permute-start | bytes 393224 | tf_op jit(solution)/shard_map/ppermute | solution.py:213
  105.1 16.2 %collective-permute-start.16 = (bf16[512,128]{1,0:T(8,128)(2,1)S(1)}, bf16[512,128]{1,0:T(8,128)(2,1)S(1)}, u32[]{:S(2)}, u32[]{:S(2)}) collective-permute-start(bf16[512,128]{1,0:T(8,128)(2,1)S(1)} %get-tuple-element.55.value_ref), channel_id=1, source_target_pairs={{0,24},{1,25},{2,26},{3,27},{4,28},{5,29},{6,30},{7,31}} | collective-permute-start | bytes 393224 | tf_op jit(solution)/shard_map/ppermute | solution.py:213
  106.5 14.9 %collective-permute-start.15 = (bf16[512,128]{1,0:T(8,128)(2,1)S(1)}, bf16[512,128]{1,0:T(8,128)(2,1)S(1)}, u32[]{:S(2)}, u32[]{:S(2)}) collective-permute-start(bf16[512,128]{1,0:T(8,128)(2,1)S(1)} %get-tuple-element.55.value_ref), channel_id=1, source_target_pairs={{0,8},{1,9},{2,10},{3,11},{4,12},{5,13},{6,14},{7,15}} | collective-permute-start | bytes 393224 | tf_op jit(solution)/shard_map/ppermute | solution.py:213
  120.7 6.0 %collective-permute-start.34 = (bf16[512,128]{1,0:T(8,128)(2,1)S(1)}, bf16[512,128]{1,0:T(8,128)(2,1)S(1)}, u32[]{:S(2)}, u32[]{:S(2)}) collective-permute-start(bf16[512,128]{1,0:T(8,128)(2,1)S(1)} %get-tuple-element.75.value_ref), channel_id=1, source_target_pairs={{8,24},{9,25},{10,26},{11,27},{12,28},{13,29},{14,30},{15,31}} | collective-permute-start | bytes 393224 | tf_op jit(solution)/shard_map/ppermute | solution.py:213
  122.1 5.9 %collective-permute-start.33 = (bf16[512,128]{1,0:T(8,128)(2,1)S(1)}, bf16[512,128]{1,0:T(8,128)(2,1)S(1)}, u32[]{:S(2)}, u32[]{:S(2)}) collective-permute-start(bf16[512,128]{1,0:T(8,128)(2,1)S(1)} %get-tuple-element.75.value_ref), channel_id=1, source_target_pairs={{8,0},{9,1},{10,2},{11,3},{12,4},{13,5},{14,6},{15,7}} | collective-permute-start | bytes 393224 | tf_op jit(solution)/shard_map/ppermute | solution.py:213
  124.0 7.2 %collective-permute-start.26 = (bf16[512,128]{1,0:T(8,128)(2,1)S(1)}, bf16[512,128]{1,0:T(8,128)(2,1)S(1)}, u32[]{:S(2)}, u32[]{:S(2)}) collective-permute-start(bf16[512,128]{1,0:T(8,128)(2,1)S(1)} %picked.2.rest_0_), channel_id=1, source_target_pairs={{0,64},{1,65},{2,66},{3,67},{4,68},{5,69},{6,70},{7,71},{8,72},{9,... | collective-permute-start | bytes 393224 | tf_op jit(solution)/shard_map/ppermute | solution.py:213
  125.3 7.2 %collective-permute-start.25 = (bf16[512,128]{1,0:T(8,128)(2,1)S(1)}, bf16[512,128]{1,0:T(8,128)(2,1)S(1)}, u32[]{:S(2)}, u32[]{:S(2)}) collective-permute-start(bf16[512,128]{1,0:T(8,128)(2,1)S(1)} %picked.2.rest_0_), channel_id=1, source_target_pairs={{0,96},{1,97},{2,98},{3,99},{4,100},{5,101},{6,102},{7,103},{8,104... | collective-permute-start | bytes 393224 | tf_op jit(solution)/shard_map/ppermute | solution.py:213
  126.7 5.9 %collective-permute-start.24 = (bf16[512,128]{1,0:T(8,128)(2,1)S(1)}, bf16[512,128]{1,0:T(8,128)(2,1)S(1)}, u32[]{:S(2)}, u32[]{:S(2)}) collective-permute-start(bf16[512,128]{1,0:T(8,128)(2,1)S(1)} %picked.2.rest_0_), channel_id=1, source_target_pairs={{0,32},{1,33},{2,34},{3,35},{4,36},{5,37},{6,38},{7,39},{8,40},{9,... | collective-permute-start | bytes 393224 | tf_op jit(solution)/shard_map/ppermute | solution.py:213
  128.7 5.1 %collective-permute-start.37 = (bf16[512,128]{1,0:T(8,128)(2,1)S(1)}, bf16[512,128]{1,0:T(8,128)(2,1)S(1)}, u32[]{:S(2)}, u32[]{:S(2)}) collective-permute-start(bf16[512,128]{1,0:T(8,128)(2,1)S(1)} %picked.3.rest_4_), channel_id=1, source_target_pairs={{0,64},{1,65},{2,66},{3,67},{4,68},{5,69},{6,70},{7,71},{8,72},{9,... | collective-permute-start | bytes 393224 | tf_op jit(solution)/shard_map/ppermute | solution.py:213
  (8 other events, 60.4 us)

commit v8 on v6

--- a/solution.py
+++ b/solution.py
@@ -336,18 +336,18 @@
     p30, p40 = products(0, (3, 4), kept)
     x2, packed, mixed12, kept = solve(1, pieces, [x1], ("value", "packed", "mixed", "kept"))
     pieces = onward(2, x2, packed)
-    mixed12, pieces[3] = after((mixed12, pieces[3]))
     mixed12 = spread_x(mixed12, 0)
     p30, p40 = to_column(p30, 0, 2), to_column(p40, 0, 3)
     pieces, kept = after((pieces, kept))
     p41, = products(1, (4,), kept)
+    pieces, p40, mixed12 = after((pieces, p40, mixed12))
+    mixed12 = pick(column(0, 0, 0), table, mixed12[0], mixed12[1:])
     pieces, mixed12 = after((pieces, mixed12))
-    mixed12 = pick(column(0, 0, 0), table, mixed12[0], mixed12[1:])
     x3, packed = solve(2, pieces, [p30], ("value", "packed"))
     pieces = onward(3, x3, packed)
-    mixed12, pieces[3] = after((mixed12, pieces[3]))
+    p41 = to_column(p41, 1, 3)
+    mixed12, x3, p41 = after((mixed12, x3, p41))
     spread12 = spread_y(mixed12)
-    p41 = to_column(p41, 1, 3)
     pieces, spread12 = after((pieces, spread12))
     x4, mixed34 = solve(3, pieces, [x3, p40, p41], ("value", "mixed"))
     mixed34 = spread_x(mixed34, 1)

time: 149 us -> 146 us (0.980)
  starting transfers between devices: 61.4 us -> 51 us
  waiting for transfers between devices: 32.1 us -> 40.7 us
    ppermute x27, starting transfers between devices: 41.4 us -> 30.1 us  [send(): return lax.ppermute(value, AXES, pairs)]
    ppermute x27, waiting for transfers between devices: 19.4 us -> 29.8 us  [send(): return lax.ppermute(value, AXES, pairs)]
    ppermute x9, starting transfers between devices: 14.7 us -> 16.4 us  [to_row(): return lax.ppermute(value, 'row', [(z, (z + step) % NZ) for z in range(NZ)])]
  transfers between devices with their start and end apart: 39 -> 39, of which waited for: 15 -> 20; matrix products, arithmetic and copies ran while one was open for 1% -> 1% of each run, Pallas kernels for 2% -> 3%
where the time goes in v8:
time: 146 us; the launch traced here: 144 us
  starting transfers between devices  51 us (35%)
  waiting for transfers between devices  40.7 us (28%)
  blocking collectives  28 us (19%)
  Pallas kernels  22 us (15%)
    ppermute x27, starting transfers between devices, send(): return lax.ppermute(value, AXES, pairs)  30.1 us
    ppermute x27, waiting for transfers between devices, send(): return lax.ppermute(value, AXES, pairs)  29.8 us
    all_to_all x2, blocking collectives, over_plane(): lax.all_to_all(value, 'col', 0, 0, axis_index_groups=groups, tiled=True)  28 us
    pallas_call x15, Pallas kernels, call(): pl.pallas_call(body, out_shape=outs, in_specs=in_specs, out_specs=out_spe...  22 us
    ppermute x9, starting transfers between devices, to_row(): return lax.ppermute(value, 'row', [(z, (z + step) % NZ) for z in range(NZ)])  16.4 us
    ppermute x9, waiting for transfers between devices, to_row(): return lax.ppermute(value, 'row', [(z, (z + step) % NZ) for z in range(NZ)])  7.28 us
    ppermute x3, starting transfers between devices, other_core(): return lax.ppermute(value, 'col', [(c, c ^ 1) for c in range(NX * NY * 2)])  4.58 us
    ppermute x3, waiting for transfers between devices, other_core(): return lax.ppermute(value, 'col', [(c, c ^ 1) for c in range(NX * NY * 2)])  3.67 us
  transfers between devices with their start and end apart: 39, of which 20 were waited for; matrix products, arithmetic and copies ran while one was open for 1% of the time, Pallas kernels for 3%

profile of v8, /device:TPU:1, one launch (start us, length us, event | category | flops | bytes accessed | tf_op | source)
XLA Modules:
  0.0 144.5 jit_solution(12501221592197984430)
XLA Ops:
  0.6 2.7 %base_solve.1 = (f32[2,512,128]{2,1,0:T(8,128)}, bf16[512,128]{1,0:T(8,128)(2,1)S(1)}, bf16[512,128]{1,0:T(8,128)(2,1)S(1)}) custom-call(bf16[2,512,512]{2,1,0:T(8,128)(2,1)} %inverse_ref.1, f32[2,512,128]{2,1,0:T(8,128)} %rhs_ref.1), custom_call_target="tpu_custom_call" | custom-call | flops 134217728 | bytes 1835008 | tf_op jit(solution)/shard_map/base_solve/pallas_call | solution.py:32
  3.3 2.5 %collective-permute-start = (bf16[512,128]{1,0:T(8,128)(2,1)S(1)}, bf16[512,128]{1,0:T(8,128)(2,1)S(1)}, u32[]{:S(2)}, u32[]{:S(2)}) collective-permute-start(bf16[512,128]{1,0:T(8,128)(2,1)S(1)} %get-tuple-element.59.rest_0_), channel_id=1, source_target_pairs={{0,1},{1,2},{2,3},{3,0},{4,5},{5,6},{6,7},{7,4},{8,9},{9,10},{10,1... | collective-permute-start | bytes 393224 | tf_op jit(solution)/shard_map/ppermute | solution.py:221
  5.9 2.2 %collective-permute-start.3 = (bf16[512,128]{1,0:T(8,128)(2,1)S(1)}, bf16[512,128]{1,0:T(8,128)(2,1)S(1)}, u32[]{:S(2)}, u32[]{:S(2)}) collective-permute-start(bf16[512,128]{1,0:T(8,128)(2,1)S(1)} %get-tuple-element.60.rest_1_), channel_id=1, source_target_pairs={{0,3},{1,0},{2,1},{3,2},{4,7},{5,4},{6,5},{7,6},{8,11},{9,8},{10,9... | collective-permute-start | bytes 393224 | tf_op jit(solution)/shard_map/ppermute | solution.py:221
  8.1 2.7 %collective-permute-start.5 = (bf16[512,128]{1,0:T(8,128)(2,1)S(1)}, bf16[512,128]{1,0:T(8,128)(2,1)S(1)}, u32[]{:S(2)}, u32[]{:S(2)}) collective-permute-start(bf16[512,128]{1,0:T(8,128)(2,1)S(1)} %get-tuple-element.59.rest_0_), channel_id=1, source_target_pairs={{0,3},{1,0},{2,1},{3,2},{4,7},{5,4},{6,5},{7,6},{8,11},{9,8},{10,9... | collective-permute-start | bytes 393224 | tf_op jit(solution)/shard_map/ppermute | solution.py:221
  11.2 2.7 %collective-permute-start.4 = (bf16[512,128]{1,0:T(8,128)(2,1)S(1)}, bf16[512,128]{1,0:T(8,128)(2,1)S(1)}, u32[]{:S(2)}, u32[]{:S(2)}) collective-permute-start(bf16[512,128]{1,0:T(8,128)(2,1)S(1)} %collective-permute-done.3.rest_7_), channel_id=1, source_target_pairs={{0,3},{1,0},{2,1},{3,2},{4,7},{5,4},{6,5},{7,6},{8,11},{9,8},{10,9... | collective-permute-start | bytes 393224 | tf_op jit(solution)/shard_map/ppermute | solution.py:221
  16.3 5.1 %base_products.1 = (f32[16,80,128]{2,1,0:T(8,128)S(1)}, bf16[16,80,128]{2,1,0:T(8,128)(2,1)S(1)}, bf16[30,512,512]{2,1,0:T(8,128)(2,1)S(1)}, bf16[5,512,512]{2,1,0:T(8,128)(2,1)S(1)}) custom-call(s32[6,7]{1,0:T(8,128)S(1)} %pad_add_fusion.table, bf16[5,6,512,512]{3,2,1,0:T(8,128)(2,1)} %factor_ref.1, bf16[5,512,512]{2,1,0:T(8,128)(2,1)} %bitcast.11, ...), custom_call_target="tpu_custom_call" | custom-call | flops 1006632960 | bytes 15728640 | tf_op jit(solution)/shard_map/base_products/pallas_call | solution.py:32
  24.0 17.3 %all_to_all.10.in_ref = bf16[16,80,128]{2,1,0:T(8,128)(2,1)S(1)} all-to-all(bf16[16,80,128]{2,1,0:T(8,128)(2,1)S(1)} %pair_sums.1), channel_id=1, replica_groups={{0,8,16,24,32,40,48,56,64,72,80,88,96,104,112,120},{4,12,20,28,36,44,52..., dimensions={0} | all-to-all | bytes 655360 | tf_op jit(solution)/shard_map/all_to_all | solution.py:230
  41.3 10.7 %all_to_all.11.half_ref = bf16[16,80,128]{2,1,0:T(8,128)(2,1)S(1)} all-to-all(bf16[16,80,128]{2,1,0:T(8,128)(2,1)S(1)} %sum_shares.1), channel_id=1, replica_groups={{0,8,16,24,32,40,48,56,64,72,80,88,96,104,112,120},{4,12,20,28,36,44,52..., dimensions={0} | all-to-all | bytes 655360 | tf_op jit(solution)/shard_map/all_to_all | solution.py:230
  52.1 2.7 %collective-permute-start.7 = (bf16[16,80,128]{2,1,0:T(8,128)(2,1)S(1)}, bf16[16,80,128]{2,1,0:T(8,128)(2,1)S(1)}, u32[]{:S(2)}, u32[]{:S(2)}) collective-permute-start(bf16[16,80,128]{2,1,0:T(8,128)(2,1)S(1)} %all_to_all.11.half_ref), channel_id=1, source_target_pairs={{0,4},{4,0},{8,12},{12,8},{16,20},{20,16},{24,28},{28,24},{32,36},... | collective-permute-start | bytes 983048 | tf_op jit(solution)/shard_map/ppermute | solution.py:225
  57.1 2.2 %collective-permute-start.8 = (bf16[512,128]{1,0:T(8,128)(2,1)S(1)}, bf16[512,128]{1,0:T(8,128)(2,1)S(1)}, u32[]{:S(2)}, u32[]{:S(2)}) collective-permute-start(bf16[512,128]{1,0:T(8,128)(2,1)S(1)} %get-tuple-element.64.rest_0_.first_ref), channel_id=1, source_target_pairs={{0,1},{1,2},{2,3},{3,0},{4,5},{5,6},{6,7},{7,4},{8,9},{9,10},{10,1... | collective-permute-start | bytes 393224 | tf_op jit(solution)/shard_map/ppermute | solution.py:221
  59.2 4.1 %collective-permute-start.9 = (bf16[512,128]{1,0:T(8,128)(2,1)S(1)}, bf16[512,128]{1,0:T(8,128)(2,1)S(1)}, u32[]{:S(2)}, u32[]{:S(2)}) collective-permute-start(bf16[512,128]{1,0:T(8,128)(2,1)S(1)} %get-tuple-element.64.rest_0_.first_ref), channel_id=1, source_target_pairs={{0,2},{1,3},{2,0},{3,1},{4,6},{5,7},{6,4},{7,5},{8,10},{9,11},{10,... | collective-permute-start | bytes 393224 | tf_op jit(solution)/shard_map/ppermute | solution.py:221
  63.3 2.4 %collective-permute-done.8.rest_1_ = bf16[512,128]{1,0:T(8,128)(2,1)S(1)} collective-permute-done((bf16[512,128]{1,0:T(8,128)(2,1)S(1)}, bf16[512,128]{1,0:T(8,128)(2,1)S(1)}, u32[]{:S(2)}, u32[]{:S(2)}) %collective-permute-start.8) | collective-permute-done | bytes 131104 | tf_op jit(solution)/shard_map/ppermute | solution.py:221
  65.7 3.7 %collective-permute-done.9.rest_2_ = bf16[512,128]{1,0:T(8,128)(2,1)S(1)} collective-permute-done((bf16[512,128]{1,0:T(8,128)(2,1)S(1)}, bf16[512,128]{1,0:T(8,128)(2,1)S(1)}, u32[]{:S(2)}, u32[]{:S(2)}) %collective-permute-start.9) | collective-permute-done | bytes 131104 | tf_op jit(solution)/shard_map/ppermute | solution.py:221
  75.9 4.2 %collective-permute-done.12.rest_1_ = bf16[512,128]{1,0:T(8,128)(2,1)S(1)} collective-permute-done((bf16[512,128]{1,0:T(8,128)(2,1)S(1)}, bf16[512,128]{1,0:T(8,128)(2,1)S(1)}, u32[]{:S(2)}, u32[]{:S(2)}) %collective-permute-start.12) | collective-permute-done | bytes 131104 | tf_op jit(solution)/shard_map/ppermute | solution.py:213
  80.1 1.9 %collective-permute-done.13.rest_2_ = bf16[512,128]{1,0:T(8,128)(2,1)S(1)} collective-permute-done((bf16[512,128]{1,0:T(8,128)(2,1)S(1)}, bf16[512,128]{1,0:T(8,128)(2,1)S(1)}, u32[]{:S(2)}, u32[]{:S(2)}) %collective-permute-start.13) | collective-permute-done | bytes 131104 | tf_op jit(solution)/shard_map/ppermute | solution.py:213
  82.7 2.9 %solve_2.1 = (bf16[512,128]{1,0:T(8,128)(2,1)S(1)}, bf16[2,512,128]{2,1,0:T(8,128)(2,1)S(1)}, bf16[512,128]{1,0:T(8,128)(2,1)S(1)}, bf16[4,512,128]{2,1,0:T(8,128)(2,1)S(1)}) custom-call(s32[6,7]{1,0:T(8,128)S(1)} %pad_add_fusion.table, bf16[30,512,512]{2,1,0:T(8,128)(2,1)S(1)} %get-tuple-element.65.held_ref, ...), custom_call_target="tpu_custom_call" | custom-call | flops 335544320 | tf_op jit(solution)/shard_map/solve_2/pallas_call | solution.py:32
  85.6 1.3 collective-permute-start.15
  86.9 1.3 collective-permute-start.16
  88.2 1.3 collective-permute-start.17
  89.5 1.3 collective-permute-start.18
  101.0 1.4 collective-permute-start.28
  102.4 1.3 solve_3.1
  106.5 1.3 collective-permute-start.29
  107.8 1.3 collective-permute-start.30
  111.0 1.3 collective-permute-done.31.rest_3_
  112.3 1.7 %solve_4.1 = (bf16[512,128]{1,0:T(8,128)(2,1)}, bf16[512,128]{1,0:T(8,128)(2,1)S(1)}) custom-call(s32[6,7]{1,0:T(8,128)S(1)} %pad_add_fusion.table, bf16[30,512,512]{2,1,0:T(8,128)(2,1)S(1)} %get-tuple-element.65.held_ref, f32[4,512,128]{2,1,0:T(8,128)S(1)} %get-tuple-element.66.ahead_ref, bf16[5,512,512]{2,1,0:T(8,128)(2,1)S(1)} %get-tuple-element.63.inverse_ref, ...), custom_call_target="tpu_custom_call" | custom-call | flops 335544320 | tf_op jit(solution)/shard_map/solve_4/pallas_call | solution.py:32
  116.7 15.5 %collective-permute-done.33.rest_1_ = bf16[512,128]{1,0:T(8,128)(2,1)S(1)} collective-permute-done((bf16[512,128]{1,0:T(8,128)(2,1)S(1)}, bf16[512,128]{1,0:T(8,128)(2,1)S(1)}, u32[]{:S(2)}, u32[]{:S(2)}) %collective-permute-start.33) | collective-permute-done | bytes 131104 | tf_op jit(solution)/shard_map/ppermute | solution.py:213
  132.9 1.3 collective-permute-start.35
  134.2 1.3 collective-permute-start.36
  137.2 1.3 collective-permute-done.36.rest_6_
  138.5 1.6 %collective-permute-done.37.rest_7_ = bf16[512,128]{1,0:T(8,128)(2,1)S(1)} collective-permute-done((bf16[512,128]{1,0:T(8,128)(2,1)S(1)}, bf16[512,128]{1,0:T(8,128)(2,1)S(1)}, u32[]{:S(2)}, u32[]{:S(2)}) %collective-permute-start.37) | collective-permute-done | bytes 131104 | tf_op jit(solution)/shard_map/ppermute | solution.py:213
  142.7 1.8 %final.1 = f32[5,512,128]{2,1,0:T(8,128)} custom-call(s32[6,7]{1,0:T(8,128)S(1)} %pad_add_fusion.table, bf16[512,128]{1,0:T(8,128)(2,1)S(1)} %get-tuple-element.64.rest_0_.first_ref, bf16[2,512,128]{2,1,0:T(8,128)(2,1)S(1)} %merged.1.mine_ref, bf16[2,512,128]{2,1,0:T(8,128)(2,1)S(1)} %collective-permute-done.38.other_ref), custom_call_target="tpu_custom_call" | custom-call | tf_op jit(solution)/shard_map/final/pallas_call | solution.py:32
  (69 shorter events, 37.0 us)
Async XLA Ops:
  3.3 7.9 %collective-permute-start = (bf16[512,128]{1,0:T(8,128)(2,1)S(1)}, bf16[512,128]{1,0:T(8,128)(2,1)S(1)}, u32[]{:S(2)}, u32[]{:S(2)}) collective-permute-start(bf16[512,128]{1,0:T(8,128)(2,1)S(1)} %get-tuple-element.59.rest_0_), channel_id=1, source_target_pairs={{0,1},{1,2},{2,3},{3,0},{4,5},{5,6},{6,7},{7,4},{8,9},{9,10},{10,1... | collective-permute-start | bytes 393224 | tf_op jit(solution)/shard_map/ppermute | solution.py:221
  5.9 5.3 %collective-permute-start.3 = (bf16[512,128]{1,0:T(8,128)(2,1)S(1)}, bf16[512,128]{1,0:T(8,128)(2,1)S(1)}, u32[]{:S(2)}, u32[]{:S(2)}) collective-permute-start(bf16[512,128]{1,0:T(8,128)(2,1)S(1)} %get-tuple-element.60.rest_1_), channel_id=1, source_target_pairs={{0,3},{1,0},{2,1},{3,2},{4,7},{5,4},{6,5},{7,6},{8,11},{9,8},{10,9... | collective-permute-start | bytes 393224 | tf_op jit(solution)/shard_map/ppermute | solution.py:221
  8.1 7.3 %collective-permute-start.1 = (bf16[512,128]{1,0:T(8,128)(2,1)S(1)}, bf16[512,128]{1,0:T(8,128)(2,1)S(1)}, u32[]{:S(2)}, u32[]{:S(2)}) collective-permute-start(bf16[512,128]{1,0:T(8,128)(2,1)S(1)} %get-tuple-element.60.rest_1_), channel_id=1, source_target_pairs={{0,1},{1,2},{2,3},{3,0},{4,5},{5,6},{6,7},{7,4},{8,9},{9,10},{10,1... | collective-permute-start | bytes 393224 | tf_op jit(solution)/shard_map/ppermute | solution.py:221
  8.1 7.3 %collective-permute-start.5 = (bf16[512,128]{1,0:T(8,128)(2,1)S(1)}, bf16[512,128]{1,0:T(8,128)(2,1)S(1)}, u32[]{:S(2)}, u32[]{:S(2)}) collective-permute-start(bf16[512,128]{1,0:T(8,128)(2,1)S(1)} %get-tuple-element.59.rest_0_), channel_id=1, source_target_pairs={{0,3},{1,0},{2,1},{3,2},{4,7},{5,4},{6,5},{7,6},{8,11},{9,8},{10,9... | collective-permute-start | bytes 393224 | tf_op jit(solution)/shard_map/ppermute | solution.py:221
  11.2 5.0 %collective-permute-start.2 = (bf16[512,128]{1,0:T(8,128)(2,1)S(1)}, bf16[512,128]{1,0:T(8,128)(2,1)S(1)}, u32[]{:S(2)}, u32[]{:S(2)}) collective-permute-start(bf16[512,128]{1,0:T(8,128)(2,1)S(1)} %collective-permute-done.rest_2_), channel_id=1, source_target_pairs={{0,1},{1,2},{2,3},{3,0},{4,5},{5,6},{6,7},{7,4},{8,9},{9,10},{10,1... | collective-permute-start | bytes 393224 | tf_op jit(solution)/shard_map/ppermute | solution.py:221
  11.2 5.0 %collective-permute-start.4 = (bf16[512,128]{1,0:T(8,128)(2,1)S(1)}, bf16[512,128]{1,0:T(8,128)(2,1)S(1)}, u32[]{:S(2)}, u32[]{:S(2)}) collective-permute-start(bf16[512,128]{1,0:T(8,128)(2,1)S(1)} %collective-permute-done.3.rest_7_), channel_id=1, source_target_pairs={{0,3},{1,0},{2,1},{3,2},{4,7},{5,4},{6,5},{7,6},{8,11},{9,8},{10,9... | collective-permute-start | bytes 393224 | tf_op jit(solution)/shard_map/ppermute | solution.py:221
  52.1 3.9 %collective-permute-start.7 = (bf16[16,80,128]{2,1,0:T(8,128)(2,1)S(1)}, bf16[16,80,128]{2,1,0:T(8,128)(2,1)S(1)}, u32[]{:S(2)}, u32[]{:S(2)}) collective-permute-start(bf16[16,80,128]{2,1,0:T(8,128)(2,1)S(1)} %all_to_all.11.half_ref), channel_id=1, source_target_pairs={{0,4},{4,0},{8,12},{12,8},{16,20},{20,16},{24,28},{28,24},{32,36},... | collective-permute-start | bytes 983048 | tf_op jit(solution)/shard_map/ppermute | solution.py:225
  57.1 8.7 %collective-permute-start.8 = (bf16[512,128]{1,0:T(8,128)(2,1)S(1)}, bf16[512,128]{1,0:T(8,128)(2,1)S(1)}, u32[]{:S(2)}, u32[]{:S(2)}) collective-permute-start(bf16[512,128]{1,0:T(8,128)(2,1)S(1)} %get-tuple-element.64.rest_0_.first_ref), channel_id=1, source_target_pairs={{0,1},{1,2},{2,3},{3,0},{4,5},{5,6},{6,7},{7,4},{8,9},{9,10},{10,1... | collective-permute-start | bytes 393224 | tf_op jit(solution)/shard_map/ppermute | solution.py:221
  59.2 10.1 %collective-permute-start.9 = (bf16[512,128]{1,0:T(8,128)(2,1)S(1)}, bf16[512,128]{1,0:T(8,128)(2,1)S(1)}, u32[]{:S(2)}, u32[]{:S(2)}) collective-permute-start(bf16[512,128]{1,0:T(8,128)(2,1)S(1)} %get-tuple-element.64.rest_0_.first_ref), channel_id=1, source_target_pairs={{0,2},{1,3},{2,0},{3,1},{4,6},{5,7},{6,4},{7,5},{8,10},{9,11},{10,... | collective-permute-start | bytes 393224 | tf_op jit(solution)/shard_map/ppermute | solution.py:221
  63.3 6.1 %collective-permute-start.10 = (bf16[512,128]{1,0:T(8,128)(2,1)S(1)}, bf16[512,128]{1,0:T(8,128)(2,1)S(1)}, u32[]{:S(2)}, u32[]{:S(2)}) collective-permute-start(bf16[512,128]{1,0:T(8,128)(2,1)S(1)} %get-tuple-element.64.rest_0_.first_ref), channel_id=1, source_target_pairs={{0,3},{1,0},{2,1},{3,2},{4,7},{5,4},{6,5},{7,6},{8,11},{9,8},{10,9... | collective-permute-start | bytes 393224 | tf_op jit(solution)/shard_map/ppermute | solution.py:221
  70.7 12.0 %collective-permute-start.11 = (bf16[2,512,128]{2,1,0:T(8,128)(2,1)S(1)}, bf16[2,512,128]{2,1,0:T(8,128)(2,1)S(1)}, u32[]{:S(2)}, u32[]{:S(2)}) collective-permute-start(bf16[2,512,128]{2,1,0:T(8,128)(2,1)S(1)} %get-tuple-element.67), channel_id=1, source_target_pairs={{0,4},{1,5},{2,6},{3,7}} | collective-permute-start | bytes 786440 | tf_op jit(solution)/shard_map/ppermute | solution.py:213
  72.0 8.1 %collective-permute-start.12 = (bf16[512,128]{1,0:T(8,128)(2,1)S(1)}, bf16[512,128]{1,0:T(8,128)(2,1)S(1)}, u32[]{:S(2)}, u32[]{:S(2)}) collective-permute-start(bf16[512,128]{1,0:T(8,128)(2,1)S(1)} %get-tuple-element.68.rest_4_), channel_id=1, source_target_pairs={{0,5},{1,6},{2,7},{3,4}} | collective-permute-start | bytes 393224 | tf_op jit(solution)/shard_map/ppermute | solution.py:213
  73.3 8.7 %collective-permute-start.13 = (bf16[512,128]{1,0:T(8,128)(2,1)S(1)}, bf16[512,128]{1,0:T(8,128)(2,1)S(1)}, u32[]{:S(2)}, u32[]{:S(2)}) collective-permute-start(bf16[512,128]{1,0:T(8,128)(2,1)S(1)} %get-tuple-element.68.rest_4_), channel_id=1, source_target_pairs={{0,6},{1,7},{2,4},{3,5}} | collective-permute-start | bytes 393224 | tf_op jit(solution)/shard_map/ppermute | solution.py:213
  74.6 8.1 %collective-permute-start.14 = (bf16[512,128]{1,0:T(8,128)(2,1)S(1)}, bf16[512,128]{1,0:T(8,128)(2,1)S(1)}, u32[]{:S(2)}, u32[]{:S(2)}) collective-permute-start(bf16[512,128]{1,0:T(8,128)(2,1)S(1)} %get-tuple-element.68.rest_4_), channel_id=1, source_target_pairs={{0,7},{1,4},{2,5},{3,6}} | collective-permute-start | bytes 393224 | tf_op jit(solution)/shard_map/ppermute | solution.py:213
  85.6 11.6 %collective-permute-start.15 = (bf16[2,512,128]{2,1,0:T(8,128)(2,1)S(1)}, bf16[2,512,128]{2,1,0:T(8,128)(2,1)S(1)}, u32[]{:S(2)}, u32[]{:S(2)}) collective-permute-start(bf16[2,512,128]{2,1,0:T(8,128)(2,1)S(1)} %get-tuple-element.74), channel_id=1, source_target_pairs={{4,8},{5,9},{6,10},{7,11}} | collective-permute-start | bytes 786440 | tf_op jit(solution)/shard_map/ppermute | solution.py:213
  86.9 6.1 %collective-permute-start.16 = (bf16[512,128]{1,0:T(8,128)(2,1)S(1)}, bf16[512,128]{1,0:T(8,128)(2,1)S(1)}, u32[]{:S(2)}, u32[]{:S(2)}) collective-permute-start(bf16[512,128]{1,0:T(8,128)(2,1)S(1)} %get-tuple-element.75), channel_id=1, source_target_pairs={{4,9},{5,10},{6,11},{7,8}} | collective-permute-start | bytes 393224 | tf_op jit(solution)/shard_map/ppermute | solution.py:213
  88.2 6.2 %collective-permute-start.17 = (bf16[512,128]{1,0:T(8,128)(2,1)S(1)}, bf16[512,128]{1,0:T(8,128)(2,1)S(1)}, u32[]{:S(2)}, u32[]{:S(2)}) collective-permute-start(bf16[512,128]{1,0:T(8,128)(2,1)S(1)} %get-tuple-element.75), channel_id=1, source_target_pairs={{4,10},{5,11},{6,8},{7,9}} | collective-permute-start | bytes 393224 | tf_op jit(solution)/shard_map/ppermute | solution.py:213
  89.5 6.3 %collective-permute-start.18 = (bf16[512,128]{1,0:T(8,128)(2,1)S(1)}, bf16[512,128]{1,0:T(8,128)(2,1)S(1)}, u32[]{:S(2)}, u32[]{:S(2)}) collective-permute-start(bf16[512,128]{1,0:T(8,128)(2,1)S(1)} %get-tuple-element.75), channel_id=1, source_target_pairs={{4,11},{5,8},{6,9},{7,10}} | collective-permute-start | bytes 393224 | tf_op jit(solution)/shard_map/ppermute | solution.py:213
  91.6 6.2 %collective-permute-start.19 = (bf16[512,128]{1,0:T(8,128)(2,1)S(1)}, bf16[512,128]{1,0:T(8,128)(2,1)S(1)}, u32[]{:S(2)}, u32[]{:S(2)}) collective-permute-start(bf16[512,128]{1,0:T(8,128)(2,1)S(1)} %get-tuple-element.82), channel_id=1, source_target_pairs={{0,12},{1,13},{2,14},{3,15}} | collective-permute-start | bytes 393224 | tf_op jit(solution)/shard_map/ppermute | solution.py:213
  93.0 4.8 %collective-permute-start.20 = (bf16[512,128]{1,0:T(8,128)(2,1)S(1)}, bf16[512,128]{1,0:T(8,128)(2,1)S(1)}, u32[]{:S(2)}, u32[]{:S(2)}) collective-permute-start(bf16[512,128]{1,0:T(8,128)(2,1)S(1)} %get-tuple-element.88.value_ref), channel_id=1, source_target_pairs={{0,8},{1,9},{2,10},{3,11},{4,12},{5,13},{6,14},{7,15}} | collective-permute-start | bytes 393224 | tf_op jit(solution)/shard_map/ppermute | solution.py:213
  94.4 3.4 %collective-permute-start.21 = (bf16[512,128]{1,0:T(8,128)(2,1)S(1)}, bf16[512,128]{1,0:T(8,128)(2,1)S(1)}, u32[]{:S(2)}, u32[]{:S(2)}) collective-permute-start(bf16[512,128]{1,0:T(8,128)(2,1)S(1)} %get-tuple-element.88.value_ref), channel_id=1, source_target_pairs={{0,24},{1,25},{2,26},{3,27},{4,28},{5,29},{6,30},{7,31}} | collective-permute-start | bytes 393224 | tf_op jit(solution)/shard_map/ppermute | solution.py:213
  97.1 5.3 %collective-permute-start.23 = (bf16[512,128]{1,0:T(8,128)(2,1)S(1)}, bf16[512,128]{1,0:T(8,128)(2,1)S(1)}, u32[]{:S(2)}, u32[]{:S(2)}) collective-permute-start(bf16[512,128]{1,0:T(8,128)(2,1)S(1)} %get-tuple-element.96), channel_id=1, source_target_pairs={{0,8},{1,9},{2,10},{3,11}} | collective-permute-start | bytes 393224 | tf_op jit(solution)/shard_map/ppermute | solution.py:213
  101.0 5.5 %collective-permute-start.28 = (bf16[512,128]{1,0:T(8,128)(2,1)S(1)}, bf16[512,128]{1,0:T(8,128)(2,1)S(1)}, u32[]{:S(2)}, u32[]{:S(2)}) collective-permute-start(bf16[512,128]{1,0:T(8,128)(2,1)S(1)} %later_1.1), channel_id=1, source_target_pairs={{4,12},{5,13},{6,14},{7,15}} | collective-permute-start | bytes 393224 | tf_op jit(solution)/shard_map/ppermute | solution.py:213
  103.7 6.7 %collective-permute-start.24 = (bf16[2,512,128]{2,1,0:T(8,128)(2,1)S(1)}, bf16[2,512,128]{2,1,0:T(8,128)(2,1)S(1)}, u32[]{:S(2)}, u32[]{:S(2)}) collective-permute-start(bf16[2,512,128]{2,1,0:T(8,128)(2,1)S(1)} %get-tuple-element.97), channel_id=1, source_target_pairs={{8,12},{9,13},{10,14},{11,15}} | collective-permute-start | bytes 786440 | tf_op jit(solution)/shard_map/ppermute | solution.py:213
  105.1 4.0 %collective-permute-start.26 = (bf16[512,128]{1,0:T(8,128)(2,1)S(1)}, bf16[512,128]{1,0:T(8,128)(2,1)S(1)}, u32[]{:S(2)}, u32[]{:S(2)}) collective-permute-start(bf16[512,128]{1,0:T(8,128)(2,1)S(1)} %get-tuple-element.110.rest_4_), channel_id=1, source_target_pairs={{8,14},{9,15},{10,12},{11,13}} | collective-permute-start | bytes 393224 | tf_op jit(solution)/shard_map/ppermute | solution.py:213
  105.8 4.6 %collective-permute-start.27 = (bf16[512,128]{1,0:T(8,128)(2,1)S(1)}, bf16[512,128]{1,0:T(8,128)(2,1)S(1)}, u32[]{:S(2)}, u32[]{:S(2)}) collective-permute-start(bf16[512,128]{1,0:T(8,128)(2,1)S(1)} %get-tuple-element.110.rest_4_), channel_id=1, source_target_pairs={{8,15},{9,12},{10,13},{11,14}} | collective-permute-start | bytes 393224 | tf_op jit(solution)/shard_map/ppermute | solution.py:213
  106.5 4.0 %collective-permute-start.29 = (bf16[512,128]{1,0:T(8,128)(2,1)S(1)}, bf16[512,128]{1,0:T(8,128)(2,1)S(1)}, u32[]{:S(2)}, u32[]{:S(2)}) collective-permute-start(bf16[512,128]{1,0:T(8,128)(2,1)S(1)} %picked.2.rest_0_), channel_id=1, source_target_pairs={{0,32},{1,33},{2,34},{3,35},{4,36},{5,37},{6,38},{7,39},{8,40},{9,... | collective-permute-start | bytes 393224 | tf_op jit(solution)/shard_map/ppermute | solution.py:213
  114.7 17.5 %collective-permute-start.33 = (bf16[512,128]{1,0:T(8,128)(2,1)S(1)}, bf16[512,128]{1,0:T(8,128)(2,1)S(1)}, u32[]{:S(2)}, u32[]{:S(2)}) collective-permute-start(bf16[512,128]{1,0:T(8,128)(2,1)S(1)} %get-tuple-element.113.value_ref), channel_id=1, source_target_pairs={{8,0},{9,1},{10,2},{11,3},{12,4},{13,5},{14,6},{15,7}} | collective-permute-start | bytes 393224 | tf_op jit(solution)/shard_map/ppermute | solution.py:213
  116.0 16.2 %collective-permute-start.34 = (bf16[512,128]{1,0:T(8,128)(2,1)S(1)}, bf16[512,128]{1,0:T(8,128)(2,1)S(1)}, u32[]{:S(2)}, u32[]{:S(2)}) collective-permute-start(bf16[512,128]{1,0:T(8,128)(2,1)S(1)} %get-tuple-element.113.value_ref), channel_id=1, source_target_pairs={{8,24},{9,25},{10,26},{11,27},{12,28},{13,29},{14,30},{15,31}} | collective-permute-start | bytes 393224 | tf_op jit(solution)/shard_map/ppermute | solution.py:213
  132.9 4.3 %collective-permute-start.35 = (bf16[512,128]{1,0:T(8,128)(2,1)S(1)}, bf16[512,128]{1,0:T(8,128)(2,1)S(1)}, u32[]{:S(2)}, u32[]{:S(2)}) collective-permute-start(bf16[512,128]{1,0:T(8,128)(2,1)S(1)} %picked.3.rest_4_), channel_id=1, source_target_pairs={{0,32},{1,33},{2,34},{3,35},{4,36},{5,37},{6,38},{7,39},{8,40},{9,... | collective-permute-start | bytes 393224 | tf_op jit(solution)/shard_map/ppermute | solution.py:213
  134.2 4.3 %collective-permute-start.36 = (bf16[512,128]{1,0:T(8,128)(2,1)S(1)}, bf16[512,128]{1,0:T(8,128)(2,1)S(1)}, u32[]{:S(2)}, u32[]{:S(2)}) collective-permute-start(bf16[512,128]{1,0:T(8,128)(2,1)S(1)} %picked.3.rest_4_), channel_id=1, source_target_pairs={{0,96},{1,97},{2,98},{3,99},{4,100},{5,101},{6,102},{7,103},{8,104... | collective-permute-start | bytes 393224 | tf_op jit(solution)/shard_map/ppermute | solution.py:213
  135.5 4.6 %collective-permute-start.37 = (bf16[512,128]{1,0:T(8,128)(2,1)S(1)}, bf16[512,128]{1,0:T(8,128)(2,1)S(1)}, u32[]{:S(2)}, u32[]{:S(2)}) collective-permute-start(bf16[512,128]{1,0:T(8,128)(2,1)S(1)} %picked.3.rest_4_), channel_id=1, source_target_pairs={{0,64},{1,65},{2,66},{3,67},{4,68},{5,69},{6,70},{7,71},{8,72},{9,... | collective-permute-start | bytes 393224 | tf_op jit(solution)/shard_map/ppermute | solution.py:213
  (8 other events, 54.6 us)

commit v9 on v7

--- a/solution.py
+++ b/solution.py
@@ -145,14 +145,15 @@
     lists = (table, held_ref)
     total[...] = nearest[1].astype(F32) if chained else jnp.zeros_like(total)
     for ref in more[1 if "mixed" in named else 0 :]:
-        total[...] += ref[...].astype(F32)
+        total[...] += (ref[0] if len(ref.shape) == 3 else ref[...]).astype(F32)
     add_products(total, level, slots, low, low + NZ, lambda q: operands[q], *lists)
     correction = (ahead_ref[level - 1] - total[...]).astype(BF16)
     value = dot(inverse_ref[level], correction).astype(BF16)
     named["value"][...] = value
     if "packed" in named:
         named["packed"][0] = value
-        total[...] = jnp.zeros_like(total)
+        carried = [ref for ref in more if len(ref.shape) == 3]
+        total[...] = carried[0][1].astype(F32) if carried else jnp.zeros_like(total)
         add_products(total, level + 1, slots, low, low + NZ, lambda q: operands[q], *lists)
         named["packed"][1] = total[...].astype(BF16)
     if "mixed" in named:
@@ -162,12 +163,11 @@
             named["kept"][v] = operands[v]
 
 
-def later_kernel(levels, slots, low, table, held_ref, operands, *rest):
-    out_refs, total = rest[:-1], rest[-1]
-    for level, out_ref in zip(levels, out_refs):
+def later_kernel(levels, slots, low, table, held_ref, operands, out_ref, total):
+    for i, level in enumerate(levels):
         total[...] = jnp.zeros_like(total)
         add_products(total, level, slots, low, low + NZ, lambda q: operands[q], table, held_ref)
-        out_ref[...] = total[...].astype(BF16)
+        out_ref[i] = total[...].astype(BF16)
 
 
 def pair_kernel(keep_ref, got_ref, out_ref):
@@ -323,7 +323,7 @@
     def products(u, levels_made, kept):
         return call(
             functools.partial(later_kernel, levels_made, slots, low(u)), f"later_{u}",
-            (full,) * len(levels_made), [SMEM] + [VMEM] * 2, (*lists, kept),
+            jax.ShapeDtypeStruct((len(levels_made), size, samples), BF16), [SMEM] + [VMEM] * 2, (*lists, kept),
             scratch=[acc], flops=4 * len(levels_made) * one,
         )
 
@@ -333,20 +333,19 @@
     x1, packed, kept = solve(0, [first] + [to_row(first, k) for k in (1, 2, 3)], [], ("value", "packed", "kept"))
     pieces = onward(1, x1, packed)
     pieces, kept = after((pieces, kept))
-    p30, p40 = products(0, (3, 4), kept)
+    carried = products(0, (3, 4), kept)
     x2, packed, mixed12, kept = solve(1, pieces, [x1], ("value", "packed", "mixed", "kept"))
     pieces = onward(2, x2, packed)
     mixed12 = spread_x(mixed12, 0)
     mixed12 = pick(column(0, 0, 0), table, mixed12[0], mixed12[1:])
-    p30, p40 = to_column(p30, 0, 2), to_column(p40, 0, 3)
+    carried = to_column(carried, 0, 2)
     pieces, kept = after((pieces, kept))
-    p41, = products(1, (4,), kept)
-    pieces, p40 = after((pieces, p40))
-    x3, packed = solve(2, pieces, [p30], ("value", "packed"))
+    p41 = products(1, (4,), kept)
+    x3, packed = solve(2, pieces, [carried], ("value", "packed"))
     pieces = onward(3, x3, packed)
     spread12 = spread_y(after((mixed12, x3))[0])
     p41 = to_column(p41, 1, 3)
-    x4, mixed34 = solve(3, pieces, [x3, p40, p41], ("value", "mixed"))
+    x4, mixed34 = solve(3, pieces, [x3, p41], ("value", "mixed"))
     mixed34 = spread_x(mixed34, 1)
     spread34 = spread_y(pick(column(1, 0, 0), table, mixed34[0], mixed34[1:]))
     spreads = spread12 + spread34

time: 142 us -> 140 us (0.986); the launches traced: 140 us -> 140 us
  waiting for transfers between devices: 29.3 us -> 32 us
  starting transfers between devices: 59.3 us -> 57.6 us
    ppermute x27 -> x26, starting transfers between devices: 41.4 us -> 37.5 us  [send(): return lax.ppermute(value, AXES, pairs)]
    ppermute x27 -> x26, waiting for transfers between devices: 12.9 us -> 15.9 us  [send(): return lax.ppermute(value, AXES, pairs)]
    ppermute x3, starting transfers between devices: 4.87 us -> 6.82 us  [other_core(): return lax.ppermute(value, 'col', [(c, c ^ 1) for c in range(NX * NY * 2)])]
  transfers between devices with their start and end apart: 39 -> 38, of which waited for: 16 -> 18; matrix products, arithmetic and copies ran while one was open for 1% -> 1% of each run, Pallas kernels for 4% -> 4%
where the time goes in v9:
time: 140 us
  starting transfers between devices  57.6 us (41%)
  waiting for transfers between devices  32 us (23%)
  blocking collectives  26.9 us (19%)
  Pallas kernels  20.6 us (15%)
    ppermute x26, starting transfers between devices, send(): return lax.ppermute(value, AXES, pairs)  37.5 us
    all_to_all x2, blocking collectives, over_plane(): lax.all_to_all(value, 'col', 0, 0, axis_index_groups=groups, tiled=True)  26.9 us
    pallas_call x15, Pallas kernels, call(): pl.pallas_call(body, out_shape=outs, in_specs=in_specs, out_specs=out_spe...  20.6 us
    ppermute x26, waiting for transfers between devices, send(): return lax.ppermute(value, AXES, pairs)  15.9 us
    ppermute x9, starting transfers between devices, to_row(): return lax.ppermute(value, 'row', [(z, (z + step) % NZ) for z in range(NZ)])  13.3 us
    ppermute x9, waiting for transfers between devices, to_row(): return lax.ppermute(value, 'row', [(z, (z + step) % NZ) for z in range(NZ)])  12.4 us
    ppermute x3, starting transfers between devices, other_core(): return lax.ppermute(value, 'col', [(c, c ^ 1) for c in range(NX * NY * 2)])  6.82 us
    ppermute x3, waiting for transfers between devices, other_core(): return lax.ppermute(value, 'col', [(c, c ^ 1) for c in range(NX * NY * 2)])  3.67 us
  transfers between devices with their start and end apart: 38, of which 18 were waited for; matrix products, arithmetic and copies ran while one was open for 1% of the time, Pallas kernels for 4%

profile of v9, /device:TPU:1, one launch (start us, length us, event | category | flops | bytes accessed | tf_op | source)
XLA Modules:
  0.0 139.8 jit_solution(8416379327979608015)
XLA Ops:
  0.6 2.7 %base_solve.1 = (f32[2,512,128]{2,1,0:T(8,128)}, bf16[512,128]{1,0:T(8,128)(2,1)S(1)}, bf16[512,128]{1,0:T(8,128)(2,1)S(1)}) custom-call(bf16[2,512,512]{2,1,0:T(8,128)(2,1)} %inverse_ref.1, f32[2,512,128]{2,1,0:T(8,128)} %rhs_ref.1), custom_call_target="tpu_custom_call" | custom-call | flops 134217728 | bytes 1835008 | tf_op jit(solution)/shard_map/base_solve/pallas_call | solution.py:32
  3.3 2.5 %collective-permute-start = (bf16[512,128]{1,0:T(8,128)(2,1)S(1)}, bf16[512,128]{1,0:T(8,128)(2,1)S(1)}, u32[]{:S(2)}, u32[]{:S(2)}) collective-permute-start(bf16[512,128]{1,0:T(8,128)(2,1)S(1)} %get-tuple-element.33.rest_0_), channel_id=1, source_target_pairs={{0,1},{1,2},{2,3},{3,0},{4,5},{5,6},{6,7},{7,4},{8,9},{9,10},{10,1... | collective-permute-start | bytes 393224 | tf_op jit(solution)/shard_map/ppermute | solution.py:221
  5.9 2.2 %collective-permute-start.3 = (bf16[512,128]{1,0:T(8,128)(2,1)S(1)}, bf16[512,128]{1,0:T(8,128)(2,1)S(1)}, u32[]{:S(2)}, u32[]{:S(2)}) collective-permute-start(bf16[512,128]{1,0:T(8,128)(2,1)S(1)} %get-tuple-element.34.rest_1_), channel_id=1, source_target_pairs={{0,3},{1,0},{2,1},{3,2},{4,7},{5,4},{6,5},{7,6},{8,11},{9,8},{10,9... | collective-permute-start | bytes 393224 | tf_op jit(solution)/shard_map/ppermute | solution.py:221
  8.1 1.4 collective-permute-start.5
  9.6 1.6 %collective-permute-done.rest_2_ = bf16[512,128]{1,0:T(8,128)(2,1)S(1)} collective-permute-done((bf16[512,128]{1,0:T(8,128)(2,1)S(1)}, bf16[512,128]{1,0:T(8,128)(2,1)S(1)}, u32[]{:S(2)}, u32[]{:S(2)}) %collective-permute-start) | collective-permute-done | bytes 131104 | tf_op jit(solution)/shard_map/ppermute | solution.py:221
  11.2 2.7 %collective-permute-start.4 = (bf16[512,128]{1,0:T(8,128)(2,1)S(1)}, bf16[512,128]{1,0:T(8,128)(2,1)S(1)}, u32[]{:S(2)}, u32[]{:S(2)}) collective-permute-start(bf16[512,128]{1,0:T(8,128)(2,1)S(1)} %collective-permute-done.3.rest_7_), channel_id=1, source_target_pairs={{0,3},{1,0},{2,1},{3,2},{4,7},{5,4},{6,5},{7,6},{8,11},{9,8},{10,9... | collective-permute-start | bytes 393224 | tf_op jit(solution)/shard_map/ppermute | solution.py:221
  15.4 2.3 %collective-permute-done.2.rest_4_ = bf16[512,128]{1,0:T(8,128)(2,1)S(1)} collective-permute-done((bf16[512,128]{1,0:T(8,128)(2,1)S(1)}, bf16[512,128]{1,0:T(8,128)(2,1)S(1)}, u32[]{:S(2)}, u32[]{:S(2)}) %collective-permute-start.2) | collective-permute-done | bytes 131104 | tf_op jit(solution)/shard_map/ppermute | solution.py:221
  17.7 4.5 %base_products.1 = (f32[16,80,128]{2,1,0:T(8,128)S(1)}, bf16[16,80,128]{2,1,0:T(8,128)(2,1)S(1)}, bf16[30,512,512]{2,1,0:T(8,128)(2,1)S(1)}, bf16[5,512,512]{2,1,0:T(8,128)(2,1)S(1)}) custom-call(s32[6,7]{1,0:T(8,128)S(1)} %pad_add_fusion.table, bf16[5,6,512,512]{3,2,1,0:T(8,128)(2,1)} %factor_ref.1, bf16[5,512,512]{2,1,0:T(8,128)(2,1)} %bitcast.11, ...), custom_call_target="tpu_custom_call" | custom-call | flops 1006632960 | bytes 15728640 | tf_op jit(solution)/shard_map/base_products/pallas_call | solution.py:32
  22.3 3.0 %collective-permute-start.6 = (bf16[16,80,128]{2,1,0:T(8,128)(2,1)S(1)}, bf16[16,80,128]{2,1,0:T(8,128)(2,1)S(1)}, u32[]{:S(2)}, u32[]{:S(2)}) collective-permute-start(bf16[16,80,128]{2,1,0:T(8,128)(2,1)S(1)} %get-tuple-element.36), channel_id=1, source_target_pairs={{0,4},{4,0},{8,12},{12,8},{16,20},{20,16},{24,28},{28,24},{32,36},... | collective-permute-start | bytes 983048 | tf_op jit(solution)/shard_map/ppermute | solution.py:225
  26.6 16.2 %all_to_all.10.in_ref = bf16[16,80,128]{2,1,0:T(8,128)(2,1)S(1)} all-to-all(bf16[16,80,128]{2,1,0:T(8,128)(2,1)S(1)} %pair_sums.1), channel_id=1, replica_groups={{0,8,16,24,32,40,48,56,64,72,80,88,96,104,112,120},{4,12,20,28,36,44,52..., dimensions={0} | all-to-all | bytes 655360 | tf_op jit(solution)/shard_map/all_to_all | solution.py:230
  42.9 10.7 %all_to_all.11.half_ref = bf16[16,80,128]{2,1,0:T(8,128)(2,1)S(1)} all-to-all(bf16[16,80,128]{2,1,0:T(8,128)(2,1)S(1)} %sum_shares.1), channel_id=1, replica_groups={{0,8,16,24,32,40,48,56,64,72,80,88,96,104,112,120},{4,12,20,28,36,44,52..., dimensions={0} | all-to-all | bytes 655360 | tf_op jit(solution)/shard_map/all_to_all | solution.py:230
  53.6 2.7 %collective-permute-start.7 = (bf16[16,80,128]{2,1,0:T(8,128)(2,1)S(1)}, bf16[16,80,128]{2,1,0:T(8,128)(2,1)S(1)}, u32[]{:S(2)}, u32[]{:S(2)}) collective-permute-start(bf16[16,80,128]{2,1,0:T(8,128)(2,1)S(1)} %all_to_all.11.half_ref), channel_id=1, source_target_pairs={{0,4},{4,0},{8,12},{12,8},{16,20},{20,16},{24,28},{28,24},{32,36},... | collective-permute-start | bytes 983048 | tf_op jit(solution)/shard_map/ppermute | solution.py:225
  58.6 3.7 %collective-permute-start.10 = (bf16[512,128]{1,0:T(8,128)(2,1)S(1)}, bf16[512,128]{1,0:T(8,128)(2,1)S(1)}, u32[]{:S(2)}, u32[]{:S(2)}) collective-permute-start(bf16[512,128]{1,0:T(8,128)(2,1)S(1)} %get-tuple-element.38.rest_0_.first_ref), channel_id=1, source_target_pairs={{0,3},{1,0},{2,1},{3,2},{4,7},{5,4},{6,5},{7,6},{8,11},{9,8},{10,9... | collective-permute-start | bytes 393224 | tf_op jit(solution)/shard_map/ppermute | solution.py:221
  63.0 5.0 %collective-permute-done.10.rest_3_ = bf16[512,128]{1,0:T(8,128)(2,1)S(1)} collective-permute-done((bf16[512,128]{1,0:T(8,128)(2,1)S(1)}, bf16[512,128]{1,0:T(8,128)(2,1)S(1)}, u32[]{:S(2)}, u32[]{:S(2)}) %collective-permute-start.10) | collective-permute-done | bytes 131104 | tf_op jit(solution)/shard_map/ppermute | solution.py:221
  68.3 3.2 %collective-permute-done.8.rest_1_ = bf16[512,128]{1,0:T(8,128)(2,1)S(1)} collective-permute-done((bf16[512,128]{1,0:T(8,128)(2,1)S(1)}, bf16[512,128]{1,0:T(8,128)(2,1)S(1)}, u32[]{:S(2)}, u32[]{:S(2)}) %collective-permute-start.8) | collective-permute-done | bytes 131104 | tf_op jit(solution)/shard_map/ppermute | solution.py:221
  77.9 2.4 %collective-permute-done.14.rest_3_ = bf16[512,128]{1,0:T(8,128)(2,1)S(1)} collective-permute-done((bf16[512,128]{1,0:T(8,128)(2,1)S(1)}, bf16[512,128]{1,0:T(8,128)(2,1)S(1)}, u32[]{:S(2)}, u32[]{:S(2)}) %collective-permute-start.14) | collective-permute-done | bytes 131104 | tf_op jit(solution)/shard_map/ppermute | solution.py:213
  80.3 2.8 %collective-permute-done.13.rest_2_ = bf16[512,128]{1,0:T(8,128)(2,1)S(1)} collective-permute-done((bf16[512,128]{1,0:T(8,128)(2,1)S(1)}, bf16[512,128]{1,0:T(8,128)(2,1)S(1)}, u32[]{:S(2)}, u32[]{:S(2)}) %collective-permute-start.13) | collective-permute-done | bytes 131104 | tf_op jit(solution)/shard_map/ppermute | solution.py:213
  83.2 1.4 collective-permute-done.12.rest_1_
  84.5 2.3 %solve_2.1 = (bf16[512,128]{1,0:T(8,128)(2,1)S(1)}, bf16[2,512,128]{2,1,0:T(8,128)(2,1)S(1)}, bf16[512,128]{1,0:T(8,128)(2,1)S(1)}, bf16[4,512,128]{2,1,0:T(8,128)(2,1)S(1)}) custom-call(s32[6,7]{1,0:T(8,128)S(1)} %pad_add_fusion.table, bf16[30,512,512]{2,1,0:T(8,128)(2,1)S(1)} %get-tuple-element.39.held_ref, ...), custom_call_target="tpu_custom_call" | custom-call | flops 335544320 | tf_op jit(solution)/shard_map/solve_2/pallas_call | solution.py:32
  86.8 1.3 collective-permute-start.18
  89.6 1.3 collective-permute-start.21
  90.9 1.3 collective-permute-start.20
  93.5 2.1 %collective-permute-done.21.rest_3_ = bf16[512,128]{1,0:T(8,128)(2,1)S(1)} collective-permute-done((bf16[512,128]{1,0:T(8,128)(2,1)S(1)}, bf16[512,128]{1,0:T(8,128)(2,1)S(1)}, u32[]{:S(2)}, u32[]{:S(2)}) %collective-permute-start.21) | collective-permute-done | bytes 131104 | tf_op jit(solution)/shard_map/ppermute | solution.py:213
  95.6 1.4 %collective-permute-done.20.rest_2_ = bf16[512,128]{1,0:T(8,128)(2,1)S(1)} collective-permute-done((bf16[512,128]{1,0:T(8,128)(2,1)S(1)}, bf16[512,128]{1,0:T(8,128)(2,1)S(1)}, u32[]{:S(2)}, u32[]{:S(2)}) %collective-permute-start.20) | collective-permute-done | bytes 131104 | tf_op jit(solution)/shard_map/ppermute | solution.py:213
  97.0 1.4 %collective-permute-done.19.rest_1_ = bf16[512,128]{1,0:T(8,128)(2,1)S(1)} collective-permute-done((bf16[512,128]{1,0:T(8,128)(2,1)S(1)}, bf16[512,128]{1,0:T(8,128)(2,1)S(1)}, u32[]{:S(2)}, u32[]{:S(2)}) %collective-permute-start.19) | collective-permute-done | bytes 131104 | tf_op jit(solution)/shard_map/ppermute | solution.py:213
  106.4 1.3 collective-permute-start.16
  107.7 9.3 %collective-permute-start.15 = (bf16[512,128]{1,0:T(8,128)(2,1)S(1)}, bf16[512,128]{1,0:T(8,128)(2,1)S(1)}, u32[]{:S(2)}, u32[]{:S(2)}) collective-permute-start(bf16[512,128]{1,0:T(8,128)(2,1)S(1)} %get-tuple-element.48.value_ref), channel_id=1, source_target_pairs={{0,8},{1,9},{2,10},{3,11},{4,12},{5,13},{6,14},{7,15}} | collective-permute-start | bytes 393224 | tf_op jit(solution)/shard_map/ppermute | solution.py:213
  117.0 1.7 %solve_4.1 = (bf16[512,128]{1,0:T(8,128)(2,1)}, bf16[512,128]{1,0:T(8,128)(2,1)S(1)}) custom-call(s32[6,7]{1,0:T(8,128)S(1)} %pad_add_fusion.table, bf16[30,512,512]{2,1,0:T(8,128)(2,1)S(1)} %get-tuple-element.39.held_ref, f32[4,512,128]{2,1,0:T(8,128)S(1)} %get-tuple-element.40.ahead_ref, bf16[5,512,512]{2,1,0:T(8,128)(2,1)S(1)} %get-tuple-element.37.inverse_ref, ...), custom_call_target="tpu_custom_call" | custom-call | flops 335544320 | tf_op jit(solution)/shard_map/solve_4/pallas_call | solution.py:32
  123.7 1.3 collective-permute-start.24
  130.8 1.3 collective-permute-start.34
  133.3 1.7 %collective-permute-done.34.rest_5_ = bf16[512,128]{1,0:T(8,128)(2,1)S(1)} collective-permute-done((bf16[512,128]{1,0:T(8,128)(2,1)S(1)}, bf16[512,128]{1,0:T(8,128)(2,1)S(1)}, u32[]{:S(2)}, u32[]{:S(2)}) %collective-permute-start.34) | collective-permute-done | bytes 131104 | tf_op jit(solution)/shard_map/ppermute | solution.py:213
  138.0 1.8 %final.1 = f32[5,512,128]{2,1,0:T(8,128)} custom-call(s32[6,7]{1,0:T(8,128)S(1)} %pad_add_fusion.table, bf16[512,128]{1,0:T(8,128)(2,1)S(1)} %get-tuple-element.38.rest_0_.first_ref, bf16[2,512,128]{2,1,0:T(8,128)(2,1)S(1)} %merged.1.mine_ref, bf16[2,512,128]{2,1,0:T(8,128)(2,1)S(1)} %collective-permute-done.37.other_ref), custom_call_target="tpu_custom_call" | custom-call | tf_op jit(solution)/shard_map/final/pallas_call | solution.py:32
  (67 shorter events, 38.2 us)
Async XLA Ops:
  3.3 7.9 %collective-permute-start = (bf16[512,128]{1,0:T(8,128)(2,1)S(1)}, bf16[512,128]{1,0:T(8,128)(2,1)S(1)}, u32[]{:S(2)}, u32[]{:S(2)}) collective-permute-start(bf16[512,128]{1,0:T(8,128)(2,1)S(1)} %get-tuple-element.33.rest_0_), channel_id=1, source_target_pairs={{0,1},{1,2},{2,3},{3,0},{4,5},{5,6},{6,7},{7,4},{8,9},{9,10},{10,1... | collective-permute-start | bytes 393224 | tf_op jit(solution)/shard_map/ppermute | solution.py:221
  5.9 5.3 %collective-permute-start.3 = (bf16[512,128]{1,0:T(8,128)(2,1)S(1)}, bf16[512,128]{1,0:T(8,128)(2,1)S(1)}, u32[]{:S(2)}, u32[]{:S(2)}) collective-permute-start(bf16[512,128]{1,0:T(8,128)(2,1)S(1)} %get-tuple-element.34.rest_1_), channel_id=1, source_target_pairs={{0,3},{1,0},{2,1},{3,2},{4,7},{5,4},{6,5},{7,6},{8,11},{9,8},{10,9... | collective-permute-start | bytes 393224 | tf_op jit(solution)/shard_map/ppermute | solution.py:221
  8.1 7.3 %collective-permute-start.5 = (bf16[512,128]{1,0:T(8,128)(2,1)S(1)}, bf16[512,128]{1,0:T(8,128)(2,1)S(1)}, u32[]{:S(2)}, u32[]{:S(2)}) collective-permute-start(bf16[512,128]{1,0:T(8,128)(2,1)S(1)} %get-tuple-element.33.rest_0_), channel_id=1, source_target_pairs={{0,3},{1,0},{2,1},{3,2},{4,7},{5,4},{6,5},{7,6},{8,11},{9,8},{10,9... | collective-permute-start | bytes 393224 | tf_op jit(solution)/shard_map/ppermute | solution.py:221
  9.5 6.0 %collective-permute-start.1 = (bf16[512,128]{1,0:T(8,128)(2,1)S(1)}, bf16[512,128]{1,0:T(8,128)(2,1)S(1)}, u32[]{:S(2)}, u32[]{:S(2)}) collective-permute-start(bf16[512,128]{1,0:T(8,128)(2,1)S(1)} %get-tuple-element.34.rest_1_), channel_id=1, source_target_pairs={{0,1},{1,2},{2,3},{3,0},{4,5},{5,6},{6,7},{7,4},{8,9},{9,10},{10,1... | collective-permute-start | bytes 393224 | tf_op jit(solution)/shard_map/ppermute | solution.py:221
  11.2 6.5 %collective-permute-start.2 = (bf16[512,128]{1,0:T(8,128)(2,1)S(1)}, bf16[512,128]{1,0:T(8,128)(2,1)S(1)}, u32[]{:S(2)}, u32[]{:S(2)}) collective-permute-start(bf16[512,128]{1,0:T(8,128)(2,1)S(1)} %collective-permute-done.rest_2_), channel_id=1, source_target_pairs={{0,1},{1,2},{2,3},{3,0},{4,5},{5,6},{6,7},{7,4},{8,9},{9,10},{10,1... | collective-permute-start | bytes 393224 | tf_op jit(solution)/shard_map/ppermute | solution.py:221
  11.2 6.5 %collective-permute-start.4 = (bf16[512,128]{1,0:T(8,128)(2,1)S(1)}, bf16[512,128]{1,0:T(8,128)(2,1)S(1)}, u32[]{:S(2)}, u32[]{:S(2)}) collective-permute-start(bf16[512,128]{1,0:T(8,128)(2,1)S(1)} %collective-permute-done.3.rest_7_), channel_id=1, source_target_pairs={{0,3},{1,0},{2,1},{3,2},{4,7},{5,4},{6,5},{7,6},{8,11},{9,8},{10,9... | collective-permute-start | bytes 393224 | tf_op jit(solution)/shard_map/ppermute | solution.py:221
  22.3 4.2 %collective-permute-start.6 = (bf16[16,80,128]{2,1,0:T(8,128)(2,1)S(1)}, bf16[16,80,128]{2,1,0:T(8,128)(2,1)S(1)}, u32[]{:S(2)}, u32[]{:S(2)}) collective-permute-start(bf16[16,80,128]{2,1,0:T(8,128)(2,1)S(1)} %get-tuple-element.36), channel_id=1, source_target_pairs={{0,4},{4,0},{8,12},{12,8},{16,20},{20,16},{24,28},{28,24},{32,36},... | collective-permute-start | bytes 983048 | tf_op jit(solution)/shard_map/ppermute | solution.py:225
  58.6 9.4 %collective-permute-start.10 = (bf16[512,128]{1,0:T(8,128)(2,1)S(1)}, bf16[512,128]{1,0:T(8,128)(2,1)S(1)}, u32[]{:S(2)}, u32[]{:S(2)}) collective-permute-start(bf16[512,128]{1,0:T(8,128)(2,1)S(1)} %get-tuple-element.38.rest_0_.first_ref), channel_id=1, source_target_pairs={{0,3},{1,0},{2,1},{3,2},{4,7},{5,4},{6,5},{7,6},{8,11},{9,8},{10,9... | collective-permute-start | bytes 393224 | tf_op jit(solution)/shard_map/ppermute | solution.py:221
  62.3 6.0 %collective-permute-start.9 = (bf16[512,128]{1,0:T(8,128)(2,1)S(1)}, bf16[512,128]{1,0:T(8,128)(2,1)S(1)}, u32[]{:S(2)}, u32[]{:S(2)}) collective-permute-start(bf16[512,128]{1,0:T(8,128)(2,1)S(1)} %get-tuple-element.38.rest_0_.first_ref), channel_id=1, source_target_pairs={{0,2},{1,3},{2,0},{3,1},{4,6},{5,7},{6,4},{7,5},{8,10},{9,11},{10,... | collective-permute-start | bytes 393224 | tf_op jit(solution)/shard_map/ppermute | solution.py:221
  62.3 9.1 %collective-permute-start.8 = (bf16[512,128]{1,0:T(8,128)(2,1)S(1)}, bf16[512,128]{1,0:T(8,128)(2,1)S(1)}, u32[]{:S(2)}, u32[]{:S(2)}) collective-permute-start(bf16[512,128]{1,0:T(8,128)(2,1)S(1)} %get-tuple-element.38.rest_0_.first_ref), channel_id=1, source_target_pairs={{0,1},{1,2},{2,3},{3,0},{4,5},{5,6},{6,7},{7,4},{8,9},{9,10},{10,1... | collective-permute-start | bytes 393224 | tf_op jit(solution)/shard_map/ppermute | solution.py:221
  72.7 11.8 %collective-permute-start.11 = (bf16[2,512,128]{2,1,0:T(8,128)(2,1)S(1)}, bf16[2,512,128]{2,1,0:T(8,128)(2,1)S(1)}, u32[]{:S(2)}, u32[]{:S(2)}) collective-permute-start(bf16[2,512,128]{2,1,0:T(8,128)(2,1)S(1)} %get-tuple-element.41), channel_id=1, source_target_pairs={{0,4},{1,5},{2,6},{3,7}} | collective-permute-start | bytes 786440 | tf_op jit(solution)/shard_map/ppermute | solution.py:213
  74.0 6.3 %collective-permute-start.14 = (bf16[512,128]{1,0:T(8,128)(2,1)S(1)}, bf16[512,128]{1,0:T(8,128)(2,1)S(1)}, u32[]{:S(2)}, u32[]{:S(2)}) collective-permute-start(bf16[512,128]{1,0:T(8,128)(2,1)S(1)} %get-tuple-element.42.rest_4_), channel_id=1, source_target_pairs={{0,7},{1,4},{2,5},{3,6}} | collective-permute-start | bytes 393224 | tf_op jit(solution)/shard_map/ppermute | solution.py:213
  75.3 7.8 %collective-permute-start.13 = (bf16[512,128]{1,0:T(8,128)(2,1)S(1)}, bf16[512,128]{1,0:T(8,128)(2,1)S(1)}, u32[]{:S(2)}, u32[]{:S(2)}) collective-permute-start(bf16[512,128]{1,0:T(8,128)(2,1)S(1)} %get-tuple-element.42.rest_4_), channel_id=1, source_target_pairs={{0,6},{1,7},{2,4},{3,5}} | collective-permute-start | bytes 393224 | tf_op jit(solution)/shard_map/ppermute | solution.py:213
  76.6 7.9 %collective-permute-start.12 = (bf16[512,128]{1,0:T(8,128)(2,1)S(1)}, bf16[512,128]{1,0:T(8,128)(2,1)S(1)}, u32[]{:S(2)}, u32[]{:S(2)}) collective-permute-start(bf16[512,128]{1,0:T(8,128)(2,1)S(1)} %get-tuple-element.42.rest_4_), channel_id=1, source_target_pairs={{0,5},{1,6},{2,7},{3,4}} | collective-permute-start | bytes 393224 | tf_op jit(solution)/shard_map/ppermute | solution.py:213
  86.8 11.6 %collective-permute-start.18 = (bf16[2,512,128]{2,1,0:T(8,128)(2,1)S(1)}, bf16[2,512,128]{2,1,0:T(8,128)(2,1)S(1)}, u32[]{:S(2)}, u32[]{:S(2)}) collective-permute-start(bf16[2,512,128]{2,1,0:T(8,128)(2,1)S(1)} %get-tuple-element.49), channel_id=1, source_target_pairs={{4,8},{5,9},{6,10},{7,11}} | collective-permute-start | bytes 786440 | tf_op jit(solution)/shard_map/ppermute | solution.py:213
  88.9 9.6 %collective-permute-start.22 = (bf16[2,512,128]{2,1,0:T(8,128)(2,1)S(1)}, bf16[2,512,128]{2,1,0:T(8,128)(2,1)S(1)}, u32[]{:S(2)}, u32[]{:S(2)}) collective-permute-start(bf16[2,512,128]{2,1,0:T(8,128)(2,1)S(1)} %later_0.1), channel_id=1, source_target_pairs={{0,8},{1,9},{2,10},{3,11}} | collective-permute-start | bytes 786440 | tf_op jit(solution)/shard_map/ppermute | solution.py:213
  89.6 6.0 %collective-permute-start.21 = (bf16[512,128]{1,0:T(8,128)(2,1)S(1)}, bf16[512,128]{1,0:T(8,128)(2,1)S(1)}, u32[]{:S(2)}, u32[]{:S(2)}) collective-permute-start(bf16[512,128]{1,0:T(8,128)(2,1)S(1)} %get-tuple-element.50), channel_id=1, source_target_pairs={{4,11},{5,8},{6,9},{7,10}} | collective-permute-start | bytes 393224 | tf_op jit(solution)/shard_map/ppermute | solution.py:213
  90.9 6.1 %collective-permute-start.20 = (bf16[512,128]{1,0:T(8,128)(2,1)S(1)}, bf16[512,128]{1,0:T(8,128)(2,1)S(1)}, u32[]{:S(2)}, u32[]{:S(2)}) collective-permute-start(bf16[512,128]{1,0:T(8,128)(2,1)S(1)} %get-tuple-element.50), channel_id=1, source_target_pairs={{4,10},{5,11},{6,8},{7,9}} | collective-permute-start | bytes 393224 | tf_op jit(solution)/shard_map/ppermute | solution.py:213
  92.2 6.2 %collective-permute-start.19 = (bf16[512,128]{1,0:T(8,128)(2,1)S(1)}, bf16[512,128]{1,0:T(8,128)(2,1)S(1)}, u32[]{:S(2)}, u32[]{:S(2)}) collective-permute-start(bf16[512,128]{1,0:T(8,128)(2,1)S(1)} %get-tuple-element.50), channel_id=1, source_target_pairs={{4,9},{5,10},{6,11},{7,8}} | collective-permute-start | bytes 393224 | tf_op jit(solution)/shard_map/ppermute | solution.py:213
  99.5 17.5 %collective-permute-start.26 = (bf16[2,512,128]{2,1,0:T(8,128)(2,1)S(1)}, bf16[2,512,128]{2,1,0:T(8,128)(2,1)S(1)}, u32[]{:S(2)}, u32[]{:S(2)}) collective-permute-start(bf16[2,512,128]{2,1,0:T(8,128)(2,1)S(1)} %get-tuple-element.59), channel_id=1, source_target_pairs={{8,12},{9,13},{10,14},{11,15}} | collective-permute-start | bytes 786440 | tf_op jit(solution)/shard_map/ppermute | solution.py:213
  103.7 4.0 %collective-permute-start.28 = (bf16[512,128]{1,0:T(8,128)(2,1)S(1)}, bf16[512,128]{1,0:T(8,128)(2,1)S(1)}, u32[]{:S(2)}, u32[]{:S(2)}) collective-permute-start(bf16[512,128]{1,0:T(8,128)(2,1)S(1)} %get-tuple-element.57.rest_4_), channel_id=1, source_target_pairs={{8,14},{9,15},{10,12},{11,13}} | collective-permute-start | bytes 393224 | tf_op jit(solution)/shard_map/ppermute | solution.py:213
  104.4 12.6 %collective-permute-start.27 = (bf16[512,128]{1,0:T(8,128)(2,1)S(1)}, bf16[512,128]{1,0:T(8,128)(2,1)S(1)}, u32[]{:S(2)}, u32[]{:S(2)}) collective-permute-start(bf16[512,128]{1,0:T(8,128)(2,1)S(1)} %get-tuple-element.57.rest_4_), channel_id=1, source_target_pairs={{8,13},{9,14},{10,15},{11,12}} | collective-permute-start | bytes 393224 | tf_op jit(solution)/shard_map/ppermute | solution.py:213
  105.1 14.3 %collective-permute-start.17 = (bf16[512,128]{1,0:T(8,128)(2,1)S(1)}, bf16[512,128]{1,0:T(8,128)(2,1)S(1)}, u32[]{:S(2)}, u32[]{:S(2)}) collective-permute-start(bf16[512,128]{1,0:T(8,128)(2,1)S(1)} %get-tuple-element.48.value_ref), channel_id=1, source_target_pairs={{0,16},{1,17},{2,18},{3,19},{4,20},{5,21},{6,22},{7,23}} | collective-permute-start | bytes 393224 | tf_op jit(solution)/shard_map/ppermute | solution.py:213
  106.4 13.0 %collective-permute-start.16 = (bf16[512,128]{1,0:T(8,128)(2,1)S(1)}, bf16[512,128]{1,0:T(8,128)(2,1)S(1)}, u32[]{:S(2)}, u32[]{:S(2)}) collective-permute-start(bf16[512,128]{1,0:T(8,128)(2,1)S(1)} %get-tuple-element.48.value_ref), channel_id=1, source_target_pairs={{0,24},{1,25},{2,26},{3,27},{4,28},{5,29},{6,30},{7,31}} | collective-permute-start | bytes 393224 | tf_op jit(solution)/shard_map/ppermute | solution.py:213
  107.7 12.1 %collective-permute-start.15 = (bf16[512,128]{1,0:T(8,128)(2,1)S(1)}, bf16[512,128]{1,0:T(8,128)(2,1)S(1)}, u32[]{:S(2)}, u32[]{:S(2)}) collective-permute-start(bf16[512,128]{1,0:T(8,128)(2,1)S(1)} %get-tuple-element.48.value_ref), channel_id=1, source_target_pairs={{0,8},{1,9},{2,10},{3,11},{4,12},{5,13},{6,14},{7,15}} | collective-permute-start | bytes 393224 | tf_op jit(solution)/shard_map/ppermute | solution.py:213
  118.7 6.3 %collective-permute-start.33 = (bf16[512,128]{1,0:T(8,128)(2,1)S(1)}, bf16[512,128]{1,0:T(8,128)(2,1)S(1)}, u32[]{:S(2)}, u32[]{:S(2)}) collective-permute-start(bf16[512,128]{1,0:T(8,128)(2,1)S(1)} %get-tuple-element.61.value_ref), channel_id=1, source_target_pairs={{8,24},{9,25},{10,26},{11,27},{12,28},{13,29},{14,30},{15,31}} | collective-permute-start | bytes 393224 | tf_op jit(solution)/shard_map/ppermute | solution.py:213
  120.4 7.1 %collective-permute-start.32 = (bf16[512,128]{1,0:T(8,128)(2,1)S(1)}, bf16[512,128]{1,0:T(8,128)(2,1)S(1)}, u32[]{:S(2)}, u32[]{:S(2)}) collective-permute-start(bf16[512,128]{1,0:T(8,128)(2,1)S(1)} %get-tuple-element.61.value_ref), channel_id=1, source_target_pairs={{8,0},{9,1},{10,2},{11,3},{12,4},{13,5},{14,6},{15,7}} | collective-permute-start | bytes 393224 | tf_op jit(solution)/shard_map/ppermute | solution.py:213
  121.7 5.8 %collective-permute-start.31 = (bf16[512,128]{1,0:T(8,128)(2,1)S(1)}, bf16[512,128]{1,0:T(8,128)(2,1)S(1)}, u32[]{:S(2)}, u32[]{:S(2)}) collective-permute-start(bf16[512,128]{1,0:T(8,128)(2,1)S(1)} %get-tuple-element.61.value_ref), channel_id=1, source_target_pairs={{8,16},{9,17},{10,18},{11,19},{12,20},{13,21},{14,22},{15,23}} | collective-permute-start | bytes 393224 | tf_op jit(solution)/shard_map/ppermute | solution.py:213
  122.4 8.4 %collective-permute-start.25 = (bf16[512,128]{1,0:T(8,128)(2,1)S(1)}, bf16[512,128]{1,0:T(8,128)(2,1)S(1)}, u32[]{:S(2)}, u32[]{:S(2)}) collective-permute-start(bf16[512,128]{1,0:T(8,128)(2,1)S(1)} %picked.2.rest_0_), channel_id=1, source_target_pairs={{0,64},{1,65},{2,66},{3,67},{4,68},{5,69},{6,70},{7,71},{8,72},{9,... | collective-permute-start | bytes 393224 | tf_op jit(solution)/shard_map/ppermute | solution.py:213
  123.7 8.4 %collective-permute-start.24 = (bf16[512,128]{1,0:T(8,128)(2,1)S(1)}, bf16[512,128]{1,0:T(8,128)(2,1)S(1)}, u32[]{:S(2)}, u32[]{:S(2)}) collective-permute-start(bf16[512,128]{1,0:T(8,128)(2,1)S(1)} %picked.2.rest_0_), channel_id=1, source_target_pairs={{0,96},{1,97},{2,98},{3,99},{4,100},{5,101},{6,102},{7,103},{8,104... | collective-permute-start | bytes 393224 | tf_op jit(solution)/shard_map/ppermute | solution.py:213
  125.0 7.1 %collective-permute-start.23 = (bf16[512,128]{1,0:T(8,128)(2,1)S(1)}, bf16[512,128]{1,0:T(8,128)(2,1)S(1)}, u32[]{:S(2)}, u32[]{:S(2)}) collective-permute-start(bf16[512,128]{1,0:T(8,128)(2,1)S(1)} %picked.2.rest_0_), channel_id=1, source_target_pairs={{0,32},{1,33},{2,34},{3,35},{4,36},{5,37},{6,38},{7,39},{8,40},{9,... | collective-permute-start | bytes 393224 | tf_op jit(solution)/shard_map/ppermute | solution.py:213
  130.8 4.1 %collective-permute-start.34 = (bf16[512,128]{1,0:T(8,128)(2,1)S(1)}, bf16[512,128]{1,0:T(8,128)(2,1)S(1)}, u32[]{:S(2)}, u32[]{:S(2)}) collective-permute-start(bf16[512,128]{1,0:T(8,128)(2,1)S(1)} %picked.3.rest_4_), channel_id=1, source_target_pairs={{0,32},{1,33},{2,34},{3,35},{4,36},{5,37},{6,38},{7,39},{8,40},{9,... | collective-permute-start | bytes 393224 | tf_op jit(solution)/shard_map/ppermute | solution.py:213
  (7 other events, 56.3 us)

commit v10 on v9

--- a/solution.py
+++ b/solution.py
@@ -337,17 +337,20 @@
     x2, packed, mixed12, kept = solve(1, pieces, [x1], ("value", "packed", "mixed", "kept"))
     pieces = onward(2, x2, packed)
     mixed12 = spread_x(mixed12, 0)
-    mixed12 = pick(column(0, 0, 0), table, mixed12[0], mixed12[1:])
     carried = to_column(carried, 0, 2)
     pieces, kept = after((pieces, kept))
     p41 = products(1, (4,), kept)
     x3, packed = solve(2, pieces, [carried], ("value", "packed"))
     pieces = onward(3, x3, packed)
-    spread12 = spread_y(after((mixed12, x3))[0])
     p41 = to_column(p41, 1, 3)
     x4, mixed34 = solve(3, pieces, [x3, p41], ("value", "mixed"))
     mixed34 = spread_x(mixed34, 1)
-    spread34 = spread_y(pick(column(1, 0, 0), table, mixed34[0], mixed34[1:]))
+
+    mixed34 = pick(column(1, 0, 0), table, mixed34[0], mixed34[1:])
+    mixed12 = pick(column(0, 0, 0), table, mixed12[0], mixed12[1:])
+    mixed12, mixed34 = after((mixed12, mixed34))
+    spread34 = spread_y(mixed34)
+    spread12 = spread_y(mixed12)
     spreads = spread12 + spread34
     mine = call(
         functools.partial(merge_kernel, levels), "merged", two, [SMEM] + [VMEM] * len(spreads), (table, *spreads)

time: 140 us -> 145 us (1.036)
  waiting for transfers between devices: 32 us -> 36.5 us
    ppermute x26, waiting for transfers between devices: 15.9 us -> 20.5 us  [send(): return lax.ppermute(value, AXES, pairs)]
  transfers between devices with their start and end apart: 38 -> 38, of which waited for: 18 -> 18; matrix products, arithmetic and copies ran while one was open for 1% -> 1% of each run, Pallas kernels for 4% -> 3%
where the time goes in v10:
time: 145 us; the launch traced here: 144 us
  starting transfers between devices  57.4 us (40%)
  waiting for transfers between devices  36.5 us (25%)
  blocking collectives  27.7 us (19%)
  Pallas kernels  20 us (14%)
    ppermute x26, starting transfers between devices, send(): return lax.ppermute(value, AXES, pairs)  36.1 us
    all_to_all x2, blocking collectives, over_plane(): lax.all_to_all(value, 'col', 0, 0, axis_index_groups=groups, tiled=True)  27.7 us
    ppermute x26, waiting for transfers between devices, send(): return lax.ppermute(value, AXES, pairs)  20.5 us
    pallas_call x15, Pallas kernels, call(): pl.pallas_call(body, out_shape=outs, in_specs=in_specs, out_specs=out_spe...  20 us
    ppermute x9, starting transfers between devices, to_row(): return lax.ppermute(value, 'row', [(z, (z + step) % NZ) for z in range(NZ)])  14.6 us
    ppermute x9, waiting for transfers between devices, to_row(): return lax.ppermute(value, 'row', [(z, (z + step) % NZ) for z in range(NZ)])  12.3 us
    ppermute x3, starting transfers between devices, other_core(): return lax.ppermute(value, 'col', [(c, c ^ 1) for c in range(NX * NY * 2)])  6.7 us
    ppermute x3, waiting for transfers between devices, other_core(): return lax.ppermute(value, 'col', [(c, c ^ 1) for c in range(NX * NY * 2)])  3.67 us
  transfers between devices with their start and end apart: 38, of which 18 were waited for; matrix products, arithmetic and copies ran while one was open for 1% of the time, Pallas kernels for 3%

profile of v10, /device:TPU:1, one launch (start us, length us, event | category | flops | bytes accessed | tf_op | source)
XLA Modules:
  0.0 144.2 jit_solution(15220165335844121298)
XLA Ops:
  0.6 2.7 %base_solve.1 = (f32[2,512,128]{2,1,0:T(8,128)}, bf16[512,128]{1,0:T(8,128)(2,1)S(1)}, bf16[512,128]{1,0:T(8,128)(2,1)S(1)}) custom-call(bf16[2,512,512]{2,1,0:T(8,128)(2,1)} %inverse_ref.1, f32[2,512,128]{2,1,0:T(8,128)} %rhs_ref.1), custom_call_target="tpu_custom_call" | custom-call | flops 134217728 | bytes 1835008 | tf_op jit(solution)/shard_map/base_solve/pallas_call | solution.py:32
  3.3 2.5 %collective-permute-start = (bf16[512,128]{1,0:T(8,128)(2,1)S(1)}, bf16[512,128]{1,0:T(8,128)(2,1)S(1)}, u32[]{:S(2)}, u32[]{:S(2)}) collective-permute-start(bf16[512,128]{1,0:T(8,128)(2,1)S(1)} %get-tuple-element.34.rest_0_), channel_id=1, source_target_pairs={{0,1},{1,2},{2,3},{3,0},{4,5},{5,6},{6,7},{7,4},{8,9},{9,10},{10,1... | collective-permute-start | bytes 393224 | tf_op jit(solution)/shard_map/ppermute | solution.py:221
  5.9 2.2 %collective-permute-start.3 = (bf16[512,128]{1,0:T(8,128)(2,1)S(1)}, bf16[512,128]{1,0:T(8,128)(2,1)S(1)}, u32[]{:S(2)}, u32[]{:S(2)}) collective-permute-start(bf16[512,128]{1,0:T(8,128)(2,1)S(1)} %get-tuple-element.35.rest_1_), channel_id=1, source_target_pairs={{0,3},{1,0},{2,1},{3,2},{4,7},{5,4},{6,5},{7,6},{8,11},{9,8},{10,9... | collective-permute-start | bytes 393224 | tf_op jit(solution)/shard_map/ppermute | solution.py:221
  8.1 1.4 collective-permute-start.5
  9.6 1.6 %collective-permute-done.rest_2_ = bf16[512,128]{1,0:T(8,128)(2,1)S(1)} collective-permute-done((bf16[512,128]{1,0:T(8,128)(2,1)S(1)}, bf16[512,128]{1,0:T(8,128)(2,1)S(1)}, u32[]{:S(2)}, u32[]{:S(2)}) %collective-permute-start) | collective-permute-done | bytes 131104 | tf_op jit(solution)/shard_map/ppermute | solution.py:221
  11.2 2.7 %collective-permute-start.4 = (bf16[512,128]{1,0:T(8,128)(2,1)S(1)}, bf16[512,128]{1,0:T(8,128)(2,1)S(1)}, u32[]{:S(2)}, u32[]{:S(2)}) collective-permute-start(bf16[512,128]{1,0:T(8,128)(2,1)S(1)} %collective-permute-done.3.rest_7_), channel_id=1, source_target_pairs={{0,3},{1,0},{2,1},{3,2},{4,7},{5,4},{6,5},{7,6},{8,11},{9,8},{10,9... | collective-permute-start | bytes 393224 | tf_op jit(solution)/shard_map/ppermute | solution.py:221
  15.4 2.3 %collective-permute-done.2.rest_4_ = bf16[512,128]{1,0:T(8,128)(2,1)S(1)} collective-permute-done((bf16[512,128]{1,0:T(8,128)(2,1)S(1)}, bf16[512,128]{1,0:T(8,128)(2,1)S(1)}, u32[]{:S(2)}, u32[]{:S(2)}) %collective-permute-start.2) | collective-permute-done | bytes 131104 | tf_op jit(solution)/shard_map/ppermute | solution.py:221
  17.7 3.9 %base_products.1 = (f32[16,80,128]{2,1,0:T(8,128)S(1)}, bf16[16,80,128]{2,1,0:T(8,128)(2,1)S(1)}, bf16[30,512,512]{2,1,0:T(8,128)(2,1)S(1)}, bf16[5,512,512]{2,1,0:T(8,128)(2,1)S(1)}) custom-call(s32[6,7]{1,0:T(8,128)S(1)} %pad_add_fusion.table, bf16[5,6,512,512]{3,2,1,0:T(8,128)(2,1)} %factor_ref.1, bf16[5,512,512]{2,1,0:T(8,128)(2,1)} %bitcast.11, ...), custom_call_target="tpu_custom_call" | custom-call | flops 1006632960 | bytes 15728640 | tf_op jit(solution)/shard_map/base_products/pallas_call | solution.py:32
  21.7 3.3 %collective-permute-start.6 = (bf16[16,80,128]{2,1,0:T(8,128)(2,1)S(1)}, bf16[16,80,128]{2,1,0:T(8,128)(2,1)S(1)}, u32[]{:S(2)}, u32[]{:S(2)}) collective-permute-start(bf16[16,80,128]{2,1,0:T(8,128)(2,1)S(1)} %get-tuple-element.37), channel_id=1, source_target_pairs={{0,4},{4,0},{8,12},{12,8},{16,20},{20,16},{24,28},{28,24},{32,36},... | collective-permute-start | bytes 983048 | tf_op jit(solution)/shard_map/ppermute | solution.py:225
  26.3 17.0 %all_to_all.10.in_ref = bf16[16,80,128]{2,1,0:T(8,128)(2,1)S(1)} all-to-all(bf16[16,80,128]{2,1,0:T(8,128)(2,1)S(1)} %pair_sums.1), channel_id=1, replica_groups={{0,8,16,24,32,40,48,56,64,72,80,88,96,104,112,120},{4,12,20,28,36,44,52..., dimensions={0} | all-to-all | bytes 655360 | tf_op jit(solution)/shard_map/all_to_all | solution.py:230
  43.3 10.7 %all_to_all.11.half_ref = bf16[16,80,128]{2,1,0:T(8,128)(2,1)S(1)} all-to-all(bf16[16,80,128]{2,1,0:T(8,128)(2,1)S(1)} %sum_shares.1), channel_id=1, replica_groups={{0,8,16,24,32,40,48,56,64,72,80,88,96,104,112,120},{4,12,20,28,36,44,52..., dimensions={0} | all-to-all | bytes 655360 | tf_op jit(solution)/shard_map/all_to_all | solution.py:230
  54.1 2.7 %collective-permute-start.7 = (bf16[16,80,128]{2,1,0:T(8,128)(2,1)S(1)}, bf16[16,80,128]{2,1,0:T(8,128)(2,1)S(1)}, u32[]{:S(2)}, u32[]{:S(2)}) collective-permute-start(bf16[16,80,128]{2,1,0:T(8,128)(2,1)S(1)} %all_to_all.11.half_ref), channel_id=1, source_target_pairs={{0,4},{4,0},{8,12},{12,8},{16,20},{20,16},{24,28},{28,24},{32,36},... | collective-permute-start | bytes 983048 | tf_op jit(solution)/shard_map/ppermute | solution.py:225
  59.1 4.3 %collective-permute-start.10 = (bf16[512,128]{1,0:T(8,128)(2,1)S(1)}, bf16[512,128]{1,0:T(8,128)(2,1)S(1)}, u32[]{:S(2)}, u32[]{:S(2)}) collective-permute-start(bf16[512,128]{1,0:T(8,128)(2,1)S(1)} %get-tuple-element.39.rest_0_.first_ref), channel_id=1, source_target_pairs={{0,3},{1,0},{2,1},{3,2},{4,7},{5,4},{6,5},{7,6},{8,11},{9,8},{10,9... | collective-permute-start | bytes 393224 | tf_op jit(solution)/shard_map/ppermute | solution.py:221
  64.8 3.8 %collective-permute-done.10.rest_3_ = bf16[512,128]{1,0:T(8,128)(2,1)S(1)} collective-permute-done((bf16[512,128]{1,0:T(8,128)(2,1)S(1)}, bf16[512,128]{1,0:T(8,128)(2,1)S(1)}, u32[]{:S(2)}, u32[]{:S(2)}) %collective-permute-start.10) | collective-permute-done | bytes 131104 | tf_op jit(solution)/shard_map/ppermute | solution.py:221
  69.3 3.8 %collective-permute-done.8.rest_1_ = bf16[512,128]{1,0:T(8,128)(2,1)S(1)} collective-permute-done((bf16[512,128]{1,0:T(8,128)(2,1)S(1)}, bf16[512,128]{1,0:T(8,128)(2,1)S(1)}, u32[]{:S(2)}, u32[]{:S(2)}) %collective-permute-start.8) | collective-permute-done | bytes 131104 | tf_op jit(solution)/shard_map/ppermute | solution.py:221
  79.6 2.4 %collective-permute-done.14.rest_3_ = bf16[512,128]{1,0:T(8,128)(2,1)S(1)} collective-permute-done((bf16[512,128]{1,0:T(8,128)(2,1)S(1)}, bf16[512,128]{1,0:T(8,128)(2,1)S(1)}, u32[]{:S(2)}, u32[]{:S(2)}) %collective-permute-start.14) | collective-permute-done | bytes 131104 | tf_op jit(solution)/shard_map/ppermute | solution.py:213
  82.0 2.8 %collective-permute-done.13.rest_2_ = bf16[512,128]{1,0:T(8,128)(2,1)S(1)} collective-permute-done((bf16[512,128]{1,0:T(8,128)(2,1)S(1)}, bf16[512,128]{1,0:T(8,128)(2,1)S(1)}, u32[]{:S(2)}, u32[]{:S(2)}) %collective-permute-start.13) | collective-permute-done | bytes 131104 | tf_op jit(solution)/shard_map/ppermute | solution.py:213
  84.8 1.4 collective-permute-done.12.rest_1_
  86.2 2.3 %solve_2.1 = (bf16[512,128]{1,0:T(8,128)(2,1)S(1)}, bf16[2,512,128]{2,1,0:T(8,128)(2,1)S(1)}, bf16[512,128]{1,0:T(8,128)(2,1)S(1)}, bf16[4,512,128]{2,1,0:T(8,128)(2,1)S(1)}) custom-call(s32[6,7]{1,0:T(8,128)S(1)} %pad_add_fusion.table, bf16[30,512,512]{2,1,0:T(8,128)(2,1)S(1)} %get-tuple-element.40.held_ref, ...), custom_call_target="tpu_custom_call" | custom-call | flops 335544320 | tf_op jit(solution)/shard_map/solve_2/pallas_call | solution.py:32
  88.5 1.3 collective-permute-start.18
  92.6 1.3 collective-permute-start.20
  93.9 1.3 collective-permute-start.19
  95.2 2.1 %collective-permute-done.21.rest_3_ = bf16[512,128]{1,0:T(8,128)(2,1)S(1)} collective-permute-done((bf16[512,128]{1,0:T(8,128)(2,1)S(1)}, bf16[512,128]{1,0:T(8,128)(2,1)S(1)}, u32[]{:S(2)}, u32[]{:S(2)}) %collective-permute-start.21) | collective-permute-done | bytes 131104 | tf_op jit(solution)/shard_map/ppermute | solution.py:213
  97.3 1.4 collective-permute-done.20.rest_2_
  98.7 1.4 collective-permute-done.19.rest_1_
  103.2 1.3 collective-permute-start.27
  109.5 7.9 %collective-permute-start.15 = (bf16[512,128]{1,0:T(8,128)(2,1)S(1)}, bf16[512,128]{1,0:T(8,128)(2,1)S(1)}, u32[]{:S(2)}, u32[]{:S(2)}) collective-permute-start(bf16[512,128]{1,0:T(8,128)(2,1)S(1)} %get-tuple-element.49.value_ref), channel_id=1, source_target_pairs={{0,8},{1,9},{2,10},{3,11},{4,12},{5,13},{6,14},{7,15}} | collective-permute-start | bytes 393224 | tf_op jit(solution)/shard_map/ppermute | solution.py:213
  117.4 1.7 %solve_4.1 = (bf16[512,128]{1,0:T(8,128)(2,1)}, bf16[512,128]{1,0:T(8,128)(2,1)S(1)}) custom-call(s32[6,7]{1,0:T(8,128)S(1)} %pad_add_fusion.table, bf16[30,512,512]{2,1,0:T(8,128)(2,1)S(1)} %get-tuple-element.40.held_ref, f32[4,512,128]{2,1,0:T(8,128)S(1)} %get-tuple-element.41.ahead_ref, bf16[5,512,512]{2,1,0:T(8,128)(2,1)S(1)} %get-tuple-element.38.inverse_ref, ...), custom_call_target="tpu_custom_call" | custom-call | flops 335544320 | tf_op jit(solution)/shard_map/solve_4/pallas_call | solution.py:32
  122.4 3.9 %collective-permute-done.29.rest_1_ = bf16[512,128]{1,0:T(8,128)(2,1)S(1)} collective-permute-done((bf16[512,128]{1,0:T(8,128)(2,1)S(1)}, bf16[512,128]{1,0:T(8,128)(2,1)S(1)}, u32[]{:S(2)}, u32[]{:S(2)}) %collective-permute-start.29) | collective-permute-done | bytes 131104 | tf_op jit(solution)/shard_map/ppermute | solution.py:213
  134.9 2.1 %collective-permute-done.36.rest_7_ = bf16[512,128]{1,0:T(8,128)(2,1)S(1)} collective-permute-done((bf16[512,128]{1,0:T(8,128)(2,1)S(1)}, bf16[512,128]{1,0:T(8,128)(2,1)S(1)}, u32[]{:S(2)}, u32[]{:S(2)}) %collective-permute-start.36) | collective-permute-done | bytes 131104 | tf_op jit(solution)/shard_map/ppermute | solution.py:213
  137.0 2.8 %collective-permute-done.34.rest_5_ = bf16[512,128]{1,0:T(8,128)(2,1)S(1)} collective-permute-done((bf16[512,128]{1,0:T(8,128)(2,1)S(1)}, bf16[512,128]{1,0:T(8,128)(2,1)S(1)}, u32[]{:S(2)}, u32[]{:S(2)}) %collective-permute-start.34) | collective-permute-done | bytes 131104 | tf_op jit(solution)/shard_map/ppermute | solution.py:213
  142.4 1.8 %final.1 = f32[5,512,128]{2,1,0:T(8,128)} custom-call(s32[6,7]{1,0:T(8,128)S(1)} %pad_add_fusion.table, bf16[512,128]{1,0:T(8,128)(2,1)S(1)} %get-tuple-element.39.rest_0_.first_ref, bf16[2,512,128]{2,1,0:T(8,128)(2,1)S(1)} %merged.1.mine_ref, bf16[2,512,128]{2,1,0:T(8,128)(2,1)S(1)} %collective-permute-done.37.other_ref), custom_call_target="tpu_custom_call" | custom-call | tf_op jit(solution)/shard_map/final/pallas_call | solution.py:32
  (67 shorter events, 38.9 us)
Async XLA Ops:
  3.3 7.9 %collective-permute-start = (bf16[512,128]{1,0:T(8,128)(2,1)S(1)}, bf16[512,128]{1,0:T(8,128)(2,1)S(1)}, u32[]{:S(2)}, u32[]{:S(2)}) collective-permute-start(bf16[512,128]{1,0:T(8,128)(2,1)S(1)} %get-tuple-element.34.rest_0_), channel_id=1, source_target_pairs={{0,1},{1,2},{2,3},{3,0},{4,5},{5,6},{6,7},{7,4},{8,9},{9,10},{10,1... | collective-permute-start | bytes 393224 | tf_op jit(solution)/shard_map/ppermute | solution.py:221
  5.9 5.3 %collective-permute-start.3 = (bf16[512,128]{1,0:T(8,128)(2,1)S(1)}, bf16[512,128]{1,0:T(8,128)(2,1)S(1)}, u32[]{:S(2)}, u32[]{:S(2)}) collective-permute-start(bf16[512,128]{1,0:T(8,128)(2,1)S(1)} %get-tuple-element.35.rest_1_), channel_id=1, source_target_pairs={{0,3},{1,0},{2,1},{3,2},{4,7},{5,4},{6,5},{7,6},{8,11},{9,8},{10,9... | collective-permute-start | bytes 393224 | tf_op jit(solution)/shard_map/ppermute | solution.py:221
  8.1 7.3 %collective-permute-start.5 = (bf16[512,128]{1,0:T(8,128)(2,1)S(1)}, bf16[512,128]{1,0:T(8,128)(2,1)S(1)}, u32[]{:S(2)}, u32[]{:S(2)}) collective-permute-start(bf16[512,128]{1,0:T(8,128)(2,1)S(1)} %get-tuple-element.34.rest_0_), channel_id=1, source_target_pairs={{0,3},{1,0},{2,1},{3,2},{4,7},{5,4},{6,5},{7,6},{8,11},{9,8},{10,9... | collective-permute-start | bytes 393224 | tf_op jit(solution)/shard_map/ppermute | solution.py:221
  9.5 6.0 %collective-permute-start.1 = (bf16[512,128]{1,0:T(8,128)(2,1)S(1)}, bf16[512,128]{1,0:T(8,128)(2,1)S(1)}, u32[]{:S(2)}, u32[]{:S(2)}) collective-permute-start(bf16[512,128]{1,0:T(8,128)(2,1)S(1)} %get-tuple-element.35.rest_1_), channel_id=1, source_target_pairs={{0,1},{1,2},{2,3},{3,0},{4,5},{5,6},{6,7},{7,4},{8,9},{9,10},{10,1... | collective-permute-start | bytes 393224 | tf_op jit(solution)/shard_map/ppermute | solution.py:221
  11.2 6.5 %collective-permute-start.2 = (bf16[512,128]{1,0:T(8,128)(2,1)S(1)}, bf16[512,128]{1,0:T(8,128)(2,1)S(1)}, u32[]{:S(2)}, u32[]{:S(2)}) collective-permute-start(bf16[512,128]{1,0:T(8,128)(2,1)S(1)} %collective-permute-done.rest_2_), channel_id=1, source_target_pairs={{0,1},{1,2},{2,3},{3,0},{4,5},{5,6},{6,7},{7,4},{8,9},{9,10},{10,1... | collective-permute-start | bytes 393224 | tf_op jit(solution)/shard_map/ppermute | solution.py:221
  11.2 6.5 %collective-permute-start.4 = (bf16[512,128]{1,0:T(8,128)(2,1)S(1)}, bf16[512,128]{1,0:T(8,128)(2,1)S(1)}, u32[]{:S(2)}, u32[]{:S(2)}) collective-permute-start(bf16[512,128]{1,0:T(8,128)(2,1)S(1)} %collective-permute-done.3.rest_7_), channel_id=1, source_target_pairs={{0,3},{1,0},{2,1},{3,2},{4,7},{5,4},{6,5},{7,6},{8,11},{9,8},{10,9... | collective-permute-start | bytes 393224 | tf_op jit(solution)/shard_map/ppermute | solution.py:221
  21.7 4.6 %collective-permute-start.6 = (bf16[16,80,128]{2,1,0:T(8,128)(2,1)S(1)}, bf16[16,80,128]{2,1,0:T(8,128)(2,1)S(1)}, u32[]{:S(2)}, u32[]{:S(2)}) collective-permute-start(bf16[16,80,128]{2,1,0:T(8,128)(2,1)S(1)} %get-tuple-element.37), channel_id=1, source_target_pairs={{0,4},{4,0},{8,12},{12,8},{16,20},{20,16},{24,28},{28,24},{32,36},... | collective-permute-start | bytes 983048 | tf_op jit(solution)/shard_map/ppermute | solution.py:225
  59.1 9.5 %collective-permute-start.10 = (bf16[512,128]{1,0:T(8,128)(2,1)S(1)}, bf16[512,128]{1,0:T(8,128)(2,1)S(1)}, u32[]{:S(2)}, u32[]{:S(2)}) collective-permute-start(bf16[512,128]{1,0:T(8,128)(2,1)S(1)} %get-tuple-element.39.rest_0_.first_ref), channel_id=1, source_target_pairs={{0,3},{1,0},{2,1},{3,2},{4,7},{5,4},{6,5},{7,6},{8,11},{9,8},{10,9... | collective-permute-start | bytes 393224 | tf_op jit(solution)/shard_map/ppermute | solution.py:221
  63.4 5.9 %collective-permute-start.9 = (bf16[512,128]{1,0:T(8,128)(2,1)S(1)}, bf16[512,128]{1,0:T(8,128)(2,1)S(1)}, u32[]{:S(2)}, u32[]{:S(2)}) collective-permute-start(bf16[512,128]{1,0:T(8,128)(2,1)S(1)} %get-tuple-element.39.rest_0_.first_ref), channel_id=1, source_target_pairs={{0,2},{1,3},{2,0},{3,1},{4,6},{5,7},{6,4},{7,5},{8,10},{9,11},{10,... | collective-permute-start | bytes 393224 | tf_op jit(solution)/shard_map/ppermute | solution.py:221
  64.0 9.1 %collective-permute-start.8 = (bf16[512,128]{1,0:T(8,128)(2,1)S(1)}, bf16[512,128]{1,0:T(8,128)(2,1)S(1)}, u32[]{:S(2)}, u32[]{:S(2)}) collective-permute-start(bf16[512,128]{1,0:T(8,128)(2,1)S(1)} %get-tuple-element.39.rest_0_.first_ref), channel_id=1, source_target_pairs={{0,1},{1,2},{2,3},{3,0},{4,5},{5,6},{6,7},{7,4},{8,9},{9,10},{10,1... | collective-permute-start | bytes 393224 | tf_op jit(solution)/shard_map/ppermute | solution.py:221
  74.4 11.8 %collective-permute-start.11 = (bf16[2,512,128]{2,1,0:T(8,128)(2,1)S(1)}, bf16[2,512,128]{2,1,0:T(8,128)(2,1)S(1)}, u32[]{:S(2)}, u32[]{:S(2)}) collective-permute-start(bf16[2,512,128]{2,1,0:T(8,128)(2,1)S(1)} %get-tuple-element.42), channel_id=1, source_target_pairs={{0,4},{1,5},{2,6},{3,7}} | collective-permute-start | bytes 786440 | tf_op jit(solution)/shard_map/ppermute | solution.py:213
  75.7 6.3 %collective-permute-start.14 = (bf16[512,128]{1,0:T(8,128)(2,1)S(1)}, bf16[512,128]{1,0:T(8,128)(2,1)S(1)}, u32[]{:S(2)}, u32[]{:S(2)}) collective-permute-start(bf16[512,128]{1,0:T(8,128)(2,1)S(1)} %get-tuple-element.43.rest_4_), channel_id=1, source_target_pairs={{0,7},{1,4},{2,5},{3,6}} | collective-permute-start | bytes 393224 | tf_op jit(solution)/shard_map/ppermute | solution.py:213
  77.0 7.8 %collective-permute-start.13 = (bf16[512,128]{1,0:T(8,128)(2,1)S(1)}, bf16[512,128]{1,0:T(8,128)(2,1)S(1)}, u32[]{:S(2)}, u32[]{:S(2)}) collective-permute-start(bf16[512,128]{1,0:T(8,128)(2,1)S(1)} %get-tuple-element.43.rest_4_), channel_id=1, source_target_pairs={{0,6},{1,7},{2,4},{3,5}} | collective-permute-start | bytes 393224 | tf_op jit(solution)/shard_map/ppermute | solution.py:213
  78.3 7.9 %collective-permute-start.12 = (bf16[512,128]{1,0:T(8,128)(2,1)S(1)}, bf16[512,128]{1,0:T(8,128)(2,1)S(1)}, u32[]{:S(2)}, u32[]{:S(2)}) collective-permute-start(bf16[512,128]{1,0:T(8,128)(2,1)S(1)} %get-tuple-element.43.rest_4_), channel_id=1, source_target_pairs={{0,5},{1,6},{2,7},{3,4}} | collective-permute-start | bytes 393224 | tf_op jit(solution)/shard_map/ppermute | solution.py:213
  88.5 11.6 %collective-permute-start.18 = (bf16[2,512,128]{2,1,0:T(8,128)(2,1)S(1)}, bf16[2,512,128]{2,1,0:T(8,128)(2,1)S(1)}, u32[]{:S(2)}, u32[]{:S(2)}) collective-permute-start(bf16[2,512,128]{2,1,0:T(8,128)(2,1)S(1)} %get-tuple-element.50), channel_id=1, source_target_pairs={{4,8},{5,9},{6,10},{7,11}} | collective-permute-start | bytes 786440 | tf_op jit(solution)/shard_map/ppermute | solution.py:213
  90.6 9.5 %collective-permute-start.22 = (bf16[2,512,128]{2,1,0:T(8,128)(2,1)S(1)}, bf16[2,512,128]{2,1,0:T(8,128)(2,1)S(1)}, u32[]{:S(2)}, u32[]{:S(2)}) collective-permute-start(bf16[2,512,128]{2,1,0:T(8,128)(2,1)S(1)} %later_0.1), channel_id=1, source_target_pairs={{0,8},{1,9},{2,10},{3,11}} | collective-permute-start | bytes 786440 | tf_op jit(solution)/shard_map/ppermute | solution.py:213
  91.3 6.0 %collective-permute-start.21 = (bf16[512,128]{1,0:T(8,128)(2,1)S(1)}, bf16[512,128]{1,0:T(8,128)(2,1)S(1)}, u32[]{:S(2)}, u32[]{:S(2)}) collective-permute-start(bf16[512,128]{1,0:T(8,128)(2,1)S(1)} %get-tuple-element.51), channel_id=1, source_target_pairs={{4,11},{5,8},{6,9},{7,10}} | collective-permute-start | bytes 393224 | tf_op jit(solution)/shard_map/ppermute | solution.py:213
  92.6 6.1 %collective-permute-start.20 = (bf16[512,128]{1,0:T(8,128)(2,1)S(1)}, bf16[512,128]{1,0:T(8,128)(2,1)S(1)}, u32[]{:S(2)}, u32[]{:S(2)}) collective-permute-start(bf16[512,128]{1,0:T(8,128)(2,1)S(1)} %get-tuple-element.51), channel_id=1, source_target_pairs={{4,10},{5,11},{6,8},{7,9}} | collective-permute-start | bytes 393224 | tf_op jit(solution)/shard_map/ppermute | solution.py:213
  93.9 6.2 %collective-permute-start.19 = (bf16[512,128]{1,0:T(8,128)(2,1)S(1)}, bf16[512,128]{1,0:T(8,128)(2,1)S(1)}, u32[]{:S(2)}, u32[]{:S(2)}) collective-permute-start(bf16[512,128]{1,0:T(8,128)(2,1)S(1)} %get-tuple-element.51), channel_id=1, source_target_pairs={{4,9},{5,10},{6,11},{7,8}} | collective-permute-start | bytes 393224 | tf_op jit(solution)/shard_map/ppermute | solution.py:213
  101.2 16.2 %collective-permute-start.23 = (bf16[2,512,128]{2,1,0:T(8,128)(2,1)S(1)}, bf16[2,512,128]{2,1,0:T(8,128)(2,1)S(1)}, u32[]{:S(2)}, u32[]{:S(2)}) collective-permute-start(bf16[2,512,128]{2,1,0:T(8,128)(2,1)S(1)} %get-tuple-element.58), channel_id=1, source_target_pairs={{8,12},{9,13},{10,14},{11,15}} | collective-permute-start | bytes 786440 | tf_op jit(solution)/shard_map/ppermute | solution.py:213
  106.1 11.3 %collective-permute-start.24 = (bf16[512,128]{1,0:T(8,128)(2,1)S(1)}, bf16[512,128]{1,0:T(8,128)(2,1)S(1)}, u32[]{:S(2)}, u32[]{:S(2)}) collective-permute-start(bf16[512,128]{1,0:T(8,128)(2,1)S(1)} %get-tuple-element.59.rest_4_), channel_id=1, source_target_pairs={{8,13},{9,14},{10,15},{11,12}} | collective-permute-start | bytes 393224 | tf_op jit(solution)/shard_map/ppermute | solution.py:213
  106.9 14.2 %collective-permute-start.17 = (bf16[512,128]{1,0:T(8,128)(2,1)S(1)}, bf16[512,128]{1,0:T(8,128)(2,1)S(1)}, u32[]{:S(2)}, u32[]{:S(2)}) collective-permute-start(bf16[512,128]{1,0:T(8,128)(2,1)S(1)} %get-tuple-element.49.value_ref), channel_id=1, source_target_pairs={{0,16},{1,17},{2,18},{3,19},{4,20},{5,21},{6,22},{7,23}} | collective-permute-start | bytes 393224 | tf_op jit(solution)/shard_map/ppermute | solution.py:213
  108.2 13.6 %collective-permute-start.16 = (bf16[512,128]{1,0:T(8,128)(2,1)S(1)}, bf16[512,128]{1,0:T(8,128)(2,1)S(1)}, u32[]{:S(2)}, u32[]{:S(2)}) collective-permute-start(bf16[512,128]{1,0:T(8,128)(2,1)S(1)} %get-tuple-element.49.value_ref), channel_id=1, source_target_pairs={{0,24},{1,25},{2,26},{3,27},{4,28},{5,29},{6,30},{7,31}} | collective-permute-start | bytes 393224 | tf_op jit(solution)/shard_map/ppermute | solution.py:213
  109.5 12.3 %collective-permute-start.15 = (bf16[512,128]{1,0:T(8,128)(2,1)S(1)}, bf16[512,128]{1,0:T(8,128)(2,1)S(1)}, u32[]{:S(2)}, u32[]{:S(2)}) collective-permute-start(bf16[512,128]{1,0:T(8,128)(2,1)S(1)} %get-tuple-element.49.value_ref), channel_id=1, source_target_pairs={{0,8},{1,9},{2,10},{3,11},{4,12},{5,13},{6,14},{7,15}} | collective-permute-start | bytes 393224 | tf_op jit(solution)/shard_map/ppermute | solution.py:213
  119.7 6.6 %collective-permute-start.29 = (bf16[512,128]{1,0:T(8,128)(2,1)S(1)}, bf16[512,128]{1,0:T(8,128)(2,1)S(1)}, u32[]{:S(2)}, u32[]{:S(2)}) collective-permute-start(bf16[512,128]{1,0:T(8,128)(2,1)S(1)} %get-tuple-element.61.value_ref), channel_id=1, source_target_pairs={{8,0},{9,1},{10,2},{11,3},{12,4},{13,5},{14,6},{15,7}} | collective-permute-start | bytes 393224 | tf_op jit(solution)/shard_map/ppermute | solution.py:213
  121.1 5.3 %collective-permute-start.28 = (bf16[512,128]{1,0:T(8,128)(2,1)S(1)}, bf16[512,128]{1,0:T(8,128)(2,1)S(1)}, u32[]{:S(2)}, u32[]{:S(2)}) collective-permute-start(bf16[512,128]{1,0:T(8,128)(2,1)S(1)} %get-tuple-element.61.value_ref), channel_id=1, source_target_pairs={{8,16},{9,17},{10,18},{11,19},{12,20},{13,21},{14,22},{15,23}} | collective-permute-start | bytes 393224 | tf_op jit(solution)/shard_map/ppermute | solution.py:213
  127.0 6.5 %collective-permute-start.33 = (bf16[512,128]{1,0:T(8,128)(2,1)S(1)}, bf16[512,128]{1,0:T(8,128)(2,1)S(1)}, u32[]{:S(2)}, u32[]{:S(2)}) collective-permute-start(bf16[512,128]{1,0:T(8,128)(2,1)S(1)} %picked.2.rest_0_), channel_id=1, source_target_pairs={{0,64},{1,65},{2,66},{3,67},{4,68},{5,69},{6,70},{7,71},{8,72},{9,... | collective-permute-start | bytes 393224 | tf_op jit(solution)/shard_map/ppermute | solution.py:213
  128.3 6.5 %collective-permute-start.32 = (bf16[512,128]{1,0:T(8,128)(2,1)S(1)}, bf16[512,128]{1,0:T(8,128)(2,1)S(1)}, u32[]{:S(2)}, u32[]{:S(2)}) collective-permute-start(bf16[512,128]{1,0:T(8,128)(2,1)S(1)} %picked.2.rest_0_), channel_id=1, source_target_pairs={{0,96},{1,97},{2,98},{3,99},{4,100},{5,101},{6,102},{7,103},{8,104... | collective-permute-start | bytes 393224 | tf_op jit(solution)/shard_map/ppermute | solution.py:213
  129.6 5.2 %collective-permute-start.31 = (bf16[512,128]{1,0:T(8,128)(2,1)S(1)}, bf16[512,128]{1,0:T(8,128)(2,1)S(1)}, u32[]{:S(2)}, u32[]{:S(2)}) collective-permute-start(bf16[512,128]{1,0:T(8,128)(2,1)S(1)} %picked.2.rest_0_), channel_id=1, source_target_pairs={{0,32},{1,33},{2,34},{3,35},{4,36},{5,37},{6,38},{7,39},{8,40},{9,... | collective-permute-start | bytes 393224 | tf_op jit(solution)/shard_map/ppermute | solution.py:213
  130.9 6.1 %collective-permute-start.36 = (bf16[512,128]{1,0:T(8,128)(2,1)S(1)}, bf16[512,128]{1,0:T(8,128)(2,1)S(1)}, u32[]{:S(2)}, u32[]{:S(2)}) collective-permute-start(bf16[512,128]{1,0:T(8,128)(2,1)S(1)} %picked.3.rest_4_), channel_id=1, source_target_pairs={{0,64},{1,65},{2,66},{3,67},{4,68},{5,69},{6,70},{7,71},{8,72},{9,... | collective-permute-start | bytes 393224 | tf_op jit(solution)/shard_map/ppermute | solution.py:213
  132.2 4.8 %collective-permute-start.35 = (bf16[512,128]{1,0:T(8,128)(2,1)S(1)}, bf16[512,128]{1,0:T(8,128)(2,1)S(1)}, u32[]{:S(2)}, u32[]{:S(2)}) collective-permute-start(bf16[512,128]{1,0:T(8,128)(2,1)S(1)} %picked.3.rest_4_), channel_id=1, source_target_pairs={{0,96},{1,97},{2,98},{3,99},{4,100},{5,101},{6,102},{7,103},{8,104... | collective-permute-start | bytes 393224 | tf_op jit(solution)/shard_map/ppermute | solution.py:213
  133.5 6.3 %collective-permute-start.34 = (bf16[512,128]{1,0:T(8,128)(2,1)S(1)}, bf16[512,128]{1,0:T(8,128)(2,1)S(1)}, u32[]{:S(2)}, u32[]{:S(2)}) collective-permute-start(bf16[512,128]{1,0:T(8,128)(2,1)S(1)} %picked.3.rest_4_), channel_id=1, source_target_pairs={{0,32},{1,33},{2,34},{3,35},{4,36},{5,37},{6,38},{7,39},{8,40},{9,... | collective-permute-start | bytes 393224 | tf_op jit(solution)/shard_map/ppermute | solution.py:213
  (7 other events, 56.9 us)

commit v11 on v9

--- a/solution.py
+++ b/solution.py
@@ -28,13 +28,14 @@
     return jnp.dot(a, b, preferred_element_type=F32)
 
 
-def call(body, name, outs, in_specs, args, scratch=(), flops=0, nbytes=0, out_specs=None):
+def call(body, name, outs, in_specs, args, scratch=(), flops=0, nbytes=0, out_specs=None, aliases=None):
     return pl.pallas_call(
         body,
         out_shape=outs,
         in_specs=in_specs,
         out_specs=out_specs or jax.tree.map(lambda _: VMEM, outs),
         scratch_shapes=list(scratch),
+        input_output_aliases=aliases or {},
         compiler_params=pltpu.CompilerParams(vmem_limit_bytes=24 * 1024 * 1024),
         cost_estimate=pl.CostEstimate(flops=flops, bytes_accessed=nbytes, transcendentals=0),
         name=name,
@@ -193,13 +194,22 @@
         out_ref[i] = jnp.where(table[levels, 2] < 2 * NX, value[...], came)
 
 
-def final_kernel(table, first_ref, mine_ref, other_ref, out_ref):
-    levels = out_ref.shape[0]
+def output_kernel(start, levels, table, *rest):
+    refs, (out_ref, value, sem) = rest[:-3], rest[-3:]
+    mine_ref, other_ref = refs[-2:]
     core = table[levels, 1]
-    out_ref[0] = first_ref[...].astype(F32)
-    for level in range(1, levels):
-        i, side = (level - 1) // 2, (level - 1) % 2
-        out_ref[level] = jnp.where(core == side, mine_ref[i], other_ref[i]).astype(F32)
+    count = value.shape[0]
+    if count == 3:
+        value[0] = refs[0][...].astype(F32)
+    for side in BOTH:
+        value[count - 2 + side] = jnp.where(core == side, mine_ref[0], other_ref[0]).astype(F32)
+    copy = pltpu.make_async_copy(value, out_ref.at[pl.ds(start, count)], sem)
+    copy.start()
+    copy.wait()
+
+
+def rest_kernel(levels, table, out_before, mine_ref, other_ref, out_ref, value, sem):
+    output_kernel(levels - 2, levels, table, mine_ref, other_ref, out_ref, value, sem)
 
 
 def pick(column_of, table, value, got):
@@ -348,13 +358,23 @@
     x4, mixed34 = solve(3, pieces, [x3, p41], ("value", "mixed"))
     mixed34 = spread_x(mixed34, 1)
     spread34 = spread_y(pick(column(1, 0, 0), table, mixed34[0], mixed34[1:]))
-    spreads = spread12 + spread34
-    mine = call(
-        functools.partial(merge_kernel, levels), "merged", two, [SMEM] + [VMEM] * len(spreads), (table, *spreads)
-    )
+    def merged(spread, name):
+        single = jax.ShapeDtypeStruct((1, size, samples), BF16)
+        value = call(
+            functools.partial(merge_kernel, levels), name, single, [SMEM] + [VMEM] * len(spread), (table, *spread)
+        )
+        return value, other_core(value)
+
+    shape = jax.ShapeDtypeStruct((levels, size, samples), F32)
     out = call(
-        final_kernel, "final", jax.ShapeDtypeStruct((levels, size, samples), F32), [SMEM] + [VMEM] * 3,
-        (table, first, mine, other_core(mine)),
+        functools.partial(output_kernel, 0, levels), "output_first", shape, [SMEM] + [VMEM] * 3,
+        (table, first, *merged(spread12, "merged_first")), out_specs=HBM,
+        scratch=[pltpu.VMEM((3, size, samples), F32), pltpu.SemaphoreType.DMA],
+    )
+    out = call(
+        functools.partial(rest_kernel, levels), "output_rest", shape, [SMEM, HBM] + [VMEM] * 2,
+        (table, out, *merged(spread34, "merged_rest")), out_specs=HBM, aliases={1: 0},
+        scratch=[pltpu.VMEM((2, size, samples), F32), pltpu.SemaphoreType.DMA],
     )
     return base_solution, out[:, None]
 

time: 140 us -> 141 us (level); the launches traced: 140 us -> 139 us
  blocking collectives: 26.9 us -> 32.3 us
  starting transfers between devices: 57.6 us -> 53.3 us
  waiting for transfers between devices: 32 us -> 29.4 us
    all_to_all x2, blocking collectives: 26.9 us -> 32.3 us  [over_plane(): lax.all_to_all(value, 'col', 0, 0, axis_index_groups=groups, tiled=True)]
    ppermute x9, starting transfers between devices: 13.3 us -> 10.4 us  [to_row(): return lax.ppermute(value, 'row', [(z, (z + step) % NZ) for z in range(NZ)])]
    ppermute x3 -> x4, waiting for transfers between devices: 3.67 us -> 2.52 us  [other_core(): return lax.ppermute(value, 'col', [(c, c ^ 1) for c in range(NX * NY * 2)])]
    pallas_call x15 -> x17, Pallas kernels: 20.6 us -> 21.3 us  [call(): pl.pallas_call(body, out_shape=outs, in_specs=in_specs, out_specs=out_spe...]
    ppermute x3 -> x4, starting transfers between devices: 6.82 us -> 6.49 us  [other_core(): return lax.ppermute(value, 'col', [(c, c ^ 1) for c in range(NX * NY * 2)])]
  transfers between devices with their start and end apart: 38 -> 39, of which waited for: 18 -> 16; matrix products, arithmetic and copies ran while one was open for 1% -> 1% of each run, Pallas kernels for 4% -> 5%
where the time goes in v11:
time: 141 us; the launch traced here: 139 us
  starting transfers between devices  53.3 us (38%)
  blocking collectives  32.3 us (23%)
  waiting for transfers between devices  29.4 us (21%)
  Pallas kernels  21.3 us (15%)
    ppermute x26, starting transfers between devices, send(): return lax.ppermute(value, AXES, pairs)  36.4 us
    all_to_all x2, blocking collectives, over_plane(): lax.all_to_all(value, 'col', 0, 0, axis_index_groups=groups, tiled=True)  32.3 us
    pallas_call x17, Pallas kernels, call(): pl.pallas_call(body, out_shape=outs, in_specs=in_specs, out_specs=out_spe...  21.3 us
    ppermute x26, waiting for transfers between devices, send(): return lax.ppermute(value, AXES, pairs)  14.6 us
    ppermute x9, waiting for transfers between devices, to_row(): return lax.ppermute(value, 'row', [(z, (z + step) % NZ) for z in range(NZ)])  12.3 us
    ppermute x9, starting transfers between devices, to_row(): return lax.ppermute(value, 'row', [(z, (z + step) % NZ) for z in range(NZ)])  10.4 us
    ppermute x4, starting transfers between devices, other_core(): return lax.ppermute(value, 'col', [(c, c ^ 1) for c in range(NX * NY * 2)])  6.49 us
  transfers between devices with their start and end apart: 39, of which 16 were waited for; matrix products, arithmetic and copies ran while one was open for 1% of the time, Pallas kernels for 5%

profile of v11, /device:TPU:1, one launch (start us, length us, event | category | flops | bytes accessed | tf_op | source)
XLA Modules:
  0.0 139.1 jit_solution(7489133865836629536)
XLA Ops:
  0.6 2.7 %base_solve.1 = (f32[2,512,128]{2,1,0:T(8,128)}, bf16[512,128]{1,0:T(8,128)(2,1)S(1)}, bf16[512,128]{1,0:T(8,128)(2,1)S(1)}) custom-call(bf16[2,512,512]{2,1,0:T(8,128)(2,1)} %inverse_ref.1, f32[2,512,128]{2,1,0:T(8,128)} %rhs_ref.1), custom_call_target="tpu_custom_call" | custom-call | flops 134217728 | bytes 1835008 | tf_op jit(solution)/shard_map/base_solve/pallas_call | solution.py:32
  3.3 2.5 %collective-permute-start = (bf16[512,128]{1,0:T(8,128)(2,1)S(1)}, bf16[512,128]{1,0:T(8,128)(2,1)S(1)}, u32[]{:S(2)}, u32[]{:S(2)}) collective-permute-start(bf16[512,128]{1,0:T(8,128)(2,1)S(1)} %get-tuple-element.33.rest_0_), channel_id=1, source_target_pairs={{0,1},{1,2},{2,3},{3,0},{4,5},{5,6},{6,7},{7,4},{8,9},{9,10},{10,1... | collective-permute-start | bytes 393224 | tf_op jit(solution)/shard_map/ppermute | solution.py:231
  5.9 2.2 %collective-permute-start.3 = (bf16[512,128]{1,0:T(8,128)(2,1)S(1)}, bf16[512,128]{1,0:T(8,128)(2,1)S(1)}, u32[]{:S(2)}, u32[]{:S(2)}) collective-permute-start(bf16[512,128]{1,0:T(8,128)(2,1)S(1)} %get-tuple-element.34.rest_1_), channel_id=1, source_target_pairs={{0,3},{1,0},{2,1},{3,2},{4,7},{5,4},{6,5},{7,6},{8,11},{9,8},{10,9... | collective-permute-start | bytes 393224 | tf_op jit(solution)/shard_map/ppermute | solution.py:231
  8.1 1.4 collective-permute-start.5
  9.6 1.6 %collective-permute-done.rest_2_ = bf16[512,128]{1,0:T(8,128)(2,1)S(1)} collective-permute-done((bf16[512,128]{1,0:T(8,128)(2,1)S(1)}, bf16[512,128]{1,0:T(8,128)(2,1)S(1)}, u32[]{:S(2)}, u32[]{:S(2)}) %collective-permute-start) | collective-permute-done | bytes 131104 | tf_op jit(solution)/shard_map/ppermute | solution.py:231
  11.2 2.7 %collective-permute-start.4 = (bf16[512,128]{1,0:T(8,128)(2,1)S(1)}, bf16[512,128]{1,0:T(8,128)(2,1)S(1)}, u32[]{:S(2)}, u32[]{:S(2)}) collective-permute-start(bf16[512,128]{1,0:T(8,128)(2,1)S(1)} %collective-permute-done.3.rest_7_), channel_id=1, source_target_pairs={{0,3},{1,0},{2,1},{3,2},{4,7},{5,4},{6,5},{7,6},{8,11},{9,8},{10,9... | collective-permute-start | bytes 393224 | tf_op jit(solution)/shard_map/ppermute | solution.py:231
  15.4 2.3 %collective-permute-done.2.rest_4_ = bf16[512,128]{1,0:T(8,128)(2,1)S(1)} collective-permute-done((bf16[512,128]{1,0:T(8,128)(2,1)S(1)}, bf16[512,128]{1,0:T(8,128)(2,1)S(1)}, u32[]{:S(2)}, u32[]{:S(2)}) %collective-permute-start.2) | collective-permute-done | bytes 131104 | tf_op jit(solution)/shard_map/ppermute | solution.py:231
  17.7 4.4 %base_products.1 = (f32[16,80,128]{2,1,0:T(8,128)S(1)}, bf16[16,80,128]{2,1,0:T(8,128)(2,1)S(1)}, bf16[30,512,512]{2,1,0:T(8,128)(2,1)S(1)}, bf16[5,512,512]{2,1,0:T(8,128)(2,1)S(1)}) custom-call(s32[6,7]{1,0:T(8,128)S(1)} %pad_add_fusion.table, bf16[5,6,512,512]{3,2,1,0:T(8,128)(2,1)} %factor_ref.1, bf16[5,512,512]{2,1,0:T(8,128)(2,1)} %bitcast.12, ...), custom_call_target="tpu_custom_call" | custom-call | flops 1006632960 | bytes 15728640 | tf_op jit(solution)/shard_map/base_products/pallas_call | solution.py:32
  22.1 1.8 %collective-permute-start.6 = (bf16[16,80,128]{2,1,0:T(8,128)(2,1)S(1)}, bf16[16,80,128]{2,1,0:T(8,128)(2,1)S(1)}, u32[]{:S(2)}, u32[]{:S(2)}) collective-permute-start(bf16[16,80,128]{2,1,0:T(8,128)(2,1)S(1)} %get-tuple-element.36), channel_id=1, source_target_pairs={{0,4},{4,0},{8,12},{12,8},{16,20},{20,16},{24,28},{28,24},{32,36},... | collective-permute-start | bytes 983048 | tf_op jit(solution)/shard_map/ppermute | solution.py:235
  25.3 21.6 %all_to_all.10.in_ref = bf16[16,80,128]{2,1,0:T(8,128)(2,1)S(1)} all-to-all(bf16[16,80,128]{2,1,0:T(8,128)(2,1)S(1)} %pair_sums.1), channel_id=1, replica_groups={{0,8,16,24,32,40,48,56,64,72,80,88,96,104,112,120},{4,12,20,28,36,44,52..., dimensions={0} | all-to-all | bytes 655360 | tf_op jit(solution)/shard_map/all_to_all | solution.py:240
  46.9 10.7 %all_to_all.11.half_ref = bf16[16,80,128]{2,1,0:T(8,128)(2,1)S(1)} all-to-all(bf16[16,80,128]{2,1,0:T(8,128)(2,1)S(1)} %sum_shares.1), channel_id=1, replica_groups={{0,8,16,24,32,40,48,56,64,72,80,88,96,104,112,120},{4,12,20,28,36,44,52..., dimensions={0} | all-to-all | bytes 655360 | tf_op jit(solution)/shard_map/all_to_all | solution.py:240
  57.6 2.7 %collective-permute-start.7 = (bf16[16,80,128]{2,1,0:T(8,128)(2,1)S(1)}, bf16[16,80,128]{2,1,0:T(8,128)(2,1)S(1)}, u32[]{:S(2)}, u32[]{:S(2)}) collective-permute-start(bf16[16,80,128]{2,1,0:T(8,128)(2,1)S(1)} %all_to_all.11.half_ref), channel_id=1, source_target_pairs={{0,4},{4,0},{8,12},{12,8},{16,20},{20,16},{24,28},{28,24},{32,36},... | collective-permute-start | bytes 983048 | tf_op jit(solution)/shard_map/ppermute | solution.py:235
  62.8 1.4 collective-permute-start.8
  64.1 3.2 %collective-permute-done.10.rest_3_ = bf16[512,128]{1,0:T(8,128)(2,1)S(1)} collective-permute-done((bf16[512,128]{1,0:T(8,128)(2,1)S(1)}, bf16[512,128]{1,0:T(8,128)(2,1)S(1)}, u32[]{:S(2)}, u32[]{:S(2)}) %collective-permute-start.10) | collective-permute-done | bytes 131104 | tf_op jit(solution)/shard_map/ppermute | solution.py:231
  67.4 1.6 %collective-permute-done.9.rest_2_ = bf16[512,128]{1,0:T(8,128)(2,1)S(1)} collective-permute-done((bf16[512,128]{1,0:T(8,128)(2,1)S(1)}, bf16[512,128]{1,0:T(8,128)(2,1)S(1)}, u32[]{:S(2)}, u32[]{:S(2)}) %collective-permute-start.9) | collective-permute-done | bytes 131104 | tf_op jit(solution)/shard_map/ppermute | solution.py:231
  69.0 3.5 %collective-permute-done.8.rest_1_ = bf16[512,128]{1,0:T(8,128)(2,1)S(1)} collective-permute-done((bf16[512,128]{1,0:T(8,128)(2,1)S(1)}, bf16[512,128]{1,0:T(8,128)(2,1)S(1)}, u32[]{:S(2)}, u32[]{:S(2)}) %collective-permute-start.8) | collective-permute-done | bytes 131104 | tf_op jit(solution)/shard_map/ppermute | solution.py:231
  79.0 2.4 %collective-permute-done.14.rest_3_ = bf16[512,128]{1,0:T(8,128)(2,1)S(1)} collective-permute-done((bf16[512,128]{1,0:T(8,128)(2,1)S(1)}, bf16[512,128]{1,0:T(8,128)(2,1)S(1)}, u32[]{:S(2)}, u32[]{:S(2)}) %collective-permute-start.14) | collective-permute-done | bytes 131104 | tf_op jit(solution)/shard_map/ppermute | solution.py:223
  81.4 2.8 %collective-permute-done.13.rest_2_ = bf16[512,128]{1,0:T(8,128)(2,1)S(1)} collective-permute-done((bf16[512,128]{1,0:T(8,128)(2,1)S(1)}, bf16[512,128]{1,0:T(8,128)(2,1)S(1)}, u32[]{:S(2)}, u32[]{:S(2)}) %collective-permute-start.13) | collective-permute-done | bytes 131104 | tf_op jit(solution)/shard_map/ppermute | solution.py:223
  84.2 1.4 collective-permute-done.12.rest_1_
  85.6 1.7 %solve_2.1 = (bf16[512,128]{1,0:T(8,128)(2,1)S(1)}, bf16[2,512,128]{2,1,0:T(8,128)(2,1)S(1)}, bf16[512,128]{1,0:T(8,128)(2,1)S(1)}, bf16[4,512,128]{2,1,0:T(8,128)(2,1)S(1)}) custom-call(s32[6,7]{1,0:T(8,128)S(1)} %pad_add_fusion.table, bf16[30,512,512]{2,1,0:T(8,128)(2,1)S(1)} %get-tuple-element.39.held_ref, ...), custom_call_target="tpu_custom_call" | custom-call | flops 335544320 | tf_op jit(solution)/shard_map/solve_2/pallas_call | solution.py:32
  87.3 1.3 collective-permute-start.18
  90.0 1.3 collective-permute-start.21
  91.3 1.3 collective-permute-start.20
  94.0 2.0 %collective-permute-done.21.rest_3_ = bf16[512,128]{1,0:T(8,128)(2,1)S(1)} collective-permute-done((bf16[512,128]{1,0:T(8,128)(2,1)S(1)}, bf16[512,128]{1,0:T(8,128)(2,1)S(1)}, u32[]{:S(2)}, u32[]{:S(2)}) %collective-permute-start.21) | collective-permute-done | bytes 131104 | tf_op jit(solution)/shard_map/ppermute | solution.py:223
  96.0 1.4 %collective-permute-done.20.rest_2_ = bf16[512,128]{1,0:T(8,128)(2,1)S(1)} collective-permute-done((bf16[512,128]{1,0:T(8,128)(2,1)S(1)}, bf16[512,128]{1,0:T(8,128)(2,1)S(1)}, u32[]{:S(2)}, u32[]{:S(2)}) %collective-permute-start.20) | collective-permute-done | bytes 131104 | tf_op jit(solution)/shard_map/ppermute | solution.py:223
  97.4 1.7 %collective-permute-done.19.rest_1_ = bf16[512,128]{1,0:T(8,128)(2,1)S(1)} collective-permute-done((bf16[512,128]{1,0:T(8,128)(2,1)S(1)}, bf16[512,128]{1,0:T(8,128)(2,1)S(1)}, u32[]{:S(2)}, u32[]{:S(2)}) %collective-permute-start.19) | collective-permute-done | bytes 131104 | tf_op jit(solution)/shard_map/ppermute | solution.py:223
  106.8 1.3 collective-permute-start.16
  108.1 8.1 %collective-permute-start.15 = (bf16[512,128]{1,0:T(8,128)(2,1)S(1)}, bf16[512,128]{1,0:T(8,128)(2,1)S(1)}, u32[]{:S(2)}, u32[]{:S(2)}) collective-permute-start(bf16[512,128]{1,0:T(8,128)(2,1)S(1)} %get-tuple-element.48.value_ref), channel_id=1, source_target_pairs={{0,8},{1,9},{2,10},{3,11},{4,12},{5,13},{6,14},{7,15}} | collective-permute-start | bytes 393224 | tf_op jit(solution)/shard_map/ppermute | solution.py:223
  116.2 1.7 %solve_4.1 = (bf16[512,128]{1,0:T(8,128)(2,1)}, bf16[512,128]{1,0:T(8,128)(2,1)S(1)}) custom-call(s32[6,7]{1,0:T(8,128)S(1)} %pad_add_fusion.table, bf16[30,512,512]{2,1,0:T(8,128)(2,1)S(1)} %get-tuple-element.39.held_ref, f32[4,512,128]{2,1,0:T(8,128)S(1)} %get-tuple-element.40.ahead_ref, bf16[5,512,512]{2,1,0:T(8,128)(2,1)S(1)} %get-tuple-element.37.inverse_ref, ...), custom_call_target="tpu_custom_call" | custom-call | flops 335544320 | tf_op jit(solution)/shard_map/solve_4/pallas_call | solution.py:32
  121.5 1.3 collective-permute-start.25
  135.9 1.6 %output_first.1.out_before = f32[5,512,128]{2,1,0:T(8,128)} custom-call(s32[6,7]{1,0:T(8,128)S(1)} %pad_add_fusion.table, bf16[512,128]{1,0:T(8,128)(2,1)S(1)} %get-tuple-element.38.rest_0_, bf16[1,512,128]{2,1,0:T(8,128)(2,1)S(1)} %merged_first.1.rest_1_, bf16[1,512,128]{2,1,0:T(8,128)(2,1)S(1)} %collective-permute-done.26.rest_2_), custom_call_target="tpu_custom_call" | custom-call | tf_op jit(solution)/shard_map/output_first/pallas_call | solution.py:32
  137.4 1.5 %output_rest.1 = f32[5,512,128]{2,1,0:T(8,128)} custom-call(s32[6,7]{1,0:T(8,128)S(1)} %pad_add_fusion.table, f32[5,512,128]{2,1,0:T(8,128)} %output_first.1.out_before, bf16[1,512,128]{2,1,0:T(8,128)(2,1)S(1)} %merged_rest.1.mine_ref, bf16[1,512,128]{2,1,0:T(8,128)(2,1)S(1)} %collective-permute-done.38.other_ref), custom_call_target="tpu_custom_call", output_to_operand_aliasing={{}: (1, {})} | custom-call | tf_op jit(solution)/shard_map/output_rest/pallas_call | solution.py:32
  (71 shorter events, 38.8 us)
Async XLA Ops:
  3.3 7.9 %collective-permute-start = (bf16[512,128]{1,0:T(8,128)(2,1)S(1)}, bf16[512,128]{1,0:T(8,128)(2,1)S(1)}, u32[]{:S(2)}, u32[]{:S(2)}) collective-permute-start(bf16[512,128]{1,0:T(8,128)(2,1)S(1)} %get-tuple-element.33.rest_0_), channel_id=1, source_target_pairs={{0,1},{1,2},{2,3},{3,0},{4,5},{5,6},{6,7},{7,4},{8,9},{9,10},{10,1... | collective-permute-start | bytes 393224 | tf_op jit(solution)/shard_map/ppermute | solution.py:231
  5.9 5.3 %collective-permute-start.3 = (bf16[512,128]{1,0:T(8,128)(2,1)S(1)}, bf16[512,128]{1,0:T(8,128)(2,1)S(1)}, u32[]{:S(2)}, u32[]{:S(2)}) collective-permute-start(bf16[512,128]{1,0:T(8,128)(2,1)S(1)} %get-tuple-element.34.rest_1_), channel_id=1, source_target_pairs={{0,3},{1,0},{2,1},{3,2},{4,7},{5,4},{6,5},{7,6},{8,11},{9,8},{10,9... | collective-permute-start | bytes 393224 | tf_op jit(solution)/shard_map/ppermute | solution.py:231
  8.1 7.3 %collective-permute-start.5 = (bf16[512,128]{1,0:T(8,128)(2,1)S(1)}, bf16[512,128]{1,0:T(8,128)(2,1)S(1)}, u32[]{:S(2)}, u32[]{:S(2)}) collective-permute-start(bf16[512,128]{1,0:T(8,128)(2,1)S(1)} %get-tuple-element.33.rest_0_), channel_id=1, source_target_pairs={{0,3},{1,0},{2,1},{3,2},{4,7},{5,4},{6,5},{7,6},{8,11},{9,8},{10,9... | collective-permute-start | bytes 393224 | tf_op jit(solution)/shard_map/ppermute | solution.py:231
  9.5 6.0 %collective-permute-start.1 = (bf16[512,128]{1,0:T(8,128)(2,1)S(1)}, bf16[512,128]{1,0:T(8,128)(2,1)S(1)}, u32[]{:S(2)}, u32[]{:S(2)}) collective-permute-start(bf16[512,128]{1,0:T(8,128)(2,1)S(1)} %get-tuple-element.34.rest_1_), channel_id=1, source_target_pairs={{0,1},{1,2},{2,3},{3,0},{4,5},{5,6},{6,7},{7,4},{8,9},{9,10},{10,1... | collective-permute-start | bytes 393224 | tf_op jit(solution)/shard_map/ppermute | solution.py:231
  11.2 6.5 %collective-permute-start.2 = (bf16[512,128]{1,0:T(8,128)(2,1)S(1)}, bf16[512,128]{1,0:T(8,128)(2,1)S(1)}, u32[]{:S(2)}, u32[]{:S(2)}) collective-permute-start(bf16[512,128]{1,0:T(8,128)(2,1)S(1)} %collective-permute-done.rest_2_), channel_id=1, source_target_pairs={{0,1},{1,2},{2,3},{3,0},{4,5},{5,6},{6,7},{7,4},{8,9},{9,10},{10,1... | collective-permute-start | bytes 393224 | tf_op jit(solution)/shard_map/ppermute | solution.py:231
  11.2 6.5 %collective-permute-start.4 = (bf16[512,128]{1,0:T(8,128)(2,1)S(1)}, bf16[512,128]{1,0:T(8,128)(2,1)S(1)}, u32[]{:S(2)}, u32[]{:S(2)}) collective-permute-start(bf16[512,128]{1,0:T(8,128)(2,1)S(1)} %collective-permute-done.3.rest_7_), channel_id=1, source_target_pairs={{0,3},{1,0},{2,1},{3,2},{4,7},{5,4},{6,5},{7,6},{8,11},{9,8},{10,9... | collective-permute-start | bytes 393224 | tf_op jit(solution)/shard_map/ppermute | solution.py:231
  62.6 4.8 %collective-permute-start.10 = (bf16[512,128]{1,0:T(8,128)(2,1)S(1)}, bf16[512,128]{1,0:T(8,128)(2,1)S(1)}, u32[]{:S(2)}, u32[]{:S(2)}) collective-permute-start(bf16[512,128]{1,0:T(8,128)(2,1)S(1)} %get-tuple-element.38.rest_0_), channel_id=1, source_target_pairs={{0,3},{1,0},{2,1},{3,2},{4,7},{5,4},{6,5},{7,6},{8,11},{9,8},{10,9... | collective-permute-start | bytes 393224 | tf_op jit(solution)/shard_map/ppermute | solution.py:231
  62.7 6.3 %collective-permute-start.9 = (bf16[512,128]{1,0:T(8,128)(2,1)S(1)}, bf16[512,128]{1,0:T(8,128)(2,1)S(1)}, u32[]{:S(2)}, u32[]{:S(2)}) collective-permute-start(bf16[512,128]{1,0:T(8,128)(2,1)S(1)} %get-tuple-element.38.rest_0_), channel_id=1, source_target_pairs={{0,2},{1,3},{2,0},{3,1},{4,6},{5,7},{6,4},{7,5},{8,10},{9,11},{10,... | collective-permute-start | bytes 393224 | tf_op jit(solution)/shard_map/ppermute | solution.py:231
  62.8 9.7 %collective-permute-start.8 = (bf16[512,128]{1,0:T(8,128)(2,1)S(1)}, bf16[512,128]{1,0:T(8,128)(2,1)S(1)}, u32[]{:S(2)}, u32[]{:S(2)}) collective-permute-start(bf16[512,128]{1,0:T(8,128)(2,1)S(1)} %get-tuple-element.38.rest_0_), channel_id=1, source_target_pairs={{0,1},{1,2},{2,3},{3,0},{4,5},{5,6},{6,7},{7,4},{8,9},{9,10},{10,1... | collective-permute-start | bytes 393224 | tf_op jit(solution)/shard_map/ppermute | solution.py:231
  73.8 11.8 %collective-permute-start.11 = (bf16[2,512,128]{2,1,0:T(8,128)(2,1)S(1)}, bf16[2,512,128]{2,1,0:T(8,128)(2,1)S(1)}, u32[]{:S(2)}, u32[]{:S(2)}) collective-permute-start(bf16[2,512,128]{2,1,0:T(8,128)(2,1)S(1)} %get-tuple-element.41), channel_id=1, source_target_pairs={{0,4},{1,5},{2,6},{3,7}} | collective-permute-start | bytes 786440 | tf_op jit(solution)/shard_map/ppermute | solution.py:223
  75.1 6.3 %collective-permute-start.14 = (bf16[512,128]{1,0:T(8,128)(2,1)S(1)}, bf16[512,128]{1,0:T(8,128)(2,1)S(1)}, u32[]{:S(2)}, u32[]{:S(2)}) collective-permute-start(bf16[512,128]{1,0:T(8,128)(2,1)S(1)} %get-tuple-element.42.rest_4_), channel_id=1, source_target_pairs={{0,7},{1,4},{2,5},{3,6}} | collective-permute-start | bytes 393224 | tf_op jit(solution)/shard_map/ppermute | solution.py:223
  76.4 7.8 %collective-permute-start.13 = (bf16[512,128]{1,0:T(8,128)(2,1)S(1)}, bf16[512,128]{1,0:T(8,128)(2,1)S(1)}, u32[]{:S(2)}, u32[]{:S(2)}) collective-permute-start(bf16[512,128]{1,0:T(8,128)(2,1)S(1)} %get-tuple-element.42.rest_4_), channel_id=1, source_target_pairs={{0,6},{1,7},{2,4},{3,5}} | collective-permute-start | bytes 393224 | tf_op jit(solution)/shard_map/ppermute | solution.py:223
  77.7 7.9 %collective-permute-start.12 = (bf16[512,128]{1,0:T(8,128)(2,1)S(1)}, bf16[512,128]{1,0:T(8,128)(2,1)S(1)}, u32[]{:S(2)}, u32[]{:S(2)}) collective-permute-start(bf16[512,128]{1,0:T(8,128)(2,1)S(1)} %get-tuple-element.42.rest_4_), channel_id=1, source_target_pairs={{0,5},{1,6},{2,7},{3,4}} | collective-permute-start | bytes 393224 | tf_op jit(solution)/shard_map/ppermute | solution.py:223
  87.3 11.8 %collective-permute-start.18 = (bf16[2,512,128]{2,1,0:T(8,128)(2,1)S(1)}, bf16[2,512,128]{2,1,0:T(8,128)(2,1)S(1)}, u32[]{:S(2)}, u32[]{:S(2)}) collective-permute-start(bf16[2,512,128]{2,1,0:T(8,128)(2,1)S(1)} %get-tuple-element.49), channel_id=1, source_target_pairs={{4,8},{5,9},{6,10},{7,11}} | collective-permute-start | bytes 786440 | tf_op jit(solution)/shard_map/ppermute | solution.py:223
  89.3 9.8 %collective-permute-start.22 = (bf16[2,512,128]{2,1,0:T(8,128)(2,1)S(1)}, bf16[2,512,128]{2,1,0:T(8,128)(2,1)S(1)}, u32[]{:S(2)}, u32[]{:S(2)}) collective-permute-start(bf16[2,512,128]{2,1,0:T(8,128)(2,1)S(1)} %later_0.1), channel_id=1, source_target_pairs={{0,8},{1,9},{2,10},{3,11}} | collective-permute-start | bytes 786440 | tf_op jit(solution)/shard_map/ppermute | solution.py:223
  90.0 5.9 %collective-permute-start.21 = (bf16[512,128]{1,0:T(8,128)(2,1)S(1)}, bf16[512,128]{1,0:T(8,128)(2,1)S(1)}, u32[]{:S(2)}, u32[]{:S(2)}) collective-permute-start(bf16[512,128]{1,0:T(8,128)(2,1)S(1)} %get-tuple-element.50), channel_id=1, source_target_pairs={{4,11},{5,8},{6,9},{7,10}} | collective-permute-start | bytes 393224 | tf_op jit(solution)/shard_map/ppermute | solution.py:223
  91.3 6.0 %collective-permute-start.20 = (bf16[512,128]{1,0:T(8,128)(2,1)S(1)}, bf16[512,128]{1,0:T(8,128)(2,1)S(1)}, u32[]{:S(2)}, u32[]{:S(2)}) collective-permute-start(bf16[512,128]{1,0:T(8,128)(2,1)S(1)} %get-tuple-element.50), channel_id=1, source_target_pairs={{4,10},{5,11},{6,8},{7,9}} | collective-permute-start | bytes 393224 | tf_op jit(solution)/shard_map/ppermute | solution.py:223
  92.6 6.5 %collective-permute-start.19 = (bf16[512,128]{1,0:T(8,128)(2,1)S(1)}, bf16[512,128]{1,0:T(8,128)(2,1)S(1)}, u32[]{:S(2)}, u32[]{:S(2)}) collective-permute-start(bf16[512,128]{1,0:T(8,128)(2,1)S(1)} %get-tuple-element.50), channel_id=1, source_target_pairs={{4,9},{5,10},{6,11},{7,8}} | collective-permute-start | bytes 393224 | tf_op jit(solution)/shard_map/ppermute | solution.py:223
  100.2 16.0 %collective-permute-start.27 = (bf16[2,512,128]{2,1,0:T(8,128)(2,1)S(1)}, bf16[2,512,128]{2,1,0:T(8,128)(2,1)S(1)}, u32[]{:S(2)}, u32[]{:S(2)}) collective-permute-start(bf16[2,512,128]{2,1,0:T(8,128)(2,1)S(1)} %get-tuple-element.59), channel_id=1, source_target_pairs={{8,12},{9,13},{10,14},{11,15}} | collective-permute-start | bytes 786440 | tf_op jit(solution)/shard_map/ppermute | solution.py:223
  104.8 11.4 %collective-permute-start.28 = (bf16[512,128]{1,0:T(8,128)(2,1)S(1)}, bf16[512,128]{1,0:T(8,128)(2,1)S(1)}, u32[]{:S(2)}, u32[]{:S(2)}) collective-permute-start(bf16[512,128]{1,0:T(8,128)(2,1)S(1)} %get-tuple-element.57.rest_4_), channel_id=1, source_target_pairs={{8,13},{9,14},{10,15},{11,12}} | collective-permute-start | bytes 393224 | tf_op jit(solution)/shard_map/ppermute | solution.py:223
  105.4 13.1 %collective-permute-start.17 = (bf16[512,128]{1,0:T(8,128)(2,1)S(1)}, bf16[512,128]{1,0:T(8,128)(2,1)S(1)}, u32[]{:S(2)}, u32[]{:S(2)}) collective-permute-start(bf16[512,128]{1,0:T(8,128)(2,1)S(1)} %get-tuple-element.48.value_ref), channel_id=1, source_target_pairs={{0,16},{1,17},{2,18},{3,19},{4,20},{5,21},{6,22},{7,23}} | collective-permute-start | bytes 393224 | tf_op jit(solution)/shard_map/ppermute | solution.py:223
  106.8 11.8 %collective-permute-start.16 = (bf16[512,128]{1,0:T(8,128)(2,1)S(1)}, bf16[512,128]{1,0:T(8,128)(2,1)S(1)}, u32[]{:S(2)}, u32[]{:S(2)}) collective-permute-start(bf16[512,128]{1,0:T(8,128)(2,1)S(1)} %get-tuple-element.48.value_ref), channel_id=1, source_target_pairs={{0,24},{1,25},{2,26},{3,27},{4,28},{5,29},{6,30},{7,31}} | collective-permute-start | bytes 393224 | tf_op jit(solution)/shard_map/ppermute | solution.py:223
  108.1 10.8 %collective-permute-start.15 = (bf16[512,128]{1,0:T(8,128)(2,1)S(1)}, bf16[512,128]{1,0:T(8,128)(2,1)S(1)}, u32[]{:S(2)}, u32[]{:S(2)}) collective-permute-start(bf16[512,128]{1,0:T(8,128)(2,1)S(1)} %get-tuple-element.48.value_ref), channel_id=1, source_target_pairs={{0,8},{1,9},{2,10},{3,11},{4,12},{5,13},{6,14},{7,15}} | collective-permute-start | bytes 393224 | tf_op jit(solution)/shard_map/ppermute | solution.py:223
  117.9 6.3 %collective-permute-start.34 = (bf16[512,128]{1,0:T(8,128)(2,1)S(1)}, bf16[512,128]{1,0:T(8,128)(2,1)S(1)}, u32[]{:S(2)}, u32[]{:S(2)}) collective-permute-start(bf16[512,128]{1,0:T(8,128)(2,1)S(1)} %get-tuple-element.61.value_ref), channel_id=1, source_target_pairs={{8,24},{9,25},{10,26},{11,27},{12,28},{13,29},{14,30},{15,31}} | collective-permute-start | bytes 393224 | tf_op jit(solution)/shard_map/ppermute | solution.py:223
  119.6 7.1 %collective-permute-start.33 = (bf16[512,128]{1,0:T(8,128)(2,1)S(1)}, bf16[512,128]{1,0:T(8,128)(2,1)S(1)}, u32[]{:S(2)}, u32[]{:S(2)}) collective-permute-start(bf16[512,128]{1,0:T(8,128)(2,1)S(1)} %get-tuple-element.61.value_ref), channel_id=1, source_target_pairs={{8,0},{9,1},{10,2},{11,3},{12,4},{13,5},{14,6},{15,7}} | collective-permute-start | bytes 393224 | tf_op jit(solution)/shard_map/ppermute | solution.py:223
  120.9 5.8 %collective-permute-start.32 = (bf16[512,128]{1,0:T(8,128)(2,1)S(1)}, bf16[512,128]{1,0:T(8,128)(2,1)S(1)}, u32[]{:S(2)}, u32[]{:S(2)}) collective-permute-start(bf16[512,128]{1,0:T(8,128)(2,1)S(1)} %get-tuple-element.61.value_ref), channel_id=1, source_target_pairs={{8,16},{9,17},{10,18},{11,19},{12,20},{13,21},{14,22},{15,23}} | collective-permute-start | bytes 393224 | tf_op jit(solution)/shard_map/ppermute | solution.py:223
  121.5 8.4 %collective-permute-start.25 = (bf16[512,128]{1,0:T(8,128)(2,1)S(1)}, bf16[512,128]{1,0:T(8,128)(2,1)S(1)}, u32[]{:S(2)}, u32[]{:S(2)}) collective-permute-start(bf16[512,128]{1,0:T(8,128)(2,1)S(1)} %picked.2.rest_0_), channel_id=1, source_target_pairs={{0,64},{1,65},{2,66},{3,67},{4,68},{5,69},{6,70},{7,71},{8,72},{9,... | collective-permute-start | bytes 393224 | tf_op jit(solution)/shard_map/ppermute | solution.py:223
  122.9 8.4 %collective-permute-start.24 = (bf16[512,128]{1,0:T(8,128)(2,1)S(1)}, bf16[512,128]{1,0:T(8,128)(2,1)S(1)}, u32[]{:S(2)}, u32[]{:S(2)}) collective-permute-start(bf16[512,128]{1,0:T(8,128)(2,1)S(1)} %picked.2.rest_0_), channel_id=1, source_target_pairs={{0,96},{1,97},{2,98},{3,99},{4,100},{5,101},{6,102},{7,103},{8,104... | collective-permute-start | bytes 393224 | tf_op jit(solution)/shard_map/ppermute | solution.py:223
  124.2 7.1 %collective-permute-start.23 = (bf16[512,128]{1,0:T(8,128)(2,1)S(1)}, bf16[512,128]{1,0:T(8,128)(2,1)S(1)}, u32[]{:S(2)}, u32[]{:S(2)}) collective-permute-start(bf16[512,128]{1,0:T(8,128)(2,1)S(1)} %picked.2.rest_0_), channel_id=1, source_target_pairs={{0,32},{1,33},{2,34},{3,35},{4,36},{5,37},{6,38},{7,39},{8,40},{9,... | collective-permute-start | bytes 393224 | tf_op jit(solution)/shard_map/ppermute | solution.py:223
  127.3 5.4 %collective-permute-start.37 = (bf16[512,128]{1,0:T(8,128)(2,1)S(1)}, bf16[512,128]{1,0:T(8,128)(2,1)S(1)}, u32[]{:S(2)}, u32[]{:S(2)}) collective-permute-start(bf16[512,128]{1,0:T(8,128)(2,1)S(1)} %picked.3.rest_0_), channel_id=1, source_target_pairs={{0,64},{1,65},{2,66},{3,67},{4,68},{5,69},{6,70},{7,71},{8,72},{9,... | collective-permute-start | bytes 393224 | tf_op jit(solution)/shard_map/ppermute | solution.py:223
  128.6 4.1 %collective-permute-start.36 = (bf16[512,128]{1,0:T(8,128)(2,1)S(1)}, bf16[512,128]{1,0:T(8,128)(2,1)S(1)}, u32[]{:S(2)}, u32[]{:S(2)}) collective-permute-start(bf16[512,128]{1,0:T(8,128)(2,1)S(1)} %picked.3.rest_0_), channel_id=1, source_target_pairs={{0,96},{1,97},{2,98},{3,99},{4,100},{5,101},{6,102},{7,103},{8,104... | collective-permute-start | bytes 393224 | tf_op jit(solution)/shard_map/ppermute | solution.py:223
  129.9 4.1 %collective-permute-start.35 = (bf16[512,128]{1,0:T(8,128)(2,1)S(1)}, bf16[512,128]{1,0:T(8,128)(2,1)S(1)}, u32[]{:S(2)}, u32[]{:S(2)}) collective-permute-start(bf16[512,128]{1,0:T(8,128)(2,1)S(1)} %picked.3.rest_0_), channel_id=1, source_target_pairs={{0,32},{1,33},{2,34},{3,35},{4,36},{5,37},{6,38},{7,39},{8,40},{9,... | collective-permute-start | bytes 393224 | tf_op jit(solution)/shard_map/ppermute | solution.py:223
  (8 other events, 64.3 us)

commit v12 on v11

--- a/solution.py
+++ b/solution.py
@@ -340,7 +340,8 @@
     def onward(u, value, packed):
         return [to_column(packed, u - 1, u)] + [to_column(value, u - 1, u, k) for k in (1, 2, 3)]
 
-    x1, packed, kept = solve(0, [first] + [to_row(first, k) for k in (1, 2, 3)], [], ("value", "packed", "kept"))
+    after_one, before_one, across = (to_row(first, k) for k in (1, 3, 2))
+    x1, packed, kept = solve(0, [first, after_one, across, before_one], [], ("value", "packed", "kept"))
     pieces = onward(1, x1, packed)
     pieces, kept = after((pieces, kept))
     carried = products(0, (3, 4), kept)

time: 141 us -> 141 us (level)
  Pallas kernels: 21.3 us -> 23.3 us
  blocking collectives: 32.3 us -> 30.4 us
    pallas_call x17, Pallas kernels: 21.3 us -> 23.3 us  [call(): pl.pallas_call(body, out_shape=outs, in_specs=in_specs, out_specs=out_spe...]
    all_to_all x2, blocking collectives: 32.3 us -> 30.4 us  [over_plane(): lax.all_to_all(value, 'col', 0, 0, axis_index_groups=groups, tiled=True)]
    ppermute x26, waiting for transfers between devices: 14.6 us -> 13.1 us  [send(): return lax.ppermute(value, AXES, pairs)]
  transfers between devices with their start and end apart: 39 -> 39, of which waited for: 16 -> 16; matrix products, arithmetic and copies ran while one was open for 1% -> 1% of each run, Pallas kernels for 5% -> 6%
where the time goes in v12:
time: 141 us; the launch traced here: 138 us
  starting transfers between devices  53.6 us (38%)
  blocking collectives  30.4 us (22%)
  waiting for transfers between devices  28.2 us (20%)
  Pallas kernels  23.3 us (17%)
    ppermute x26, starting transfers between devices, send(): return lax.ppermute(value, AXES, pairs)  35.9 us
    all_to_all x2, blocking collectives, over_plane(): lax.all_to_all(value, 'col', 0, 0, axis_index_groups=groups, tiled=True)  30.4 us
    pallas_call x17, Pallas kernels, call(): pl.pallas_call(body, out_shape=outs, in_specs=in_specs, out_specs=out_spe...  23.3 us
    ppermute x26, waiting for transfers between devices, send(): return lax.ppermute(value, AXES, pairs)  13.1 us
    ppermute x9, waiting for transfers between devices, to_row(): return lax.ppermute(value, 'row', [(z, (z + step) % NZ) for z in range(NZ)])  12.6 us
    ppermute x9, starting transfers between devices, to_row(): return lax.ppermute(value, 'row', [(z, (z + step) % NZ) for z in range(NZ)])  11.7 us
    ppermute x4, starting transfers between devices, other_core(): return lax.ppermute(value, 'col', [(c, c ^ 1) for c in range(NX * NY * 2)])  6.03 us
  transfers between devices with their start and end apart: 39, of which 16 were waited for; matrix products, arithmetic and copies ran while one was open for 1% of the time, Pallas kernels for 6%

profile of v12, /device:TPU:1, one launch (start us, length us, event | category | flops | bytes accessed | tf_op | source)
XLA Modules:
  0.0 138.3 jit_solution(7489133865836629536)
XLA Ops:
  0.6 2.7 %base_solve.1 = (f32[2,512,128]{2,1,0:T(8,128)}, bf16[512,128]{1,0:T(8,128)(2,1)S(1)}, bf16[512,128]{1,0:T(8,128)(2,1)S(1)}) custom-call(bf16[2,512,512]{2,1,0:T(8,128)(2,1)} %inverse_ref.1, f32[2,512,128]{2,1,0:T(8,128)} %rhs_ref.1), custom_call_target="tpu_custom_call" | custom-call | flops 134217728 | bytes 1835008 | tf_op jit(solution)/shard_map/base_solve/pallas_call | solution.py:32
  3.3 2.5 %collective-permute-start = (bf16[512,128]{1,0:T(8,128)(2,1)S(1)}, bf16[512,128]{1,0:T(8,128)(2,1)S(1)}, u32[]{:S(2)}, u32[]{:S(2)}) collective-permute-start(bf16[512,128]{1,0:T(8,128)(2,1)S(1)} %get-tuple-element.33.rest_0_), channel_id=1, source_target_pairs={{0,1},{1,2},{2,3},{3,0},{4,5},{5,6},{6,7},{7,4},{8,9},{9,10},{10,1... | collective-permute-start | bytes 393224 | tf_op jit(solution)/shard_map/ppermute | solution.py:231
  5.9 2.2 %collective-permute-start.3 = (bf16[512,128]{1,0:T(8,128)(2,1)S(1)}, bf16[512,128]{1,0:T(8,128)(2,1)S(1)}, u32[]{:S(2)}, u32[]{:S(2)}) collective-permute-start(bf16[512,128]{1,0:T(8,128)(2,1)S(1)} %get-tuple-element.34.rest_1_), channel_id=1, source_target_pairs={{0,3},{1,0},{2,1},{3,2},{4,7},{5,4},{6,5},{7,6},{8,11},{9,8},{10,9... | collective-permute-start | bytes 393224 | tf_op jit(solution)/shard_map/ppermute | solution.py:231
  8.1 1.4 %collective-permute-start.5 = (bf16[512,128]{1,0:T(8,128)(2,1)S(1)}, bf16[512,128]{1,0:T(8,128)(2,1)S(1)}, u32[]{:S(2)}, u32[]{:S(2)}) collective-permute-start(bf16[512,128]{1,0:T(8,128)(2,1)S(1)} %get-tuple-element.33.rest_0_), channel_id=1, source_target_pairs={{0,3},{1,0},{2,1},{3,2},{4,7},{5,4},{6,5},{7,6},{8,11},{9,8},{10,9... | collective-permute-start | bytes 393224 | tf_op jit(solution)/shard_map/ppermute | solution.py:231
  9.6 1.6 %collective-permute-done.rest_2_ = bf16[512,128]{1,0:T(8,128)(2,1)S(1)} collective-permute-done((bf16[512,128]{1,0:T(8,128)(2,1)S(1)}, bf16[512,128]{1,0:T(8,128)(2,1)S(1)}, u32[]{:S(2)}, u32[]{:S(2)}) %collective-permute-start) | collective-permute-done | bytes 131104 | tf_op jit(solution)/shard_map/ppermute | solution.py:231
  11.2 2.7 %collective-permute-start.4 = (bf16[512,128]{1,0:T(8,128)(2,1)S(1)}, bf16[512,128]{1,0:T(8,128)(2,1)S(1)}, u32[]{:S(2)}, u32[]{:S(2)}) collective-permute-start(bf16[512,128]{1,0:T(8,128)(2,1)S(1)} %collective-permute-done.3.rest_7_), channel_id=1, source_target_pairs={{0,3},{1,0},{2,1},{3,2},{4,7},{5,4},{6,5},{7,6},{8,11},{9,8},{10,9... | collective-permute-start | bytes 393224 | tf_op jit(solution)/shard_map/ppermute | solution.py:231
  15.4 2.3 %collective-permute-done.2.rest_4_ = bf16[512,128]{1,0:T(8,128)(2,1)S(1)} collective-permute-done((bf16[512,128]{1,0:T(8,128)(2,1)S(1)}, bf16[512,128]{1,0:T(8,128)(2,1)S(1)}, u32[]{:S(2)}, u32[]{:S(2)}) %collective-permute-start.2) | collective-permute-done | bytes 131104 | tf_op jit(solution)/shard_map/ppermute | solution.py:231
  17.7 4.8 %base_products.1 = (f32[16,80,128]{2,1,0:T(8,128)S(1)}, bf16[16,80,128]{2,1,0:T(8,128)(2,1)S(1)}, bf16[30,512,512]{2,1,0:T(8,128)(2,1)S(1)}, bf16[5,512,512]{2,1,0:T(8,128)(2,1)S(1)}) custom-call(s32[6,7]{1,0:T(8,128)S(1)} %pad_add_fusion.table, bf16[5,6,512,512]{3,2,1,0:T(8,128)(2,1)} %factor_ref.1, bf16[5,512,512]{2,1,0:T(8,128)(2,1)} %bitcast.12, ...), custom_call_target="tpu_custom_call" | custom-call | flops 1006632960 | bytes 15728640 | tf_op jit(solution)/shard_map/base_products/pallas_call | solution.py:32
  24.8 19.7 %all_to_all.10.in_ref = bf16[16,80,128]{2,1,0:T(8,128)(2,1)S(1)} all-to-all(bf16[16,80,128]{2,1,0:T(8,128)(2,1)S(1)} %pair_sums.1), channel_id=1, replica_groups={{0,8,16,24,32,40,48,56,64,72,80,88,96,104,112,120},{4,12,20,28,36,44,52..., dimensions={0} | all-to-all | bytes 655360 | tf_op jit(solution)/shard_map/all_to_all | solution.py:240
  44.5 10.7 %all_to_all.11.half_ref = bf16[16,80,128]{2,1,0:T(8,128)(2,1)S(1)} all-to-all(bf16[16,80,128]{2,1,0:T(8,128)(2,1)S(1)} %sum_shares.1), channel_id=1, replica_groups={{0,8,16,24,32,40,48,56,64,72,80,88,96,104,112,120},{4,12,20,28,36,44,52..., dimensions={0} | all-to-all | bytes 655360 | tf_op jit(solution)/shard_map/all_to_all | solution.py:240
  55.2 2.7 %collective-permute-start.7 = (bf16[16,80,128]{2,1,0:T(8,128)(2,1)S(1)}, bf16[16,80,128]{2,1,0:T(8,128)(2,1)S(1)}, u32[]{:S(2)}, u32[]{:S(2)}) collective-permute-start(bf16[16,80,128]{2,1,0:T(8,128)(2,1)S(1)} %all_to_all.11.half_ref), channel_id=1, source_target_pairs={{0,4},{4,0},{8,12},{12,8},{16,20},{20,16},{24,28},{28,24},{32,36},... | collective-permute-start | bytes 983048 | tf_op jit(solution)/shard_map/ppermute | solution.py:235
  60.2 1.7 %collective-permute-start.10 = (bf16[512,128]{1,0:T(8,128)(2,1)S(1)}, bf16[512,128]{1,0:T(8,128)(2,1)S(1)}, u32[]{:S(2)}, u32[]{:S(2)}) collective-permute-start(bf16[512,128]{1,0:T(8,128)(2,1)S(1)} %get-tuple-element.38.rest_0_), channel_id=1, source_target_pairs={{0,3},{1,0},{2,1},{3,2},{4,7},{5,4},{6,5},{7,6},{8,11},{9,8},{10,9... | collective-permute-start | bytes 393224 | tf_op jit(solution)/shard_map/ppermute | solution.py:231
  63.0 2.0 %collective-permute-done.10.rest_3_ = bf16[512,128]{1,0:T(8,128)(2,1)S(1)} collective-permute-done((bf16[512,128]{1,0:T(8,128)(2,1)S(1)}, bf16[512,128]{1,0:T(8,128)(2,1)S(1)}, u32[]{:S(2)}, u32[]{:S(2)}) %collective-permute-start.10) | collective-permute-done | bytes 131104 | tf_op jit(solution)/shard_map/ppermute | solution.py:231
  65.0 2.8 %collective-permute-done.9.rest_2_ = bf16[512,128]{1,0:T(8,128)(2,1)S(1)} collective-permute-done((bf16[512,128]{1,0:T(8,128)(2,1)S(1)}, bf16[512,128]{1,0:T(8,128)(2,1)S(1)}, u32[]{:S(2)}, u32[]{:S(2)}) %collective-permute-start.9) | collective-permute-done | bytes 131104 | tf_op jit(solution)/shard_map/ppermute | solution.py:231
  67.8 3.8 %collective-permute-done.8.rest_1_ = bf16[512,128]{1,0:T(8,128)(2,1)S(1)} collective-permute-done((bf16[512,128]{1,0:T(8,128)(2,1)S(1)}, bf16[512,128]{1,0:T(8,128)(2,1)S(1)}, u32[]{:S(2)}, u32[]{:S(2)}) %collective-permute-start.8) | collective-permute-done | bytes 131104 | tf_op jit(solution)/shard_map/ppermute | solution.py:231
  78.1 2.4 %collective-permute-done.14.rest_3_ = bf16[512,128]{1,0:T(8,128)(2,1)S(1)} collective-permute-done((bf16[512,128]{1,0:T(8,128)(2,1)S(1)}, bf16[512,128]{1,0:T(8,128)(2,1)S(1)}, u32[]{:S(2)}, u32[]{:S(2)}) %collective-permute-start.14) | collective-permute-done | bytes 131104 | tf_op jit(solution)/shard_map/ppermute | solution.py:223
  80.5 2.8 %collective-permute-done.13.rest_2_ = bf16[512,128]{1,0:T(8,128)(2,1)S(1)} collective-permute-done((bf16[512,128]{1,0:T(8,128)(2,1)S(1)}, bf16[512,128]{1,0:T(8,128)(2,1)S(1)}, u32[]{:S(2)}, u32[]{:S(2)}) %collective-permute-start.13) | collective-permute-done | bytes 131104 | tf_op jit(solution)/shard_map/ppermute | solution.py:223
  83.4 1.4 collective-permute-done.12.rest_1_
  84.7 2.3 %solve_2.1 = (bf16[512,128]{1,0:T(8,128)(2,1)S(1)}, bf16[2,512,128]{2,1,0:T(8,128)(2,1)S(1)}, bf16[512,128]{1,0:T(8,128)(2,1)S(1)}, bf16[4,512,128]{2,1,0:T(8,128)(2,1)S(1)}) custom-call(s32[6,7]{1,0:T(8,128)S(1)} %pad_add_fusion.table, bf16[30,512,512]{2,1,0:T(8,128)(2,1)S(1)} %get-tuple-element.39.held_ref, ...), custom_call_target="tpu_custom_call" | custom-call | flops 335544320 | tf_op jit(solution)/shard_map/solve_2/pallas_call | solution.py:32
  87.0 1.3 collective-permute-start.18
  89.8 1.3 collective-permute-start.21
  91.1 1.3 collective-permute-start.20
  94.5 1.4 %collective-permute-done.20.rest_2_ = bf16[512,128]{1,0:T(8,128)(2,1)S(1)} collective-permute-done((bf16[512,128]{1,0:T(8,128)(2,1)S(1)}, bf16[512,128]{1,0:T(8,128)(2,1)S(1)}, u32[]{:S(2)}, u32[]{:S(2)}) %collective-permute-start.20) | collective-permute-done | bytes 131104 | tf_op jit(solution)/shard_map/ppermute | solution.py:223
  95.9 1.7 %collective-permute-done.19.rest_1_ = bf16[512,128]{1,0:T(8,128)(2,1)S(1)} collective-permute-done((bf16[512,128]{1,0:T(8,128)(2,1)S(1)}, bf16[512,128]{1,0:T(8,128)(2,1)S(1)}, u32[]{:S(2)}, u32[]{:S(2)}) %collective-permute-start.19) | collective-permute-done | bytes 131104 | tf_op jit(solution)/shard_map/ppermute | solution.py:223
  99.4 1.8 %later_1.1 = bf16[1,512,128]{2,1,0:T(8,128)(2,1)S(1)} custom-call(s32[6,7]{1,0:T(8,128)S(1)} %pad_add_fusion.table, bf16[30,512,512]{2,1,0:T(8,128)(2,1)S(1)} %get-tuple-element.39.held_ref, bf16[4,512,128]{2,1,0:T(8,128)(2,1)S(1)} %get-tuple-element.60.operands), custom_call_target="tpu_custom_call" | custom-call | flops 268435456 | tf_op jit(solution)/shard_map/later_1/pallas_call | solution.py:32
  101.3 1.3 collective-permute-start.31
  104.8 1.3 collective-permute-start.17
  107.5 7.6 %collective-permute-start.15 = (bf16[512,128]{1,0:T(8,128)(2,1)S(1)}, bf16[512,128]{1,0:T(8,128)(2,1)S(1)}, u32[]{:S(2)}, u32[]{:S(2)}) collective-permute-start(bf16[512,128]{1,0:T(8,128)(2,1)S(1)} %get-tuple-element.48.value_ref), channel_id=1, source_target_pairs={{0,8},{1,9},{2,10},{3,11},{4,12},{5,13},{6,14},{7,15}} | collective-permute-start | bytes 393224 | tf_op jit(solution)/shard_map/ppermute | solution.py:223
  115.2 1.7 %solve_4.1 = (bf16[512,128]{1,0:T(8,128)(2,1)}, bf16[512,128]{1,0:T(8,128)(2,1)S(1)}) custom-call(s32[6,7]{1,0:T(8,128)S(1)} %pad_add_fusion.table, bf16[30,512,512]{2,1,0:T(8,128)(2,1)S(1)} %get-tuple-element.39.held_ref, f32[4,512,128]{2,1,0:T(8,128)S(1)} %get-tuple-element.40.ahead_ref, bf16[5,512,512]{2,1,0:T(8,128)(2,1)S(1)} %get-tuple-element.37.inverse_ref, ...), custom_call_target="tpu_custom_call" | custom-call | flops 335544320 | tf_op jit(solution)/shard_map/solve_4/pallas_call | solution.py:32
  133.7 1.4 collective-permute-start.38
  135.1 1.6 %output_first.1.out_before = f32[5,512,128]{2,1,0:T(8,128)} custom-call(s32[6,7]{1,0:T(8,128)S(1)} %pad_add_fusion.table, bf16[512,128]{1,0:T(8,128)(2,1)S(1)} %get-tuple-element.38.rest_0_, bf16[1,512,128]{2,1,0:T(8,128)(2,1)S(1)} %merged_first.1.rest_1_, bf16[1,512,128]{2,1,0:T(8,128)(2,1)S(1)} %collective-permute-done.26.rest_2_), custom_call_target="tpu_custom_call" | custom-call | tf_op jit(solution)/shard_map/output_first/pallas_call | solution.py:32
  136.7 1.5 %output_rest.1 = f32[5,512,128]{2,1,0:T(8,128)} custom-call(s32[6,7]{1,0:T(8,128)S(1)} %pad_add_fusion.table, f32[5,512,128]{2,1,0:T(8,128)} %output_first.1.out_before, bf16[1,512,128]{2,1,0:T(8,128)(2,1)S(1)} %merged_rest.1.mine_ref, bf16[1,512,128]{2,1,0:T(8,128)(2,1)S(1)} %collective-permute-done.38.other_ref), custom_call_target="tpu_custom_call", output_to_operand_aliasing={{}: (1, {})} | custom-call | tf_op jit(solution)/shard_map/output_rest/pallas_call | solution.py:32
  (71 shorter events, 39.3 us)
Async XLA Ops:
  3.3 7.9 %collective-permute-start = (bf16[512,128]{1,0:T(8,128)(2,1)S(1)}, bf16[512,128]{1,0:T(8,128)(2,1)S(1)}, u32[]{:S(2)}, u32[]{:S(2)}) collective-permute-start(bf16[512,128]{1,0:T(8,128)(2,1)S(1)} %get-tuple-element.33.rest_0_), channel_id=1, source_target_pairs={{0,1},{1,2},{2,3},{3,0},{4,5},{5,6},{6,7},{7,4},{8,9},{9,10},{10,1... | collective-permute-start | bytes 393224 | tf_op jit(solution)/shard_map/ppermute | solution.py:231
  5.9 5.3 %collective-permute-start.3 = (bf16[512,128]{1,0:T(8,128)(2,1)S(1)}, bf16[512,128]{1,0:T(8,128)(2,1)S(1)}, u32[]{:S(2)}, u32[]{:S(2)}) collective-permute-start(bf16[512,128]{1,0:T(8,128)(2,1)S(1)} %get-tuple-element.34.rest_1_), channel_id=1, source_target_pairs={{0,3},{1,0},{2,1},{3,2},{4,7},{5,4},{6,5},{7,6},{8,11},{9,8},{10,9... | collective-permute-start | bytes 393224 | tf_op jit(solution)/shard_map/ppermute | solution.py:231
  8.1 7.3 %collective-permute-start.5 = (bf16[512,128]{1,0:T(8,128)(2,1)S(1)}, bf16[512,128]{1,0:T(8,128)(2,1)S(1)}, u32[]{:S(2)}, u32[]{:S(2)}) collective-permute-start(bf16[512,128]{1,0:T(8,128)(2,1)S(1)} %get-tuple-element.33.rest_0_), channel_id=1, source_target_pairs={{0,3},{1,0},{2,1},{3,2},{4,7},{5,4},{6,5},{7,6},{8,11},{9,8},{10,9... | collective-permute-start | bytes 393224 | tf_op jit(solution)/shard_map/ppermute | solution.py:231
  9.5 6.0 %collective-permute-start.1 = (bf16[512,128]{1,0:T(8,128)(2,1)S(1)}, bf16[512,128]{1,0:T(8,128)(2,1)S(1)}, u32[]{:S(2)}, u32[]{:S(2)}) collective-permute-start(bf16[512,128]{1,0:T(8,128)(2,1)S(1)} %get-tuple-element.34.rest_1_), channel_id=1, source_target_pairs={{0,1},{1,2},{2,3},{3,0},{4,5},{5,6},{6,7},{7,4},{8,9},{9,10},{10,1... | collective-permute-start | bytes 393224 | tf_op jit(solution)/shard_map/ppermute | solution.py:231
  11.2 6.5 %collective-permute-start.2 = (bf16[512,128]{1,0:T(8,128)(2,1)S(1)}, bf16[512,128]{1,0:T(8,128)(2,1)S(1)}, u32[]{:S(2)}, u32[]{:S(2)}) collective-permute-start(bf16[512,128]{1,0:T(8,128)(2,1)S(1)} %collective-permute-done.rest_2_), channel_id=1, source_target_pairs={{0,1},{1,2},{2,3},{3,0},{4,5},{5,6},{6,7},{7,4},{8,9},{9,10},{10,1... | collective-permute-start | bytes 393224 | tf_op jit(solution)/shard_map/ppermute | solution.py:231
  11.2 6.5 %collective-permute-start.4 = (bf16[512,128]{1,0:T(8,128)(2,1)S(1)}, bf16[512,128]{1,0:T(8,128)(2,1)S(1)}, u32[]{:S(2)}, u32[]{:S(2)}) collective-permute-start(bf16[512,128]{1,0:T(8,128)(2,1)S(1)} %collective-permute-done.3.rest_7_), channel_id=1, source_target_pairs={{0,3},{1,0},{2,1},{3,2},{4,7},{5,4},{6,5},{7,6},{8,11},{9,8},{10,9... | collective-permute-start | bytes 393224 | tf_op jit(solution)/shard_map/ppermute | solution.py:231
  60.2 4.8 %collective-permute-start.10 = (bf16[512,128]{1,0:T(8,128)(2,1)S(1)}, bf16[512,128]{1,0:T(8,128)(2,1)S(1)}, u32[]{:S(2)}, u32[]{:S(2)}) collective-permute-start(bf16[512,128]{1,0:T(8,128)(2,1)S(1)} %get-tuple-element.38.rest_0_), channel_id=1, source_target_pairs={{0,3},{1,0},{2,1},{3,2},{4,7},{5,4},{6,5},{7,6},{8,11},{9,8},{10,9... | collective-permute-start | bytes 393224 | tf_op jit(solution)/shard_map/ppermute | solution.py:231
  61.9 5.9 %collective-permute-start.9 = (bf16[512,128]{1,0:T(8,128)(2,1)S(1)}, bf16[512,128]{1,0:T(8,128)(2,1)S(1)}, u32[]{:S(2)}, u32[]{:S(2)}) collective-permute-start(bf16[512,128]{1,0:T(8,128)(2,1)S(1)} %get-tuple-element.38.rest_0_), channel_id=1, source_target_pairs={{0,2},{1,3},{2,0},{3,1},{4,6},{5,7},{6,4},{7,5},{8,10},{9,11},{10,... | collective-permute-start | bytes 393224 | tf_op jit(solution)/shard_map/ppermute | solution.py:231
  62.2 9.4 %collective-permute-start.8 = (bf16[512,128]{1,0:T(8,128)(2,1)S(1)}, bf16[512,128]{1,0:T(8,128)(2,1)S(1)}, u32[]{:S(2)}, u32[]{:S(2)}) collective-permute-start(bf16[512,128]{1,0:T(8,128)(2,1)S(1)} %get-tuple-element.38.rest_0_), channel_id=1, source_target_pairs={{0,1},{1,2},{2,3},{3,0},{4,5},{5,6},{6,7},{7,4},{8,9},{9,10},{10,1... | collective-permute-start | bytes 393224 | tf_op jit(solution)/shard_map/ppermute | solution.py:231
  72.9 11.8 %collective-permute-start.11 = (bf16[2,512,128]{2,1,0:T(8,128)(2,1)S(1)}, bf16[2,512,128]{2,1,0:T(8,128)(2,1)S(1)}, u32[]{:S(2)}, u32[]{:S(2)}) collective-permute-start(bf16[2,512,128]{2,1,0:T(8,128)(2,1)S(1)} %get-tuple-element.41), channel_id=1, source_target_pairs={{0,4},{1,5},{2,6},{3,7}} | collective-permute-start | bytes 786440 | tf_op jit(solution)/shard_map/ppermute | solution.py:223
  74.2 6.3 %collective-permute-start.14 = (bf16[512,128]{1,0:T(8,128)(2,1)S(1)}, bf16[512,128]{1,0:T(8,128)(2,1)S(1)}, u32[]{:S(2)}, u32[]{:S(2)}) collective-permute-start(bf16[512,128]{1,0:T(8,128)(2,1)S(1)} %get-tuple-element.42.rest_4_), channel_id=1, source_target_pairs={{0,7},{1,4},{2,5},{3,6}} | collective-permute-start | bytes 393224 | tf_op jit(solution)/shard_map/ppermute | solution.py:223
  75.5 7.8 %collective-permute-start.13 = (bf16[512,128]{1,0:T(8,128)(2,1)S(1)}, bf16[512,128]{1,0:T(8,128)(2,1)S(1)}, u32[]{:S(2)}, u32[]{:S(2)}) collective-permute-start(bf16[512,128]{1,0:T(8,128)(2,1)S(1)} %get-tuple-element.42.rest_4_), channel_id=1, source_target_pairs={{0,6},{1,7},{2,4},{3,5}} | collective-permute-start | bytes 393224 | tf_op jit(solution)/shard_map/ppermute | solution.py:223
  76.8 7.9 %collective-permute-start.12 = (bf16[512,128]{1,0:T(8,128)(2,1)S(1)}, bf16[512,128]{1,0:T(8,128)(2,1)S(1)}, u32[]{:S(2)}, u32[]{:S(2)}) collective-permute-start(bf16[512,128]{1,0:T(8,128)(2,1)S(1)} %get-tuple-element.42.rest_4_), channel_id=1, source_target_pairs={{0,5},{1,6},{2,7},{3,4}} | collective-permute-start | bytes 393224 | tf_op jit(solution)/shard_map/ppermute | solution.py:223
  87.0 10.6 %collective-permute-start.18 = (bf16[2,512,128]{2,1,0:T(8,128)(2,1)S(1)}, bf16[2,512,128]{2,1,0:T(8,128)(2,1)S(1)}, u32[]{:S(2)}, u32[]{:S(2)}) collective-permute-start(bf16[2,512,128]{2,1,0:T(8,128)(2,1)S(1)} %get-tuple-element.49), channel_id=1, source_target_pairs={{4,8},{5,9},{6,10},{7,11}} | collective-permute-start | bytes 786440 | tf_op jit(solution)/shard_map/ppermute | solution.py:223
  89.1 8.5 %collective-permute-start.22 = (bf16[2,512,128]{2,1,0:T(8,128)(2,1)S(1)}, bf16[2,512,128]{2,1,0:T(8,128)(2,1)S(1)}, u32[]{:S(2)}, u32[]{:S(2)}) collective-permute-start(bf16[2,512,128]{2,1,0:T(8,128)(2,1)S(1)} %later_0.1), channel_id=1, source_target_pairs={{0,8},{1,9},{2,10},{3,11}} | collective-permute-start | bytes 786440 | tf_op jit(solution)/shard_map/ppermute | solution.py:223
  89.8 4.7 %collective-permute-start.21 = (bf16[512,128]{1,0:T(8,128)(2,1)S(1)}, bf16[512,128]{1,0:T(8,128)(2,1)S(1)}, u32[]{:S(2)}, u32[]{:S(2)}) collective-permute-start(bf16[512,128]{1,0:T(8,128)(2,1)S(1)} %get-tuple-element.50), channel_id=1, source_target_pairs={{4,11},{5,8},{6,9},{7,10}} | collective-permute-start | bytes 393224 | tf_op jit(solution)/shard_map/ppermute | solution.py:223
  91.1 4.8 %collective-permute-start.20 = (bf16[512,128]{1,0:T(8,128)(2,1)S(1)}, bf16[512,128]{1,0:T(8,128)(2,1)S(1)}, u32[]{:S(2)}, u32[]{:S(2)}) collective-permute-start(bf16[512,128]{1,0:T(8,128)(2,1)S(1)} %get-tuple-element.50), channel_id=1, source_target_pairs={{4,10},{5,11},{6,8},{7,9}} | collective-permute-start | bytes 393224 | tf_op jit(solution)/shard_map/ppermute | solution.py:223
  92.4 5.2 %collective-permute-start.19 = (bf16[512,128]{1,0:T(8,128)(2,1)S(1)}, bf16[512,128]{1,0:T(8,128)(2,1)S(1)}, u32[]{:S(2)}, u32[]{:S(2)}) collective-permute-start(bf16[512,128]{1,0:T(8,128)(2,1)S(1)} %get-tuple-element.50), channel_id=1, source_target_pairs={{4,9},{5,10},{6,11},{7,8}} | collective-permute-start | bytes 393224 | tf_op jit(solution)/shard_map/ppermute | solution.py:223
  98.7 16.4 %collective-permute-start.27 = (bf16[2,512,128]{2,1,0:T(8,128)(2,1)S(1)}, bf16[2,512,128]{2,1,0:T(8,128)(2,1)S(1)}, u32[]{:S(2)}, u32[]{:S(2)}) collective-permute-start(bf16[2,512,128]{2,1,0:T(8,128)(2,1)S(1)} %get-tuple-element.59), channel_id=1, source_target_pairs={{8,12},{9,13},{10,14},{11,15}} | collective-permute-start | bytes 786440 | tf_op jit(solution)/shard_map/ppermute | solution.py:223
  104.2 11.0 %collective-permute-start.28 = (bf16[512,128]{1,0:T(8,128)(2,1)S(1)}, bf16[512,128]{1,0:T(8,128)(2,1)S(1)}, u32[]{:S(2)}, u32[]{:S(2)}) collective-permute-start(bf16[512,128]{1,0:T(8,128)(2,1)S(1)} %get-tuple-element.57.rest_4_), channel_id=1, source_target_pairs={{8,13},{9,14},{10,15},{11,12}} | collective-permute-start | bytes 393224 | tf_op jit(solution)/shard_map/ppermute | solution.py:223
  104.8 12.7 %collective-permute-start.17 = (bf16[512,128]{1,0:T(8,128)(2,1)S(1)}, bf16[512,128]{1,0:T(8,128)(2,1)S(1)}, u32[]{:S(2)}, u32[]{:S(2)}) collective-permute-start(bf16[512,128]{1,0:T(8,128)(2,1)S(1)} %get-tuple-element.48.value_ref), channel_id=1, source_target_pairs={{0,16},{1,17},{2,18},{3,19},{4,20},{5,21},{6,22},{7,23}} | collective-permute-start | bytes 393224 | tf_op jit(solution)/shard_map/ppermute | solution.py:223
  106.2 11.4 %collective-permute-start.16 = (bf16[512,128]{1,0:T(8,128)(2,1)S(1)}, bf16[512,128]{1,0:T(8,128)(2,1)S(1)}, u32[]{:S(2)}, u32[]{:S(2)}) collective-permute-start(bf16[512,128]{1,0:T(8,128)(2,1)S(1)} %get-tuple-element.48.value_ref), channel_id=1, source_target_pairs={{0,24},{1,25},{2,26},{3,27},{4,28},{5,29},{6,30},{7,31}} | collective-permute-start | bytes 393224 | tf_op jit(solution)/shard_map/ppermute | solution.py:223
  107.5 10.8 %collective-permute-start.15 = (bf16[512,128]{1,0:T(8,128)(2,1)S(1)}, bf16[512,128]{1,0:T(8,128)(2,1)S(1)}, u32[]{:S(2)}, u32[]{:S(2)}) collective-permute-start(bf16[512,128]{1,0:T(8,128)(2,1)S(1)} %get-tuple-element.48.value_ref), channel_id=1, source_target_pairs={{0,8},{1,9},{2,10},{3,11},{4,12},{5,13},{6,14},{7,15}} | collective-permute-start | bytes 393224 | tf_op jit(solution)/shard_map/ppermute | solution.py:223
  116.8 6.7 %collective-permute-start.34 = (bf16[512,128]{1,0:T(8,128)(2,1)S(1)}, bf16[512,128]{1,0:T(8,128)(2,1)S(1)}, u32[]{:S(2)}, u32[]{:S(2)}) collective-permute-start(bf16[512,128]{1,0:T(8,128)(2,1)S(1)} %get-tuple-element.61.value_ref), channel_id=1, source_target_pairs={{8,24},{9,25},{10,26},{11,27},{12,28},{13,29},{14,30},{15,31}} | collective-permute-start | bytes 393224 | tf_op jit(solution)/shard_map/ppermute | solution.py:223
  119.0 6.8 %collective-permute-start.33 = (bf16[512,128]{1,0:T(8,128)(2,1)S(1)}, bf16[512,128]{1,0:T(8,128)(2,1)S(1)}, u32[]{:S(2)}, u32[]{:S(2)}) collective-permute-start(bf16[512,128]{1,0:T(8,128)(2,1)S(1)} %get-tuple-element.61.value_ref), channel_id=1, source_target_pairs={{8,0},{9,1},{10,2},{11,3},{12,4},{13,5},{14,6},{15,7}} | collective-permute-start | bytes 393224 | tf_op jit(solution)/shard_map/ppermute | solution.py:223
  120.3 5.5 %collective-permute-start.32 = (bf16[512,128]{1,0:T(8,128)(2,1)S(1)}, bf16[512,128]{1,0:T(8,128)(2,1)S(1)}, u32[]{:S(2)}, u32[]{:S(2)}) collective-permute-start(bf16[512,128]{1,0:T(8,128)(2,1)S(1)} %get-tuple-element.61.value_ref), channel_id=1, source_target_pairs={{8,16},{9,17},{10,18},{11,19},{12,20},{13,21},{14,22},{15,23}} | collective-permute-start | bytes 393224 | tf_op jit(solution)/shard_map/ppermute | solution.py:223
  120.9 8.1 %collective-permute-start.25 = (bf16[512,128]{1,0:T(8,128)(2,1)S(1)}, bf16[512,128]{1,0:T(8,128)(2,1)S(1)}, u32[]{:S(2)}, u32[]{:S(2)}) collective-permute-start(bf16[512,128]{1,0:T(8,128)(2,1)S(1)} %picked.2.rest_0_), channel_id=1, source_target_pairs={{0,64},{1,65},{2,66},{3,67},{4,68},{5,69},{6,70},{7,71},{8,72},{9,... | collective-permute-start | bytes 393224 | tf_op jit(solution)/shard_map/ppermute | solution.py:223
  122.3 8.1 %collective-permute-start.24 = (bf16[512,128]{1,0:T(8,128)(2,1)S(1)}, bf16[512,128]{1,0:T(8,128)(2,1)S(1)}, u32[]{:S(2)}, u32[]{:S(2)}) collective-permute-start(bf16[512,128]{1,0:T(8,128)(2,1)S(1)} %picked.2.rest_0_), channel_id=1, source_target_pairs={{0,96},{1,97},{2,98},{3,99},{4,100},{5,101},{6,102},{7,103},{8,104... | collective-permute-start | bytes 393224 | tf_op jit(solution)/shard_map/ppermute | solution.py:223
  123.6 6.8 %collective-permute-start.23 = (bf16[512,128]{1,0:T(8,128)(2,1)S(1)}, bf16[512,128]{1,0:T(8,128)(2,1)S(1)}, u32[]{:S(2)}, u32[]{:S(2)}) collective-permute-start(bf16[512,128]{1,0:T(8,128)(2,1)S(1)} %picked.2.rest_0_), channel_id=1, source_target_pairs={{0,32},{1,33},{2,34},{3,35},{4,36},{5,37},{6,38},{7,39},{8,40},{9,... | collective-permute-start | bytes 393224 | tf_op jit(solution)/shard_map/ppermute | solution.py:223
  126.4 5.7 %collective-permute-start.37 = (bf16[512,128]{1,0:T(8,128)(2,1)S(1)}, bf16[512,128]{1,0:T(8,128)(2,1)S(1)}, u32[]{:S(2)}, u32[]{:S(2)}) collective-permute-start(bf16[512,128]{1,0:T(8,128)(2,1)S(1)} %picked.3.rest_0_), channel_id=1, source_target_pairs={{0,64},{1,65},{2,66},{3,67},{4,68},{5,69},{6,70},{7,71},{8,72},{9,... | collective-permute-start | bytes 393224 | tf_op jit(solution)/shard_map/ppermute | solution.py:223
  127.7 4.4 %collective-permute-start.36 = (bf16[512,128]{1,0:T(8,128)(2,1)S(1)}, bf16[512,128]{1,0:T(8,128)(2,1)S(1)}, u32[]{:S(2)}, u32[]{:S(2)}) collective-permute-start(bf16[512,128]{1,0:T(8,128)(2,1)S(1)} %picked.3.rest_0_), channel_id=1, source_target_pairs={{0,96},{1,97},{2,98},{3,99},{4,100},{5,101},{6,102},{7,103},{8,104... | collective-permute-start | bytes 393224 | tf_op jit(solution)/shard_map/ppermute | solution.py:223
  131.1 4.1 %collective-permute-start.26 = (bf16[1,512,128]{2,1,0:T(8,128)(2,1)S(1)}, bf16[1,512,128]{2,1,0:T(8,128)(2,1)S(1)}, u32[]{:S(2)}, u32[]{:S(2)}) collective-permute-start(bf16[1,512,128]{2,1,0:T(8,128)(2,1)S(1)} %merged_first.1.rest_1_), channel_id=1, source_target_pairs={{0,4},{4,0},{8,12},{12,8},{16,20},{20,16},{24,28},{28,24},{32,36},... | collective-permute-start | bytes 393224 | tf_op jit(solution)/shard_map/ppermute | solution.py:235
  (8 other events, 60.7 us)
